TPU v7x, 256 devices: a whole 4x4x8 slice. The times are simulated.
256 devices in a mesh: dp: 64 (over x, z, core), mp: 4 (over y).
Axes of the slice: x: 4, y: 4, z: 8, core: 2. Of those that a mesh axis runs over, the one named last changes fastest.
Arguments:
- inputs: bfloat16 [64, 512, 4096], P('dp'), may hold values from -16 to 16
- w_query: bfloat16 [4096, 2048], P(None, 'mp'), may hold values from -0.09375 to 0.09375
- cache_kv: bfloat16 [512, 2, 128, 2048], P('dp', None, None, 'mp'), may hold values from -240 to 240
- nb_owner: int32 [64, 8, 2], P('dp'), may hold values from 0 to 63, as said below
- nb_row: int32 [64, 8, 2], P('dp'), may hold values from 0 to 7
- out_grad: bfloat16 [64, 512, 2048], P('dp', None, 'mp'), may hold values from -6 to 6
Outputs:
- attended: bfloat16 [64, 512, 2048], P('dp', None, 'mp')
- input_grad: bfloat16 [64, 512, 4096], P('dp', None, 'mp')
- query_grad: float32 [4096, 2048], P('dp', 'mp')
Inputs may be any that keep to these rules, and one draw needn't show every extreme that they name: `nb_owner`: within one sequence no owner is named more than 1 times; one owner, the same for every sequence, is named exactly 1 times by each sequence.
All inputs are finite; a program needn't handle non-finite values.
Results may differ from a plain program's by a relative error of at most 0.02.
The roundings to bfloat16 on the way count: a program that leaves them out, or rounds other values in their place, can miss the bound.
Values may be sent and summed in bfloat16 or wider, within the bound.
No kernel may reach another device: no remote copies, remote signals or barrier semaphores. Data moves between devices by JAX's collectives and lax.ppermute only.
A program may use at most 128 MiB of HBM per device.

v0:
```python
import jax
import jax.numpy as jnp
from jax import lax
from jax.sharding import PartitionSpec as P

HEAD_DIM = 128
STRETCH = 64


def local(inputs, w_query, cache_kv, nb_owner, nb_row, out_grad):
    dp_count = lax.axis_size("dp")
    tokens = inputs[0]
    grad_rows = out_grad[0]
    stretch_count = nb_owner.shape[1]
    neigh_count = nb_owner.shape[2]
    owners = nb_owner.reshape(-1)
    picked_rows = nb_row.reshape(-1)
    request_count = owners.shape[0]
    capacity = max(1, -(-request_count // dp_count))
    request_order = jnp.arange(request_count, dtype=jnp.int32)
    earlier = (owners[None, :] == owners[:, None]) & (
        request_order[None, :] < request_order[:, None]
    )
    slot_rank = jnp.sum(earlier.astype(jnp.int32), axis=1)
    slot_index = owners * capacity + slot_rank
    slot_grid = jnp.arange(dp_count * capacity, dtype=jnp.int32)
    slot_match = (slot_index[:, None] == slot_grid[None, :]).astype(jnp.int32)
    wanted = jnp.sum(slot_match * picked_rows[:, None], axis=0)
    asked_rows = lax.all_to_all(wanted, "dp", split_axis=0, concat_axis=0, tiled=True)
    att_width = w_query.shape[1]
    local_heads = att_width // HEAD_DIM
    key_span = cache_kv.shape[2]
    queries = jnp.dot(tokens, w_query, preferred_element_type=jnp.float32).astype(jnp.bfloat16)
    fetched_kv = lax.all_to_all(cache_kv[asked_rows], "dp", split_axis=0, concat_axis=0, tiled=True)
    keys_got = fetched_kv[:, 0]
    values_got = fetched_kv[:, 1]
    keys = keys_got[slot_index].reshape(
        stretch_count, neigh_count * key_span, local_heads, HEAD_DIM
    )
    values = values_got[slot_index].reshape(
        stretch_count, neigh_count * key_span, local_heads, HEAD_DIM
    )
    lead_rows = STRETCH - 1
    score_scale = HEAD_DIM ** (-0.5)

    def shifted(array):
        tail = jnp.zeros((lead_rows, array.shape[1]), array.dtype)
        return jnp.concatenate([array[lead_rows:], tail], 0).reshape(
            -1, STRETCH, local_heads, HEAD_DIM
        )

    def unshift(array):
        flat = array.reshape(-1, att_width)
        head = jnp.zeros((lead_rows, att_width), flat.dtype)
        return jnp.concatenate([head, flat[: flat.shape[0] - lead_rows]], 0)

    q_blocks = shifted(queries)
    g_blocks = shifted(grad_rows)
    scores = (
        jnp.einsum("cqhd,ckhd->chqk", q_blocks, keys, preferred_element_type=jnp.float32)
        * score_scale
    )
    row_max = jnp.max(scores, axis=-1, keepdims=True)
    exp_scores = jnp.exp(scores - row_max)
    probs = exp_scores / jnp.sum(exp_scores, axis=-1, keepdims=True)
    probs_bf = probs.astype(jnp.bfloat16)
    outputs = jnp.einsum("chqk,ckhd->cqhd", probs_bf, values, preferred_element_type=jnp.float32)
    attended = unshift(outputs).astype(jnp.bfloat16)
    dprob = jnp.einsum("cqhd,ckhd->chqk", g_blocks, values, preferred_element_type=jnp.float32)
    delta = jnp.sum(dprob * probs, axis=-1, keepdims=True)
    dscore = (probs * (dprob - delta) * score_scale).astype(jnp.bfloat16)
    dquery_blocks = jnp.einsum("chqk,ckhd->cqhd", dscore, keys, preferred_element_type=jnp.float32)
    dquery = unshift(dquery_blocks).astype(jnp.bfloat16)
    query_grad = lax.psum_scatter(
        lax.dot_general(
            tokens, dquery, (((0,), (0,)), ((), ())), preferred_element_type=jnp.float32
        ),
        "dp",
        scatter_dimension=0,
        tiled=True,
    )
    partial_value = lax.dot_general(
        dquery, w_query, (((1,), (1,)), ((), ())), preferred_element_type=jnp.float32
    )
    input_grad = lax.psum_scatter(
        partial_value.astype(jnp.bfloat16), "mp", scatter_dimension=1, tiled=True
    )
    return (attended[None], input_grad[None], query_grad)


def solution(mesh):
    return jax.shard_map(
        local,
        mesh=mesh,
        in_specs=(
            P("dp", None, None),
            P(None, "mp"),
            P("dp", None, None, "mp"),
            P("dp", None, None),
            P("dp", None, None),
            P("dp", None, "mp"),
        ),
        out_specs=(P("dp", None, "mp"), P("dp", None, "mp"), P("dp", "mp")),
        check_vma=False,
    )
```

profile of v0, /device:TPU:32, one launch (start us, length us, event | category | flops | bytes accessed | tf_op | source)
XLA Modules:
  0.0 673.5 jit_solution(3518784578080070567)
XLA Ops:
  7.2 0.9 copy.56
  8.4 0.8 copy.57
  9.4 19.9 %all_to_all.17 = s32[64,1,1]{2,1,0:T(1,128)S(1)} all-to-all(s32[64,1,1]{2,1,0:T(1,128)S(1)} %copy.58), channel_id=1, replica_groups=mesh['dp'=64,'mp'=4] {'dp'}, dimensions={0} | all-to-all | bytes 512 | tf_op jit(solution)/shard_map/all_to_all | solution.py:29
  29.3 1.2 reduce
  30.6 7.4 %gather_fusion = bf16[64,2,128,512]{3,2,1,0:T(8,128)(2,1)} fusion(bf16[8,2,128,512]{3,2,1,0:T(8,128)(2,1)S(1)} %copy-done, s32[1024]{0:T(1024)S(1)} %pad_clamp_fusion.1), kind=kCustom, calls=%fused_computation | custom fusion | bytes 33554688 | tf_op jit(solution)/shard_map/gather | solution.py:34
  37.9 6.6 all-to-all-start.1
  44.9 5.8 fusion.3
  52.0 356.3 %all-to-all-done.1 = bf16[64,2,128,512]{3,2,1,0:T(8,128)(2,1)} async-done(((bf16[64,2,128,512]{3,2,1,0:T(8,128)(2,1)}), bf16[64,2,128,512]{3,2,1,0:T(8,128)(2,1)}, u32[]{:S(2)}, u32[]{:S(2)}) %all-to-all-start.1) | async-done | bytes 16777248 | tf_op jit(solution)/shard_map/all_to_all | solution.py:34
  408.4 11.6 %slice_bitcast_fusion.1 = (bf16[64,128,512]{2,1,0:T(8,128)(2,1)}, bf16[64,128,512]{2,1,0:T(8,128)(2,1)}) fusion(bf16[64,2,128,512]{3,2,1,0:T(8,128)(2,1)} %all-to-all-done.1), kind=kLoop, calls=%fused_computation.6 | loop fusion | bytes 33554432 | tf_op jit(solution)/shard_map/squeeze | solution.py:35
  420.0 4.1 gather_fusion.2
  424.0 2.1 reshape.100
  426.1 2.4 fusion.15
  428.6 2.1 fusion.54
  430.6 5.4 gather_fusion.1
  436.0 2.5 reshape.98
  438.6 2.2 fusion.9
  440.8 15.3 %fusion.30 = bf16[8,64,4,128]{3,1,2,0:T(8,128)(2,1)S(1)} fusion(bf16[8,256,4,128]{3,2,1,0:T(4,128)(2,1)} %reshape.100, f32[8,4,64,256]{3,2,1,0:T(8,128)} %fusion.9, f32[8,4,64,256]{3,2,1,0:T(8,128)} %get-tuple-element.21, f32[8,4,64]{2,1,0:T(4,128)S(1)} %get-tuple-element.20), kind=kOutput, calls=%fused_computation.29 | convolution fusion | flops 138152192 | bytes 6823936 | tf_op jit(solution)/shard_map/chqk,ckhd->cqhd/dot_general | solution.py:72
  456.6 6.5 convolution_convert_fusion
  463.4 7.8 %convolution_bitcast_fusion = f32[4096,512]{0,1:T(8,128)} fusion(bf16[1,512,4096]{2,1,0:T(8,128)(2,1)} %param.6, bf16[449,512]{1,0:T(8,128)(2,1)S(1)} %slice.40), kind=kOutput, calls=%fused_computation.7 | convolution fusion | flops 2147483648 | bytes 13042688 | tf_op jit(solution)/shard_map/dot_general | solution.py:75
  471.2 9.1 %copy.69 = f32[4096,512]{1,0:T(8,128)} copy(f32[4096,512]{0,1:T(8,128)} %convolution_bitcast_fusion) | data formatting | bytes 16777216
  480.3 6.1 fusion.27
  486.9 0.9 pad_bitcast_fusion
  487.8 23.6 %reduce-scatter.5.cloned.1.call-done = bf16[512,1024]{1,0:T(8,128)(2,1)} async-done(((bf16[512,4096]{1,0:T(8,128)(2,1)}), bf16[512,1024]{1,0:T(8,128)(2,1)}) %reduce-scatter.5.cloned.1.call-update) | async-done | bytes 1048592 | tf_op jit(solution)/shard_map/reduce_scatter | solution.py:85
  511.4 155.2 %reduce-scatter.7.cloned.1.call-done = f32[64,512]{1,0:T(8,128)} async-done(((f32[4096,512]{1,0:T(8,128)}), f32[64,512]{1,0:T(8,128)}) %reduce-scatter.7.cloned.1.call-update) | async-done | bytes 131088
  (37 shorter events, 3.5 us)
Async XLA Ops:
  7.2 23.4 %copy-start = (bf16[8,2,128,512]{3,2,1,0:T(8,128)(2,1)S(1)}, bf16[8,2,128,512]{3,2,1,0:T(8,128)(2,1)}, u32[]{:S(2)}) copy-start(bf16[8,2,128,512]{3,2,1,0:T(8,128)(2,1)} %param.8) | copy-start | bytes 6291460
  37.9 370.4 %all-to-all-start.1 = ((bf16[64,2,128,512]{3,2,1,0:T(8,128)(2,1)}), bf16[64,2,128,512]{3,2,1,0:T(8,128)(2,1)}, u32[]{:S(2)}, u32[]{:S(2)}) async-start(bf16[64,2,128,512]{3,2,1,0:T(8,128)(2,1)} %gather_fusion), calls=%async_computation.1 | async-start | bytes 33554432 | tf_op jit(solution)/shard_map/all_to_all | solution.py:34
  44.6 466.9 %reduce-scatter.5.cloned.1.call-start = ((), (), s32[]{:S(2)}) async-start(), calls=%async_computation.4 | async-start | bytes 5242880 | tf_op jit(solution)/shard_map/reduce_scatter | solution.py:85
  50.7 1.0 copy-start.4
  428.6 2.1 copy-start.2
  438.6 2.2 copy-start.3
  463.1 203.5 %reduce-scatter.7.cloned.1.call-start = ((), (), s32[]{:S(2)}) async-start(), calls=%async_computation.5 | async-start | bytes 8519680
  480.3 186.4 %copy-start.1 = (bf16[8,2,128,512]{3,2,1,0:T(8,128)(2,1)S(1)}, bf16[8,2,128,512]{3,2,1,0:T(8,128)(2,1)}, u32[]{:S(2)}) copy-start(bf16[8,2,128,512]{3,2,1,0:T(8,128)(2,1)} %param.8) | copy-start | bytes 6291460
Sparse Core Ops, SparseCore 0:
  463.3 48.1 reduce-scatter.4
  516.8 149.8 reduce-scatter.6
where the time goes:
time: 675 us; the launch traced here: 673 us
  waiting for transfers between devices  535 us (79%)
  local copies, waits for them, and re-layouts  47.4 us (7%)
  matrix products  46 us (7%)
  blocking collectives  19.9 us (3%)
  between operations  14.2 us (2%)
  starting transfers between devices  7.09 us (1%)
    all_to_all x1, waiting for transfers between devices, local(): lax.all_to_all(cache_kv[asked_rows], 'dp', split_axis=0, concat_axis=0, t...  356 us
    unnamed x3, waiting for transfers between devices  155 us
    reduce_scatter x1, waiting for transfers between devices, local(): lax.psum_scatter(partial_value.astype(jnp.bfloat16), 'mp', scatter_dimens...  23.6 us
    all_to_all x1, blocking collectives, local(): lax.all_to_all(wanted, 'dp', split_axis=0, concat_axis=0, tiled=True)  19.9 us
    dot_general x1, matrix products, local(): jnp.einsum('chqk,ckhd->cqhd', dscore, keys, preferred_element_type=jnp.fl...  15.3 us
  transfers between devices with their start and end apart: 3, of which 3 were waited for; matrix products, arithmetic and copies ran while one was open for 5% of the time, Pallas kernels for 0%

commit v1 on v0

v1 whole, which is shorter than its diff:
```python
import functools

import jax
import jax.numpy as jnp
from jax import lax
from jax.experimental import pallas as pl
from jax.experimental.pallas import tpu as pltpu
from jax.sharding import Mesh
from jax.sharding import PartitionSpec as P

HEAD_DIM = 128
STRETCH = 64
LEAD = STRETCH - 1
TILE = 16
PLANE = ("x", "core")
DP = ("x", "z", "core")
CHUNKS = ((0, 3), (3, 6), (6, 8))
BF16, F32 = jnp.bfloat16, jnp.float32


def pick_kernel(ids_ref, tiles_ref, out_ref, *, slots):
    seq = pl.program_id(0)

    for slot in range(slots):
        out_ref[0, slot] = tiles_ref[ids_ref[seq * slots + slot]]


def pick(ids, tiles):
    seqs, slots = ids.shape
    return pl.pallas_call(
        functools.partial(pick_kernel, slots=slots),
        grid_spec=pltpu.PrefetchScalarGridSpec(
            num_scalar_prefetch=1,
            grid=(seqs,),
            in_specs=[pl.BlockSpec(tiles.shape, lambda s, ids: (0, 0, 0))],
            out_specs=pl.BlockSpec((1, slots) + tiles.shape[1:], lambda s, ids: (s, 0, 0, 0)),
        ),
        out_shape=jax.ShapeDtypeStruct((seqs, slots) + tiles.shape[1:], tiles.dtype),
        compiler_params=pltpu.CompilerParams(vmem_limit_bytes=32 << 20),
        cost_estimate=pl.CostEstimate(flops=0, bytes_accessed=6 << 20, transcendentals=0),
        name="pick",
    )(ids.reshape(-1), tiles)


def attend_kernel(q_ref, g_ref, kv_ref, out_ref, dq_ref, *, heads):
    scale = HEAD_DIM ** (-0.5)
    both = (((1,), (1,)), ((), ()))
    for head in range(heads):
        cols = slice(head * HEAD_DIM, (head + 1) * HEAD_DIM)
        keys = kv_ref[0, head].reshape(-1, HEAD_DIM)
        values = kv_ref[1, head].reshape(-1, HEAD_DIM)
        scores = lax.dot_general(q_ref[:, cols], keys, both, preferred_element_type=F32) * scale
        exps = jnp.exp(scores - jnp.max(scores, axis=-1, keepdims=True))
        probs = exps / jnp.sum(exps, axis=-1, keepdims=True)
        out_ref[:, cols] = jnp.dot(
            probs.astype(BF16), values, preferred_element_type=F32
        ).astype(BF16)
        dprob = lax.dot_general(g_ref[:, cols], values, both, preferred_element_type=F32)
        delta = jnp.sum(dprob * probs, axis=-1, keepdims=True)
        dscore = (probs * (dprob - delta) * scale).astype(BF16)
        dq_ref[:, cols] = jnp.dot(dscore, keys, preferred_element_type=F32).astype(BF16)


def attend(q, g, kv, neigh):
    rows, width = q.shape
    count = rows // STRETCH
    _, heads, tiles, slots, _, _ = kv.shape
    block = pl.BlockSpec((STRETCH, width), lambda c: (c, 0))
    return pl.pallas_call(
        functools.partial(attend_kernel, heads=heads),
        grid=(count,),
        in_specs=[
            block,
            block,
            pl.BlockSpec((2, heads, tiles, neigh, TILE, HEAD_DIM), lambda c: (0, 0, 0, c, 0, 0)),
        ],
        out_specs=[block, block],
        out_shape=[jax.ShapeDtypeStruct(q.shape, BF16)] * 2,
        compiler_params=pltpu.CompilerParams(vmem_limit_bytes=32 << 20),
        cost_estimate=pl.CostEstimate(
            flops=10 * rows * width * neigh * tiles * TILE, bytes_accessed=kv.size * 2, transcendentals=0
        ),
        name="attend",
    )(q, g, kv)


def local(inputs, w_query, cache_kv, nb_owner, nb_row, out_grad):
    nx, nz, nc = (lax.axis_size(a) for a in DP)
    ndp = nx * nz * nc
    tokens, grad_rows = inputs[0], out_grad[0]
    length, d = tokens.shape
    width = w_query.shape[1]
    heads = width // HEAD_DIM
    db_rows, _, nb_len, _ = cache_kv.shape
    _, stretches, neigh = nb_owner.shape
    tiles = nb_len // TILE

    own_ids = (nb_owner * db_rows + nb_row).reshape(-1)
    ids = lax.all_gather(own_ids, DP, tiled=False)

    cut = cache_kv.reshape(db_rows, 2, tiles, TILE, heads, HEAD_DIM)
    cut = cut.transpose(1, 4, 2, 0, 3, 5).reshape(ndp, db_rows, TILE, HEAD_DIM)
    held = lax.all_to_all(cut, DP, split_axis=0, concat_axis=0, tiled=True)
    held = held.reshape(ndp * db_rows, TILE, HEAD_DIM)

    def shifted(array):
        return jnp.concatenate([array[LEAD:], jnp.zeros((LEAD, array.shape[1]), array.dtype)], 0)

    moved = shifted(tokens)
    q = jnp.dot(moved, w_query, preferred_element_type=F32).astype(BF16)
    g = shifted(grad_rows)

    share = moved.reshape(length, nx, nz, nc, -1).transpose(1, 3, 0, 2, 4).reshape(nx * nc, length, -1)
    share = lax.all_to_all(share, PLANE, split_axis=0, concat_axis=0, tiled=True)

    outs, grads, total = [], [], 0.0
    for first, last in CHUNKS:
        lo, hi = first * STRETCH, last * STRETCH
        slots = slice(first * neigh, last * neigh)
        send = pick(ids[:, slots], held)
        got = lax.all_to_all(send, DP, split_axis=0, concat_axis=0, tiled=True)
        got = got.reshape(2, heads, tiles, (last - first) * neigh, TILE, HEAD_DIM)
        out, dq = attend(q[lo:hi], g[lo:hi], got, neigh)
        rows = min(hi, length - LEAD) - lo
        keep = -(-rows // TILE) * TILE
        dq = jnp.where(jnp.arange(keep)[:, None] < rows, dq[:keep], 0)
        outs.append(out[:rows])
        part = lax.dot_general(
            dq, w_query, (((1,), (1,)), ((), ())), preferred_element_type=F32
        ).astype(BF16)
        part = part.reshape(keep, lax.axis_size("mp"), -1).transpose(1, 0, 2)
        part = lax.all_to_all(part, "mp", split_axis=0, concat_axis=0, tiled=True)
        part = jnp.sum(part.astype(F32), axis=0).astype(BF16)
        grads.append(part[:rows])
        plane_dq = lax.all_gather(dq, PLANE, tiled=False)
        total += jnp.einsum("std,stf->df", share[:, lo : lo + keep], plane_dq, preferred_element_type=F32)

    query_grad = lax.psum_scatter(total, "z", scatter_dimension=0, tiled=True)
    attended = jnp.concatenate([jnp.zeros((LEAD, width), BF16)] + outs, 0)
    input_grad = jnp.concatenate([jnp.zeros((LEAD, d // lax.axis_size("mp")), BF16)] + grads, 0)
    return attended[None], input_grad[None], query_grad


def solution(mesh):
    fine = Mesh(mesh.devices.reshape(4, 8, 2, 4), ("x", "z", "core", "mp"))
    return jax.shard_map(
        local,
        mesh=fine,
        in_specs=(
            P(DP, None, None),
            P(None, "mp"),
            P(DP, None, None, "mp"),
            P(DP, None, None),
            P(DP, None, None),
            P(DP, None, "mp"),
        ),
        out_specs=(P(DP, None, "mp"), P(DP, None, "mp"), P(DP, "mp")),
        check_vma=False,
    )
```

time: 675 us -> 387 us (0.57)
  waiting for transfers between devices: 535 us -> 72.7 us
  blocking collectives: 19.9 us -> 136 us
  Pallas kernels: 0 us -> 44.3 us
  starting transfers between devices: 7.09 us -> 50.2 us
  matrix products: 46 us -> 27.9 us
  local copies, waits for them, and re-layouts: 47.4 us -> 34.3 us
    all_to_all x1 -> x8, waiting for transfers between devices: 356 us -> 72.1 us  [the longest x3 43.6 us: local(): got = lax.all_to_all(send, DP, split_axis=0, concat_axis=0, tiled=True)]
    unnamed x3, waiting for transfers between devices: 155 us -> 0.55 us
    all_gather x0 -> x2, blocking collectives: none -> 136 us  [the longest x1 79.9 us: local(): ids = lax.all_gather(own_ids, DP, tiled=False)]
    pallas_call x0 -> x6, Pallas kernels: none -> 44.3 us  [the longest x3 23.3 us: pick(): pl.pallas_call(functools.partial(pick_kernel, slots=slots), grid_spec=plt...]
    all_to_all x1 -> x8, starting transfers between devices: 6.61 us -> 49.8 us  [the longest x3 21.1 us: local(): got = lax.all_to_all(send, DP, split_axis=0, concat_axis=0, tiled=True)]
    reduce_scatter x1, waiting for transfers between devices: 23.6 us -> 0.01 us  [local(): query_grad = lax.psum_scatter(total, 'z', scatter_dimension=0, tiled=True)]
    all_to_all x1 -> x0, blocking collectives: 19.9 us -> none  [local(): lax.all_to_all(wanted, 'dp', split_axis=0, concat_axis=0, tiled=True)]
    dot_general x7, matrix products: 46 us -> 27.9 us  [the longest x3 11 us: local(): jnp.einsum('std,stf->df', share[:, lo:lo + keep], plane_dq, preferred_ele...]
  transfers between devices with their start and end apart: 3 -> 11, of which waited for: 3 -> 5; matrix products, arithmetic and copies ran while one was open for 5% -> 16% of each run, Pallas kernels for 0% -> 11%
where the time goes in v1:
time: 387 us; the launch traced here: 385 us
  blocking collectives  136 us (35%)
  waiting for transfers between devices  72.7 us (19%)
  starting transfers between devices  50.2 us (13%)
  Pallas kernels  44.3 us (11%)
  local copies, waits for them, and re-layouts  34.3 us (9%)
  matrix products  27.9 us (7%)
  between operations  14.1 us (4%)
  other arithmetic  5.37 us (1%)
    all_gather x1, blocking collectives, local(): ids = lax.all_gather(own_ids, DP, tiled=False)  79.9 us
    all_gather x1, blocking collectives, local(): plane_dq = lax.all_gather(dq, PLANE, tiled=False)  56.4 us
    all_to_all x3, waiting for transfers between devices, local(): got = lax.all_to_all(send, DP, split_axis=0, concat_axis=0, tiled=True)  43.6 us
    all_to_all x3, waiting for transfers between devices, local(): part = lax.all_to_all(part, 'mp', split_axis=0, concat_axis=0, tiled=True)  28.5 us
    pallas_call x3, Pallas kernels, pick(): pl.pallas_call(functools.partial(pick_kernel, slots=slots), grid_spec=plt...  23.3 us
    all_to_all x3, starting transfers between devices, local(): got = lax.all_to_all(send, DP, split_axis=0, concat_axis=0, tiled=True)  21.1 us
    pallas_call x3, Pallas kernels, attend(): pl.pallas_call(functools.partial(attend_kernel, heads=heads), grid=(count...  21 us
    all_to_all x3, starting transfers between devices, local(): part = lax.all_to_all(part, 'mp', split_axis=0, concat_axis=0, tiled=True)  12.4 us
  transfers between devices with their start and end apart: 11, of which 5 were waited for; matrix products, arithmetic and copies ran while one was open for 16% of the time, Pallas kernels for 11%

profile of v1, /device:TPU:32, one launch (start us, length us, event | category | flops | bytes accessed | tf_op | source)
XLA Modules:
  0.0 385.1 jit_solution(2242495801863551607)
XLA Ops:
  11.6 11.7 %all-to-all-start = ((bf16[64,8,16,128]{3,2,1,0:T(8,128)(2,1)}), bf16[64,8,16,128]{3,2,1,0:T(8,128)(2,1)S(1)}, u32[]{:S(2)}, u32[]{:S(2)}) async-start(bf16[64,8,16,128]{3,2,1,0:T(8,128)(2,1)} %bitcast.76), calls=%async_computation | async-start | bytes 4194304 | tf_op jit(solution)/shard_map/all_to_all | solution.py:103
  23.5 79.9 %all-gather.3 = s32[64,1,16]{2,1,0:T(1,128)S(1)} all-gather(s32[1,1,16]{2,1,0:T(1,128)S(1)} %reshape.79), channel_id=1, replica_groups=mesh['x'=4,'z'=8,'core'=2,'mp'=4] {'x','z','core'}, dimensions={0}, use_global_device_ids=true | all-gather | bytes 4160 | tf_op jit(solution)/shard_map/all_gather | solution.py:99
  106.4 7.3 %all-to-all-start.2 = ((bf16[64,6,16,128]{3,2,1,0:T(8,128)(2,1)}), bf16[64,6,16,128]{3,2,1,0:T(8,128)(2,1)}, u32[]{:S(2)}, u32[]{:S(2)}) async-start(bf16[64,6,16,128]{3,2,1,0:T(8,128)(2,1)} %copy-done.1), calls=%async_computation.2 | async-start | bytes 3145728 | tf_op jit(solution)/shard_map/all_to_all | solution.py:121
  116.7 36.0 %all-to-all-done.2 = bf16[64,6,16,128]{3,2,1,0:T(8,128)(2,1)} async-done(((bf16[64,6,16,128]{3,2,1,0:T(8,128)(2,1)}), bf16[64,6,16,128]{3,2,1,0:T(8,128)(2,1)}, u32[]{:S(2)}, u32[]{:S(2)}) %all-to-all-start.2) | async-done | bytes 1572896 | tf_op jit(solution)/shard_map/all_to_all | solution.py:121
  152.8 7.0 %all-to-all-start.1 = ((bf16[64,6,16,128]{3,2,1,0:T(8,128)(2,1)}), bf16[64,6,16,128]{3,2,1,0:T(8,128)(2,1)}, u32[]{:S(2)}, u32[]{:S(2)}) async-start(bf16[64,6,16,128]{3,2,1,0:T(8,128)(2,1)} %copy-done), calls=%async_computation.1 | async-start | bytes 3145728 | tf_op jit(solution)/shard_map/all_to_all | solution.py:121
  159.8 4.9 %slice.65 = bf16[1,449,4096]{2,1,0:T(8,128)(2,1)} slice(bf16[1,512,4096]{2,1,0:T(8,128)(2,1)} %param.6), slice={[0:1], [63:512], [0:4096]} | slice | bytes 7356416 | tf_op jit(solution)/shard_map/slice | solution.py:107
  164.7 6.4 %copy.25 = bf16[1,449,4096]{1,2,0:T(8,128)(2,1)} copy(bf16[1,449,4096]{2,1,0:T(8,128)(2,1)} %slice.65) | data formatting | bytes 7356416
  171.2 20.0 %pick.5 = bf16[64,4,16,128]{3,2,1,0:T(8,128)(2,1)} custom-call(s32[256]{0:T(256)S(1)} %reshape.69.ids_ref, bf16[512,16,128]{2,1,0:T(8,128)(2,1)S(1)} %bitcast.70), custom_call_target="tpu_custom_call" | custom-call | bytes 6291456 | tf_op jit(solution)/shard_map/pick/pallas_call | solution.py:30
  191.2 7.6 %all-to-all-done.1 = bf16[64,6,16,128]{3,2,1,0:T(8,128)(2,1)} async-done(((bf16[64,6,16,128]{3,2,1,0:T(8,128)(2,1)}), bf16[64,6,16,128]{3,2,1,0:T(8,128)(2,1)}, u32[]{:S(2)}, u32[]{:S(2)}) %all-to-all-start.1) | async-done | bytes 1572896 | tf_op jit(solution)/shard_map/all_to_all | solution.py:121
  198.8 6.8 %all-to-all-start.3 = ((bf16[64,4,16,128]{3,2,1,0:T(8,128)(2,1)}), bf16[64,4,16,128]{3,2,1,0:T(8,128)(2,1)S(1)}, u32[]{:S(2)}, u32[]{:S(2)}) async-start(bf16[64,4,16,128]{3,2,1,0:T(8,128)(2,1)} %pick.5), calls=%async_computation.3 | async-start | bytes 2097152 | tf_op jit(solution)/shard_map/all_to_all | solution.py:121
  205.7 5.9 %convolution_convert_fusion.3 = bf16[512,512]{1,0:T(8,128)(2,1)S(1)} fusion(bf16[4096,512]{1,0:T(8,128)(2,1)} %param.7, bf16[449,4096]{0,1:T(8,128)(2,1)} %bitcast.74), kind=kOutput, calls=%fused_computation.14 | convolution fusion | flops 2147745792 | bytes 8396800 | tf_op jit(solution)/shard_map/dot_general | solution.py:110
  211.7 8.1 %attend.4 = (bf16[192,512]{1,0:T(8,128)(2,1)S(1)}, bf16[192,512]{1,0:T(8,128)(2,1)S(1)}) custom-call(bf16[192,512]{1,0:T(8,128)(2,1)S(1)} %get-tuple-element.18.q_ref, bf16[192,512]{1,0:T(8,128)(2,1)S(1)} %get-tuple-element.16.g_ref, bf16[2,4,8,6,16,128]{5,4,3,2,1,0:T(8,128)(2,1)} %bitcast.8.kv_ref), custom_call_target="tpu_custom_call" | custom-call | flops 251658240 | bytes 1572864 | tf_op jit(solution)/shard_map/attend/pallas_call | solution.py:69
  219.8 8.1 %attend.3 = (bf16[192,512]{1,0:T(8,128)(2,1)S(1)}, bf16[192,512]{1,0:T(8,128)(2,1)S(1)}) custom-call(bf16[192,512]{1,0:T(8,128)(2,1)S(1)} %get-tuple-element.17.q_ref, bf16[192,512]{1,0:T(8,128)(2,1)S(1)} %get-tuple-element.15.g_ref, bf16[2,4,8,6,16,128]{5,4,3,2,1,0:T(8,128)(2,1)} %bitcast.6.kv_ref), custom_call_target="tpu_custom_call" | custom-call | flops 251658240 | bytes 1572864 | tf_op jit(solution)/shard_map/attend/pallas_call | solution.py:69
  234.0 6.5 %copy.24 = bf16[8,512,512]{2,1,0:T(8,128)(2,1)} copy(bf16[8,512,512]{1,2,0:T(8,128)(2,1)} %bitcast.73) | data formatting | bytes 8388608 | tf_op jit(solution)/shard_map/reshape | solution.py:113
  240.5 4.6 %all-to-all-start.7 = ((bf16[8,512,512]{2,1,0:T(8,128)(2,1)}), bf16[8,512,512]{2,1,0:T(8,128)(2,1)}, u32[]{:S(2)}, u32[]{:S(2)}) async-start(bf16[8,512,512]{2,1,0:T(8,128)(2,1)} %copy.24), calls=%async_computation.7 | async-start | bytes 8388608 | tf_op jit(solution)/shard_map/all_to_all | solution.py:114
  246.0 4.8 %attend.5 = (bf16[128,512]{1,0:T(8,128)(2,1)S(1)}, bf16[128,512]{1,0:T(8,128)(2,1)S(1)}) custom-call(bf16[128,512]{1,0:T(8,128)(2,1)S(1)} %slice.90.q_ref, bf16[128,512]{1,0:T(8,128)(2,1)S(1)} %pad_slice_fusion.g_ref, bf16[2,4,8,4,16,128]{5,4,3,2,1,0:T(8,128)(2,1)S(1)} %bitcast.71), custom_call_target="tpu_custom_call" | custom-call | flops 167772160 | bytes 1048576 | tf_op jit(solution)/shard_map/attend/pallas_call | solution.py:69
  255.4 56.4 %all-gather.2 = bf16[640,512]{1,0:T(8,128)(2,1)S(1)} all-gather(bf16[80,512]{1,0:T(8,128)(2,1)S(1)} %slice_select_fusion), channel_id=4, replica_groups=mesh['x'=4,'z'=8,'core'=2,'mp'=4] {'x','core'}, dimensions={0}, use_global_device_ids=true | all-gather | bytes 737280 | tf_op jit(solution)/shard_map/all_gather | solution.py:135
  311.8 4.5 %all-to-all-start.6 = ((bf16[4,80,1024]{2,1,0:T(8,128)(2,1)}), bf16[4,80,1024]{2,1,0:T(8,128)(2,1)S(1)}, u32[]{:S(2)}, u32[]{:S(2)}) async-start(bf16[4,80,1024]{2,1,0:T(8,128)(2,1)} %bitcast.67), calls=%async_computation.6 | async-start | bytes 1310720 | tf_op jit(solution)/shard_map/all_to_all | solution.py:132
  331.4 3.9 %fusion.4 = f32[512,512]{1,0:T(8,128)} fusion(bf16[8,192,512]{2,1,0:T(8,128)(2,1)} %bitcast.83, bf16[8,512,512]{2,1,0:T(8,128)(2,1)} %all-to-all-done.7), kind=kOutput, calls=%fused_computation.9 | convolution fusion | flops 805306368 | bytes 4194304 | tf_op jit(solution)/shard_map/std,stf->df/dot_general | solution.py:136
  335.3 4.5 %fusion.13 = f32[512,512]{1,0:T(8,128)} fusion(f32[512,512]{1,0:T(8,128)} %convolution_bitcast_fusion, f32[512,512]{1,0:T(8,128)} %fusion.4, bf16[8,192,512]{2,1,0:T(8,128)(2,1)} %bitcast.87, bf16[8,512,512]{2,1,0:T(8,128)(2,1)} %all-to-all-done.7), kind=kOutput, calls=%fused_computation.13 | convolution fusion | flops 805830656 | bytes 6291456 | tf_op jit(solution)/shard_map/std,stf->df/dot_general | solution.py:136
  339.8 3.7 convolution_convert_fusion.1
  344.9 6.8 %all-to-all-done.5 = bf16[4,192,1024]{2,1,0:T(8,128)(2,1)S(1)} async-done(((bf16[4,192,1024]{2,1,0:T(8,128)(2,1)}), bf16[4,192,1024]{2,1,0:T(8,128)(2,1)S(1)}, u32[]{:S(2)}, u32[]{:S(2)}) %all-to-all-start.5) | async-done | bytes 1572896 | tf_op jit(solution)/shard_map/all_to_all | solution.py:132
  351.7 4.4 %all-to-all-start.4 = ((bf16[4,192,1024]{2,1,0:T(8,128)(2,1)}), bf16[4,192,1024]{2,1,0:T(8,128)(2,1)}, u32[]{:S(2)}, u32[]{:S(2)}) async-start(bf16[4,192,1024]{2,1,0:T(8,128)(2,1)} %bitcast.79), calls=%async_computation.4 | async-start | bytes 3145728 | tf_op jit(solution)/shard_map/all_to_all | solution.py:132
  357.5 18.0 %all-to-all-done.4 = bf16[4,192,1024]{2,1,0:T(8,128)(2,1)} async-done(((bf16[4,192,1024]{2,1,0:T(8,128)(2,1)}), bf16[4,192,1024]{2,1,0:T(8,128)(2,1)}, u32[]{:S(2)}, u32[]{:S(2)}) %all-to-all-start.4) | async-done | bytes 1572896 | tf_op jit(solution)/shard_map/all_to_all | solution.py:132
  (66 shorter events, 43.3 us)
Async XLA Ops:
  11.6 11.7 %copy-start.5 = (s32[1,8,2]{1,2,0:T(2,128)S(1)}, s32[1,8,2]{1,2,0:T(2,128)}, u32[]{:S(2)}) copy-start(s32[1,8,2]{1,2,0:T(2,128)} %param.10) | copy-start | bytes 196
  11.6 11.7 %copy-start.6 = (s32[1,8,2]{1,2,0:T(2,128)S(1)}, s32[1,8,2]{1,2,0:T(2,128)}, u32[]{:S(2)}) copy-start(s32[1,8,2]{1,2,0:T(2,128)} %param.9) | copy-start | bytes 196
  11.6 92.0 %all-to-all-start = ((bf16[64,8,16,128]{3,2,1,0:T(8,128)(2,1)}), bf16[64,8,16,128]{3,2,1,0:T(8,128)(2,1)S(1)}, u32[]{:S(2)}, u32[]{:S(2)}) async-start(bf16[64,8,16,128]{3,2,1,0:T(8,128)(2,1)} %bitcast.76), calls=%async_computation | async-start | bytes 4194304 | tf_op jit(solution)/shard_map/all_to_all | solution.py:103
  105.3 1.1 copy-start.1
  106.4 46.3 %all-to-all-start.2 = ((bf16[64,6,16,128]{3,2,1,0:T(8,128)(2,1)}), bf16[64,6,16,128]{3,2,1,0:T(8,128)(2,1)}, u32[]{:S(2)}, u32[]{:S(2)}) async-start(bf16[64,6,16,128]{3,2,1,0:T(8,128)(2,1)} %copy-done.1), calls=%async_computation.2 | async-start | bytes 3145728 | tf_op jit(solution)/shard_map/all_to_all | solution.py:121
  115.5 1.2 copy-start
  152.8 46.0 %all-to-all-start.1 = ((bf16[64,6,16,128]{3,2,1,0:T(8,128)(2,1)}), bf16[64,6,16,128]{3,2,1,0:T(8,128)(2,1)}, u32[]{:S(2)}, u32[]{:S(2)}) async-start(bf16[64,6,16,128]{3,2,1,0:T(8,128)(2,1)} %copy-done), calls=%async_computation.1 | async-start | bytes 3145728 | tf_op jit(solution)/shard_map/all_to_all | solution.py:121
  198.8 41.7 %all-to-all-start.3 = ((bf16[64,4,16,128]{3,2,1,0:T(8,128)(2,1)}), bf16[64,4,16,128]{3,2,1,0:T(8,128)(2,1)S(1)}, u32[]{:S(2)}, u32[]{:S(2)}) async-start(bf16[64,4,16,128]{3,2,1,0:T(8,128)(2,1)} %pick.5), calls=%async_computation.3 | async-start | bytes 2097152 | tf_op jit(solution)/shard_map/all_to_all | solution.py:121
  205.6 125.8 %all-gather.7.cloned.1.call-start = ((), (), s32[]{:S(2)}) async-start(), calls=%async_computation.10 | async-start | bytes 1769472 | tf_op jit(solution)/shard_map/all_gather | solution.py:135
  205.7 5.9 %copy-start.4 = (bf16[1,512,512]{2,1,0:T(8,128)(2,1)S(1)}, bf16[1,512,512]{2,1,0:T(8,128)(2,1)}, u32[]{:S(2)}) copy-start(bf16[1,512,512]{2,1,0:T(8,128)(2,1)} %param.11) | copy-start | bytes 1572868
  240.5 71.4 %all-to-all-start.7 = ((bf16[8,512,512]{2,1,0:T(8,128)(2,1)}), bf16[8,512,512]{2,1,0:T(8,128)(2,1)}, u32[]{:S(2)}, u32[]{:S(2)}) async-start(bf16[8,512,512]{2,1,0:T(8,128)(2,1)} %copy.24), calls=%async_computation.7 | async-start | bytes 8388608 | tf_op jit(solution)/shard_map/all_to_all | solution.py:114
  245.1 90.2 %all-gather.9.cloned.1.call-start = ((), (), s32[]{:S(2)}) async-start(), calls=%async_computation.11 | async-start | bytes 1769472 | tf_op jit(solution)/shard_map/all_gather | solution.py:135
  311.8 7.2 %copy-start.3 = (bf16[192,512]{1,0:T(8,128)(2,1)S(1)}, bf16[192,512]{1,0:T(8,128)(2,1)}, u32[]{:S(2)}) copy-start(bf16[192,512]{1,0:T(8,128)(2,1)} %get-tuple-element.22) | copy-start | bytes 589828
  311.8 15.9 %all-to-all-start.6 = ((bf16[4,80,1024]{2,1,0:T(8,128)(2,1)}), bf16[4,80,1024]{2,1,0:T(8,128)(2,1)S(1)}, u32[]{:S(2)}, u32[]{:S(2)}) async-start(bf16[4,80,1024]{2,1,0:T(8,128)(2,1)} %bitcast.67), calls=%async_computation.6 | async-start | bytes 1310720 | tf_op jit(solution)/shard_map/all_to_all | solution.py:132
  327.7 23.9 %all-to-all-start.5 = ((bf16[4,192,1024]{2,1,0:T(8,128)(2,1)}), bf16[4,192,1024]{2,1,0:T(8,128)(2,1)S(1)}, u32[]{:S(2)}, u32[]{:S(2)}) async-start(bf16[4,192,1024]{2,1,0:T(8,128)(2,1)} %bitcast.78), calls=%async_computation.5 | async-start | bytes 3145728 | tf_op jit(solution)/shard_map/all_to_all | solution.py:132
  331.3 47.3 %reduce-scatter.2.cloned.1.call-start = ((), (), s32[]{:S(2)}) async-start(), calls=%async_computation.9 | async-start | bytes 1179648 | tf_op jit(solution)/shard_map/reduce_scatter | solution.py:138
  335.3 4.5 %copy-start.2 = (bf16[192,512]{1,0:T(8,128)(2,1)S(1)}, bf16[192,512]{1,0:T(8,128)(2,1)}, u32[]{:S(2)}) copy-start(bf16[192,512]{1,0:T(8,128)(2,1)} %get-tuple-element.21) | copy-start | bytes 589828
  351.7 23.9 %all-to-all-start.4 = ((bf16[4,192,1024]{2,1,0:T(8,128)(2,1)}), bf16[4,192,1024]{2,1,0:T(8,128)(2,1)}, u32[]{:S(2)}, u32[]{:S(2)}) async-start(bf16[4,192,1024]{2,1,0:T(8,128)(2,1)} %bitcast.79), calls=%async_computation.4 | async-start | bytes 3145728 | tf_op jit(solution)/shard_map/all_to_all | solution.py:132
Sparse Core Ops, SparseCore 0:
  228.9 34.1 all-gather.6
  265.0 41.8 all-gather.8
  339.9 38.1 reduce-scatter.1

commit v2 on v1

v2 whole, which is shorter than its diff:
```python
import functools

import jax
import jax.numpy as jnp
from jax import lax
from jax.experimental import pallas as pl
from jax.experimental.pallas import tpu as pltpu
from jax.sharding import Mesh
from jax.sharding import PartitionSpec as P

HEAD_DIM = 128
STRETCH = 64
LEAD = STRETCH - 1
TILE = 16
SKIP = LEAD // TILE * TILE
DP = ("x", "z", "core")
VMEM = 56 << 20
BF16, F32 = jnp.bfloat16, jnp.float32
BOTH_LAST = (((1,), (1,)), ((), ()))
BOTH_FIRST = (((0,), (0,)), ((), ()))


def cut_kernel(owner_ref, row_ref, cache_ref, out_ref):
    rows = cache_ref.shape[0]
    stretches, neigh = owner_ref.shape
    lane = lax.broadcasted_iota(jnp.int32, (TILE, HEAD_DIM), 1)
    named = jnp.zeros((TILE, HEAD_DIM), F32)
    for s in range(stretches):
        for n in range(neigh):
            at = s * neigh + n
            named = jnp.where(lane == at, owner_ref[s, n].astype(F32), named)
            named = jnp.where(lane == at + stretches * neigh, row_ref[s, n].astype(F32), named)
    for tile in range(out_ref.shape[0]):
        out_ref[tile, :rows] = cache_ref[:, 0, tile * TILE : (tile + 1) * TILE]
        out_ref[tile, rows] = named.astype(BF16)


def cut(nb_owner, nb_row, cache):
    rows, _, nb_len, width = cache.shape
    tiles, heads = nb_len // TILE, width // HEAD_DIM
    return pl.pallas_call(
        cut_kernel,
        grid=(2, heads),
        in_specs=[
            pl.BlockSpec(memory_space=pltpu.SMEM),
            pl.BlockSpec(memory_space=pltpu.SMEM),
            pl.BlockSpec((rows, 1, nb_len, HEAD_DIM), lambda a, h: (0, a, 0, h)),
        ],
        out_specs=pl.BlockSpec((tiles, rows + 1, TILE, HEAD_DIM), lambda a, h: (a * heads + h, 0, 0, 0)),
        out_shape=jax.ShapeDtypeStruct((2 * heads * tiles, rows + 1, TILE, HEAD_DIM), BF16),
        compiler_params=pltpu.CompilerParams(vmem_limit_bytes=VMEM),
        cost_estimate=pl.CostEstimate(flops=0, bytes_accessed=4 << 20, transcendentals=0),
        name="cut",
    )(nb_owner, nb_row, cache)


def pick_kernel(ids_ref, tiles_ref, out_ref, *, slots):
    base = pl.program_id(0) * slots
    for slot in range(slots):
        out_ref[slot] = tiles_ref[ids_ref[base + slot]]


def pick(ids, tiles):
    count, slots = ids.shape[0], 64
    return pl.pallas_call(
        functools.partial(pick_kernel, slots=slots),
        grid_spec=pltpu.PrefetchScalarGridSpec(
            num_scalar_prefetch=1,
            grid=(count // slots,),
            in_specs=[pl.BlockSpec(tiles.shape, lambda s, ids: (0, 0, 0))],
            out_specs=pl.BlockSpec((slots,) + tiles.shape[1:], lambda s, ids: (s, 0, 0)),
        ),
        out_shape=jax.ShapeDtypeStruct((count,) + tiles.shape[1:], tiles.dtype),
        compiler_params=pltpu.CompilerParams(vmem_limit_bytes=VMEM),
        cost_estimate=pl.CostEstimate(flops=0, bytes_accessed=6 << 20, transcendentals=0),
        name="pick",
    )(ids, tiles)


def attend_kernel(q_ref, g_ref, kv_ref, out_ref, dq_ref, *, heads):
    scale = HEAD_DIM ** (-0.5)
    cols = [slice(h * HEAD_DIM, (h + 1) * HEAD_DIM) for h in range(heads)]
    keys = [kv_ref[0, h].reshape(-1, HEAD_DIM) for h in range(heads)]
    values = [kv_ref[1, h].reshape(-1, HEAD_DIM) for h in range(heads)]
    scores = [
        lax.dot_general(q_ref[:, c], k, BOTH_LAST, preferred_element_type=F32)
        for c, k in zip(cols, keys)
    ]
    dprobs = [
        lax.dot_general(g_ref[:, c], v, BOTH_LAST, preferred_element_type=F32)
        for c, v in zip(cols, values)
    ]
    probs, dscores = [], []
    for score, dprob in zip(scores, dprobs):
        score = score * scale
        exps = jnp.exp(score - jnp.max(score, axis=-1, keepdims=True))
        prob = exps * (1.0 / jnp.sum(exps, axis=-1, keepdims=True))
        delta = jnp.sum(dprob * prob, axis=-1, keepdims=True)
        probs.append(prob.astype(BF16))
        dscores.append((prob * (dprob - delta) * scale).astype(BF16))
    for c, k, v, prob, dscore in zip(cols, keys, values, probs, dscores):
        out_ref[:, c] = jnp.dot(prob, v, preferred_element_type=F32).astype(BF16)
        dq_ref[:, c] = jnp.dot(dscore, k, preferred_element_type=F32).astype(BF16)


def attend(q, g, kv, neigh):
    rows, width = q.shape
    count = rows // STRETCH
    _, heads, tiles, slots, _, _ = kv.shape
    block = pl.BlockSpec((STRETCH, width), lambda c: (c, 0))
    return pl.pallas_call(
        functools.partial(attend_kernel, heads=heads),
        grid=(count,),
        in_specs=[
            block,
            block,
            pl.BlockSpec((2, heads, tiles, neigh, TILE, HEAD_DIM), lambda c: (0, 0, 0, c, 0, 0)),
        ],
        out_specs=[block, block],
        out_shape=[jax.ShapeDtypeStruct(q.shape, BF16)] * 2,
        compiler_params=pltpu.CompilerParams(vmem_limit_bytes=VMEM),
        cost_estimate=pl.CostEstimate(
            flops=10 * rows * width * neigh * tiles * TILE, bytes_accessed=kv.size * 2, transcendentals=0
        ),
        name="attend",
    )(q, g, kv)


def step(array, axis, by):
    size = lax.axis_size(axis)
    return lax.ppermute(array, axis, [(i, (i + by) % size) for i in range(size)])


def local(inputs, w_query, cache_kv, nb_owner, nb_row, out_grad):
    nx, nz, nc = (lax.axis_size(a) for a in DP)
    ndp, nmp = nx * nz * nc, lax.axis_size("mp")
    mx, mz, mc = (lax.axis_index(a) for a in DP)
    my = lax.axis_index("mp")
    tokens, grad_rows = inputs[0], out_grad[0]
    length, d = tokens.shape
    width = w_query.shape[1]
    heads = width // HEAD_DIM
    db_rows, _, nb_len, _ = cache_kv.shape
    _, stretches, neigh = nb_owner.shape
    requests = stretches * neigh
    tiles = nb_len // TILE
    real = length - LEAD

    message = cut(nb_owner[0], nb_row[0], cache_kv)
    held = lax.all_to_all(message, DP, split_axis=0, concat_axis=0, tiled=True)
    named = held[:, db_rows, 0, : 2 * requests].astype(jnp.int32)
    ids = named[:, :requests] * (db_rows + 1) + named[:, requests:]
    send = pick(ids.reshape(-1), held.reshape(-1, TILE, HEAD_DIM))
    got = lax.all_to_all(
        send.reshape(ndp, requests, TILE, HEAD_DIM), DP, split_axis=0, concat_axis=0, tiled=True
    )

    def shifted(array):
        return jnp.concatenate([array[LEAD:], jnp.zeros((LEAD, array.shape[1]), array.dtype)], 0)

    q = shifted(jnp.dot(tokens, w_query, preferred_element_type=F32).astype(BF16))
    g = shifted(grad_rows)

    late, weights, _ = lax.optimization_barrier((tokens, w_query, held))
    block = d // nx
    share = [lax.dynamic_slice(late, (SKIP, (mx + by) % nx * block), (length - SKIP, block)) for by in range(nx)]
    share = [step(a, "x", by) if by else a for by, a in enumerate(share)]
    block = d // nmp
    fans = [lax.dynamic_slice(weights, ((my + by) % nmp * block, 0), (block, width)) for by in range(nmp)]
    fans = [step(a, "mp", by) if by else a for by, a in enumerate(fans)]

    out, dq = attend(q, g, got.reshape(2, heads, tiles, requests, TILE, HEAD_DIM), neigh)
    dq = jnp.concatenate([jnp.zeros((LEAD - SKIP, width), BF16), dq[:real]], 0)

    total = 0.0
    for by in range(nx):
        near = step(dq, "x", by) if by else dq
        total += lax.dot_general(share[by], near, BOTH_FIRST, preferred_element_type=F32)
    total = total.reshape(nz, nc, -1, width)
    mine = lax.dynamic_index_in_dim(total, mc, 1, keepdims=False)
    mine += step(lax.dynamic_index_in_dim(total, 1 - mc, 1, keepdims=False), "core", 1)
    query_grad = lax.dynamic_index_in_dim(mine, mz, 0, keepdims=False)
    for by in range(1, nz):
        query_grad += step(lax.dynamic_index_in_dim(mine, (mz + by) % nz, 0, keepdims=False), "z", by)

    part = 0.0
    for by in range(nmp):
        near = step(dq, "mp", by) if by else dq
        part += lax.dot_general(near, fans[by], BOTH_LAST, preferred_element_type=F32).astype(BF16).astype(F32)
    part = part.astype(BF16)
    attended = jnp.concatenate([jnp.zeros((LEAD, width), BF16), out[:real]], 0)
    input_grad = jnp.concatenate([jnp.zeros((SKIP, d // nmp), BF16), part], 0)
    return attended[None], input_grad[None], query_grad


def solution(mesh):
    fine = Mesh(mesh.devices.reshape(4, 8, 2, 4), ("x", "z", "core", "mp"))
    return jax.shard_map(
        local,
        mesh=fine,
        in_specs=(
            P(DP, None, None),
            P(None, "mp"),
            P(DP, None, None, "mp"),
            P(DP, None, None),
            P(DP, None, None),
            P(DP, None, "mp"),
        ),
        out_specs=(P(DP, None, "mp"), P(DP, None, "mp"), P(DP, "mp")),
        check_vma=False,
    )
```

time: 387 us -> 327 us (0.84)
  waiting for transfers between devices: 72.7 us -> 151 us
  blocking collectives: 136 us -> 68.3 us
  Pallas kernels: 44.3 us -> 23.1 us
  local copies, waits for them, and re-layouts: 34.3 us -> 16.8 us
  between operations: 14.1 us -> 0.9 us
  matrix products: 27.9 us -> 17.8 us
  starting transfers between devices: 50.2 us -> 42.5 us
    all_gather x2 -> x0, blocking collectives: 136 us -> none  [the longest x1 79.9 us: local(): ids = lax.all_gather(own_ids, DP, tiled=False)]
    ppermute x0 -> x20, waiting for transfers between devices: none -> 70.1 us  [step(): lax.ppermute(array, axis, [(i, (i + by) % size) for i in range(size)])]
    all_to_all x0 -> x1, blocking collectives: none -> 68.3 us  [local(): held = lax.all_to_all(message, DP, split_axis=0, concat_axis=0, tiled=True)]
    all_to_all x8 -> x1, starting transfers between devices: 49.8 us -> 6.47 us  [local(): lax.all_to_all(send.reshape(ndp, requests, TILE, HEAD_DIM), DP, split_axi...]
    ppermute x0 -> x20, starting transfers between devices: none -> 36 us  [step(): lax.ppermute(array, axis, [(i, (i + by) % size) for i in range(size)])]
    pallas_call x3 -> x1, Pallas kernels: 23.3 us -> 8.69 us  [pick(): pl.pallas_call(functools.partial(pick_kernel, slots=slots), grid_spec=plt...]
    pallas_call x3 -> x1, Pallas kernels: 21 us -> 8.58 us  [attend(): pl.pallas_call(functools.partial(attend_kernel, heads=heads), grid=(count...]
    reshape x8 -> x1, local copies, waits for them, and re-layouts: 13 us -> 0.85 us  [local(): send = pick(ids.reshape(-1), held.reshape(-1, TILE, HEAD_DIM))]
  transfers between devices with their start and end apart: 11 -> 21, of which waited for: 5 -> 12; matrix products, arithmetic and copies ran while one was open for 16% -> 10% of each run, Pallas kernels for 11% -> 3%
where the time goes in v2:
time: 327 us; the launch traced here: 323 us
  waiting for transfers between devices  151 us (46%)
  blocking collectives  68.3 us (21%)
  starting transfers between devices  42.5 us (13%)
  Pallas kernels  23.1 us (7%)
  matrix products  17.8 us (5%)
  local copies, waits for them, and re-layouts  16.8 us (5%)
    all_to_all x1, waiting for transfers between devices, local(): lax.all_to_all(send.reshape(ndp, requests, TILE, HEAD_DIM), DP, split_axi...  80.8 us
    ppermute x20, waiting for transfers between devices, step(): lax.ppermute(array, axis, [(i, (i + by) % size) for i in range(size)])  70.1 us
    all_to_all x1, blocking collectives, local(): held = lax.all_to_all(message, DP, split_axis=0, concat_axis=0, tiled=True)  68.3 us
    ppermute x20, starting transfers between devices, step(): lax.ppermute(array, axis, [(i, (i + by) % size) for i in range(size)])  36 us
    pallas_call x1, Pallas kernels, pick(): pl.pallas_call(functools.partial(pick_kernel, slots=slots), grid_spec=plt...  8.69 us
    pallas_call x1, Pallas kernels, attend(): pl.pallas_call(functools.partial(attend_kernel, heads=heads), grid=(count...  8.58 us
    dot_general x4, matrix products, local(): lax.dot_general(share[by], near, BOTH_FIRST, preferred_element_type=F32)  6.67 us
    dot_general x4, matrix products, local(): lax.dot_general(near, fans[by], BOTH_LAST, preferred_element_type=F32)  6.62 us
  transfers between devices with their start and end apart: 21, of which 12 were waited for; matrix products, arithmetic and copies ran while one was open for 10% of the time, Pallas kernels for 3%

profile of v2, /device:TPU:32, one launch (start us, length us, event | category | flops | bytes accessed | tf_op | source)
XLA Modules:
  0.0 322.7 jit_solution(2467508779555644867)
XLA Ops:
  3.3 5.8 %cut.1 = bf16[64,9,16,128]{3,2,1,0:T(8,128)(2,1)} custom-call(s32[8,2]{1,0:T(8,128)} %copy.11.owner_ref, s32[8,2]{1,0:T(8,128)} %copy.12.row_ref, bf16[8,2,128,512]{3,2,1,0:T(8,128)(2,1)} %cache_ref.1), custom_call_target="tpu_custom_call" | custom-call | bytes 4194304 | tf_op jit(solution)/shard_map/cut/pallas_call | solution.py:41
  9.1 68.3 %all_to_all.10 = bf16[64,9,16,128]{3,2,1,0:T(8,128)(2,1)S(1)} all-to-all(bf16[64,9,16,128]{3,2,1,0:T(8,128)(2,1)} %cut.1), channel_id=1, replica_groups=mesh['x'=4,'z'=8,'core'=2,'mp'=4] {'x','z','core'}, dimensions={0} | all-to-all | bytes 4718592 | tf_op jit(solution)/shard_map/all_to_all | solution.py:150
  78.9 8.7 %pick.1 = bf16[1024,16,128]{2,1,0:T(8,128)(2,1)} custom-call(s32[1024]{0:T(1024)} %reshape.24.ids_ref, bf16[576,16,128]{2,1,0:T(8,128)(2,1)} %bitcast.62), custom_call_target="tpu_custom_call" | custom-call | bytes 6291456 | tf_op jit(solution)/shard_map/pick/pallas_call | solution.py:65
  87.5 6.5 %all-to-all-start.1 = ((bf16[64,16,16,128]{3,2,1,0:T(8,128)(2,1)}), bf16[64,16,16,128]{3,2,1,0:T(8,128)(2,1)}, u32[]{:S(2)}, u32[]{:S(2)}) async-start(bf16[64,16,16,128]{3,2,1,0:T(8,128)(2,1)} %bitcast.61), calls=%async_computation.1 | async-start | bytes 8388608 | tf_op jit(solution)/shard_map/all_to_all | solution.py:154
  97.9 4.5 %fusion.11 = bf16[512,512]{1,0:T(8,128)(2,1)S(1)} fusion(bf16[4096,512]{1,0:T(8,128)(2,1)} %param.7, bf16[1,512,4096]{2,1,0:T(8,128)(2,1)S(1)} %copy-done.1), kind=kOutput, calls=%fused_computation.40 | convolution fusion | flops 2147483648 | bytes 8912896 | tf_op jit(solution)/shard_map/dot_general | solution.py:161
  102.4 3.0 collective-permute-start.8
  107.3 80.8 %all-to-all-done.1 = bf16[64,16,16,128]{3,2,1,0:T(8,128)(2,1)} async-done(((bf16[64,16,16,128]{3,2,1,0:T(8,128)(2,1)}), bf16[64,16,16,128]{3,2,1,0:T(8,128)(2,1)}, u32[]{:S(2)}, u32[]{:S(2)}) %all-to-all-start.1) | async-done | bytes 4194336 | tf_op jit(solution)/shard_map/all_to_all | solution.py:154
  188.1 8.6 %attend.1 = (bf16[512,512]{1,0:T(8,128)(2,1)}, bf16[512,512]{1,0:T(8,128)(2,1)}) custom-call(bf16[512,512]{1,0:T(8,128)(2,1)} %concatenate.15.q_ref, bf16[512,512]{1,0:T(8,128)(2,1)} %concatenate.16.g_ref, bf16[2,4,8,16,16,128]{5,4,3,2,1,0:T(8,128)(2,1)} %bitcast.7.kv_ref), custom_call_target="tpu_custom_call" | custom-call | flops 671088640 | bytes 4194304 | tf_op jit(solution)/shard_map/attend/pallas_call | solution.py:111
  201.9 3.6 %constant_dynamic-slice_fusion = (bf16[1024,512]{1,0:T(8,128)(2,1)}, bf16[1024,512]{1,0:T(8,128)(2,1)}, bf16[1024,512]{1,0:T(8,128)(2,1)}) fusion(bf16[4096,512]{1,0:T(8,128)(2,1)} %param.7, s32[]{:T(128)S(6)} %select_n.126, s32[]{:T(128)S(6)} %select_n.124, s32[]{:T(128)S(6)} %select_n.122), kind=kLoop, calls=%fused_computation.32 | loop fusion | bytes 6291468 | tf_op jit(solution)/shard_map/dynamic_slice | solution.py:169
  210.8 3.0 collective-permute-done.7
  217.5 3.3 %collective-permute-start.3 = (bf16[1024,512]{1,0:T(8,128)(2,1)}, bf16[1024,512]{1,0:T(8,128)(2,1)}, u32[]{:S(2)}, u32[]{:S(2)}) collective-permute-start(bf16[1024,512]{1,0:T(8,128)(2,1)} %get-tuple-element.15), channel_id=1, source_target_pairs={{0,2},{1,3},{2,0},{3,1},{4,6},{5,7},{6,4},{7,5},{8,10},{9,11},{10,... | collective-permute-start | bytes 3145736 | tf_op jit(solution)/shard_map/ppermute | solution.py:131
  220.8 4.2 %collective-permute-done.9 = bf16[464,512]{1,0:T(8,128)(2,1)S(1)} collective-permute-done((bf16[464,512]{1,0:T(8,128)(2,1)}, bf16[464,512]{1,0:T(8,128)(2,1)S(1)}, u32[]{:S(2)}, u32[]{:S(2)}) %collective-permute-start.9) | collective-permute-done | bytes 475168 | tf_op jit(solution)/shard_map/ppermute | solution.py:131
  228.4 4.8 %collective-permute-done.10 = bf16[464,1024]{1,0:T(8,128)(2,1)S(1)} collective-permute-done((bf16[464,1024]{1,0:T(8,128)(2,1)S(1)}, bf16[464,1024]{1,0:T(8,128)(2,1)S(1)}, u32[]{:S(2)}, u32[]{:S(2)}) %collective-permute-start.10) | collective-permute-done | bytes 950304 | tf_op jit(solution)/shard_map/ppermute | solution.py:131
  233.2 10.9 %collective-permute-done.11 = bf16[464,512]{1,0:T(8,128)(2,1)S(1)} collective-permute-done((bf16[464,512]{1,0:T(8,128)(2,1)}, bf16[464,512]{1,0:T(8,128)(2,1)S(1)}, u32[]{:S(2)}, u32[]{:S(2)}) %collective-permute-start.11) | collective-permute-done | bytes 475168 | tf_op jit(solution)/shard_map/ppermute | solution.py:131
  246.0 3.2 collective-permute-start.2
  253.2 15.5 %collective-permute-done = bf16[464,512]{1,0:T(8,128)(2,1)} collective-permute-done((bf16[464,512]{1,0:T(8,128)(2,1)}, bf16[464,512]{1,0:T(8,128)(2,1)}, u32[]{:S(2)}, u32[]{:S(2)}) %collective-permute-start) | collective-permute-done | bytes 475168 | tf_op jit(solution)/shard_map/ppermute | solution.py:131
  268.7 2.5 collective-permute-start.4
  273.3 6.7 %collective-permute-done.2 = bf16[464,512]{1,0:T(8,128)(2,1)S(1)} collective-permute-done((bf16[464,512]{1,0:T(8,128)(2,1)}, bf16[464,512]{1,0:T(8,128)(2,1)S(1)}, u32[]{:S(2)}, u32[]{:S(2)}) %collective-permute-start.2) | collective-permute-done | bytes 475168 | tf_op jit(solution)/shard_map/ppermute | solution.py:131
  285.0 9.0 %collective-permute-done.4 = bf16[464,512]{1,0:T(8,128)(2,1)S(1)} collective-permute-done((bf16[464,512]{1,0:T(8,128)(2,1)}, bf16[464,512]{1,0:T(8,128)(2,1)S(1)}, u32[]{:S(2)}, u32[]{:S(2)}) %collective-permute-start.4) | collective-permute-done | bytes 475168 | tf_op jit(solution)/shard_map/ppermute | solution.py:131
  296.5 4.2 %collective-permute-start.16 = (f32[64,512]{1,0:T(8,128)S(1)}, f32[64,512]{1,0:T(8,128)S(1)}, u32[]{:S(2)}, u32[]{:S(2)}) collective-permute-start(f32[64,512]{1,0:T(8,128)S(1)} %get-tuple-element.21), channel_id=1, source_target_pairs={{0,32},{8,40},{16,48},{24,56},{32,0},{40,8},{48,16},{56,24},{1,33}... | collective-permute-start | bytes 393224 | tf_op jit(solution)/shard_map/ppermute | solution.py:131
  302.4 2.4 collective-permute-start.19
  307.8 2.7 collective-permute-done.16
  310.5 8.2 %collective-permute-done.17 = f32[64,512]{1,0:T(8,128)S(1)} collective-permute-done((f32[64,512]{1,0:T(8,128)S(1)}, f32[64,512]{1,0:T(8,128)S(1)}, u32[]{:S(2)}, u32[]{:S(2)}) %collective-permute-start.17) | collective-permute-done | bytes 131104 | tf_op jit(solution)/shard_map/ppermute | solution.py:131
  318.7 3.3 %collective-permute-done.19 = f32[64,512]{1,0:T(8,128)S(1)} collective-permute-done((f32[64,512]{1,0:T(8,128)S(1)}, f32[64,512]{1,0:T(8,128)S(1)}, u32[]{:S(2)}, u32[]{:S(2)}) %collective-permute-start.19) | collective-permute-done | bytes 131104 | tf_op jit(solution)/shard_map/ppermute | solution.py:131
  (61 shorter events, 48.3 us)
Async XLA Ops:
  87.5 100.6 %all-to-all-start.1 = ((bf16[64,16,16,128]{3,2,1,0:T(8,128)(2,1)}), bf16[64,16,16,128]{3,2,1,0:T(8,128)(2,1)}, u32[]{:S(2)}, u32[]{:S(2)}) async-start(bf16[64,16,16,128]{3,2,1,0:T(8,128)(2,1)} %bitcast.61), calls=%async_computation.1 | async-start | bytes 8388608 | tf_op jit(solution)/shard_map/all_to_all | solution.py:154
  96.3 9.1 %copy-start.3 = (bf16[1,512,512]{2,1,0:T(8,128)(2,1)S(1)}, bf16[1,512,512]{2,1,0:T(8,128)(2,1)}, u32[]{:S(2)}) copy-start(bf16[1,512,512]{2,1,0:T(8,128)(2,1)} %param.11) | copy-start | bytes 1572868
  96.3 112.8 %collective-permute-start.6 = (bf16[464,1024]{1,0:T(8,128)(2,1)S(1)}, bf16[464,1024]{1,0:T(8,128)(2,1)}, u32[]{:S(2)}, u32[]{:S(2)}) collective-permute-start(bf16[464,1024]{1,0:T(8,128)(2,1)S(1)} %get-tuple-element.11), channel_id=1, source_target_pairs={{0,64},{64,128},{128,192},{192,0},{1,65},{65,129},{129,193},{193,1... | collective-permute-start | bytes 2850824 | tf_op jit(solution)/shard_map/ppermute | solution.py:131
  102.4 115.0 %collective-permute-start.8 = (bf16[464,1024]{1,0:T(8,128)(2,1)S(1)}, bf16[464,1024]{1,0:T(8,128)(2,1)}, u32[]{:S(2)}, u32[]{:S(2)}) collective-permute-start(bf16[464,1024]{1,0:T(8,128)(2,1)S(1)} %get-tuple-element.13), channel_id=1, source_target_pairs={{0,128},{64,192},{128,0},{192,64},{1,129},{65,193},{129,1},{193,65... | collective-permute-start | bytes 2850824 | tf_op jit(solution)/shard_map/ppermute | solution.py:131
  198.6 15.2 %collective-permute-start.7 = (bf16[464,512]{1,0:T(8,128)(2,1)}, bf16[464,512]{1,0:T(8,128)(2,1)}, u32[]{:S(2)}, u32[]{:S(2)}) collective-permute-start(bf16[464,512]{1,0:T(8,128)(2,1)} %concatenate.18), channel_id=1, source_target_pairs={{0,64},{64,128},{128,192},{192,0},{1,65},{65,129},{129,193},{193,1... | collective-permute-start | bytes 1425416 | tf_op jit(solution)/shard_map/ppermute | solution.py:131
  200.0 33.2 %collective-permute-start.10 = (bf16[464,1024]{1,0:T(8,128)(2,1)S(1)}, bf16[464,1024]{1,0:T(8,128)(2,1)S(1)}, u32[]{:S(2)}, u32[]{:S(2)}) collective-permute-start(bf16[464,1024]{1,0:T(8,128)(2,1)S(1)} %get-tuple-element.12), channel_id=1, source_target_pairs={{0,192},{64,0},{128,64},{192,128},{1,193},{65,1},{129,65},{193,129... | collective-permute-start | bytes 2850824 | tf_op jit(solution)/shard_map/ppermute | solution.py:131
  205.4 19.5 %collective-permute-start.9 = (bf16[464,512]{1,0:T(8,128)(2,1)}, bf16[464,512]{1,0:T(8,128)(2,1)S(1)}, u32[]{:S(2)}, u32[]{:S(2)}) collective-permute-start(bf16[464,512]{1,0:T(8,128)(2,1)} %concatenate.18), channel_id=1, source_target_pairs={{0,128},{64,192},{128,0},{192,64},{1,129},{65,193},{129,1},{193,65... | collective-permute-start | bytes 1425416 | tf_op jit(solution)/shard_map/ppermute | solution.py:131
  209.2 42.0 %collective-permute-start.1 = (bf16[1024,512]{1,0:T(8,128)(2,1)}, bf16[1024,512]{1,0:T(8,128)(2,1)}, u32[]{:S(2)}, u32[]{:S(2)}) collective-permute-start(bf16[1024,512]{1,0:T(8,128)(2,1)} %get-tuple-element.16), channel_id=1, source_target_pairs={{0,1},{1,2},{2,3},{3,0},{4,5},{5,6},{6,7},{7,4},{8,9},{9,10},{10,1... | collective-permute-start | bytes 3145736 | tf_op jit(solution)/shard_map/ppermute | solution.py:131
  213.8 30.3 %collective-permute-start.11 = (bf16[464,512]{1,0:T(8,128)(2,1)}, bf16[464,512]{1,0:T(8,128)(2,1)S(1)}, u32[]{:S(2)}, u32[]{:S(2)}) collective-permute-start(bf16[464,512]{1,0:T(8,128)(2,1)} %concatenate.18), channel_id=1, source_target_pairs={{0,192},{64,0},{128,64},{192,128},{1,193},{65,1},{129,65},{193,129... | collective-permute-start | bytes 1425416 | tf_op jit(solution)/shard_map/ppermute | solution.py:131
  217.5 55.9 %collective-permute-start.3 = (bf16[1024,512]{1,0:T(8,128)(2,1)}, bf16[1024,512]{1,0:T(8,128)(2,1)}, u32[]{:S(2)}, u32[]{:S(2)}) collective-permute-start(bf16[1024,512]{1,0:T(8,128)(2,1)} %get-tuple-element.15), channel_id=1, source_target_pairs={{0,2},{1,3},{2,0},{3,1},{4,6},{5,7},{6,4},{7,5},{8,10},{9,11},{10,... | collective-permute-start | bytes 3145736 | tf_op jit(solution)/shard_map/ppermute | solution.py:131
  224.9 43.8 %collective-permute-start = (bf16[464,512]{1,0:T(8,128)(2,1)}, bf16[464,512]{1,0:T(8,128)(2,1)}, u32[]{:S(2)}, u32[]{:S(2)}) collective-permute-start(bf16[464,512]{1,0:T(8,128)(2,1)} %concatenate.18), channel_id=1, source_target_pairs={{0,1},{1,2},{2,3},{3,0},{4,5},{5,6},{6,7},{7,4},{8,9},{9,10},{10,1... | collective-permute-start | bytes 1425416 | tf_op jit(solution)/shard_map/ppermute | solution.py:131
  244.8 6.3 %copy-start.4 = (bf16[512,512]{1,0:T(8,128)(2,1)S(1)}, bf16[512,512]{1,0:T(8,128)(2,1)}, u32[]{:S(2)}) copy-start(bf16[512,512]{1,0:T(8,128)(2,1)} %get-tuple-element.7) | copy-start | bytes 1572868
  246.0 36.0 %collective-permute-start.12 = (f32[8,64,512]{2,1,0:T(8,128)}, f32[8,64,512]{2,1,0:T(8,128)}, u32[]{:S(2)}, u32[]{:S(2)}) collective-permute-start(f32[8,64,512]{2,1,0:T(8,128)} %dynamic-slice_bitcast_fusion), channel_id=1, source_target_pairs={{0,4},{4,0},{1,5},{5,1},{2,6},{6,2},{3,7},{7,3},{8,12},{12,8},{9,1... | collective-permute-start | bytes 3145736 | tf_op jit(solution)/shard_map/ppermute | solution.py:131
  246.0 5.2 %copy-start.2 = (bf16[1024,512]{1,0:T(8,128)(2,1)S(1)}, bf16[1024,512]{1,0:T(8,128)(2,1)}, u32[]{:S(2)}) copy-start(bf16[1024,512]{1,0:T(8,128)(2,1)} %get-tuple-element.14) | copy-start | bytes 3145732
  246.0 34.0 %collective-permute-start.2 = (bf16[464,512]{1,0:T(8,128)(2,1)}, bf16[464,512]{1,0:T(8,128)(2,1)S(1)}, u32[]{:S(2)}, u32[]{:S(2)}) collective-permute-start(bf16[464,512]{1,0:T(8,128)(2,1)} %concatenate.18), channel_id=1, source_target_pairs={{0,2},{1,3},{2,0},{3,1},{4,6},{5,7},{6,4},{7,5},{8,10},{9,11},{10,... | collective-permute-start | bytes 1425416 | tf_op jit(solution)/shard_map/ppermute | solution.py:131
  251.2 33.8 %collective-permute-start.5 = (bf16[1024,512]{1,0:T(8,128)(2,1)S(1)}, bf16[1024,512]{1,0:T(8,128)(2,1)S(1)}, u32[]{:S(2)}, u32[]{:S(2)}) collective-permute-start(bf16[1024,512]{1,0:T(8,128)(2,1)S(1)} %copy-done.2), channel_id=1, source_target_pairs={{0,3},{1,0},{2,1},{3,2},{4,7},{5,4},{6,5},{7,6},{8,11},{9,8},{10,9... | collective-permute-start | bytes 3145736 | tf_op jit(solution)/shard_map/ppermute | solution.py:131
  268.7 25.3 %collective-permute-start.4 = (bf16[464,512]{1,0:T(8,128)(2,1)}, bf16[464,512]{1,0:T(8,128)(2,1)S(1)}, u32[]{:S(2)}, u32[]{:S(2)}) collective-permute-start(bf16[464,512]{1,0:T(8,128)(2,1)} %concatenate.18), channel_id=1, source_target_pairs={{0,3},{1,0},{2,1},{3,2},{4,7},{5,4},{6,5},{7,6},{8,11},{9,8},{10,9... | collective-permute-start | bytes 1425416 | tf_op jit(solution)/shard_map/ppermute | solution.py:131
  283.5 18.8 %collective-permute-start.13 = (f32[64,512]{1,0:T(8,128)S(1)}, f32[64,512]{1,0:T(8,128)S(1)}, u32[]{:S(2)}, u32[]{:S(2)}) collective-permute-start(f32[64,512]{1,0:T(8,128)S(1)} %get-tuple-element.17), channel_id=1, source_target_pairs={{0,8},{8,16},{16,24},{24,32},{32,40},{40,48},{48,56},{56,0},{1,9},... | collective-permute-start | bytes 393224 | tf_op jit(solution)/shard_map/ppermute | solution.py:131
  283.6 18.8 %collective-permute-start.14 = (f32[64,512]{1,0:T(8,128)S(1)}, f32[64,512]{1,0:T(8,128)S(1)}, u32[]{:S(2)}, u32[]{:S(2)}) collective-permute-start(f32[64,512]{1,0:T(8,128)S(1)} %get-tuple-element.23), channel_id=1, source_target_pairs={{0,16},{8,24},{16,32},{24,40},{32,48},{40,56},{48,0},{56,8},{1,17}... | collective-permute-start | bytes 393224 | tf_op jit(solution)/shard_map/ppermute | solution.py:131
  294.7 13.1 %collective-permute-start.15 = (f32[64,512]{1,0:T(8,128)S(1)}, f32[64,512]{1,0:T(8,128)S(1)}, u32[]{:S(2)}, u32[]{:S(2)}) collective-permute-start(f32[64,512]{1,0:T(8,128)S(1)} %get-tuple-element.22), channel_id=1, source_target_pairs={{0,24},{8,32},{16,40},{24,48},{32,56},{40,0},{48,8},{56,16},{1,25}... | collective-permute-start | bytes 393224 | tf_op jit(solution)/shard_map/ppermute | solution.py:131
  296.5 13.9 %collective-permute-start.16 = (f32[64,512]{1,0:T(8,128)S(1)}, f32[64,512]{1,0:T(8,128)S(1)}, u32[]{:S(2)}, u32[]{:S(2)}) collective-permute-start(f32[64,512]{1,0:T(8,128)S(1)} %get-tuple-element.21), channel_id=1, source_target_pairs={{0,32},{8,40},{16,48},{24,56},{32,0},{40,8},{48,16},{56,24},{1,33}... | collective-permute-start | bytes 393224 | tf_op jit(solution)/shard_map/ppermute | solution.py:131
  300.7 17.9 %collective-permute-start.17 = (f32[64,512]{1,0:T(8,128)S(1)}, f32[64,512]{1,0:T(8,128)S(1)}, u32[]{:S(2)}, u32[]{:S(2)}) collective-permute-start(f32[64,512]{1,0:T(8,128)S(1)} %get-tuple-element.20), channel_id=1, source_target_pairs={{0,40},{8,48},{16,56},{24,0},{32,8},{40,16},{48,24},{56,32},{1,41}... | collective-permute-start | bytes 393224 | tf_op jit(solution)/shard_map/ppermute | solution.py:131
  302.3 16.4 %collective-permute-start.18 = (f32[64,512]{1,0:T(8,128)S(1)}, f32[64,512]{1,0:T(8,128)S(1)}, u32[]{:S(2)}, u32[]{:S(2)}) collective-permute-start(f32[64,512]{1,0:T(8,128)S(1)} %get-tuple-element.19), channel_id=1, source_target_pairs={{0,48},{8,56},{16,0},{24,8},{32,16},{40,24},{48,32},{56,40},{1,49}... | collective-permute-start | bytes 393224 | tf_op jit(solution)/shard_map/ppermute | solution.py:131
  302.4 19.6 %collective-permute-start.19 = (f32[64,512]{1,0:T(8,128)S(1)}, f32[64,512]{1,0:T(8,128)S(1)}, u32[]{:S(2)}, u32[]{:S(2)}) collective-permute-start(f32[64,512]{1,0:T(8,128)S(1)} %get-tuple-element.18), channel_id=1, source_target_pairs={{0,56},{8,0},{16,8},{24,16},{32,24},{40,32},{48,40},{56,48},{1,57}... | collective-permute-start | bytes 393224 | tf_op jit(solution)/shard_map/ppermute | solution.py:131
  (2 other events, 5.2 us)

commit v3 on v2

--- a/solution.py
+++ b/solution.py
@@ -14,44 +14,47 @@
 TILE = 16
 SKIP = LEAD // TILE * TILE
 DP = ("x", "z", "core")
-VMEM = 56 << 20
+VMEM = 32 << 20
 BF16, F32 = jnp.bfloat16, jnp.float32
 BOTH_LAST = (((1,), (1,)), ((), ()))
 BOTH_FIRST = (((0,), (0,)), ((), ()))
 
 
-def cut_kernel(owner_ref, row_ref, cache_ref, out_ref):
+def cut_kernel(owner_ref, row_ref, cache_ref, out_ref, named_ref):
     rows = cache_ref.shape[0]
     stretches, neigh = owner_ref.shape
-    lane = lax.broadcasted_iota(jnp.int32, (TILE, HEAD_DIM), 1)
-    named = jnp.zeros((TILE, HEAD_DIM), F32)
-    for s in range(stretches):
-        for n in range(neigh):
-            at = s * neigh + n
-            named = jnp.where(lane == at, owner_ref[s, n].astype(F32), named)
-            named = jnp.where(lane == at + stretches * neigh, row_ref[s, n].astype(F32), named)
-    for tile in range(out_ref.shape[0]):
-        out_ref[tile, :rows] = cache_ref[:, 0, tile * TILE : (tile + 1) * TILE]
-        out_ref[tile, rows] = named.astype(BF16)
+    named_ref[...] = jnp.zeros_like(named_ref)
+    named_ref[:stretches, :neigh] = owner_ref[...].astype(F32)
+    named_ref[stretches : 2 * stretches, :neigh] = row_ref[...].astype(F32)
+    _, heads, tiles, _, _, _ = out_ref.shape
+    for head in range(heads):
+        cols = slice(head * HEAD_DIM, (head + 1) * HEAD_DIM)
+        for tile in range(tiles):
+            out_ref[0, head, tile, :rows] = cache_ref[:, 0, tile * TILE : (tile + 1) * TILE, cols]
+            out_ref[0, head, tile, rows] = named_ref[...].astype(BF16)
 
 
 def cut(nb_owner, nb_row, cache):
     rows, _, nb_len, width = cache.shape
-    tiles, heads = nb_len // TILE, width // HEAD_DIM
+    tiles, heads, parts = nb_len // TILE, width // HEAD_DIM, 2
+    named = pl.BlockSpec(nb_owner.shape, lambda a, t: (0, 0))
     return pl.pallas_call(
         cut_kernel,
-        grid=(2, heads),
+        grid=(2, parts),
         in_specs=[
-            pl.BlockSpec(memory_space=pltpu.SMEM),
-            pl.BlockSpec(memory_space=pltpu.SMEM),
-            pl.BlockSpec((rows, 1, nb_len, HEAD_DIM), lambda a, h: (0, a, 0, h)),
+            named,
+            named,
+            pl.BlockSpec((rows, 1, nb_len // parts, width), lambda a, t: (0, a, t, 0)),
         ],
-        out_specs=pl.BlockSpec((tiles, rows + 1, TILE, HEAD_DIM), lambda a, h: (a * heads + h, 0, 0, 0)),
-        out_shape=jax.ShapeDtypeStruct((2 * heads * tiles, rows + 1, TILE, HEAD_DIM), BF16),
+        out_specs=pl.BlockSpec(
+            (1, heads, tiles // parts, rows + 1, TILE, HEAD_DIM), lambda a, t: (a, 0, t, 0, 0, 0)
+        ),
+        out_shape=jax.ShapeDtypeStruct((2, heads, tiles, rows + 1, TILE, HEAD_DIM), BF16),
+        scratch_shapes=[pltpu.VMEM((TILE, HEAD_DIM), F32)],
         compiler_params=pltpu.CompilerParams(vmem_limit_bytes=VMEM),
         cost_estimate=pl.CostEstimate(flops=0, bytes_accessed=4 << 20, transcendentals=0),
         name="cut",
-    )(nb_owner, nb_row, cache)
+    )(nb_owner, nb_row, cache).reshape(-1, rows + 1, TILE, HEAD_DIM)
 
 
 def pick_kernel(ids_ref, tiles_ref, out_ref, *, slots):
@@ -148,26 +151,30 @@
 
     message = cut(nb_owner[0], nb_row[0], cache_kv)
     held = lax.all_to_all(message, DP, split_axis=0, concat_axis=0, tiled=True)
-    named = held[:, db_rows, 0, : 2 * requests].astype(jnp.int32)
-    ids = named[:, :requests] * (db_rows + 1) + named[:, requests:]
+
+    block = d // nmp
+    fans = [lax.dynamic_slice(w_query, ((my + by) % nmp * block, 0), (block, width)) for by in range(nmp)]
+    fans = [step(a, "mp", by) if by else a for by, a in enumerate(fans)]
+    held, fans = lax.optimization_barrier((held, fans))
+
+    named = held[:, db_rows, : 2 * stretches, :neigh].astype(jnp.int32)
+    ids = named[:, :stretches] * (db_rows + 1) + named[:, stretches:]
     send = pick(ids.reshape(-1), held.reshape(-1, TILE, HEAD_DIM))
     got = lax.all_to_all(
         send.reshape(ndp, requests, TILE, HEAD_DIM), DP, split_axis=0, concat_axis=0, tiled=True
     )
 
-    def shifted(array):
-        return jnp.concatenate([array[LEAD:], jnp.zeros((LEAD, array.shape[1]), array.dtype)], 0)
-
-    q = shifted(jnp.dot(tokens, w_query, preferred_element_type=F32).astype(BF16))
-    g = shifted(grad_rows)
-
-    late, weights, _ = lax.optimization_barrier((tokens, w_query, held))
+    late, weights, grad_rows, _ = lax.optimization_barrier((tokens, w_query, grad_rows, held))
     block = d // nx
     share = [lax.dynamic_slice(late, (SKIP, (mx + by) % nx * block), (length - SKIP, block)) for by in range(nx)]
     share = [step(a, "x", by) if by else a for by, a in enumerate(share)]
-    block = d // nmp
-    fans = [lax.dynamic_slice(weights, ((my + by) % nmp * block, 0), (block, width)) for by in range(nmp)]
-    fans = [step(a, "mp", by) if by else a for by, a in enumerate(fans)]
+
+    def shifted(array):
+        return jnp.concatenate([array[LEAD:], jnp.zeros((LEAD, array.shape[1]), array.dtype)], 0)
+
+    q = shifted(jnp.dot(late, weights, preferred_element_type=F32).astype(BF16))
+    g = shifted(grad_rows)
+    got, share, q, g = lax.optimization_barrier((got, share, q, g))
 
     out, dq = attend(q, g, got.reshape(2, heads, tiles, requests, TILE, HEAD_DIM), neigh)
     dq = jnp.concatenate([jnp.zeros((LEAD - SKIP, width), BF16), dq[:real]], 0)

time: 327 us -> 271 us (0.83); the launches traced: 323 us -> 270 us
  blocking collectives: 68.3 us -> 0 us
  waiting for transfers between devices: 151 us -> 171 us
  Pallas kernels: 23.1 us -> 10.3 us
  starting transfers between devices: 42.5 us -> 53.1 us
  matrix products: 17.8 us -> 11.7 us
  local copies, waits for them, and re-layouts: 16.8 us -> 20.4 us
    ppermute x20, waiting for transfers between devices: 70.1 us -> 163 us  [step(): lax.ppermute(array, axis, [(i, (i + by) % size) for i in range(size)])]
    all_to_all x1, waiting for transfers between devices: 80.8 us -> 8.09 us  [local(): lax.all_to_all(send.reshape(ndp, requests, TILE, HEAD_DIM), DP, split_axi...]
    all_to_all x1 -> x0, blocking collectives: 68.3 us -> none  [local(): held = lax.all_to_all(message, DP, split_axis=0, concat_axis=0, tiled=True)]
    all_to_all x0 -> x1, starting transfers between devices: none -> 11.6 us  [local(): held = lax.all_to_all(message, DP, split_axis=0, concat_axis=0, tiled=True)]
    unnamed x10 -> x30, local copies, waits for them, and re-layouts: 0.49 us -> 9.32 us
    pallas_call x1, Pallas kernels: 8.69 us -> 1.9 us  [pick(): pl.pallas_call(functools.partial(pick_kernel, slots=slots), grid_spec=plt...]
    ppermute x20, starting transfers between devices: 36 us -> 30.9 us  [step(): lax.ppermute(array, axis, [(i, (i + by) % size) for i in range(size)])]
    pallas_call x1, Pallas kernels: 5.83 us -> 0.77 us  [cut(): pl.pallas_call(cut_kernel, grid=(2, parts), in_specs=[named, named, pl.Bl...]
  transfers between devices with their start and end apart: 21 -> 22, of which waited for: 12 -> 10; matrix products, arithmetic and copies ran while one was open for 10% -> 8% of each run, Pallas kernels for 3% -> 0%
where the time goes in v3:
time: 271 us; the launch traced here: 270 us
  waiting for transfers between devices  171 us (63%)
  starting transfers between devices  53.1 us (20%)
  local copies, waits for them, and re-layouts  20.4 us (8%)
  matrix products  11.7 us (4%)
  Pallas kernels  10.3 us (4%)
    ppermute x20, waiting for transfers between devices, step(): lax.ppermute(array, axis, [(i, (i + by) % size) for i in range(size)])  163 us
    ppermute x20, starting transfers between devices, step(): lax.ppermute(array, axis, [(i, (i + by) % size) for i in range(size)])  30.9 us
    all_to_all x1, starting transfers between devices, local(): held = lax.all_to_all(message, DP, split_axis=0, concat_axis=0, tiled=True)  11.6 us
    all_to_all x1, starting transfers between devices, local(): lax.all_to_all(send.reshape(ndp, requests, TILE, HEAD_DIM), DP, split_axi...  10.6 us
    unnamed x30, local copies, waits for them, and re-layouts  9.32 us
    all_to_all x1, waiting for transfers between devices, local(): lax.all_to_all(send.reshape(ndp, requests, TILE, HEAD_DIM), DP, split_axi...  8.09 us
    pallas_call x1, Pallas kernels, attend(): pl.pallas_call(functools.partial(attend_kernel, heads=heads), grid=(count...  7.63 us
  transfers between devices with their start and end apart: 22, of which 10 were waited for; matrix products, arithmetic and copies ran while one was open for 8% of the time, Pallas kernels for 0%

profile of v3, /device:TPU:32, one launch (start us, length us, event | category | flops | bytes accessed | tf_op | source)
XLA Modules:
  0.0 270.3 jit_solution(15203735352692317643)
XLA Ops:
  5.9 11.6 %all-to-all-start = ((bf16[64,9,16,128]{3,2,1,0:T(8,128)(2,1)}), bf16[64,9,16,128]{3,2,1,0:T(8,128)(2,1)S(1)}, u32[]{:S(2)}, u32[]{:S(2)}) async-start(bf16[64,9,16,128]{3,2,1,0:T(8,128)(2,1)} %bitcast.66), calls=%async_computation | async-start | bytes 4718592 | tf_op jit(solution)/shard_map/all_to_all | solution.py:153
  17.6 3.4 %constant_dynamic-slice_fusion = (bf16[1024,512]{1,0:T(8,128)(2,1)S(1)}, bf16[1024,512]{1,0:T(8,128)(2,1)S(1)}, bf16[1024,512]{1,0:T(8,128)(2,1)S(1)}, bf16[1024,512]{1,0:T(8,128)(2,1)}) fusion(bf16[4096,512]{1,0:T(8,128)(2,1)} %param.7, s32[]{:T(128)S(6)} %select_n.126, s32[]{:T(128)S(6)} %select_n.124, s32[]{:T(128)S(6)} %select_n.122, s32[]{:T(128)S(6)} %select_n.120), kind=kLoop, calls=%fused_computation.28 | loop fusion | bytes 8388624 | tf_op jit(solution)/shard_map/dynamic_slice | solution.py:156
  21.0 3.0 %collective-permute-start.2 = (bf16[1024,512]{1,0:T(8,128)(2,1)S(1)}, bf16[1024,512]{1,0:T(8,128)(2,1)S(1)}, u32[]{:S(2)}, u32[]{:S(2)}) collective-permute-start(bf16[1024,512]{1,0:T(8,128)(2,1)S(1)} %get-tuple-element.41), channel_id=1, source_target_pairs={{0,3},{1,0},{2,1},{3,2},{4,7},{5,4},{6,5},{7,6},{8,11},{9,8},{10,9... | collective-permute-start | bytes 3145736 | tf_op jit(solution)/shard_map/ppermute | solution.py:134
  25.6 43.6 %collective-permute-done.2 = bf16[1024,512]{1,0:T(8,128)(2,1)S(1)} collective-permute-done((bf16[1024,512]{1,0:T(8,128)(2,1)S(1)}, bf16[1024,512]{1,0:T(8,128)(2,1)S(1)}, u32[]{:S(2)}, u32[]{:S(2)}) %collective-permute-start.2) | collective-permute-done | bytes 1048608 | tf_op jit(solution)/shard_map/ppermute | solution.py:134
  75.2 2.0 copy-done
  77.3 10.6 %all-to-all-start.1 = ((bf16[64,16,16,128]{3,2,1,0:T(8,128)(2,1)}), bf16[64,16,16,128]{3,2,1,0:T(8,128)(2,1)}, u32[]{:S(2)}, u32[]{:S(2)}) async-start(bf16[64,16,16,128]{3,2,1,0:T(8,128)(2,1)} %bitcast.64), calls=%async_computation.1 | async-start | bytes 8388608 | tf_op jit(solution)/shard_map/all_to_all | solution.py:163
  88.0 2.6 constant_dynamic-slice_fusion.4
  90.6 3.0 %collective-permute-start.5 = (bf16[464,1024]{1,0:T(8,128)(2,1)S(1)}, bf16[464,1024]{1,0:T(8,128)(2,1)S(1)}, u32[]{:S(2)}, u32[]{:S(2)}) collective-permute-start(bf16[464,1024]{1,0:T(8,128)(2,1)S(1)} %get-tuple-element.37), channel_id=1, source_target_pairs={{0,192},{64,0},{128,64},{192,128},{1,193},{65,1},{129,65},{193,129... | collective-permute-start | bytes 2850824 | tf_op jit(solution)/shard_map/ppermute | solution.py:134
  95.3 2.3 fusion.11
  97.9 41.3 %collective-permute-done.5 = bf16[464,1024]{1,0:T(8,128)(2,1)S(1)} collective-permute-done((bf16[464,1024]{1,0:T(8,128)(2,1)S(1)}, bf16[464,1024]{1,0:T(8,128)(2,1)S(1)}, u32[]{:S(2)}, u32[]{:S(2)}) %collective-permute-start.5) | collective-permute-done | bytes 950304 | tf_op jit(solution)/shard_map/ppermute | solution.py:134
  140.1 33.7 %collective-permute-done.3 = bf16[464,1024]{1,0:T(8,128)(2,1)S(1)} collective-permute-done((bf16[464,1024]{1,0:T(8,128)(2,1)S(1)}, bf16[464,1024]{1,0:T(8,128)(2,1)S(1)}, u32[]{:S(2)}, u32[]{:S(2)}) %collective-permute-start.3) | collective-permute-done | bytes 950304 | tf_op jit(solution)/shard_map/ppermute | solution.py:134
  173.9 8.1 %all-to-all-done.1 = bf16[64,16,16,128]{3,2,1,0:T(8,128)(2,1)} async-done(((bf16[64,16,16,128]{3,2,1,0:T(8,128)(2,1)}), bf16[64,16,16,128]{3,2,1,0:T(8,128)(2,1)}, u32[]{:S(2)}, u32[]{:S(2)}) %all-to-all-start.1) | async-done | bytes 4194336 | tf_op jit(solution)/shard_map/all_to_all | solution.py:163
  182.0 7.6 %attend.1 = (bf16[512,512]{1,0:T(8,128)(2,1)S(1)}, bf16[512,512]{1,0:T(8,128)(2,1)S(1)}) custom-call(bf16[512,512]{1,0:T(8,128)(2,1)S(1)} %concatenate.15.q_ref, bf16[512,512]{1,0:T(8,128)(2,1)S(1)} %concatenate.16.g_ref, bf16[2,4,8,16,16,128]{5,4,3,2,1,0:T(8,128)(2,1)} %bitcast.9.kv_ref), custom_call_target="tpu_custom_call" | custom-call | flops 671088640 | bytes 4194304 | tf_op jit(solution)/shard_map/attend/pallas_call | solution.py:114
  190.5 3.0 %collective-permute-start.10 = (bf16[464,512]{1,0:T(8,128)(2,1)}, bf16[464,512]{1,0:T(8,128)(2,1)S(1)}, u32[]{:S(2)}, u32[]{:S(2)}) collective-permute-start(bf16[464,512]{1,0:T(8,128)(2,1)} %concatenate.18), channel_id=1, source_target_pairs={{0,128},{64,192},{128,0},{192,64},{1,129},{65,193},{129,1},{193,65... | collective-permute-start | bytes 1425416 | tf_op jit(solution)/shard_map/ppermute | solution.py:134
  194.2 2.6 collective-permute-start.11
  198.1 7.9 %collective-permute-done.10 = bf16[464,512]{1,0:T(8,128)(2,1)S(1)} collective-permute-done((bf16[464,512]{1,0:T(8,128)(2,1)}, bf16[464,512]{1,0:T(8,128)(2,1)S(1)}, u32[]{:S(2)}, u32[]{:S(2)}) %collective-permute-start.10) | collective-permute-done | bytes 475168 | tf_op jit(solution)/shard_map/ppermute | solution.py:134
  208.0 8.1 %collective-permute-done.9 = bf16[464,512]{1,0:T(8,128)(2,1)S(1)} collective-permute-done((bf16[464,512]{1,0:T(8,128)(2,1)}, bf16[464,512]{1,0:T(8,128)(2,1)S(1)}, u32[]{:S(2)}, u32[]{:S(2)}) %collective-permute-start.9) | collective-permute-done | bytes 475168 | tf_op jit(solution)/shard_map/ppermute | solution.py:134
  224.9 10.5 %collective-permute-done.6 = bf16[464,512]{1,0:T(8,128)(2,1)S(1)} collective-permute-done((bf16[464,512]{1,0:T(8,128)(2,1)}, bf16[464,512]{1,0:T(8,128)(2,1)S(1)}, u32[]{:S(2)}, u32[]{:S(2)}) %collective-permute-start.6) | collective-permute-done | bytes 475168 | tf_op jit(solution)/shard_map/ppermute | solution.py:134
  239.0 2.0 collective-permute-start.19
  241.8 2.1 collective-permute-start.18
  243.9 3.1 %collective-permute-start.17 = (f32[64,512]{1,0:T(8,128)S(1)}, f32[64,512]{1,0:T(8,128)S(1)}, u32[]{:S(2)}, u32[]{:S(2)}) collective-permute-start(f32[64,512]{1,0:T(8,128)S(1)} %get-tuple-element.48), channel_id=1, source_target_pairs={{0,40},{8,48},{16,56},{24,0},{32,8},{40,16},{48,24},{56,32},{1,41}... | collective-permute-start | bytes 393224 | tf_op jit(solution)/shard_map/ppermute | solution.py:134
  247.0 3.4 %collective-permute-start.16 = (f32[64,512]{1,0:T(8,128)S(1)}, f32[64,512]{1,0:T(8,128)S(1)}, u32[]{:S(2)}, u32[]{:S(2)}) collective-permute-start(f32[64,512]{1,0:T(8,128)S(1)} %get-tuple-element.49), channel_id=1, source_target_pairs={{0,32},{8,40},{16,48},{24,56},{32,0},{40,8},{48,16},{56,24},{1,33}... | collective-permute-start | bytes 393224 | tf_op jit(solution)/shard_map/ppermute | solution.py:134
  253.4 13.3 %collective-permute-done.17 = f32[64,512]{1,0:T(8,128)S(1)} collective-permute-done((f32[64,512]{1,0:T(8,128)S(1)}, f32[64,512]{1,0:T(8,128)S(1)}, u32[]{:S(2)}, u32[]{:S(2)}) %collective-permute-start.17) | collective-permute-done | bytes 131104 | tf_op jit(solution)/shard_map/ppermute | solution.py:134
  266.6 2.9 %collective-permute-done.14 = f32[64,512]{1,0:T(8,128)S(1)} collective-permute-done((f32[64,512]{1,0:T(8,128)S(1)}, f32[64,512]{1,0:T(8,128)S(1)}, u32[]{:S(2)}, u32[]{:S(2)}) %collective-permute-start.14) | collective-permute-done | bytes 131104 | tf_op jit(solution)/shard_map/ppermute | solution.py:134
  (82 shorter events, 37.4 us)
Async XLA Ops:
  5.9 67.1 %all-to-all-start = ((bf16[64,9,16,128]{3,2,1,0:T(8,128)(2,1)}), bf16[64,9,16,128]{3,2,1,0:T(8,128)(2,1)S(1)}, u32[]{:S(2)}, u32[]{:S(2)}) async-start(bf16[64,9,16,128]{3,2,1,0:T(8,128)(2,1)} %bitcast.66), calls=%async_computation | async-start | bytes 4718592 | tf_op jit(solution)/shard_map/all_to_all | solution.py:153
  21.0 48.2 %collective-permute-start.2 = (bf16[1024,512]{1,0:T(8,128)(2,1)S(1)}, bf16[1024,512]{1,0:T(8,128)(2,1)S(1)}, u32[]{:S(2)}, u32[]{:S(2)}) collective-permute-start(bf16[1024,512]{1,0:T(8,128)(2,1)S(1)} %get-tuple-element.41), channel_id=1, source_target_pairs={{0,3},{1,0},{2,1},{3,2},{4,7},{5,4},{6,5},{7,6},{8,11},{9,8},{10,9... | collective-permute-start | bytes 3145736 | tf_op jit(solution)/shard_map/ppermute | solution.py:134
  24.0 45.2 %collective-permute-start.1 = (bf16[1024,512]{1,0:T(8,128)(2,1)S(1)}, bf16[1024,512]{1,0:T(8,128)(2,1)S(1)}, u32[]{:S(2)}, u32[]{:S(2)}) collective-permute-start(bf16[1024,512]{1,0:T(8,128)(2,1)S(1)} %get-tuple-element.42), channel_id=1, source_target_pairs={{0,2},{1,3},{2,0},{3,1},{4,6},{5,7},{6,4},{7,5},{8,10},{9,11},{10,... | collective-permute-start | bytes 3145736 | tf_op jit(solution)/shard_map/ppermute | solution.py:134
  24.7 48.4 %collective-permute-start = (bf16[1024,512]{1,0:T(8,128)(2,1)S(1)}, bf16[1024,512]{1,0:T(8,128)(2,1)}, u32[]{:S(2)}, u32[]{:S(2)}) collective-permute-start(bf16[1024,512]{1,0:T(8,128)(2,1)S(1)} %get-tuple-element.43), channel_id=1, source_target_pairs={{0,1},{1,2},{2,3},{3,0},{4,5},{5,6},{6,7},{7,4},{8,9},{9,10},{10,1... | collective-permute-start | bytes 3145736 | tf_op jit(solution)/shard_map/ppermute | solution.py:134
  77.2 18.0 %copy-start.10 = (bf16[1,512,512]{2,1,0:T(8,128)(2,1)S(1)}, bf16[1,512,512]{2,1,0:T(8,128)(2,1)}, u32[]{:S(2)}) copy-start(bf16[1,512,512]{2,1,0:T(8,128)(2,1)} %param.11) | copy-start | bytes 1572868
  77.3 104.7 %all-to-all-start.1 = ((bf16[64,16,16,128]{3,2,1,0:T(8,128)(2,1)}), bf16[64,16,16,128]{3,2,1,0:T(8,128)(2,1)}, u32[]{:S(2)}, u32[]{:S(2)}) async-start(bf16[64,16,16,128]{3,2,1,0:T(8,128)(2,1)} %bitcast.64), calls=%async_computation.1 | async-start | bytes 8388608 | tf_op jit(solution)/shard_map/all_to_all | solution.py:163
  90.6 48.6 %collective-permute-start.5 = (bf16[464,1024]{1,0:T(8,128)(2,1)S(1)}, bf16[464,1024]{1,0:T(8,128)(2,1)S(1)}, u32[]{:S(2)}, u32[]{:S(2)}) collective-permute-start(bf16[464,1024]{1,0:T(8,128)(2,1)S(1)} %get-tuple-element.37), channel_id=1, source_target_pairs={{0,192},{64,0},{128,64},{192,128},{1,193},{65,1},{129,65},{193,129... | collective-permute-start | bytes 2850824 | tf_op jit(solution)/shard_map/ppermute | solution.py:134
  93.6 46.5 %collective-permute-start.4 = (bf16[464,1024]{1,0:T(8,128)(2,1)S(1)}, bf16[464,1024]{1,0:T(8,128)(2,1)}, u32[]{:S(2)}, u32[]{:S(2)}) collective-permute-start(bf16[464,1024]{1,0:T(8,128)(2,1)S(1)} %get-tuple-element.38), channel_id=1, source_target_pairs={{0,128},{64,192},{128,0},{192,64},{1,129},{65,193},{129,1},{193,65... | collective-permute-start | bytes 2850824 | tf_op jit(solution)/shard_map/ppermute | solution.py:134
  94.2 79.6 %collective-permute-start.3 = (bf16[464,1024]{1,0:T(8,128)(2,1)S(1)}, bf16[464,1024]{1,0:T(8,128)(2,1)S(1)}, u32[]{:S(2)}, u32[]{:S(2)}) collective-permute-start(bf16[464,1024]{1,0:T(8,128)(2,1)S(1)} %get-tuple-element.39), channel_id=1, source_target_pairs={{0,64},{64,128},{128,192},{192,0},{1,65},{65,129},{129,193},{193,1... | collective-permute-start | bytes 2850824 | tf_op jit(solution)/shard_map/ppermute | solution.py:134
  190.5 15.5 %collective-permute-start.10 = (bf16[464,512]{1,0:T(8,128)(2,1)}, bf16[464,512]{1,0:T(8,128)(2,1)S(1)}, u32[]{:S(2)}, u32[]{:S(2)}) collective-permute-start(bf16[464,512]{1,0:T(8,128)(2,1)} %concatenate.18), channel_id=1, source_target_pairs={{0,128},{64,192},{128,0},{192,64},{1,129},{65,193},{129,1},{193,65... | collective-permute-start | bytes 1425416 | tf_op jit(solution)/shard_map/ppermute | solution.py:134
  193.5 22.6 %collective-permute-start.9 = (bf16[464,512]{1,0:T(8,128)(2,1)}, bf16[464,512]{1,0:T(8,128)(2,1)S(1)}, u32[]{:S(2)}, u32[]{:S(2)}) collective-permute-start(bf16[464,512]{1,0:T(8,128)(2,1)} %concatenate.18), channel_id=1, source_target_pairs={{0,64},{64,128},{128,192},{192,0},{1,65},{65,129},{129,193},{193,1... | collective-permute-start | bytes 1425416 | tf_op jit(solution)/shard_map/ppermute | solution.py:134
  194.2 22.6 %collective-permute-start.11 = (bf16[464,512]{1,0:T(8,128)(2,1)}, bf16[464,512]{1,0:T(8,128)(2,1)S(1)}, u32[]{:S(2)}, u32[]{:S(2)}) collective-permute-start(bf16[464,512]{1,0:T(8,128)(2,1)} %concatenate.18), channel_id=1, source_target_pairs={{0,192},{64,0},{128,64},{192,128},{1,193},{65,1},{129,65},{193,129... | collective-permute-start | bytes 1425416 | tf_op jit(solution)/shard_map/ppermute | solution.py:134
  196.7 26.3 %collective-permute-start.7 = (bf16[464,512]{1,0:T(8,128)(2,1)}, bf16[464,512]{1,0:T(8,128)(2,1)}, u32[]{:S(2)}, u32[]{:S(2)}) collective-permute-start(bf16[464,512]{1,0:T(8,128)(2,1)} %concatenate.18), channel_id=1, source_target_pairs={{0,2},{1,3},{2,0},{3,1},{4,6},{5,7},{6,4},{7,5},{8,10},{9,11},{10,... | collective-permute-start | bytes 1425416 | tf_op jit(solution)/shard_map/ppermute | solution.py:134
  219.0 18.3 %collective-permute-start.12 = (f32[8,64,512]{2,1,0:T(8,128)S(1)}, f32[8,64,512]{2,1,0:T(8,128)}, u32[]{:S(2)}, u32[]{:S(2)}) collective-permute-start(f32[8,64,512]{2,1,0:T(8,128)S(1)} %dynamic-slice_bitcast_fusion), channel_id=1, source_target_pairs={{0,4},{4,0},{1,5},{5,1},{2,6},{6,2},{3,7},{7,3},{8,12},{12,8},{9,1... | collective-permute-start | bytes 3145736 | tf_op jit(solution)/shard_map/ppermute | solution.py:134
  219.2 21.8 %collective-permute-start.8 = (bf16[464,512]{1,0:T(8,128)(2,1)}, bf16[464,512]{1,0:T(8,128)(2,1)S(1)}, u32[]{:S(2)}, u32[]{:S(2)}) collective-permute-start(bf16[464,512]{1,0:T(8,128)(2,1)} %concatenate.18), channel_id=1, source_target_pairs={{0,3},{1,0},{2,1},{3,2},{4,7},{5,4},{6,5},{7,6},{8,11},{9,8},{10,9... | collective-permute-start | bytes 1425416 | tf_op jit(solution)/shard_map/ppermute | solution.py:134
  221.1 14.2 %collective-permute-start.6 = (bf16[464,512]{1,0:T(8,128)(2,1)}, bf16[464,512]{1,0:T(8,128)(2,1)S(1)}, u32[]{:S(2)}, u32[]{:S(2)}) collective-permute-start(bf16[464,512]{1,0:T(8,128)(2,1)} %concatenate.18), channel_id=1, source_target_pairs={{0,1},{1,2},{2,3},{3,0},{4,5},{5,6},{6,7},{7,4},{8,9},{9,10},{10,1... | collective-permute-start | bytes 1425416 | tf_op jit(solution)/shard_map/ppermute | solution.py:134
  223.0 14.3 %copy-start.4 = (f32[1024,512]{1,0:T(8,128)S(1)}, f32[1024,512]{1,0:T(8,128)}, u32[]{:S(2)}) copy-start(f32[1024,512]{1,0:T(8,128)} %copy-done.3) | copy-start | bytes 6291460
  238.9 11.4 %collective-permute-start.13 = (f32[64,512]{1,0:T(8,128)S(1)}, f32[64,512]{1,0:T(8,128)S(1)}, u32[]{:S(2)}, u32[]{:S(2)}) collective-permute-start(f32[64,512]{1,0:T(8,128)S(1)} %get-tuple-element.45), channel_id=1, source_target_pairs={{0,8},{8,16},{16,24},{24,32},{32,40},{40,48},{48,56},{56,0},{1,9},... | collective-permute-start | bytes 393224 | tf_op jit(solution)/shard_map/ppermute | solution.py:134
  239.0 12.4 %collective-permute-start.19 = (f32[64,512]{1,0:T(8,128)S(1)}, f32[64,512]{1,0:T(8,128)S(1)}, u32[]{:S(2)}, u32[]{:S(2)}) collective-permute-start(f32[64,512]{1,0:T(8,128)S(1)} %get-tuple-element.46), channel_id=1, source_target_pairs={{0,56},{8,0},{16,8},{24,16},{32,24},{40,32},{48,40},{56,48},{1,57}... | collective-permute-start | bytes 393224 | tf_op jit(solution)/shard_map/ppermute | solution.py:134
  241.8 11.6 %collective-permute-start.18 = (f32[64,512]{1,0:T(8,128)S(1)}, f32[64,512]{1,0:T(8,128)S(1)}, u32[]{:S(2)}, u32[]{:S(2)}) collective-permute-start(f32[64,512]{1,0:T(8,128)S(1)} %get-tuple-element.47), channel_id=1, source_target_pairs={{0,48},{8,56},{16,0},{24,8},{32,16},{40,24},{48,32},{56,40},{1,49}... | collective-permute-start | bytes 393224 | tf_op jit(solution)/shard_map/ppermute | solution.py:134
  243.9 22.7 %collective-permute-start.17 = (f32[64,512]{1,0:T(8,128)S(1)}, f32[64,512]{1,0:T(8,128)S(1)}, u32[]{:S(2)}, u32[]{:S(2)}) collective-permute-start(f32[64,512]{1,0:T(8,128)S(1)} %get-tuple-element.48), channel_id=1, source_target_pairs={{0,40},{8,48},{16,56},{24,0},{32,8},{40,16},{48,24},{56,32},{1,41}... | collective-permute-start | bytes 393224 | tf_op jit(solution)/shard_map/ppermute | solution.py:134
  247.0 19.7 %collective-permute-start.16 = (f32[64,512]{1,0:T(8,128)S(1)}, f32[64,512]{1,0:T(8,128)S(1)}, u32[]{:S(2)}, u32[]{:S(2)}) collective-permute-start(f32[64,512]{1,0:T(8,128)S(1)} %get-tuple-element.49), channel_id=1, source_target_pairs={{0,32},{8,40},{16,48},{24,56},{32,0},{40,8},{48,16},{56,24},{1,33}... | collective-permute-start | bytes 393224 | tf_op jit(solution)/shard_map/ppermute | solution.py:134
  250.4 16.3 %collective-permute-start.15 = (f32[64,512]{1,0:T(8,128)S(1)}, f32[64,512]{1,0:T(8,128)S(1)}, u32[]{:S(2)}, u32[]{:S(2)}) collective-permute-start(f32[64,512]{1,0:T(8,128)S(1)} %get-tuple-element.50), channel_id=1, source_target_pairs={{0,24},{8,32},{16,40},{24,48},{32,56},{40,0},{48,8},{56,16},{1,25}... | collective-permute-start | bytes 393224 | tf_op jit(solution)/shard_map/ppermute | solution.py:134
  251.4 18.1 %collective-permute-start.14 = (f32[64,512]{1,0:T(8,128)S(1)}, f32[64,512]{1,0:T(8,128)S(1)}, u32[]{:S(2)}, u32[]{:S(2)}) collective-permute-start(f32[64,512]{1,0:T(8,128)S(1)} %get-tuple-element.51), channel_id=1, source_target_pairs={{0,16},{8,24},{16,32},{24,40},{32,48},{40,56},{48,0},{56,8},{1,17}... | collective-permute-start | bytes 393224 | tf_op jit(solution)/shard_map/ppermute | solution.py:134
  (13 other events, 44.2 us)

commit v4 on v3

--- a/solution.py
+++ b/solution.py
@@ -22,10 +22,10 @@
 
 def cut_kernel(owner_ref, row_ref, cache_ref, out_ref, named_ref):
     rows = cache_ref.shape[0]
-    stretches, neigh = owner_ref.shape
+    _, stretches, neigh = owner_ref.shape
     named_ref[...] = jnp.zeros_like(named_ref)
-    named_ref[:stretches, :neigh] = owner_ref[...].astype(F32)
-    named_ref[stretches : 2 * stretches, :neigh] = row_ref[...].astype(F32)
+    named_ref[:stretches, :neigh] = owner_ref[0].astype(F32)
+    named_ref[stretches : 2 * stretches, :neigh] = row_ref[0].astype(F32)
     _, heads, tiles, _, _, _ = out_ref.shape
     for head in range(heads):
         cols = slice(head * HEAD_DIM, (head + 1) * HEAD_DIM)
@@ -37,7 +37,7 @@
 def cut(nb_owner, nb_row, cache):
     rows, _, nb_len, width = cache.shape
     tiles, heads, parts = nb_len // TILE, width // HEAD_DIM, 2
-    named = pl.BlockSpec(nb_owner.shape, lambda a, t: (0, 0))
+    named = pl.BlockSpec(nb_owner.shape, lambda a, t: (0, 0, 0))
     return pl.pallas_call(
         cut_kernel,
         grid=(2, parts),
@@ -149,7 +149,7 @@
     tiles = nb_len // TILE
     real = length - LEAD
 
-    message = cut(nb_owner[0], nb_row[0], cache_kv)
+    message = cut(nb_owner, nb_row, cache_kv)
     held = lax.all_to_all(message, DP, split_axis=0, concat_axis=0, tiled=True)
 
     block = d // nmp
@@ -186,13 +186,17 @@
     total = total.reshape(nz, nc, -1, width)
     mine = lax.dynamic_index_in_dim(total, mc, 1, keepdims=False)
     mine += step(lax.dynamic_index_in_dim(total, 1 - mc, 1, keepdims=False), "core", 1)
-    query_grad = lax.dynamic_index_in_dim(mine, mz, 0, keepdims=False)
-    for by in range(1, nz):
-        query_grad += step(lax.dynamic_index_in_dim(mine, (mz + by) % nz, 0, keepdims=False), "z", by)
-
+    groups = jnp.broadcast_to(dq[None], (nmp,) + dq.shape)
+    groups = lax.all_to_all(groups, "mp", split_axis=0, concat_axis=0, tiled=True)
+    groups, mine = lax.optimization_barrier((groups, mine))
+    terms = [lax.dynamic_index_in_dim(mine, (mz + by) % nz, 0, keepdims=False) for by in range(nz)]
+    terms = [step(a, "z", by) if by else a for by, a in enumerate(terms)]
+
+    groups, terms[1] = lax.optimization_barrier((groups, terms[1]))
+    query_grad = sum(terms)
     part = 0.0
     for by in range(nmp):
-        near = step(dq, "mp", by) if by else dq
+        near = lax.dynamic_index_in_dim(groups, (my - by) % nmp, 0, keepdims=False)
         part += lax.dot_general(near, fans[by], BOTH_LAST, preferred_element_type=F32).astype(BF16).astype(F32)
     part = part.astype(BF16)
     attended = jnp.concatenate([jnp.zeros((LEAD, width), BF16), out[:real]], 0)

time: 271 us -> 262 us (0.967)
  waiting for transfers between devices: 171 us -> 151 us
  matrix products: 11.7 us -> 16 us
  starting transfers between devices: 53.1 us -> 56.4 us
    ppermute x20 -> x17, waiting for transfers between devices: 163 us -> 143 us  [step(): lax.ppermute(array, axis, [(i, (i + by) % size) for i in range(size)])]
    all_to_all x0 -> x1, starting transfers between devices: none -> 4.41 us  [local(): lax.all_to_all(groups, 'mp', split_axis=0, concat_axis=0, tiled=True)]
    ppermute x20 -> x17, starting transfers between devices: 30.9 us -> 29.7 us  [step(): lax.ppermute(array, axis, [(i, (i + by) % size) for i in range(size)])]
    unnamed x30 -> x28, local copies, waits for them, and re-layouts: 9.32 us -> 9.49 us
  transfers between devices with their start and end apart: 22 -> 20, of which waited for: 10 -> 11; matrix products, arithmetic and copies ran while one was open for 8% -> 11% of each run, Pallas kernels for 0% -> 0%
where the time goes in v4:
time: 262 us; the launch traced here: 261 us
  waiting for transfers between devices  151 us (58%)
  starting transfers between devices  56.4 us (22%)
  local copies, waits for them, and re-layouts  22 us (8%)
  matrix products  16 us (6%)
  Pallas kernels  10.3 us (4%)
  other arithmetic  4.13 us (2%)
    ppermute x17, waiting for transfers between devices, step(): lax.ppermute(array, axis, [(i, (i + by) % size) for i in range(size)])  143 us
    ppermute x17, starting transfers between devices, step(): lax.ppermute(array, axis, [(i, (i + by) % size) for i in range(size)])  29.7 us
    all_to_all x1, starting transfers between devices, local(): held = lax.all_to_all(message, DP, split_axis=0, concat_axis=0, tiled=True)  11.6 us
    all_to_all x1, starting transfers between devices, local(): lax.all_to_all(send.reshape(ndp, requests, TILE, HEAD_DIM), DP, split_axi...  10.6 us
    unnamed x28, local copies, waits for them, and re-layouts  9.49 us
    all_to_all x1, waiting for transfers between devices, local(): lax.all_to_all(send.reshape(ndp, requests, TILE, HEAD_DIM), DP, split_axi...  7.98 us
    pallas_call x1, Pallas kernels, attend(): pl.pallas_call(functools.partial(attend_kernel, heads=heads), grid=(count...  7.63 us
    dot_general x4, matrix products, local(): lax.dot_general(near, fans[by], BOTH_LAST, preferred_element_type=F32)  7.34 us
  transfers between devices with their start and end apart: 20, of which 11 were waited for; matrix products, arithmetic and copies ran while one was open for 11% of the time, Pallas kernels for 0%

profile of v4, /device:TPU:32, one launch (start us, length us, event | category | flops | bytes accessed | tf_op | source)
XLA Modules:
  0.0 261.1 jit_solution(12295931408300386016)
XLA Ops:
  5.9 11.6 %all-to-all-start = ((bf16[64,9,16,128]{3,2,1,0:T(8,128)(2,1)}), bf16[64,9,16,128]{3,2,1,0:T(8,128)(2,1)S(1)}, u32[]{:S(2)}, u32[]{:S(2)}) async-start(bf16[64,9,16,128]{3,2,1,0:T(8,128)(2,1)} %bitcast.73), calls=%async_computation | async-start | bytes 4718592 | tf_op jit(solution)/shard_map/all_to_all | solution.py:153
  17.6 3.4 %constant_dynamic-slice_fusion = (bf16[1024,512]{1,0:T(8,128)(2,1)S(1)}, bf16[1024,512]{1,0:T(8,128)(2,1)S(1)}, bf16[1024,512]{1,0:T(8,128)(2,1)S(1)}, bf16[1024,512]{1,0:T(8,128)(2,1)}) fusion(bf16[4096,512]{1,0:T(8,128)(2,1)} %param.7, s32[]{:T(128)S(6)} %select_n.157, s32[]{:T(128)S(6)} %select_n.155, s32[]{:T(128)S(6)} %select_n.153, s32[]{:T(128)S(6)} %select_n.151), kind=kLoop, calls=%fused_computation.40 | loop fusion | bytes 8388624 | tf_op jit(solution)/shard_map/dynamic_slice | solution.py:156
  21.0 3.0 %collective-permute-start.2 = (bf16[1024,512]{1,0:T(8,128)(2,1)S(1)}, bf16[1024,512]{1,0:T(8,128)(2,1)S(1)}, u32[]{:S(2)}, u32[]{:S(2)}) collective-permute-start(bf16[1024,512]{1,0:T(8,128)(2,1)S(1)} %get-tuple-element.49), channel_id=1, source_target_pairs={{0,3},{1,0},{2,1},{3,2},{4,7},{5,4},{6,5},{7,6},{8,11},{9,8},{10,9... | collective-permute-start | bytes 3145736 | tf_op jit(solution)/shard_map/ppermute | solution.py:134
  25.6 43.6 %collective-permute-done.2 = bf16[1024,512]{1,0:T(8,128)(2,1)S(1)} collective-permute-done((bf16[1024,512]{1,0:T(8,128)(2,1)S(1)}, bf16[1024,512]{1,0:T(8,128)(2,1)S(1)}, u32[]{:S(2)}, u32[]{:S(2)}) %collective-permute-start.2) | collective-permute-done | bytes 1048608 | tf_op jit(solution)/shard_map/ppermute | solution.py:134
  77.2 10.6 %all-to-all-start.1 = ((bf16[64,16,16,128]{3,2,1,0:T(8,128)(2,1)}), bf16[64,16,16,128]{3,2,1,0:T(8,128)(2,1)}, u32[]{:S(2)}, u32[]{:S(2)}) async-start(bf16[64,16,16,128]{3,2,1,0:T(8,128)(2,1)} %bitcast.71), calls=%async_computation.1 | async-start | bytes 8388608 | tf_op jit(solution)/shard_map/all_to_all | solution.py:163
  88.0 2.6 %constant_dynamic-slice_fusion.4 = (bf16[464,1024]{1,0:T(8,128)(2,1)S(1)}, bf16[464,1024]{1,0:T(8,128)(2,1)S(1)}, bf16[464,1024]{1,0:T(8,128)(2,1)S(1)}, bf16[464,1024]{1,0:T(8,128)(2,1)S(1)}) fusion(bf16[512,4096]{1,0:T(8,128)(2,1)} %bitcast.76, s32[]{:T(128)S(6)} %select_n.165, s32[]{:T(128)S(6)} %select_n.163, s32[]{:T(128)S(6)} %select_n.161, ...), kind=kLoop, calls=%fused_computation.44 | loop fusion | bytes 7602192 | tf_op jit(solution)/shard_map/dynamic_slice | solution.py:169
  90.6 3.0 %collective-permute-start.5 = (bf16[464,1024]{1,0:T(8,128)(2,1)S(1)}, bf16[464,1024]{1,0:T(8,128)(2,1)S(1)}, u32[]{:S(2)}, u32[]{:S(2)}) collective-permute-start(bf16[464,1024]{1,0:T(8,128)(2,1)S(1)} %get-tuple-element.45), channel_id=1, source_target_pairs={{0,192},{64,0},{128,64},{192,128},{1,193},{65,1},{129,65},{193,129... | collective-permute-start | bytes 2850824 | tf_op jit(solution)/shard_map/ppermute | solution.py:134
  95.3 2.3 fusion.21
  97.9 41.3 %collective-permute-done.5 = bf16[464,1024]{1,0:T(8,128)(2,1)S(1)} collective-permute-done((bf16[464,1024]{1,0:T(8,128)(2,1)S(1)}, bf16[464,1024]{1,0:T(8,128)(2,1)S(1)}, u32[]{:S(2)}, u32[]{:S(2)}) %collective-permute-start.5) | collective-permute-done | bytes 950304 | tf_op jit(solution)/shard_map/ppermute | solution.py:134
  140.1 33.8 %collective-permute-done.3 = bf16[464,1024]{1,0:T(8,128)(2,1)} collective-permute-done((bf16[464,1024]{1,0:T(8,128)(2,1)S(1)}, bf16[464,1024]{1,0:T(8,128)(2,1)}, u32[]{:S(2)}, u32[]{:S(2)}) %collective-permute-start.3) | collective-permute-done | bytes 950304 | tf_op jit(solution)/shard_map/ppermute | solution.py:134
  174.0 8.0 %all-to-all-done.1 = bf16[64,16,16,128]{3,2,1,0:T(8,128)(2,1)} async-done(((bf16[64,16,16,128]{3,2,1,0:T(8,128)(2,1)}), bf16[64,16,16,128]{3,2,1,0:T(8,128)(2,1)}, u32[]{:S(2)}, u32[]{:S(2)}) %all-to-all-start.1) | async-done | bytes 4194336 | tf_op jit(solution)/shard_map/all_to_all | solution.py:163
  182.0 7.6 %attend.1 = (bf16[512,512]{1,0:T(8,128)(2,1)S(1)}, bf16[512,512]{1,0:T(8,128)(2,1)S(1)}) custom-call(bf16[512,512]{1,0:T(8,128)(2,1)S(1)} %concatenate.15.q_ref, bf16[512,512]{1,0:T(8,128)(2,1)S(1)} %concatenate.16.g_ref, bf16[2,4,8,16,16,128]{5,4,3,2,1,0:T(8,128)(2,1)} %bitcast.7.kv_ref), custom_call_target="tpu_custom_call" | custom-call | flops 671088640 | bytes 4194304 | tf_op jit(solution)/shard_map/attend/pallas_call | solution.py:114
  191.2 2.9 %collective-permute-start.7 = (bf16[464,512]{1,0:T(8,128)(2,1)S(1)}, bf16[464,512]{1,0:T(8,128)(2,1)}, u32[]{:S(2)}, u32[]{:S(2)}) collective-permute-start(bf16[464,512]{1,0:T(8,128)(2,1)S(1)} %concatenate.18), channel_id=1, source_target_pairs={{0,128},{64,192},{128,0},{192,64},{1,129},{65,193},{129,1},{193,65... | collective-permute-start | bytes 1425416 | tf_op jit(solution)/shard_map/ppermute | solution.py:134
  196.9 4.4 %all-to-all-start.2 = ((bf16[4,464,512]{2,1,0:T(8,128)(2,1)}), bf16[4,464,512]{2,1,0:T(8,128)(2,1)}, u32[]{:S(2)}, u32[]{:S(2)}) async-start(bf16[4,464,512]{2,1,0:T(8,128)(2,1)} %broadcast_in_dim.7), calls=%async_computation.2 | async-start | bytes 3801088 | tf_op jit(solution)/shard_map/all_to_all | solution.py:190
  202.0 2.8 %collective-permute-done.6 = bf16[464,512]{1,0:T(8,128)(2,1)} collective-permute-done((bf16[464,512]{1,0:T(8,128)(2,1)S(1)}, bf16[464,512]{1,0:T(8,128)(2,1)}, u32[]{:S(2)}, u32[]{:S(2)}) %collective-permute-start.6) | collective-permute-done | bytes 475168 | tf_op jit(solution)/shard_map/ppermute | solution.py:134
  206.9 9.2 %collective-permute-done.7 = bf16[464,512]{1,0:T(8,128)(2,1)} collective-permute-done((bf16[464,512]{1,0:T(8,128)(2,1)S(1)}, bf16[464,512]{1,0:T(8,128)(2,1)}, u32[]{:S(2)}, u32[]{:S(2)}) %collective-permute-start.7) | collective-permute-done | bytes 475168 | tf_op jit(solution)/shard_map/ppermute | solution.py:134
  220.8 2.9 %collective-permute-done.9 = f32[8,64,512]{2,1,0:T(8,128)} collective-permute-done((f32[8,64,512]{2,1,0:T(8,128)}, f32[8,64,512]{2,1,0:T(8,128)}, u32[]{:S(2)}, u32[]{:S(2)}) %collective-permute-start.9) | collective-permute-done | bytes 1048608 | tf_op jit(solution)/shard_map/ppermute | solution.py:134
  223.7 2.4 bitcast_add_fusion
  228.7 3.9 %collective-permute-start.11 = (f32[64,512]{1,0:T(8,128)S(1)}, f32[64,512]{1,0:T(8,128)S(1)}, u32[]{:S(2)}, u32[]{:S(2)}) collective-permute-start(f32[64,512]{1,0:T(8,128)S(1)} %get-tuple-element.53), channel_id=1, source_target_pairs={{0,16},{8,24},{16,32},{24,40},{32,48},{40,56},{48,0},{56,8},{1,17}... | collective-permute-start | bytes 393224 | tf_op jit(solution)/shard_map/ppermute | solution.py:134
  234.7 2.2 collective-permute-start.14
  236.9 2.4 collective-permute-start.13
  241.1 2.1 convolution_convert_fusion.2
  246.7 4.0 %collective-permute-start.12 = (f32[64,512]{1,0:T(8,128)S(1)}, f32[64,512]{1,0:T(8,128)S(1)}, u32[]{:S(2)}, u32[]{:S(2)}) collective-permute-start(f32[64,512]{1,0:T(8,128)S(1)} %get-tuple-element.58), channel_id=1, source_target_pairs={{0,24},{8,32},{16,40},{24,48},{32,56},{40,0},{48,8},{56,16},{1,25}... | collective-permute-start | bytes 393224 | tf_op jit(solution)/shard_map/ppermute | solution.py:134
  251.8 6.5 %collective-permute-done.14 = f32[64,512]{1,0:T(8,128)S(1)} collective-permute-done((f32[64,512]{1,0:T(8,128)S(1)}, f32[64,512]{1,0:T(8,128)S(1)}, u32[]{:S(2)}, u32[]{:S(2)}) %collective-permute-start.14) | collective-permute-done | bytes 131104 | tf_op jit(solution)/shard_map/ppermute | solution.py:134
  (75 shorter events, 43.3 us)
Async XLA Ops:
  5.9 67.1 %all-to-all-start = ((bf16[64,9,16,128]{3,2,1,0:T(8,128)(2,1)}), bf16[64,9,16,128]{3,2,1,0:T(8,128)(2,1)S(1)}, u32[]{:S(2)}, u32[]{:S(2)}) async-start(bf16[64,9,16,128]{3,2,1,0:T(8,128)(2,1)} %bitcast.73), calls=%async_computation | async-start | bytes 4718592 | tf_op jit(solution)/shard_map/all_to_all | solution.py:153
  21.0 48.2 %collective-permute-start.2 = (bf16[1024,512]{1,0:T(8,128)(2,1)S(1)}, bf16[1024,512]{1,0:T(8,128)(2,1)S(1)}, u32[]{:S(2)}, u32[]{:S(2)}) collective-permute-start(bf16[1024,512]{1,0:T(8,128)(2,1)S(1)} %get-tuple-element.49), channel_id=1, source_target_pairs={{0,3},{1,0},{2,1},{3,2},{4,7},{5,4},{6,5},{7,6},{8,11},{9,8},{10,9... | collective-permute-start | bytes 3145736 | tf_op jit(solution)/shard_map/ppermute | solution.py:134
  24.0 45.2 %collective-permute-start.1 = (bf16[1024,512]{1,0:T(8,128)(2,1)S(1)}, bf16[1024,512]{1,0:T(8,128)(2,1)S(1)}, u32[]{:S(2)}, u32[]{:S(2)}) collective-permute-start(bf16[1024,512]{1,0:T(8,128)(2,1)S(1)} %get-tuple-element.50), channel_id=1, source_target_pairs={{0,2},{1,3},{2,0},{3,1},{4,6},{5,7},{6,4},{7,5},{8,10},{9,11},{10,... | collective-permute-start | bytes 3145736 | tf_op jit(solution)/shard_map/ppermute | solution.py:134
  24.7 48.4 %collective-permute-start = (bf16[1024,512]{1,0:T(8,128)(2,1)S(1)}, bf16[1024,512]{1,0:T(8,128)(2,1)}, u32[]{:S(2)}, u32[]{:S(2)}) collective-permute-start(bf16[1024,512]{1,0:T(8,128)(2,1)S(1)} %get-tuple-element.51), channel_id=1, source_target_pairs={{0,1},{1,2},{2,3},{3,0},{4,5},{5,6},{6,7},{7,4},{8,9},{9,10},{10,1... | collective-permute-start | bytes 3145736 | tf_op jit(solution)/shard_map/ppermute | solution.py:134
  77.2 18.0 %copy-start.8 = (bf16[1,512,512]{2,1,0:T(8,128)(2,1)S(1)}, bf16[1,512,512]{2,1,0:T(8,128)(2,1)}, u32[]{:S(2)}) copy-start(bf16[1,512,512]{2,1,0:T(8,128)(2,1)} %param.11) | copy-start | bytes 1572868
  77.2 104.7 %all-to-all-start.1 = ((bf16[64,16,16,128]{3,2,1,0:T(8,128)(2,1)}), bf16[64,16,16,128]{3,2,1,0:T(8,128)(2,1)}, u32[]{:S(2)}, u32[]{:S(2)}) async-start(bf16[64,16,16,128]{3,2,1,0:T(8,128)(2,1)} %bitcast.71), calls=%async_computation.1 | async-start | bytes 8388608 | tf_op jit(solution)/shard_map/all_to_all | solution.py:163
  88.0 7.4 %copy-start.3 = (bf16[4096,512]{1,0:T(8,128)(2,1)S(1)}, bf16[4096,512]{1,0:T(8,128)(2,1)}, u32[]{:S(2)}) copy-start(bf16[4096,512]{1,0:T(8,128)(2,1)} %param.7) | copy-start | bytes 12582916
  90.6 48.6 %collective-permute-start.5 = (bf16[464,1024]{1,0:T(8,128)(2,1)S(1)}, bf16[464,1024]{1,0:T(8,128)(2,1)S(1)}, u32[]{:S(2)}, u32[]{:S(2)}) collective-permute-start(bf16[464,1024]{1,0:T(8,128)(2,1)S(1)} %get-tuple-element.45), channel_id=1, source_target_pairs={{0,192},{64,0},{128,64},{192,128},{1,193},{65,1},{129,65},{193,129... | collective-permute-start | bytes 2850824 | tf_op jit(solution)/shard_map/ppermute | solution.py:134
  93.6 45.6 %collective-permute-start.4 = (bf16[464,1024]{1,0:T(8,128)(2,1)S(1)}, bf16[464,1024]{1,0:T(8,128)(2,1)S(1)}, u32[]{:S(2)}, u32[]{:S(2)}) collective-permute-start(bf16[464,1024]{1,0:T(8,128)(2,1)S(1)} %get-tuple-element.46), channel_id=1, source_target_pairs={{0,128},{64,192},{128,0},{192,64},{1,129},{65,193},{129,1},{193,65... | collective-permute-start | bytes 2850824 | tf_op jit(solution)/shard_map/ppermute | solution.py:134
  94.2 79.8 %collective-permute-start.3 = (bf16[464,1024]{1,0:T(8,128)(2,1)S(1)}, bf16[464,1024]{1,0:T(8,128)(2,1)}, u32[]{:S(2)}, u32[]{:S(2)}) collective-permute-start(bf16[464,1024]{1,0:T(8,128)(2,1)S(1)} %get-tuple-element.47), channel_id=1, source_target_pairs={{0,64},{64,128},{128,192},{192,0},{1,65},{65,129},{129,193},{193,1... | collective-permute-start | bytes 2850824 | tf_op jit(solution)/shard_map/ppermute | solution.py:134
  189.8 15.0 %collective-permute-start.6 = (bf16[464,512]{1,0:T(8,128)(2,1)S(1)}, bf16[464,512]{1,0:T(8,128)(2,1)}, u32[]{:S(2)}, u32[]{:S(2)}) collective-permute-start(bf16[464,512]{1,0:T(8,128)(2,1)S(1)} %concatenate.18), channel_id=1, source_target_pairs={{0,64},{64,128},{128,192},{192,0},{1,65},{65,129},{129,193},{193,1... | collective-permute-start | bytes 1425416 | tf_op jit(solution)/shard_map/ppermute | solution.py:134
  191.2 24.8 %collective-permute-start.7 = (bf16[464,512]{1,0:T(8,128)(2,1)S(1)}, bf16[464,512]{1,0:T(8,128)(2,1)}, u32[]{:S(2)}, u32[]{:S(2)}) collective-permute-start(bf16[464,512]{1,0:T(8,128)(2,1)S(1)} %concatenate.18), channel_id=1, source_target_pairs={{0,128},{64,192},{128,0},{192,64},{1,129},{65,193},{129,1},{193,65... | collective-permute-start | bytes 1425416 | tf_op jit(solution)/shard_map/ppermute | solution.py:134
  194.1 23.7 %collective-permute-start.8 = (bf16[464,512]{1,0:T(8,128)(2,1)S(1)}, bf16[464,512]{1,0:T(8,128)(2,1)}, u32[]{:S(2)}, u32[]{:S(2)}) collective-permute-start(bf16[464,512]{1,0:T(8,128)(2,1)S(1)} %concatenate.18), channel_id=1, source_target_pairs={{0,192},{64,0},{128,64},{192,128},{1,193},{65,1},{129,65},{193,129... | collective-permute-start | bytes 1425416 | tf_op jit(solution)/shard_map/ppermute | solution.py:134
  196.9 29.3 %all-to-all-start.2 = ((bf16[4,464,512]{2,1,0:T(8,128)(2,1)}), bf16[4,464,512]{2,1,0:T(8,128)(2,1)}, u32[]{:S(2)}, u32[]{:S(2)}) async-start(bf16[4,464,512]{2,1,0:T(8,128)(2,1)} %broadcast_in_dim.7), calls=%async_computation.2 | async-start | bytes 3801088 | tf_op jit(solution)/shard_map/all_to_all | solution.py:190
  206.9 11.0 %copy-start.7 = (bf16[464,1024]{1,0:T(8,128)(2,1)S(1)}, bf16[464,1024]{1,0:T(8,128)(2,1)}, u32[]{:S(2)}) copy-start(bf16[464,1024]{1,0:T(8,128)(2,1)} %copy-done.6) | copy-start | bytes 2850820
  220.7 3.0 %collective-permute-start.9 = (f32[8,64,512]{2,1,0:T(8,128)}, f32[8,64,512]{2,1,0:T(8,128)}, u32[]{:S(2)}, u32[]{:S(2)}) collective-permute-start(f32[8,64,512]{2,1,0:T(8,128)} %dynamic-slice_bitcast_fusion), channel_id=1, source_target_pairs={{0,4},{4,0},{1,5},{5,1},{2,6},{6,2},{3,7},{7,3},{8,12},{12,8},{9,1... | collective-permute-start | bytes 3145736 | tf_op jit(solution)/shard_map/ppermute | solution.py:134
  226.1 13.2 %copy-start.12 = (bf16[1024,512]{1,0:T(8,128)(2,1)S(1)}, bf16[1024,512]{1,0:T(8,128)(2,1)}, u32[]{:S(2)}) copy-start(bf16[1024,512]{1,0:T(8,128)(2,1)} %copy-done.11) | copy-start | bytes 3145732
  227.6 9.3 %collective-permute-start.10 = (f32[64,512]{1,0:T(8,128)S(1)}, f32[64,512]{1,0:T(8,128)S(1)}, u32[]{:S(2)}, u32[]{:S(2)}) collective-permute-start(f32[64,512]{1,0:T(8,128)S(1)} %get-tuple-element.59), channel_id=1, source_target_pairs={{0,8},{8,16},{16,24},{24,32},{32,40},{40,48},{48,56},{56,0},{1,9},... | collective-permute-start | bytes 393224 | tf_op jit(solution)/shard_map/ppermute | solution.py:134
  228.7 18.0 %collective-permute-start.11 = (f32[64,512]{1,0:T(8,128)S(1)}, f32[64,512]{1,0:T(8,128)S(1)}, u32[]{:S(2)}, u32[]{:S(2)}) collective-permute-start(f32[64,512]{1,0:T(8,128)S(1)} %get-tuple-element.53), channel_id=1, source_target_pairs={{0,16},{8,24},{16,32},{24,40},{32,48},{40,56},{48,0},{56,8},{1,17}... | collective-permute-start | bytes 393224 | tf_op jit(solution)/shard_map/ppermute | solution.py:134
  232.6 19.2 %collective-permute-start.16 = (f32[64,512]{1,0:T(8,128)S(1)}, f32[64,512]{1,0:T(8,128)S(1)}, u32[]{:S(2)}, u32[]{:S(2)}) collective-permute-start(f32[64,512]{1,0:T(8,128)S(1)} %get-tuple-element.54), channel_id=1, source_target_pairs={{0,56},{8,0},{16,8},{24,16},{32,24},{40,32},{48,40},{56,48},{1,57}... | collective-permute-start | bytes 393224 | tf_op jit(solution)/shard_map/ppermute | solution.py:134
  232.6 19.2 %collective-permute-start.15 = (f32[64,512]{1,0:T(8,128)S(1)}, f32[64,512]{1,0:T(8,128)S(1)}, u32[]{:S(2)}, u32[]{:S(2)}) collective-permute-start(f32[64,512]{1,0:T(8,128)S(1)} %get-tuple-element.55), channel_id=1, source_target_pairs={{0,48},{8,56},{16,0},{24,8},{32,16},{40,24},{48,32},{56,40},{1,49}... | collective-permute-start | bytes 393224 | tf_op jit(solution)/shard_map/ppermute | solution.py:134
  234.7 23.6 %collective-permute-start.14 = (f32[64,512]{1,0:T(8,128)S(1)}, f32[64,512]{1,0:T(8,128)S(1)}, u32[]{:S(2)}, u32[]{:S(2)}) collective-permute-start(f32[64,512]{1,0:T(8,128)S(1)} %get-tuple-element.56), channel_id=1, source_target_pairs={{0,40},{8,48},{16,56},{24,0},{32,8},{40,16},{48,24},{56,32},{1,41}... | collective-permute-start | bytes 393224 | tf_op jit(solution)/shard_map/ppermute | solution.py:134
  236.9 21.4 %collective-permute-start.13 = (f32[64,512]{1,0:T(8,128)S(1)}, f32[64,512]{1,0:T(8,128)S(1)}, u32[]{:S(2)}, u32[]{:S(2)}) collective-permute-start(f32[64,512]{1,0:T(8,128)S(1)} %get-tuple-element.57), channel_id=1, source_target_pairs={{0,32},{8,40},{16,48},{24,56},{32,0},{40,8},{48,16},{56,24},{1,33}... | collective-permute-start | bytes 393224 | tf_op jit(solution)/shard_map/ppermute | solution.py:134
  246.7 12.7 %collective-permute-start.12 = (f32[64,512]{1,0:T(8,128)S(1)}, f32[64,512]{1,0:T(8,128)S(1)}, u32[]{:S(2)}, u32[]{:S(2)}) collective-permute-start(f32[64,512]{1,0:T(8,128)S(1)} %get-tuple-element.58), channel_id=1, source_target_pairs={{0,24},{8,32},{16,40},{24,48},{32,56},{40,0},{48,8},{56,16},{1,25}... | collective-permute-start | bytes 393224 | tf_op jit(solution)/shard_map/ppermute | solution.py:134
  (9 other events, 25.6 us)

commit v5 on v4

--- a/solution.py
+++ b/solution.py
@@ -20,23 +20,30 @@
 BOTH_FIRST = (((0,), (0,)), ((), ()))
 
 
-def cut_kernel(owner_ref, row_ref, cache_ref, out_ref, named_ref):
+def cut_kernel(owner_ref, row_ref, cache_ref, out_ref, owners_ref, rows_ref):
     rows = cache_ref.shape[0]
     _, stretches, neigh = owner_ref.shape
-    named_ref[...] = jnp.zeros_like(named_ref)
-    named_ref[:stretches, :neigh] = owner_ref[0].astype(F32)
-    named_ref[stretches : 2 * stretches, :neigh] = row_ref[0].astype(F32)
-    _, heads, tiles, _, _, _ = out_ref.shape
+    owners_ref[...] = jnp.zeros_like(owners_ref)
+    rows_ref[...] = jnp.zeros_like(rows_ref)
+    owners_ref[:, :neigh] = owner_ref[0].astype(F32)
+    rows_ref[:, :neigh] = row_ref[0].astype(F32)
+    named = (owners_ref[...] + pltpu.roll(rows_ref[...], neigh, 1)).astype(BF16)
+    _, heads, tiles, _, _ = out_ref.shape
     for head in range(heads):
         cols = slice(head * HEAD_DIM, (head + 1) * HEAD_DIM)
         for tile in range(tiles):
-            out_ref[0, head, tile, :rows] = cache_ref[:, 0, tile * TILE : (tile + 1) * TILE, cols]
-            out_ref[0, head, tile, rows] = named_ref[...].astype(BF16)
+            for row in range(rows):
+                out_ref[0, head, tile, row * TILE : (row + 1) * TILE] = cache_ref[
+                    row, 0, tile * TILE : (tile + 1) * TILE, cols
+                ]
+            out_ref[0, head, tile, rows * TILE :] = named
 
 
 def cut(nb_owner, nb_row, cache):
     rows, _, nb_len, width = cache.shape
     tiles, heads, parts = nb_len // TILE, width // HEAD_DIM, 2
+    stretches = nb_owner.shape[1]
+    high = rows * TILE + stretches
     named = pl.BlockSpec(nb_owner.shape, lambda a, t: (0, 0, 0))
     return pl.pallas_call(
         cut_kernel,
@@ -47,37 +54,39 @@
             pl.BlockSpec((rows, 1, nb_len // parts, width), lambda a, t: (0, a, t, 0)),
         ],
         out_specs=pl.BlockSpec(
-            (1, heads, tiles // parts, rows + 1, TILE, HEAD_DIM), lambda a, t: (a, 0, t, 0, 0, 0)
-        ),
-        out_shape=jax.ShapeDtypeStruct((2, heads, tiles, rows + 1, TILE, HEAD_DIM), BF16),
-        scratch_shapes=[pltpu.VMEM((TILE, HEAD_DIM), F32)],
+            (1, heads, tiles // parts, high, HEAD_DIM), lambda a, t: (a, 0, t, 0, 0)
+        ),
+        out_shape=jax.ShapeDtypeStruct((2, heads, tiles, high, HEAD_DIM), BF16),
+        scratch_shapes=[pltpu.VMEM((stretches, HEAD_DIM), F32)] * 2,
         compiler_params=pltpu.CompilerParams(vmem_limit_bytes=VMEM),
         cost_estimate=pl.CostEstimate(flops=0, bytes_accessed=4 << 20, transcendentals=0),
         name="cut",
-    )(nb_owner, nb_row, cache).reshape(-1, rows + 1, TILE, HEAD_DIM)
-
-
-def pick_kernel(ids_ref, tiles_ref, out_ref, *, slots):
+    )(nb_owner, nb_row, cache).reshape(-1, high, HEAD_DIM)
+
+
+def pick_kernel(ids_ref, held_ref, out_ref, *, slots, rows):
     base = pl.program_id(0) * slots
     for slot in range(slots):
-        out_ref[slot] = tiles_ref[ids_ref[base + slot]]
-
-
-def pick(ids, tiles):
+        named = ids_ref[base + slot]
+        at = pl.multiple_of(named % rows * TILE, TILE)
+        out_ref[slot] = held_ref[named // rows, pl.ds(at, TILE)]
+
+
+def pick(ids, held, rows):
     count, slots = ids.shape[0], 64
     return pl.pallas_call(
-        functools.partial(pick_kernel, slots=slots),
+        functools.partial(pick_kernel, slots=slots, rows=rows),
         grid_spec=pltpu.PrefetchScalarGridSpec(
             num_scalar_prefetch=1,
             grid=(count // slots,),
-            in_specs=[pl.BlockSpec(tiles.shape, lambda s, ids: (0, 0, 0))],
-            out_specs=pl.BlockSpec((slots,) + tiles.shape[1:], lambda s, ids: (s, 0, 0)),
-        ),
-        out_shape=jax.ShapeDtypeStruct((count,) + tiles.shape[1:], tiles.dtype),
+            in_specs=[pl.BlockSpec(held.shape, lambda s, ids: (0, 0, 0))],
+            out_specs=pl.BlockSpec((slots, TILE, HEAD_DIM), lambda s, ids: (s, 0, 0)),
+        ),
+        out_shape=jax.ShapeDtypeStruct((count, TILE, HEAD_DIM), BF16),
         compiler_params=pltpu.CompilerParams(vmem_limit_bytes=VMEM),
         cost_estimate=pl.CostEstimate(flops=0, bytes_accessed=6 << 20, transcendentals=0),
         name="pick",
-    )(ids, tiles)
+    )(ids, held)
 
 
 def attend_kernel(q_ref, g_ref, kv_ref, out_ref, dq_ref, *, heads):
@@ -157,9 +166,9 @@
     fans = [step(a, "mp", by) if by else a for by, a in enumerate(fans)]
     held, fans = lax.optimization_barrier((held, fans))
 
-    named = held[:, db_rows, : 2 * stretches, :neigh].astype(jnp.int32)
-    ids = named[:, :stretches] * (db_rows + 1) + named[:, stretches:]
-    send = pick(ids.reshape(-1), held.reshape(-1, TILE, HEAD_DIM))
+    named = held[:, db_rows * TILE :, : 2 * neigh].astype(jnp.int32)
+    ids = named[..., :neigh] * db_rows + named[..., neigh:]
+    send = pick(ids.reshape(-1), held, db_rows)
     got = lax.all_to_all(
         send.reshape(ndp, requests, TILE, HEAD_DIM), DP, split_axis=0, concat_axis=0, tiled=True
     )
@@ -169,6 +178,16 @@
     share = [lax.dynamic_slice(late, (SKIP, (mx + by) % nx * block), (length - SKIP, block)) for by in range(nx)]
     share = [step(a, "x", by) if by else a for by, a in enumerate(share)]
 
+    def ordered(array):
+        array = array.T.reshape(nz, nc, -1, array.shape[0])
+        array = jnp.concatenate([array, array], 0)
+        array = lax.dynamic_slice_in_dim(array, mz, nz, 0)
+        own = lax.dynamic_index_in_dim(array, mc, 1, keepdims=False)
+        other = lax.dynamic_index_in_dim(array, 1 - mc, 1, keepdims=False)
+        return [a.reshape(-1, a.shape[-1]) for a in (own, other)]
+
+    share = [ordered(a) for a in share]
+
     def shifted(array):
         return jnp.concatenate([array[LEAD:], jnp.zeros((LEAD, array.shape[1]), array.dtype)], 0)
 
@@ -179,17 +198,16 @@
     out, dq = attend(q, g, got.reshape(2, heads, tiles, requests, TILE, HEAD_DIM), neigh)
     dq = jnp.concatenate([jnp.zeros((LEAD - SKIP, width), BF16), dq[:real]], 0)
 
-    total = 0.0
+    mine = other = 0.0
     for by in range(nx):
         near = step(dq, "x", by) if by else dq
-        total += lax.dot_general(share[by], near, BOTH_FIRST, preferred_element_type=F32)
-    total = total.reshape(nz, nc, -1, width)
-    mine = lax.dynamic_index_in_dim(total, mc, 1, keepdims=False)
-    mine += step(lax.dynamic_index_in_dim(total, 1 - mc, 1, keepdims=False), "core", 1)
+        other += jnp.dot(share[by][1], near, preferred_element_type=F32)
+        mine += jnp.dot(share[by][0], near, preferred_element_type=F32)
+    mine += step(other, "core", 1)
     groups = jnp.broadcast_to(dq[None], (nmp,) + dq.shape)
     groups = lax.all_to_all(groups, "mp", split_axis=0, concat_axis=0, tiled=True)
     groups, mine = lax.optimization_barrier((groups, mine))
-    terms = [lax.dynamic_index_in_dim(mine, (mz + by) % nz, 0, keepdims=False) for by in range(nz)]
+    terms = jnp.split(mine, nz)
     terms = [step(a, "z", by) if by else a for by, a in enumerate(terms)]
 
     groups, terms[1] = lax.optimization_barrier((groups, terms[1]))

time: 262 us -> 275 us (1.050)
  waiting for transfers between devices: 151 us -> 127 us
  local copies, waits for them, and re-layouts: 22 us -> 41.3 us
  matrix products: 16 us -> 23.2 us
  Pallas kernels: 10.3 us -> 16.6 us
    ppermute x17, waiting for transfers between devices: 143 us -> 127 us  [step(): lax.ppermute(array, axis, [(i, (i + by) % size) for i in range(size)])]
    all_to_all x1, waiting for transfers between devices: 7.98 us -> 0.01 us  [local(): lax.all_to_all(send.reshape(ndp, requests, TILE, HEAD_DIM), DP, split_axi...]
    dynamic_slice x1 -> x4, local copies, waits for them, and re-layouts: 2.63 us -> 10.2 us  [local(): lax.dynamic_slice(late, (SKIP, (mx + by) % nx * block), (length - SKIP, b...]
    ppermute x0 -> x3, local copies, waits for them, and re-layouts: none -> 6.8 us  [step(): lax.ppermute(array, axis, [(i, (i + by) % size) for i in range(size)])]
    pallas_call x1, Pallas kernels: 1.9 us -> 8.2 us  [pick(): pl.pallas_call(functools.partial(pick_kernel, slots=slots, rows=rows), gr...]
    unnamed x28 -> x37, local copies, waits for them, and re-layouts: 9.49 us -> 14.9 us
    concatenate x0 -> x2, other arithmetic: none -> 5.12 us  [ordered(): array = jnp.concatenate([array, array], 0)]
    dot_general x1, matrix products: 2.32 us -> 5.81 us  [local(): q = shifted(jnp.dot(late, weights, preferred_element_type=F32).astype(BF16))]
  transfers between devices with their start and end apart: 20 -> 20, of which waited for: 11 -> 8; matrix products, arithmetic and copies ran while one was open for 11% -> 22% of each run, Pallas kernels for 0% -> 0%
where the time goes in v5:
time: 275 us; the launch traced here: 273 us
  waiting for transfers between devices  127 us (46%)
  starting transfers between devices  58.2 us (21%)
  local copies, waits for them, and re-layouts  41.3 us (15%)
  matrix products  23.2 us (8%)
  Pallas kernels  16.6 us (6%)
  other arithmetic  6.01 us (2%)
    ppermute x17, waiting for transfers between devices, step(): lax.ppermute(array, axis, [(i, (i + by) % size) for i in range(size)])  127 us
    ppermute x17, starting transfers between devices, step(): lax.ppermute(array, axis, [(i, (i + by) % size) for i in range(size)])  31.6 us
    unnamed x37, local copies, waits for them, and re-layouts  14.9 us
    all_to_all x1, starting transfers between devices, local(): held = lax.all_to_all(message, DP, split_axis=0, concat_axis=0, tiled=True)  11.6 us
    all_to_all x1, starting transfers between devices, local(): lax.all_to_all(send.reshape(ndp, requests, TILE, HEAD_DIM), DP, split_axi...  10.5 us
    dynamic_slice x4, local copies, waits for them, and re-layouts, local(): lax.dynamic_slice(late, (SKIP, (mx + by) % nx * block), (length - SKIP, b...  10.2 us
    pallas_call x1, Pallas kernels, pick(): pl.pallas_call(functools.partial(pick_kernel, slots=slots, rows=rows), gr...  8.2 us
    dot_general x4, matrix products, local(): lax.dot_general(near, fans[by], BOTH_LAST, preferred_element_type=F32)  7.69 us
  transfers between devices with their start and end apart: 20, of which 8 were waited for; matrix products, arithmetic and copies ran while one was open for 22% of the time, Pallas kernels for 0%

profile of v5, /device:TPU:32, one launch (start us, length us, event | category | flops | bytes accessed | tf_op | source)
XLA Modules:
  0.0 273.5 jit_solution(5586896552256159351)
XLA Ops:
  5.9 11.6 %all-to-all-start = ((bf16[64,136,128]{2,1,0:T(8,128)(2,1)}), bf16[64,136,128]{2,1,0:T(8,128)(2,1)S(1)}, u32[]{:S(2)}, u32[]{:S(2)}) async-start(bf16[64,136,128]{2,1,0:T(8,128)(2,1)} %bitcast.62), calls=%async_computation | async-start | bytes 4456448 | tf_op jit(solution)/shard_map/all_to_all | solution.py:162
  17.6 3.4 %constant_dynamic-slice_fusion = (bf16[1024,512]{1,0:T(8,128)(2,1)S(1)}, bf16[1024,512]{1,0:T(8,128)(2,1)S(1)}, bf16[1024,512]{1,0:T(8,128)(2,1)S(1)}, bf16[1024,512]{1,0:T(8,128)(2,1)}) fusion(bf16[4096,512]{1,0:T(8,128)(2,1)} %param.7, s32[]{:T(128)S(6)} %select_n.118, s32[]{:T(128)S(6)} %select_n.116, s32[]{:T(128)S(6)} %select_n.114, s32[]{:T(128)S(6)} %select_n.112), kind=kLoop, calls=%fused_computation.55 | loop fusion | bytes 8388624 | tf_op jit(solution)/shard_map/dynamic_slice | solution.py:165
  21.0 3.0 %collective-permute-start.2 = (bf16[1024,512]{1,0:T(8,128)(2,1)S(1)}, bf16[1024,512]{1,0:T(8,128)(2,1)S(1)}, u32[]{:S(2)}, u32[]{:S(2)}) collective-permute-start(bf16[1024,512]{1,0:T(8,128)(2,1)S(1)} %get-tuple-element.57), channel_id=1, source_target_pairs={{0,3},{1,0},{2,1},{3,2},{4,7},{5,4},{6,5},{7,6},{8,11},{9,8},{10,9... | collective-permute-start | bytes 3145736 | tf_op jit(solution)/shard_map/ppermute | solution.py:143
  25.6 43.6 %collective-permute-done.2 = bf16[1024,512]{1,0:T(8,128)(2,1)S(1)} collective-permute-done((bf16[1024,512]{1,0:T(8,128)(2,1)S(1)}, bf16[1024,512]{1,0:T(8,128)(2,1)S(1)}, u32[]{:S(2)}, u32[]{:S(2)}) %collective-permute-start.2) | collective-permute-done | bytes 1048608 | tf_op jit(solution)/shard_map/ppermute | solution.py:143
  73.3 8.2 %pick.1 = bf16[1024,16,128]{2,1,0:T(8,128)(2,1)S(1)} custom-call(s32[1024]{0:T(1024)S(1)} %reshape.64.ids_ref, bf16[64,136,128]{2,1,0:T(8,128)(2,1)S(1)} %all-to-all-done.held_ref), custom_call_target="tpu_custom_call" | custom-call | bytes 6291456 | tf_op jit(solution)/shard_map/pick/pallas_call | solution.py:77
  83.5 10.5 %all-to-all-start.1 = ((bf16[64,16,16,128]{3,2,1,0:T(8,128)(2,1)}), bf16[64,16,16,128]{3,2,1,0:T(8,128)(2,1)}, u32[]{:S(2)}, u32[]{:S(2)}) async-start(bf16[64,16,16,128]{3,2,1,0:T(8,128)(2,1)} %bitcast.61), calls=%async_computation.1 | async-start | bytes 8388608 | tf_op jit(solution)/shard_map/all_to_all | solution.py:172
  94.1 6.5 %copy.16 = bf16[1,512,4096]{1,2,0:T(8,128)(2,1)} copy(bf16[1,512,4096]{2,1,0:T(8,128)(2,1)} %param.6) | data formatting | bytes 8388608 | tf_op args[0]
  100.6 5.3 %constant_dynamic-slice_fusion.4 = (bf16[464,1024]{0,1:T(8,128)(2,1)S(1)}, bf16[464,1024]{0,1:T(8,128)(2,1)}, bf16[464,1024]{0,1:T(8,128)(2,1)S(1)}, bf16[464,1024]{0,1:T(8,128)(2,1)S(1)}) fusion(bf16[512,4096]{0,1:T(8,128)(2,1)} %bitcast.63, s32[]{:T(128)S(6)} %select_n.132, s32[]{:T(128)S(6)} %select_n.130, s32[]{:T(128)S(6)} %select_n.128, s32[]{:T(128)S(6)} %select_n.120), kind=kLoop, calls=%fused_computation.59 | loop fusion | bytes 7602192 | tf_op jit(solution)/shard_map/dynamic_slice | solution.py:178
  111.0 2.9 %collective-permute-start.4 = (bf16[464,1024]{1,0:T(8,128)(2,1)}, bf16[464,1024]{1,0:T(8,128)(2,1)}, u32[]{:S(2)}, u32[]{:S(2)}) collective-permute-start(bf16[464,1024]{1,0:T(8,128)(2,1)} %copy.19), channel_id=1, source_target_pairs={{0,128},{64,192},{128,0},{192,64},{1,129},{65,193},{129,1},{193,65... | collective-permute-start | bytes 2850824 | tf_op jit(solution)/shard_map/ppermute | solution.py:143
  116.6 5.8 %fusion.30 = bf16[512,512]{1,0:T(8,128)(2,1)S(1)} fusion(bf16[512,4096]{0,1:T(8,128)(2,1)} %bitcast.64, bf16[4096,512]{1,0:T(8,128)(2,1)} %param.7), kind=kOutput, calls=%fused_computation.70 | convolution fusion | flops 2147483648 | bytes 8912896 | tf_op jit(solution)/shard_map/dot_general | solution.py:194
  122.7 24.9 %collective-permute-done.3 = bf16[464,1024]{1,0:T(8,128)(2,1)} collective-permute-done((bf16[464,1024]{1,0:T(8,128)(2,1)}, bf16[464,1024]{1,0:T(8,128)(2,1)}, u32[]{:S(2)}, u32[]{:S(2)}) %collective-permute-start.3) | collective-permute-done | bytes 950304 | tf_op jit(solution)/shard_map/ppermute | solution.py:143
  149.8 37.2 %collective-permute-done.4 = bf16[464,1024]{1,0:T(8,128)(2,1)} collective-permute-done((bf16[464,1024]{1,0:T(8,128)(2,1)}, bf16[464,1024]{1,0:T(8,128)(2,1)}, u32[]{:S(2)}, u32[]{:S(2)}) %collective-permute-start.4) | collective-permute-done | bytes 950304 | tf_op jit(solution)/shard_map/ppermute | solution.py:143
  187.0 2.3 copy.20
  191.6 3.3 %fusion.7 = (bf16[8,1,64,464]{3,2,1,0:T(8,128)(2,1)}, bf16[8,1,64,464]{3,2,1,0:T(8,128)(2,1)}, bf16[8,1,64,464]{3,2,1,0:T(8,128)(2,1)}, bf16[8,1,64,464]{3,2,1,0:T(8,128)(2,1)}) fusion(s32[]{:T(128)S(6)} %select_n.122, s32[]{:T(128)S(6)} %select_n.126, bf16[8,2,64,464]{3,2,1,0:T(8,128)(2,1)} %bitcast.67, s32[]{:T(128)S(6)} %select_n.124, ...), kind=kLoop, calls=%fused_computation.34 | loop fusion | flops 950272 | bytes 3801100 | tf_op jit(solution)/shard_map/concatenate | solution.py:183
  196.7 7.6 %attend.1 = (bf16[512,512]{1,0:T(8,128)(2,1)S(1)}, bf16[512,512]{1,0:T(8,128)(2,1)S(1)}) custom-call(bf16[512,512]{1,0:T(8,128)(2,1)S(1)} %concatenate.31.q_ref, bf16[512,512]{1,0:T(8,128)(2,1)S(1)} %concatenate.32.g_ref, bf16[2,4,8,16,16,128]{5,4,3,2,1,0:T(8,128)(2,1)} %bitcast.20.kv_ref), custom_call_target="tpu_custom_call" | custom-call | flops 671088640 | bytes 4194304 | tf_op jit(solution)/shard_map/attend/pallas_call | solution.py:123
  207.8 2.5 broadcast_in_dim.7
  210.3 4.5 %all-to-all-start.2 = ((bf16[4,464,512]{2,1,0:T(8,128)(2,1)}), bf16[4,464,512]{2,1,0:T(8,128)(2,1)}, u32[]{:S(2)}, u32[]{:S(2)}) async-start(bf16[4,464,512]{2,1,0:T(8,128)(2,1)} %broadcast_in_dim.7), calls=%async_computation.2 | async-start | bytes 3801088 | tf_op jit(solution)/shard_map/all_to_all | solution.py:208
  215.3 4.1 %collective-permute-done.8 = bf16[464,512]{1,0:T(8,128)(2,1)} collective-permute-done((bf16[464,512]{1,0:T(8,128)(2,1)}, bf16[464,512]{1,0:T(8,128)(2,1)}, u32[]{:S(2)}, u32[]{:S(2)}) %collective-permute-start.8) | collective-permute-done | bytes 475168 | tf_op jit(solution)/shard_map/ppermute | solution.py:143
  220.9 8.9 %collective-permute-done.6 = bf16[464,512]{1,0:T(8,128)(2,1)} collective-permute-done((bf16[464,512]{1,0:T(8,128)(2,1)}, bf16[464,512]{1,0:T(8,128)(2,1)}, u32[]{:S(2)}, u32[]{:S(2)}) %collective-permute-start.6) | collective-permute-done | bytes 475168 | tf_op jit(solution)/shard_map/ppermute | solution.py:143
  241.3 6.0 %collective-permute-start.11 = (f32[64,512]{1,0:T(8,128)S(1)}, f32[64,512]{1,0:T(8,128)S(1)}, u32[]{:S(2)}, u32[]{:S(2)}) collective-permute-start(f32[64,512]{1,0:T(8,128)S(1)} %get-tuple-element.61), channel_id=1, source_target_pairs={{0,16},{8,24},{16,32},{24,40},{32,48},{40,56},{48,0},{56,8},{1,17}... | collective-permute-start | bytes 393224 | tf_op jit(solution)/shard_map/ppermute | solution.py:143
  247.4 4.1 %collective-permute-start.14 = (f32[64,512]{1,0:T(8,128)S(1)}, f32[64,512]{1,0:T(8,128)S(1)}, u32[]{:S(2)}, u32[]{:S(2)}) collective-permute-start(f32[64,512]{1,0:T(8,128)S(1)} %get-tuple-element.64), channel_id=1, source_target_pairs={{0,40},{8,48},{16,56},{24,0},{32,8},{40,16},{48,24},{56,32},{1,41}... | collective-permute-start | bytes 393224 | tf_op jit(solution)/shard_map/ppermute | solution.py:143
  251.5 2.4 collective-permute-start.13
  261.6 3.9 %collective-permute-start.12 = (f32[64,512]{1,0:T(8,128)S(1)}, f32[64,512]{1,0:T(8,128)S(1)}, u32[]{:S(2)}, u32[]{:S(2)}) collective-permute-start(f32[64,512]{1,0:T(8,128)S(1)} %get-tuple-element.66), channel_id=1, source_target_pairs={{0,24},{8,32},{16,40},{24,48},{32,56},{40,0},{48,8},{56,16},{1,25}... | collective-permute-start | bytes 393224 | tf_op jit(solution)/shard_map/ppermute | solution.py:143
  266.6 6.2 %collective-permute-done.14 = f32[64,512]{1,0:T(8,128)S(1)} collective-permute-done((f32[64,512]{1,0:T(8,128)S(1)}, f32[64,512]{1,0:T(8,128)S(1)}, u32[]{:S(2)}, u32[]{:S(2)}) %collective-permute-start.14) | collective-permute-done | bytes 131104 | tf_op jit(solution)/shard_map/ppermute | solution.py:143
  (94 shorter events, 53.6 us)
Async XLA Ops:
  5.9 67.1 %all-to-all-start = ((bf16[64,136,128]{2,1,0:T(8,128)(2,1)}), bf16[64,136,128]{2,1,0:T(8,128)(2,1)S(1)}, u32[]{:S(2)}, u32[]{:S(2)}) async-start(bf16[64,136,128]{2,1,0:T(8,128)(2,1)} %bitcast.62), calls=%async_computation | async-start | bytes 4456448 | tf_op jit(solution)/shard_map/all_to_all | solution.py:162
  21.0 48.2 %collective-permute-start.2 = (bf16[1024,512]{1,0:T(8,128)(2,1)S(1)}, bf16[1024,512]{1,0:T(8,128)(2,1)S(1)}, u32[]{:S(2)}, u32[]{:S(2)}) collective-permute-start(bf16[1024,512]{1,0:T(8,128)(2,1)S(1)} %get-tuple-element.57), channel_id=1, source_target_pairs={{0,3},{1,0},{2,1},{3,2},{4,7},{5,4},{6,5},{7,6},{8,11},{9,8},{10,9... | collective-permute-start | bytes 3145736 | tf_op jit(solution)/shard_map/ppermute | solution.py:143
  24.0 45.2 %collective-permute-start.1 = (bf16[1024,512]{1,0:T(8,128)(2,1)S(1)}, bf16[1024,512]{1,0:T(8,128)(2,1)S(1)}, u32[]{:S(2)}, u32[]{:S(2)}) collective-permute-start(bf16[1024,512]{1,0:T(8,128)(2,1)S(1)} %get-tuple-element.58), channel_id=1, source_target_pairs={{0,2},{1,3},{2,0},{3,1},{4,6},{5,7},{6,4},{7,5},{8,10},{9,11},{10,... | collective-permute-start | bytes 3145736 | tf_op jit(solution)/shard_map/ppermute | solution.py:143
  24.6 48.4 %collective-permute-start = (bf16[1024,512]{1,0:T(8,128)(2,1)S(1)}, bf16[1024,512]{1,0:T(8,128)(2,1)}, u32[]{:S(2)}, u32[]{:S(2)}) collective-permute-start(bf16[1024,512]{1,0:T(8,128)(2,1)S(1)} %get-tuple-element.59), channel_id=1, source_target_pairs={{0,1},{1,2},{2,3},{3,0},{4,5},{5,6},{6,7},{7,4},{8,9},{9,10},{10,1... | collective-permute-start | bytes 3145736 | tf_op jit(solution)/shard_map/ppermute | solution.py:143
  83.5 113.2 %all-to-all-start.1 = ((bf16[64,16,16,128]{3,2,1,0:T(8,128)(2,1)}), bf16[64,16,16,128]{3,2,1,0:T(8,128)(2,1)}, u32[]{:S(2)}, u32[]{:S(2)}) async-start(bf16[64,16,16,128]{3,2,1,0:T(8,128)(2,1)} %bitcast.61), calls=%async_computation.1 | async-start | bytes 8388608 | tf_op jit(solution)/shard_map/all_to_all | solution.py:172
  109.5 7.0 %copy-start.13 = (bf16[1,512,512]{2,1,0:T(8,128)(2,1)S(1)}, bf16[1,512,512]{2,1,0:T(8,128)(2,1)}, u32[]{:S(2)}) copy-start(bf16[1,512,512]{2,1,0:T(8,128)(2,1)} %param.11) | copy-start | bytes 1572868
  109.5 38.1 %collective-permute-start.3 = (bf16[464,1024]{1,0:T(8,128)(2,1)}, bf16[464,1024]{1,0:T(8,128)(2,1)}, u32[]{:S(2)}, u32[]{:S(2)}) collective-permute-start(bf16[464,1024]{1,0:T(8,128)(2,1)} %copy.17), channel_id=1, source_target_pairs={{0,64},{64,128},{128,192},{192,0},{1,65},{65,129},{129,193},{193,1... | collective-permute-start | bytes 2850824 | tf_op jit(solution)/shard_map/ppermute | solution.py:143
  111.0 76.1 %collective-permute-start.4 = (bf16[464,1024]{1,0:T(8,128)(2,1)}, bf16[464,1024]{1,0:T(8,128)(2,1)}, u32[]{:S(2)}, u32[]{:S(2)}) collective-permute-start(bf16[464,1024]{1,0:T(8,128)(2,1)} %copy.19), channel_id=1, source_target_pairs={{0,128},{64,192},{128,0},{192,64},{1,129},{65,193},{129,1},{193,65... | collective-permute-start | bytes 2850824 | tf_op jit(solution)/shard_map/ppermute | solution.py:143
  115.2 74.1 %collective-permute-start.5 = (bf16[464,1024]{1,0:T(8,128)(2,1)}, bf16[464,1024]{1,0:T(8,128)(2,1)}, u32[]{:S(2)}, u32[]{:S(2)}) collective-permute-start(bf16[464,1024]{1,0:T(8,128)(2,1)} %copy.21), channel_id=1, source_target_pairs={{0,192},{64,0},{128,64},{192,128},{1,193},{65,1},{129,65},{193,129... | collective-permute-start | bytes 2850824 | tf_op jit(solution)/shard_map/ppermute | solution.py:143
  205.3 14.1 %collective-permute-start.8 = (bf16[464,512]{1,0:T(8,128)(2,1)}, bf16[464,512]{1,0:T(8,128)(2,1)}, u32[]{:S(2)}, u32[]{:S(2)}) collective-permute-start(bf16[464,512]{1,0:T(8,128)(2,1)} %concatenate.34), channel_id=1, source_target_pairs={{0,192},{64,0},{128,64},{192,128},{1,193},{65,1},{129,65},{193,129... | collective-permute-start | bytes 1425416 | tf_op jit(solution)/shard_map/ppermute | solution.py:143
  205.3 26.0 %collective-permute-start.7 = (bf16[464,512]{1,0:T(8,128)(2,1)}, bf16[464,512]{1,0:T(8,128)(2,1)}, u32[]{:S(2)}, u32[]{:S(2)}) collective-permute-start(bf16[464,512]{1,0:T(8,128)(2,1)} %concatenate.34), channel_id=1, source_target_pairs={{0,128},{64,192},{128,0},{192,64},{1,129},{65,193},{129,1},{193,65... | collective-permute-start | bytes 1425416 | tf_op jit(solution)/shard_map/ppermute | solution.py:143
  206.8 23.0 %collective-permute-start.6 = (bf16[464,512]{1,0:T(8,128)(2,1)}, bf16[464,512]{1,0:T(8,128)(2,1)}, u32[]{:S(2)}, u32[]{:S(2)}) collective-permute-start(bf16[464,512]{1,0:T(8,128)(2,1)} %concatenate.34), channel_id=1, source_target_pairs={{0,64},{64,128},{128,192},{192,0},{1,65},{65,129},{129,193},{193,1... | collective-permute-start | bytes 1425416 | tf_op jit(solution)/shard_map/ppermute | solution.py:143
  210.3 9.2 %copy-start.10 = (bf16[8,1,64,464]{3,2,1,0:T(8,128)(2,1)S(1)}, bf16[8,1,64,464]{3,2,1,0:T(8,128)(2,1)}, u32[]{:S(2)}) copy-start(bf16[8,1,64,464]{3,2,1,0:T(8,128)(2,1)} %get-tuple-element.68) | copy-start | bytes 1425412
  210.3 27.8 %all-to-all-start.2 = ((bf16[4,464,512]{2,1,0:T(8,128)(2,1)}), bf16[4,464,512]{2,1,0:T(8,128)(2,1)}, u32[]{:S(2)}, u32[]{:S(2)}) async-start(bf16[4,464,512]{2,1,0:T(8,128)(2,1)} %broadcast_in_dim.7), calls=%async_computation.2 | async-start | bytes 3801088 | tf_op jit(solution)/shard_map/all_to_all | solution.py:208
  214.8 15.0 %copy-start.8 = (bf16[8,1,64,464]{3,2,1,0:T(8,128)(2,1)S(1)}, bf16[8,1,64,464]{3,2,1,0:T(8,128)(2,1)}, u32[]{:S(2)}) copy-start(bf16[8,1,64,464]{3,2,1,0:T(8,128)(2,1)} %get-tuple-element.72) | copy-start | bytes 1425412
  215.3 16.0 %copy-start.11 = (bf16[8,1,64,464]{3,2,1,0:T(8,128)(2,1)S(1)}, bf16[8,1,64,464]{3,2,1,0:T(8,128)(2,1)}, u32[]{:S(2)}) copy-start(bf16[8,1,64,464]{3,2,1,0:T(8,128)(2,1)} %get-tuple-element.77) | copy-start | bytes 1425412
  232.9 3.5 %collective-permute-start.9 = (f32[512,512]{1,0:T(8,128)S(1)}, f32[512,512]{1,0:T(8,128)S(1)}, u32[]{:S(2)}, u32[]{:S(2)}) collective-permute-start(f32[512,512]{1,0:T(8,128)S(1)} %fusion), channel_id=1, source_target_pairs={{0,4},{4,0},{1,5},{5,1},{2,6},{6,2},{3,7},{7,3},{8,12},{12,8},{9,1... | collective-permute-start | bytes 3145736 | tf_op jit(solution)/shard_map/ppermute | solution.py:143
  238.1 13.4 %collective-permute-start.10 = (f32[64,512]{1,0:T(8,128)S(1)}, f32[64,512]{1,0:T(8,128)S(1)}, u32[]{:S(2)}, u32[]{:S(2)}) collective-permute-start(f32[64,512]{1,0:T(8,128)S(1)} %get-tuple-element.67), channel_id=1, source_target_pairs={{0,8},{8,16},{16,24},{24,32},{32,40},{40,48},{48,56},{56,0},{1,9},... | collective-permute-start | bytes 393224 | tf_op jit(solution)/shard_map/ppermute | solution.py:143
  241.3 20.3 %collective-permute-start.11 = (f32[64,512]{1,0:T(8,128)S(1)}, f32[64,512]{1,0:T(8,128)S(1)}, u32[]{:S(2)}, u32[]{:S(2)}) collective-permute-start(f32[64,512]{1,0:T(8,128)S(1)} %get-tuple-element.61), channel_id=1, source_target_pairs={{0,16},{8,24},{16,32},{24,40},{32,48},{40,56},{48,0},{56,8},{1,17}... | collective-permute-start | bytes 393224 | tf_op jit(solution)/shard_map/ppermute | solution.py:143
  247.4 19.2 %collective-permute-start.16 = (f32[64,512]{1,0:T(8,128)S(1)}, f32[64,512]{1,0:T(8,128)S(1)}, u32[]{:S(2)}, u32[]{:S(2)}) collective-permute-start(f32[64,512]{1,0:T(8,128)S(1)} %get-tuple-element.62), channel_id=1, source_target_pairs={{0,56},{8,0},{16,8},{24,16},{32,24},{40,32},{48,40},{56,48},{1,57}... | collective-permute-start | bytes 393224 | tf_op jit(solution)/shard_map/ppermute | solution.py:143
  247.4 19.2 %collective-permute-start.15 = (f32[64,512]{1,0:T(8,128)S(1)}, f32[64,512]{1,0:T(8,128)S(1)}, u32[]{:S(2)}, u32[]{:S(2)}) collective-permute-start(f32[64,512]{1,0:T(8,128)S(1)} %get-tuple-element.63), channel_id=1, source_target_pairs={{0,48},{8,56},{16,0},{24,8},{32,16},{40,24},{48,32},{56,40},{1,49}... | collective-permute-start | bytes 393224 | tf_op jit(solution)/shard_map/ppermute | solution.py:143
  247.4 25.4 %collective-permute-start.14 = (f32[64,512]{1,0:T(8,128)S(1)}, f32[64,512]{1,0:T(8,128)S(1)}, u32[]{:S(2)}, u32[]{:S(2)}) collective-permute-start(f32[64,512]{1,0:T(8,128)S(1)} %get-tuple-element.64), channel_id=1, source_target_pairs={{0,40},{8,48},{16,56},{24,0},{32,8},{40,16},{48,24},{56,32},{1,41}... | collective-permute-start | bytes 393224 | tf_op jit(solution)/shard_map/ppermute | solution.py:143
  251.5 21.3 %collective-permute-start.13 = (f32[64,512]{1,0:T(8,128)S(1)}, f32[64,512]{1,0:T(8,128)S(1)}, u32[]{:S(2)}, u32[]{:S(2)}) collective-permute-start(f32[64,512]{1,0:T(8,128)S(1)} %get-tuple-element.65), channel_id=1, source_target_pairs={{0,32},{8,40},{16,48},{24,56},{32,0},{40,8},{48,16},{56,24},{1,33}... | collective-permute-start | bytes 393224 | tf_op jit(solution)/shard_map/ppermute | solution.py:143
  261.6 11.1 %collective-permute-start.12 = (f32[64,512]{1,0:T(8,128)S(1)}, f32[64,512]{1,0:T(8,128)S(1)}, u32[]{:S(2)}, u32[]{:S(2)}) collective-permute-start(f32[64,512]{1,0:T(8,128)S(1)} %get-tuple-element.66), channel_id=1, source_target_pairs={{0,24},{8,32},{16,40},{24,48},{32,56},{40,0},{48,8},{56,16},{1,25}... | collective-permute-start | bytes 393224 | tf_op jit(solution)/shard_map/ppermute | solution.py:143
  (13 other events, 34.6 us)

commit v6 on v4

--- a/solution.py
+++ b/solution.py
@@ -106,7 +106,7 @@
         dq_ref[:, c] = jnp.dot(dscore, k, preferred_element_type=F32).astype(BF16)
 
 
-def attend(q, g, kv, neigh):
+def attend(q, g, kv, neigh, first):
     rows, width = q.shape
     count = rows // STRETCH
     _, heads, tiles, slots, _, _ = kv.shape
@@ -117,16 +117,59 @@
         in_specs=[
             block,
             block,
-            pl.BlockSpec((2, heads, tiles, neigh, TILE, HEAD_DIM), lambda c: (0, 0, 0, c, 0, 0)),
+            pl.BlockSpec((2, heads, tiles, neigh, TILE, HEAD_DIM), lambda c: (0, 0, 0, c + first, 0, 0)),
         ],
         out_specs=[block, block],
         out_shape=[jax.ShapeDtypeStruct(q.shape, BF16)] * 2,
         compiler_params=pltpu.CompilerParams(vmem_limit_bytes=VMEM),
         cost_estimate=pl.CostEstimate(
-            flops=10 * rows * width * neigh * tiles * TILE, bytes_accessed=kv.size * 2, transcendentals=0
+            flops=128 * rows * width * neigh * tiles * TILE, bytes_accessed=kv.size, transcendentals=0
         ),
         name="attend",
     )(q, g, kv)
+
+
+def fold_kernel(at_ref, *refs, parts, rows):
+    count = (len(refs) - 3) // (1 + parts)
+    shares, nears = refs[:count], refs[count : count * (1 + parts)]
+    keep_ref, send_ref, block_ref = refs[count * (1 + parts) :]
+    blocks = keep_ref.shape[0]
+    core = at_ref[1]
+
+    @pl.loop(0, blocks)
+    def _(block):
+        at = lax.rem(at_ref[0] + block, blocks) * (2 * rows)
+        cols = pl.ds(pl.multiple_of(at, 2 * rows), 2 * rows)
+        total = jnp.zeros(block_ref.shape, F32)
+        for i, share in enumerate(shares):
+            low = 0
+            for near in nears[i * parts : (i + 1) * parts]:
+                high = low + near.shape[0]
+                total += lax.dot_general(share[low:high, cols], near[...], BOTH_FIRST, preferred_element_type=F32)
+                low = high
+        block_ref[...] = total
+        keep_ref[block] = block_ref[pl.ds(pl.multiple_of(core * rows, rows), rows)]
+        send_ref[block] = block_ref[pl.ds(pl.multiple_of((1 - core) * rows, rows), rows)]
+
+
+def fold(at, shares, nears, blocks):
+    width = nears[0][0].shape[1]
+    rows = shares[0].shape[1] // (2 * blocks)
+    whole = pl.BlockSpec(memory_space=pltpu.VMEM)
+    flat = list(shares) + [a for pair in nears for a in pair]
+    tokens = sum(a.shape[0] for a in shares)
+    return pl.pallas_call(
+        functools.partial(fold_kernel, parts=len(nears[0]), rows=rows),
+        in_specs=[pl.BlockSpec(memory_space=pltpu.SMEM)] + [whole] * len(flat),
+        out_specs=[whole] * 2,
+        out_shape=[jax.ShapeDtypeStruct((blocks, rows, width), F32)] * 2,
+        scratch_shapes=[pltpu.VMEM((2 * rows, width), F32)],
+        compiler_params=pltpu.CompilerParams(vmem_limit_bytes=VMEM),
+        cost_estimate=pl.CostEstimate(
+            flops=4 * tokens * blocks * rows * width, bytes_accessed=8 << 20, transcendentals=0
+        ),
+        name="fold",
+    )(at, *flat)
 
 
 def step(array, axis, by):
@@ -176,21 +219,23 @@
     g = shifted(grad_rows)
     got, share, q, g = lax.optimization_barrier((got, share, q, g))
 
-    out, dq = attend(q, g, got.reshape(2, heads, tiles, requests, TILE, HEAD_DIM), neigh)
-    dq = jnp.concatenate([jnp.zeros((LEAD - SKIP, width), BF16), dq[:real]], 0)
-
-    total = 0.0
-    for by in range(nx):
-        near = step(dq, "x", by) if by else dq
-        total += lax.dot_general(share[by], near, BOTH_FIRST, preferred_element_type=F32)
-    total = total.reshape(nz, nc, -1, width)
-    mine = lax.dynamic_index_in_dim(total, mc, 1, keepdims=False)
-    mine += step(lax.dynamic_index_in_dim(total, 1 - mc, 1, keepdims=False), "core", 1)
+    half = stretches // 2 * STRETCH
+    got = got.reshape(2, heads, tiles, requests, TILE, HEAD_DIM)
+    out, first = attend(q[:half], g[:half], got, neigh, 0)
+    out_late, last = attend(q[half:], g[half:], got, neigh, half // STRETCH)
+    cut_at = half - LEAD + SKIP
+    first, spill = jnp.concatenate([jnp.zeros((LEAD - SKIP, width), BF16), first[:cut_at]], 0), first[cut_at:]
+    last = jnp.concatenate([spill, last[: real - half]], 0)
+    early = [step(first, "x", by) if by else first for by in range(nx)]
+    last, early[1] = lax.optimization_barrier((last, early[1]))
+    nears = [(early[by], step(last, "x", by) if by else last) for by in range(nx)]
+    mine, other = fold(jnp.stack([mz, mc]), share, nears, nz)
+    mine += step(other, "core", 1)
+    dq = jnp.concatenate([first, last], 0)
     groups = jnp.broadcast_to(dq[None], (nmp,) + dq.shape)
     groups = lax.all_to_all(groups, "mp", split_axis=0, concat_axis=0, tiled=True)
     groups, mine = lax.optimization_barrier((groups, mine))
-    terms = [lax.dynamic_index_in_dim(mine, (mz + by) % nz, 0, keepdims=False) for by in range(nz)]
-    terms = [step(a, "z", by) if by else a for by, a in enumerate(terms)]
+    terms = [step(mine[by], "z", by) if by else mine[by] for by in range(nz)]
 
     groups, terms[1] = lax.optimization_barrier((groups, terms[1]))
     query_grad = sum(terms)
@@ -199,7 +244,7 @@
         near = lax.dynamic_index_in_dim(groups, (my - by) % nmp, 0, keepdims=False)
         part += lax.dot_general(near, fans[by], BOTH_LAST, preferred_element_type=F32).astype(BF16).astype(F32)
     part = part.astype(BF16)
-    attended = jnp.concatenate([jnp.zeros((LEAD, width), BF16), out[:real]], 0)
+    attended = jnp.concatenate([jnp.zeros((LEAD, width), BF16), out, out_late[: real - half]], 0)
     input_grad = jnp.concatenate([jnp.zeros((SKIP, d // nmp), BF16), part], 0)
     return attended[None], input_grad[None], query_grad
 

time: 262 us -> 271 us (1.034)
  local copies, waits for them, and re-layouts: 22 us -> 30.7 us
  Pallas kernels: 10.3 us -> 16.7 us
  matrix products: 16 us -> 9.76 us
    unnamed x28 -> x52, local copies, waits for them, and re-layouts: 9.49 us -> 21.4 us
    dot_general x4 -> x0, matrix products: 6.35 us -> none  [local(): lax.dot_general(share[by], near, BOTH_FIRST, preferred_element_type=F32)]
    pallas_call x0 -> x1, Pallas kernels: none -> 5.7 us  [fold(): pl.pallas_call(functools.partial(fold_kernel, parts=len(nears[0]), rows=r...]
    ppermute x17 -> x20, waiting for transfers between devices: 143 us -> 142 us  [step(): lax.ppermute(array, axis, [(i, (i + by) % size) for i in range(size)])]
    pallas_call x1 -> x2, Pallas kernels: 7.63 us -> 8.28 us  [attend(): pl.pallas_call(functools.partial(attend_kernel, heads=heads), grid=(count...]
    ppermute x17 -> x20, starting transfers between devices: 29.7 us -> 30.3 us  [step(): lax.ppermute(array, axis, [(i, (i + by) % size) for i in range(size)])]
  transfers between devices with their start and end apart: 20 -> 23, of which waited for: 11 -> 13; matrix products, arithmetic and copies ran while one was open for 11% -> 8% of each run, Pallas kernels for 0% -> 4%
where the time goes in v6:
time: 271 us; the launch traced here: 269 us
  waiting for transfers between devices  150 us (55%)
  starting transfers between devices  57 us (21%)
  local copies, waits for them, and re-layouts  30.7 us (11%)
  Pallas kernels  16.7 us (6%)
  matrix products  9.76 us (4%)
  other arithmetic  3.55 us (1%)
    ppermute x20, waiting for transfers between devices, step(): lax.ppermute(array, axis, [(i, (i + by) % size) for i in range(size)])  142 us
    ppermute x20, starting transfers between devices, step(): lax.ppermute(array, axis, [(i, (i + by) % size) for i in range(size)])  30.3 us
    unnamed x52, local copies, waits for them, and re-layouts  21.4 us
    all_to_all x1, starting transfers between devices, local(): held = lax.all_to_all(message, DP, split_axis=0, concat_axis=0, tiled=True)  11.6 us
    all_to_all x1, starting transfers between devices, local(): lax.all_to_all(send.reshape(ndp, requests, TILE, HEAD_DIM), DP, split_axi...  10.6 us
    pallas_call x2, Pallas kernels, attend(): pl.pallas_call(functools.partial(attend_kernel, heads=heads), grid=(count...  8.28 us
    dot_general x4, matrix products, local(): lax.dot_general(near, fans[by], BOTH_LAST, preferred_element_type=F32)  7.44 us
    all_to_all x1, waiting for transfers between devices, local(): lax.all_to_all(send.reshape(ndp, requests, TILE, HEAD_DIM), DP, split_axi...  7.09 us
  transfers between devices with their start and end apart: 23, of which 13 were waited for; matrix products, arithmetic and copies ran while one was open for 8% of the time, Pallas kernels for 4%

profile of v6, /device:TPU:32, one launch (start us, length us, event | category | flops | bytes accessed | tf_op | source)
XLA Modules:
  0.0 268.8 jit_solution(10818223581239217577)
XLA Ops:
  5.9 11.6 %all-to-all-start = ((bf16[64,9,16,128]{3,2,1,0:T(8,128)(2,1)}), bf16[64,9,16,128]{3,2,1,0:T(8,128)(2,1)S(1)}, u32[]{:S(2)}, u32[]{:S(2)}) async-start(bf16[64,9,16,128]{3,2,1,0:T(8,128)(2,1)} %bitcast.63), calls=%async_computation | async-start | bytes 4718592 | tf_op jit(solution)/shard_map/all_to_all | solution.py:196
  17.6 3.4 %constant_dynamic-slice_fusion = (bf16[1024,512]{1,0:T(8,128)(2,1)S(1)}, bf16[1024,512]{1,0:T(8,128)(2,1)S(1)}, bf16[1024,512]{1,0:T(8,128)(2,1)S(1)}, bf16[1024,512]{1,0:T(8,128)(2,1)}) fusion(bf16[4096,512]{1,0:T(8,128)(2,1)} %param.7, s32[]{:T(128)S(6)} %select_n.93, s32[]{:T(128)S(6)} %select_n.91, s32[]{:T(128)S(6)} %select_n.89, s32[]{:T(128)S(6)} %select_n.87), kind=kLoop, calls=%fused_computation.39 | loop fusion | bytes 8388624 | tf_op jit(solution)/shard_map/dynamic_slice | solution.py:199
  21.0 3.0 %collective-permute-start.2 = (bf16[1024,512]{1,0:T(8,128)(2,1)S(1)}, bf16[1024,512]{1,0:T(8,128)(2,1)S(1)}, u32[]{:S(2)}, u32[]{:S(2)}) collective-permute-start(bf16[1024,512]{1,0:T(8,128)(2,1)S(1)} %get-tuple-element.61), channel_id=1, source_target_pairs={{0,3},{1,0},{2,1},{3,2},{4,7},{5,4},{6,5},{7,6},{8,11},{9,8},{10,9... | collective-permute-start | bytes 3145736 | tf_op jit(solution)/shard_map/ppermute | solution.py:177
  25.6 43.6 %collective-permute-done.2 = bf16[1024,512]{1,0:T(8,128)(2,1)S(1)} collective-permute-done((bf16[1024,512]{1,0:T(8,128)(2,1)S(1)}, bf16[1024,512]{1,0:T(8,128)(2,1)S(1)}, u32[]{:S(2)}, u32[]{:S(2)}) %collective-permute-start.2) | collective-permute-done | bytes 1048608 | tf_op jit(solution)/shard_map/ppermute | solution.py:177
  77.2 10.6 %all-to-all-start.1 = ((bf16[64,16,16,128]{3,2,1,0:T(8,128)(2,1)}), bf16[64,16,16,128]{3,2,1,0:T(8,128)(2,1)}, u32[]{:S(2)}, u32[]{:S(2)}) async-start(bf16[64,16,16,128]{3,2,1,0:T(8,128)(2,1)} %bitcast.61), calls=%async_computation.1 | async-start | bytes 8388608 | tf_op jit(solution)/shard_map/all_to_all | solution.py:206
  87.9 2.6 constant_dynamic-slice_fusion.4
  90.6 3.0 %collective-permute-start.5 = (bf16[464,1024]{1,0:T(8,128)(2,1)S(1)}, bf16[464,1024]{1,0:T(8,128)(2,1)S(1)}, u32[]{:S(2)}, u32[]{:S(2)}) collective-permute-start(bf16[464,1024]{1,0:T(8,128)(2,1)S(1)} %get-tuple-element.57), channel_id=1, source_target_pairs={{0,192},{64,0},{128,64},{192,128},{1,193},{65,1},{129,65},{193,129... | collective-permute-start | bytes 2850824 | tf_op jit(solution)/shard_map/ppermute | solution.py:177
  95.3 2.3 fusion.20
  97.8 41.3 %collective-permute-done.5.refs_3_ = bf16[464,1024]{1,0:T(8,128)(2,1)S(1)} collective-permute-done((bf16[464,1024]{1,0:T(8,128)(2,1)S(1)}, bf16[464,1024]{1,0:T(8,128)(2,1)S(1)}, u32[]{:S(2)}, u32[]{:S(2)}) %collective-permute-start.5) | collective-permute-done | bytes 950304 | tf_op jit(solution)/shard_map/ppermute | solution.py:177
  141.0 32.8 %collective-permute-done.3.refs_1_ = bf16[464,1024]{1,0:T(8,128)(2,1)S(1)} collective-permute-done((bf16[464,1024]{1,0:T(8,128)(2,1)S(1)}, bf16[464,1024]{1,0:T(8,128)(2,1)S(1)}, u32[]{:S(2)}, u32[]{:S(2)}) %collective-permute-start.3) | collective-permute-done | bytes 950304 | tf_op jit(solution)/shard_map/ppermute | solution.py:177
  174.8 7.1 %all-to-all-done.1 = bf16[64,16,16,128]{3,2,1,0:T(8,128)(2,1)} async-done(((bf16[64,16,16,128]{3,2,1,0:T(8,128)(2,1)}), bf16[64,16,16,128]{3,2,1,0:T(8,128)(2,1)}, u32[]{:S(2)}, u32[]{:S(2)}) %all-to-all-start.1) | async-done | bytes 4194336 | tf_op jit(solution)/shard_map/all_to_all | solution.py:206
  182.0 4.1 %attend.2 = (bf16[256,512]{1,0:T(8,128)(2,1)S(1)}, bf16[256,512]{1,0:T(8,128)(2,1)S(1)}) custom-call(bf16[256,512]{1,0:T(8,128)(2,1)S(1)} %get-tuple-element.77.q_ref, bf16[256,512]{1,0:T(8,128)(2,1)S(1)} %get-tuple-element.72.g_ref, bf16[2,4,8,16,16,128]{5,4,3,2,1,0:T(8,128)(2,1)} %bitcast.7.kv_ref), custom_call_target="tpu_custom_call" | custom-call | flops 4294967296 | bytes 2097152 | tf_op jit(solution)/shard_map/attend/pallas_call | solution.py:114
  186.3 2.9 %collective-permute-start.10 = (bf16[256,512]{1,0:T(8,128)(2,1)S(1)}, bf16[256,512]{1,0:T(8,128)(2,1)S(1)}, u32[]{:S(2)}, u32[]{:S(2)}) collective-permute-start(bf16[256,512]{1,0:T(8,128)(2,1)S(1)} %concatenate.26.refs_4_), channel_id=1, source_target_pairs={{0,192},{64,0},{128,64},{192,128},{1,193},{65,1},{129,65},{193,129... | collective-permute-start | bytes 786440 | tf_op jit(solution)/shard_map/ppermute | solution.py:177
  190.7 4.1 %attend.3 = (bf16[256,512]{1,0:T(8,128)(2,1)S(1)}, bf16[256,512]{1,0:T(8,128)(2,1)S(1)}) custom-call(bf16[256,512]{1,0:T(8,128)(2,1)S(1)} %get-tuple-element.76.q_ref, bf16[256,512]{1,0:T(8,128)(2,1)S(1)} %get-tuple-element.73.g_ref, bf16[2,4,8,16,16,128]{5,4,3,2,1,0:T(8,128)(2,1)} %bitcast.7.kv_ref), custom_call_target="tpu_custom_call" | custom-call | flops 4294967296 | bytes 2097152 | tf_op jit(solution)/shard_map/attend/pallas_call | solution.py:114
  195.0 10.2 %collective-permute-done.6.refs_6_ = bf16[256,512]{1,0:T(8,128)(2,1)S(1)} collective-permute-done((bf16[256,512]{1,0:T(8,128)(2,1)S(1)}, bf16[256,512]{1,0:T(8,128)(2,1)S(1)}, u32[]{:S(2)}, u32[]{:S(2)}) %collective-permute-start.6) | collective-permute-done | bytes 262176 | tf_op jit(solution)/shard_map/ppermute | solution.py:177
  209.6 4.4 %all-to-all-start.2 = ((bf16[4,464,512]{2,1,0:T(8,128)(2,1)}), bf16[4,464,512]{2,1,0:T(8,128)(2,1)}, u32[]{:S(2)}, u32[]{:S(2)}) async-start(bf16[4,464,512]{2,1,0:T(8,128)(2,1)} %broadcast_in_dim.18), calls=%async_computation.2 | async-start | bytes 3801088 | tf_op jit(solution)/shard_map/all_to_all | solution.py:236
  216.9 2.4 collective-permute-done.7.refs_7_
  227.4 5.7 %fold.1 = (f32[8,64,512]{2,1,0:T(8,128)S(1)}, f32[8,64,512]{2,1,0:T(8,128)}) custom-call(s32[2]{0:T(128)S(1)} %pad_add_fusion.at_ref, bf16[464,1024]{1,0:T(8,128)(2,1)S(1)} %get-tuple-element.42.refs_0_, bf16[464,1024]{1,0:T(8,128)(2,1)S(1)} %copy-done.8, bf16[464,1024]{1,0:T(8,128)(2,1)S(1)} %copy-done.6, bf16[464,1024]{1,0:T(8,128)(2,1)S(1)} %copy-done.4, ...), custom_call_target="tpu_custom_call" | custom-call | flops 1946157056 | bytes 8388608 | tf_op jit(solution)/shard_map/fold/pallas_call | solution.py:161
  233.2 2.9 %collective-permute-done.12 = f32[8,64,512]{2,1,0:T(8,128)} collective-permute-done((f32[8,64,512]{2,1,0:T(8,128)}, f32[8,64,512]{2,1,0:T(8,128)}, u32[]{:S(2)}, u32[]{:S(2)}) %collective-permute-start.12) | collective-permute-done | bytes 1048608 | tf_op jit(solution)/shard_map/ppermute | solution.py:177
  241.5 4.0 %collective-permute-start.18 = (f32[64,512]{1,0:T(8,128)S(1)}, f32[64,512]{1,0:T(8,128)S(1)}, u32[]{:S(2)}, u32[]{:S(2)}) collective-permute-start(f32[64,512]{1,0:T(8,128)S(1)} %get-tuple-element.67), channel_id=1, source_target_pairs={{0,48},{8,56},{16,0},{24,8},{32,16},{40,24},{48,32},{56,40},{1,49}... | collective-permute-start | bytes 393224 | tf_op jit(solution)/shard_map/ppermute | solution.py:177
  247.1 2.9 %collective-permute-start.16 = (f32[64,512]{1,0:T(8,128)S(1)}, f32[64,512]{1,0:T(8,128)S(1)}, u32[]{:S(2)}, u32[]{:S(2)}) collective-permute-start(f32[64,512]{1,0:T(8,128)S(1)} %get-tuple-element.69), channel_id=1, source_target_pairs={{0,32},{8,40},{16,48},{24,56},{32,0},{40,8},{48,16},{56,24},{1,33}... | collective-permute-start | bytes 393224 | tf_op jit(solution)/shard_map/ppermute | solution.py:177
  251.7 2.1 convolution_convert_fusion.2
  257.5 3.8 %collective-permute-start.15 = (f32[64,512]{1,0:T(8,128)S(1)}, f32[64,512]{1,0:T(8,128)S(1)}, u32[]{:S(2)}, u32[]{:S(2)}) collective-permute-start(f32[64,512]{1,0:T(8,128)S(1)} %get-tuple-element.70), channel_id=1, source_target_pairs={{0,24},{8,32},{16,40},{24,48},{32,56},{40,0},{48,8},{56,16},{1,25}... | collective-permute-start | bytes 393224 | tf_op jit(solution)/shard_map/ppermute | solution.py:177
  263.8 3.4 %collective-permute-done.16 = f32[64,512]{1,0:T(8,128)S(1)} collective-permute-done((f32[64,512]{1,0:T(8,128)S(1)}, f32[64,512]{1,0:T(8,128)S(1)}, u32[]{:S(2)}, u32[]{:S(2)}) %collective-permute-start.16) | collective-permute-done | bytes 131104 | tf_op jit(solution)/shard_map/ppermute | solution.py:177
  (112 shorter events, 53.4 us)
Async XLA Ops:
  5.9 67.1 %all-to-all-start = ((bf16[64,9,16,128]{3,2,1,0:T(8,128)(2,1)}), bf16[64,9,16,128]{3,2,1,0:T(8,128)(2,1)S(1)}, u32[]{:S(2)}, u32[]{:S(2)}) async-start(bf16[64,9,16,128]{3,2,1,0:T(8,128)(2,1)} %bitcast.63), calls=%async_computation | async-start | bytes 4718592 | tf_op jit(solution)/shard_map/all_to_all | solution.py:196
  21.0 48.2 %collective-permute-start.2 = (bf16[1024,512]{1,0:T(8,128)(2,1)S(1)}, bf16[1024,512]{1,0:T(8,128)(2,1)S(1)}, u32[]{:S(2)}, u32[]{:S(2)}) collective-permute-start(bf16[1024,512]{1,0:T(8,128)(2,1)S(1)} %get-tuple-element.61), channel_id=1, source_target_pairs={{0,3},{1,0},{2,1},{3,2},{4,7},{5,4},{6,5},{7,6},{8,11},{9,8},{10,9... | collective-permute-start | bytes 3145736 | tf_op jit(solution)/shard_map/ppermute | solution.py:177
  24.0 45.2 %collective-permute-start.1 = (bf16[1024,512]{1,0:T(8,128)(2,1)S(1)}, bf16[1024,512]{1,0:T(8,128)(2,1)S(1)}, u32[]{:S(2)}, u32[]{:S(2)}) collective-permute-start(bf16[1024,512]{1,0:T(8,128)(2,1)S(1)} %get-tuple-element.62), channel_id=1, source_target_pairs={{0,2},{1,3},{2,0},{3,1},{4,6},{5,7},{6,4},{7,5},{8,10},{9,11},{10,... | collective-permute-start | bytes 3145736 | tf_op jit(solution)/shard_map/ppermute | solution.py:177
  24.6 48.4 %collective-permute-start = (bf16[1024,512]{1,0:T(8,128)(2,1)S(1)}, bf16[1024,512]{1,0:T(8,128)(2,1)}, u32[]{:S(2)}, u32[]{:S(2)}) collective-permute-start(bf16[1024,512]{1,0:T(8,128)(2,1)S(1)} %get-tuple-element.63), channel_id=1, source_target_pairs={{0,1},{1,2},{2,3},{3,0},{4,5},{5,6},{6,7},{7,4},{8,9},{9,10},{10,1... | collective-permute-start | bytes 3145736 | tf_op jit(solution)/shard_map/ppermute | solution.py:177
  77.2 18.0 %copy-start.20 = (bf16[1,512,512]{2,1,0:T(8,128)(2,1)S(1)}, bf16[1,512,512]{2,1,0:T(8,128)(2,1)}, u32[]{:S(2)}) copy-start(bf16[1,512,512]{2,1,0:T(8,128)(2,1)} %param.11) | copy-start | bytes 1572868
  77.2 104.7 %all-to-all-start.1 = ((bf16[64,16,16,128]{3,2,1,0:T(8,128)(2,1)}), bf16[64,16,16,128]{3,2,1,0:T(8,128)(2,1)}, u32[]{:S(2)}, u32[]{:S(2)}) async-start(bf16[64,16,16,128]{3,2,1,0:T(8,128)(2,1)} %bitcast.61), calls=%async_computation.1 | async-start | bytes 8388608 | tf_op jit(solution)/shard_map/all_to_all | solution.py:206
  90.6 48.6 %collective-permute-start.5 = (bf16[464,1024]{1,0:T(8,128)(2,1)S(1)}, bf16[464,1024]{1,0:T(8,128)(2,1)S(1)}, u32[]{:S(2)}, u32[]{:S(2)}) collective-permute-start(bf16[464,1024]{1,0:T(8,128)(2,1)S(1)} %get-tuple-element.57), channel_id=1, source_target_pairs={{0,192},{64,0},{128,64},{192,128},{1,193},{65,1},{129,65},{193,129... | collective-permute-start | bytes 2850824 | tf_op jit(solution)/shard_map/ppermute | solution.py:177
  93.5 46.5 %collective-permute-start.4 = (bf16[464,1024]{1,0:T(8,128)(2,1)S(1)}, bf16[464,1024]{1,0:T(8,128)(2,1)S(1)}, u32[]{:S(2)}, u32[]{:S(2)}) collective-permute-start(bf16[464,1024]{1,0:T(8,128)(2,1)S(1)} %get-tuple-element.58), channel_id=1, source_target_pairs={{0,128},{64,192},{128,0},{192,64},{1,129},{65,193},{129,1},{193,65... | collective-permute-start | bytes 2850824 | tf_op jit(solution)/shard_map/ppermute | solution.py:177
  94.2 79.6 %collective-permute-start.3 = (bf16[464,1024]{1,0:T(8,128)(2,1)S(1)}, bf16[464,1024]{1,0:T(8,128)(2,1)S(1)}, u32[]{:S(2)}, u32[]{:S(2)}) collective-permute-start(bf16[464,1024]{1,0:T(8,128)(2,1)S(1)} %get-tuple-element.59), channel_id=1, source_target_pairs={{0,64},{64,128},{128,192},{192,0},{1,65},{65,129},{129,193},{193,1... | collective-permute-start | bytes 2850824 | tf_op jit(solution)/shard_map/ppermute | solution.py:177
  186.3 27.8 %collective-permute-start.10 = (bf16[256,512]{1,0:T(8,128)(2,1)S(1)}, bf16[256,512]{1,0:T(8,128)(2,1)S(1)}, u32[]{:S(2)}, u32[]{:S(2)}) collective-permute-start(bf16[256,512]{1,0:T(8,128)(2,1)S(1)} %concatenate.26.refs_4_), channel_id=1, source_target_pairs={{0,192},{64,0},{128,64},{192,128},{1,193},{65,1},{129,65},{193,129... | collective-permute-start | bytes 786440 | tf_op jit(solution)/shard_map/ppermute | solution.py:177
  189.1 24.9 %collective-permute-start.8 = (bf16[256,512]{1,0:T(8,128)(2,1)S(1)}, bf16[256,512]{1,0:T(8,128)(2,1)S(1)}, u32[]{:S(2)}, u32[]{:S(2)}) collective-permute-start(bf16[256,512]{1,0:T(8,128)(2,1)S(1)} %concatenate.26.refs_4_), channel_id=1, source_target_pairs={{0,128},{64,192},{128,0},{192,64},{1,129},{65,193},{129,1},{193,65... | collective-permute-start | bytes 786440 | tf_op jit(solution)/shard_map/ppermute | solution.py:177
  189.8 15.4 %collective-permute-start.6 = (bf16[256,512]{1,0:T(8,128)(2,1)S(1)}, bf16[256,512]{1,0:T(8,128)(2,1)S(1)}, u32[]{:S(2)}, u32[]{:S(2)}) collective-permute-start(bf16[256,512]{1,0:T(8,128)(2,1)S(1)} %concatenate.26.refs_4_), channel_id=1, source_target_pairs={{0,64},{64,128},{128,192},{192,0},{1,65},{65,129},{129,193},{193,1... | collective-permute-start | bytes 786440 | tf_op jit(solution)/shard_map/ppermute | solution.py:177
  205.9 8.2 %collective-permute-start.11 = (bf16[208,512]{1,0:T(8,128)(2,1)S(1)}, bf16[208,512]{1,0:T(8,128)(2,1)S(1)}, u32[]{:S(2)}, u32[]{:S(2)}) collective-permute-start(bf16[208,512]{1,0:T(8,128)(2,1)S(1)} %pad_maximum_fusion.1.refs_5_), channel_id=1, source_target_pairs={{0,192},{64,0},{128,64},{192,128},{1,193},{65,1},{129,65},{193,129... | collective-permute-start | bytes 638984 | tf_op jit(solution)/shard_map/ppermute | solution.py:177
  206.5 9.7 %collective-permute-start.9 = (bf16[208,512]{1,0:T(8,128)(2,1)S(1)}, bf16[208,512]{1,0:T(8,128)(2,1)S(1)}, u32[]{:S(2)}, u32[]{:S(2)}) collective-permute-start(bf16[208,512]{1,0:T(8,128)(2,1)S(1)} %pad_maximum_fusion.1.refs_5_), channel_id=1, source_target_pairs={{0,128},{64,192},{128,0},{192,64},{1,129},{65,193},{129,1},{193,65... | collective-permute-start | bytes 638984 | tf_op jit(solution)/shard_map/ppermute | solution.py:177
  207.2 12.2 %collective-permute-start.7 = (bf16[208,512]{1,0:T(8,128)(2,1)S(1)}, bf16[208,512]{1,0:T(8,128)(2,1)S(1)}, u32[]{:S(2)}, u32[]{:S(2)}) collective-permute-start(bf16[208,512]{1,0:T(8,128)(2,1)S(1)} %pad_maximum_fusion.1.refs_5_), channel_id=1, source_target_pairs={{0,64},{64,128},{128,192},{192,0},{1,65},{65,129},{129,193},{193,1... | collective-permute-start | bytes 638984 | tf_op jit(solution)/shard_map/ppermute | solution.py:177
  209.6 28.6 %all-to-all-start.2 = ((bf16[4,464,512]{2,1,0:T(8,128)(2,1)}), bf16[4,464,512]{2,1,0:T(8,128)(2,1)}, u32[]{:S(2)}, u32[]{:S(2)}) async-start(bf16[4,464,512]{2,1,0:T(8,128)(2,1)} %broadcast_in_dim.18), calls=%async_computation.2 | async-start | bytes 3801088 | tf_op jit(solution)/shard_map/all_to_all | solution.py:236
  233.1 3.0 %collective-permute-start.12 = (f32[8,64,512]{2,1,0:T(8,128)}, f32[8,64,512]{2,1,0:T(8,128)}, u32[]{:S(2)}, u32[]{:S(2)}) collective-permute-start(f32[8,64,512]{2,1,0:T(8,128)} %get-tuple-element.48), channel_id=1, source_target_pairs={{0,4},{4,0},{1,5},{5,1},{2,6},{6,2},{3,7},{7,3},{8,12},{12,8},{9,1... | collective-permute-start | bytes 3145736 | tf_op jit(solution)/shard_map/ppermute | solution.py:177
  238.3 8.8 %collective-permute-start.13 = (f32[64,512]{1,0:T(8,128)S(1)}, f32[64,512]{1,0:T(8,128)S(1)}, u32[]{:S(2)}, u32[]{:S(2)}) collective-permute-start(f32[64,512]{1,0:T(8,128)S(1)} %get-tuple-element.71), channel_id=1, source_target_pairs={{0,8},{8,16},{16,24},{24,32},{32,40},{40,48},{48,56},{56,0},{1,9},... | collective-permute-start | bytes 393224 | tf_op jit(solution)/shard_map/ppermute | solution.py:177
  239.4 18.1 %collective-permute-start.14 = (f32[64,512]{1,0:T(8,128)S(1)}, f32[64,512]{1,0:T(8,128)S(1)}, u32[]{:S(2)}, u32[]{:S(2)}) collective-permute-start(f32[64,512]{1,0:T(8,128)S(1)} %get-tuple-element.65), channel_id=1, source_target_pairs={{0,16},{8,24},{16,32},{24,40},{32,48},{40,56},{48,0},{56,8},{1,17}... | collective-permute-start | bytes 393224 | tf_op jit(solution)/shard_map/ppermute | solution.py:177
  240.2 22.1 %collective-permute-start.19 = (f32[64,512]{1,0:T(8,128)S(1)}, f32[64,512]{1,0:T(8,128)S(1)}, u32[]{:S(2)}, u32[]{:S(2)}) collective-permute-start(f32[64,512]{1,0:T(8,128)S(1)} %get-tuple-element.66), channel_id=1, source_target_pairs={{0,56},{8,0},{16,8},{24,16},{32,24},{40,32},{48,40},{56,48},{1,57}... | collective-permute-start | bytes 393224 | tf_op jit(solution)/shard_map/ppermute | solution.py:177
  241.5 20.8 %collective-permute-start.18 = (f32[64,512]{1,0:T(8,128)S(1)}, f32[64,512]{1,0:T(8,128)S(1)}, u32[]{:S(2)}, u32[]{:S(2)}) collective-permute-start(f32[64,512]{1,0:T(8,128)S(1)} %get-tuple-element.67), channel_id=1, source_target_pairs={{0,48},{8,56},{16,0},{24,8},{32,16},{40,24},{48,32},{56,40},{1,49}... | collective-permute-start | bytes 393224 | tf_op jit(solution)/shard_map/ppermute | solution.py:177
  245.5 18.3 %collective-permute-start.17 = (f32[64,512]{1,0:T(8,128)S(1)}, f32[64,512]{1,0:T(8,128)S(1)}, u32[]{:S(2)}, u32[]{:S(2)}) collective-permute-start(f32[64,512]{1,0:T(8,128)S(1)} %get-tuple-element.68), channel_id=1, source_target_pairs={{0,40},{8,48},{16,56},{24,0},{32,8},{40,16},{48,24},{56,32},{1,41}... | collective-permute-start | bytes 393224 | tf_op jit(solution)/shard_map/ppermute | solution.py:177
  247.1 20.1 %collective-permute-start.16 = (f32[64,512]{1,0:T(8,128)S(1)}, f32[64,512]{1,0:T(8,128)S(1)}, u32[]{:S(2)}, u32[]{:S(2)}) collective-permute-start(f32[64,512]{1,0:T(8,128)S(1)} %get-tuple-element.69), channel_id=1, source_target_pairs={{0,32},{8,40},{16,48},{24,56},{32,0},{40,8},{48,16},{56,24},{1,33}... | collective-permute-start | bytes 393224 | tf_op jit(solution)/shard_map/ppermute | solution.py:177
  257.5 10.6 %collective-permute-start.15 = (f32[64,512]{1,0:T(8,128)S(1)}, f32[64,512]{1,0:T(8,128)S(1)}, u32[]{:S(2)}, u32[]{:S(2)}) collective-permute-start(f32[64,512]{1,0:T(8,128)S(1)} %get-tuple-element.70), channel_id=1, source_target_pairs={{0,24},{8,32},{16,40},{24,48},{32,56},{40,0},{48,8},{56,16},{1,25}... | collective-permute-start | bytes 393224 | tf_op jit(solution)/shard_map/ppermute | solution.py:177
  (24 other events, 50.5 us)

commit v7 on v4

--- a/solution.py
+++ b/solution.py
@@ -180,7 +180,7 @@
     dq = jnp.concatenate([jnp.zeros((LEAD - SKIP, width), BF16), dq[:real]], 0)
 
     total = 0.0
-    for by in range(nx):
+    for by in sorted(range(nx), key=lambda by: min(by, nx - by)):
         near = step(dq, "x", by) if by else dq
         total += lax.dot_general(share[by], near, BOTH_FIRST, preferred_element_type=F32)
     total = total.reshape(nz, nc, -1, width)
@@ -189,11 +189,15 @@
     groups = jnp.broadcast_to(dq[None], (nmp,) + dq.shape)
     groups = lax.all_to_all(groups, "mp", split_axis=0, concat_axis=0, tiled=True)
     groups, mine = lax.optimization_barrier((groups, mine))
-    terms = [lax.dynamic_index_in_dim(mine, (mz + by) % nz, 0, keepdims=False) for by in range(nz)]
-    terms = [step(a, "z", by) if by else a for by, a in enumerate(terms)]
-
-    groups, terms[1] = lax.optimization_barrier((groups, terms[1]))
-    query_grad = sum(terms)
+    pairs = mine.reshape(nz // 2, 2, -1, width)
+    away = lax.dynamic_index_in_dim(pairs, 1 - mz % 2, 1, keepdims=False)
+    mine = lax.dynamic_index_in_dim(pairs, mz % 2, 1, keepdims=False)
+    up = lax.ppermute(away[..., : width // 2], "z", [(i, i ^ 1) for i in range(nz)])
+    down = lax.ppermute(away[..., width // 2 :], "z", [(i, ((i + 1) ^ 1) - 1) for i in range(1, nz - 1)] + [(0, nz - 1), (nz - 1, 0)])
+    groups, up = lax.optimization_barrier((groups, up))
+    mine += jnp.concatenate([up, down], -1)
+    terms = [lax.dynamic_index_in_dim(mine, (mz // 2 + by) % (nz // 2), 0, keepdims=False) for by in range(nz // 2)]
+    query_grad = sum(step(a, "z", 2 * by) if by else a for by, a in enumerate(terms))
     part = 0.0
     for by in range(nmp):
         near = lax.dynamic_index_in_dim(groups, (my - by) % nmp, 0, keepdims=False)

time: 262 us -> 257 us (0.981)
  starting transfers between devices: 56.4 us -> 51.1 us
    ppermute x0 -> x2, waiting for transfers between devices: none -> 7.1 us  [the longest x1 5.72 us: local(): lax.ppermute(away[..., :width // 2], 'z', [(i, i ^ 1) for i in range(nz)])]
    ppermute x17 -> x13, starting transfers between devices: 29.7 us -> 23.5 us  [step(): lax.ppermute(array, axis, [(i, (i + by) % size) for i in range(size)])]
    ppermute x17 -> x13, waiting for transfers between devices: 143 us -> 137 us  [step(): lax.ppermute(array, axis, [(i, (i + by) % size) for i in range(size)])]
    unnamed x28 -> x26, local copies, waits for them, and re-layouts: 9.49 us -> 8.51 us
  transfers between devices with their start and end apart: 20 -> 18, of which waited for: 11 -> 12; matrix products, arithmetic and copies ran while one was open for 11% -> 12% of each run, Pallas kernels for 0% -> 0%
where the time goes in v7:
time: 257 us; the launch traced here: 256 us
  waiting for transfers between devices  153 us (60%)
  starting transfers between devices  51.1 us (20%)
  local copies, waits for them, and re-layouts  20.9 us (8%)
  matrix products  16.3 us (6%)
  Pallas kernels  10.3 us (4%)
  other arithmetic  3.28 us (1%)
    ppermute x13, waiting for transfers between devices, step(): lax.ppermute(array, axis, [(i, (i + by) % size) for i in range(size)])  137 us
    ppermute x13, starting transfers between devices, step(): lax.ppermute(array, axis, [(i, (i + by) % size) for i in range(size)])  23.5 us
    all_to_all x1, starting transfers between devices, local(): held = lax.all_to_all(message, DP, split_axis=0, concat_axis=0, tiled=True)  11.6 us
    all_to_all x1, starting transfers between devices, local(): lax.all_to_all(send.reshape(ndp, requests, TILE, HEAD_DIM), DP, split_axi...  10.6 us
    unnamed x26, local copies, waits for them, and re-layouts  8.51 us
    all_to_all x1, waiting for transfers between devices, local(): lax.all_to_all(send.reshape(ndp, requests, TILE, HEAD_DIM), DP, split_axi...  7.98 us
    pallas_call x1, Pallas kernels, attend(): pl.pallas_call(functools.partial(attend_kernel, heads=heads), grid=(count...  7.63 us
    dot_general x4, matrix products, local(): lax.dot_general(near, fans[by], BOTH_LAST, preferred_element_type=F32)  7.35 us
  transfers between devices with their start and end apart: 18, of which 12 were waited for; matrix products, arithmetic and copies ran while one was open for 12% of the time, Pallas kernels for 0%

profile of v7, /device:TPU:32, one launch (start us, length us, event | category | flops | bytes accessed | tf_op | source)
XLA Modules:
  0.0 256.2 jit_solution(16775211784848150715)
XLA Ops:
  5.9 11.6 %all-to-all-start = ((bf16[64,9,16,128]{3,2,1,0:T(8,128)(2,1)}), bf16[64,9,16,128]{3,2,1,0:T(8,128)(2,1)S(1)}, u32[]{:S(2)}, u32[]{:S(2)}) async-start(bf16[64,9,16,128]{3,2,1,0:T(8,128)(2,1)} %bitcast.62), calls=%async_computation | async-start | bytes 4718592 | tf_op jit(solution)/shard_map/all_to_all | solution.py:153
  17.6 3.4 %constant_dynamic-slice_fusion = (bf16[1024,512]{1,0:T(8,128)(2,1)S(1)}, bf16[1024,512]{1,0:T(8,128)(2,1)S(1)}, bf16[1024,512]{1,0:T(8,128)(2,1)S(1)}, bf16[1024,512]{1,0:T(8,128)(2,1)}) fusion(bf16[4096,512]{1,0:T(8,128)(2,1)} %param.7, s32[]{:T(128)S(6)} %select_n.149, s32[]{:T(128)S(6)} %select_n.147, s32[]{:T(128)S(6)} %select_n.145, s32[]{:T(128)S(6)} %select_n.143), kind=kLoop, calls=%fused_computation.34 | loop fusion | bytes 8388624 | tf_op jit(solution)/shard_map/dynamic_slice | solution.py:156
  21.0 3.0 %collective-permute-start.2 = (bf16[1024,512]{1,0:T(8,128)(2,1)S(1)}, bf16[1024,512]{1,0:T(8,128)(2,1)S(1)}, u32[]{:S(2)}, u32[]{:S(2)}) collective-permute-start(bf16[1024,512]{1,0:T(8,128)(2,1)S(1)} %get-tuple-element.49), channel_id=1, source_target_pairs={{0,3},{1,0},{2,1},{3,2},{4,7},{5,4},{6,5},{7,6},{8,11},{9,8},{10,9... | collective-permute-start | bytes 3145736 | tf_op jit(solution)/shard_map/ppermute | solution.py:134
  25.6 43.6 %collective-permute-done.2 = bf16[1024,512]{1,0:T(8,128)(2,1)S(1)} collective-permute-done((bf16[1024,512]{1,0:T(8,128)(2,1)S(1)}, bf16[1024,512]{1,0:T(8,128)(2,1)S(1)}, u32[]{:S(2)}, u32[]{:S(2)}) %collective-permute-start.2) | collective-permute-done | bytes 1048608 | tf_op jit(solution)/shard_map/ppermute | solution.py:134
  75.2 2.0 copy-done
  77.2 10.6 %all-to-all-start.1 = ((bf16[64,16,16,128]{3,2,1,0:T(8,128)(2,1)}), bf16[64,16,16,128]{3,2,1,0:T(8,128)(2,1)}, u32[]{:S(2)}, u32[]{:S(2)}) async-start(bf16[64,16,16,128]{3,2,1,0:T(8,128)(2,1)} %bitcast.60), calls=%async_computation.1 | async-start | bytes 8388608 | tf_op jit(solution)/shard_map/all_to_all | solution.py:163
  88.0 2.6 %constant_dynamic-slice_fusion.4 = (bf16[464,1024]{1,0:T(8,128)(2,1)S(1)}, bf16[464,1024]{1,0:T(8,128)(2,1)S(1)}, bf16[464,1024]{1,0:T(8,128)(2,1)S(1)}, bf16[464,1024]{1,0:T(8,128)(2,1)S(1)}) fusion(bf16[512,4096]{1,0:T(8,128)(2,1)} %bitcast.67, s32[]{:T(128)S(6)} %select_n.157, s32[]{:T(128)S(6)} %select_n.155, s32[]{:T(128)S(6)} %select_n.153, ...), kind=kLoop, calls=%fused_computation.38 | loop fusion | bytes 7602192 | tf_op jit(solution)/shard_map/dynamic_slice | solution.py:169
  90.6 3.0 %collective-permute-start.5 = (bf16[464,1024]{1,0:T(8,128)(2,1)S(1)}, bf16[464,1024]{1,0:T(8,128)(2,1)S(1)}, u32[]{:S(2)}, u32[]{:S(2)}) collective-permute-start(bf16[464,1024]{1,0:T(8,128)(2,1)S(1)} %get-tuple-element.45), channel_id=1, source_target_pairs={{0,192},{64,0},{128,64},{192,128},{1,193},{65,1},{129,65},{193,129... | collective-permute-start | bytes 2850824 | tf_op jit(solution)/shard_map/ppermute | solution.py:134
  95.3 2.3 fusion.18
  97.9 41.3 %collective-permute-done.5 = bf16[464,1024]{1,0:T(8,128)(2,1)S(1)} collective-permute-done((bf16[464,1024]{1,0:T(8,128)(2,1)S(1)}, bf16[464,1024]{1,0:T(8,128)(2,1)S(1)}, u32[]{:S(2)}, u32[]{:S(2)}) %collective-permute-start.5) | collective-permute-done | bytes 950304 | tf_op jit(solution)/shard_map/ppermute | solution.py:134
  139.2 34.8 %collective-permute-done.3 = bf16[464,1024]{1,0:T(8,128)(2,1)} collective-permute-done((bf16[464,1024]{1,0:T(8,128)(2,1)S(1)}, bf16[464,1024]{1,0:T(8,128)(2,1)}, u32[]{:S(2)}, u32[]{:S(2)}) %collective-permute-start.3) | collective-permute-done | bytes 950304 | tf_op jit(solution)/shard_map/ppermute | solution.py:134
  174.0 8.0 %all-to-all-done.1 = bf16[64,16,16,128]{3,2,1,0:T(8,128)(2,1)} async-done(((bf16[64,16,16,128]{3,2,1,0:T(8,128)(2,1)}), bf16[64,16,16,128]{3,2,1,0:T(8,128)(2,1)}, u32[]{:S(2)}, u32[]{:S(2)}) %all-to-all-start.1) | async-done | bytes 4194336 | tf_op jit(solution)/shard_map/all_to_all | solution.py:163
  182.0 7.6 %attend.1 = (bf16[512,512]{1,0:T(8,128)(2,1)S(1)}, bf16[512,512]{1,0:T(8,128)(2,1)S(1)}) custom-call(bf16[512,512]{1,0:T(8,128)(2,1)S(1)} %concatenate.18.q_ref, bf16[512,512]{1,0:T(8,128)(2,1)S(1)} %concatenate.19.g_ref, bf16[2,4,8,16,16,128]{5,4,3,2,1,0:T(8,128)(2,1)} %bitcast.7.kv_ref), custom_call_target="tpu_custom_call" | custom-call | flops 671088640 | bytes 4194304 | tf_op jit(solution)/shard_map/attend/pallas_call | solution.py:114
  196.2 4.4 %all-to-all-start.2 = ((bf16[4,464,512]{2,1,0:T(8,128)(2,1)}), bf16[4,464,512]{2,1,0:T(8,128)(2,1)}, u32[]{:S(2)}, u32[]{:S(2)}) async-start(bf16[4,464,512]{2,1,0:T(8,128)(2,1)} %broadcast_in_dim.7), calls=%async_computation.2 | async-start | bytes 3801088 | tf_op jit(solution)/shard_map/all_to_all | solution.py:190
  201.4 3.4 %collective-permute-done.6 = bf16[464,512]{1,0:T(8,128)(2,1)} collective-permute-done((bf16[464,512]{1,0:T(8,128)(2,1)S(1)}, bf16[464,512]{1,0:T(8,128)(2,1)}, u32[]{:S(2)}, u32[]{:S(2)}) %collective-permute-start.6) | collective-permute-done | bytes 475168 | tf_op jit(solution)/shard_map/ppermute | solution.py:134
  204.8 2.0 fusion.19
  206.8 7.4 %collective-permute-done.7 = bf16[464,512]{1,0:T(8,128)(2,1)} collective-permute-done((bf16[464,512]{1,0:T(8,128)(2,1)S(1)}, bf16[464,512]{1,0:T(8,128)(2,1)}, u32[]{:S(2)}, u32[]{:S(2)}) %collective-permute-start.7) | collective-permute-done | bytes 475168 | tf_op jit(solution)/shard_map/ppermute | solution.py:134
  216.0 2.1 add_add_fusion
  219.3 2.9 %collective-permute-done.9 = f32[8,64,512]{2,1,0:T(8,128)} collective-permute-done((f32[8,64,512]{2,1,0:T(8,128)}, f32[8,64,512]{2,1,0:T(8,128)}, u32[]{:S(2)}, u32[]{:S(2)}) %collective-permute-start.9) | collective-permute-done | bytes 1048608 | tf_op jit(solution)/shard_map/ppermute | solution.py:134
  222.2 2.4 bitcast_add_fusion
  228.7 5.7 %collective-permute-done.10 = f32[4,64,256]{2,1,0:T(8,128)S(1)} collective-permute-done((f32[4,64,256]{2,1,0:T(8,128)S(1)}, f32[4,64,256]{2,1,0:T(8,128)S(1)}, u32[]{:S(2)}, u32[]{:S(2)}) %collective-permute-start.10) | collective-permute-done | bytes 262176 | tf_op jit(solution)/shard_map/ppermute | solution.py:195
  235.9 2.9 %collective-permute-start.12 = (f32[64,512]{1,0:T(8,128)S(1)}, f32[64,512]{1,0:T(8,128)S(1)}, u32[]{:S(2)}, u32[]{:S(2)}) collective-permute-start(f32[64,512]{1,0:T(8,128)S(1)} %get-tuple-element.53), channel_id=1, source_target_pairs={{0,16},{8,24},{16,32},{24,40},{32,48},{40,56},{48,0},{56,8},{1,17}... | collective-permute-start | bytes 393224 | tf_op jit(solution)/shard_map/ppermute | solution.py:134
  240.1 4.9 %collective-permute-start.13 = (f32[64,512]{1,0:T(8,128)S(1)}, f32[64,512]{1,0:T(8,128)S(1)}, u32[]{:S(2)}, u32[]{:S(2)}) collective-permute-start(f32[64,512]{1,0:T(8,128)S(1)} %get-tuple-element.55), channel_id=1, source_target_pairs={{0,32},{8,40},{16,48},{24,56},{32,0},{40,8},{48,16},{56,24},{1,33}... | collective-permute-start | bytes 393224 | tf_op jit(solution)/shard_map/ppermute | solution.py:134
  246.8 2.1 convolution_convert_fusion.2
  (72 shorter events, 40.9 us)
Async XLA Ops:
  5.9 67.1 %all-to-all-start = ((bf16[64,9,16,128]{3,2,1,0:T(8,128)(2,1)}), bf16[64,9,16,128]{3,2,1,0:T(8,128)(2,1)S(1)}, u32[]{:S(2)}, u32[]{:S(2)}) async-start(bf16[64,9,16,128]{3,2,1,0:T(8,128)(2,1)} %bitcast.62), calls=%async_computation | async-start | bytes 4718592 | tf_op jit(solution)/shard_map/all_to_all | solution.py:153
  21.0 48.2 %collective-permute-start.2 = (bf16[1024,512]{1,0:T(8,128)(2,1)S(1)}, bf16[1024,512]{1,0:T(8,128)(2,1)S(1)}, u32[]{:S(2)}, u32[]{:S(2)}) collective-permute-start(bf16[1024,512]{1,0:T(8,128)(2,1)S(1)} %get-tuple-element.49), channel_id=1, source_target_pairs={{0,3},{1,0},{2,1},{3,2},{4,7},{5,4},{6,5},{7,6},{8,11},{9,8},{10,9... | collective-permute-start | bytes 3145736 | tf_op jit(solution)/shard_map/ppermute | solution.py:134
  24.0 45.2 %collective-permute-start.1 = (bf16[1024,512]{1,0:T(8,128)(2,1)S(1)}, bf16[1024,512]{1,0:T(8,128)(2,1)S(1)}, u32[]{:S(2)}, u32[]{:S(2)}) collective-permute-start(bf16[1024,512]{1,0:T(8,128)(2,1)S(1)} %get-tuple-element.50), channel_id=1, source_target_pairs={{0,2},{1,3},{2,0},{3,1},{4,6},{5,7},{6,4},{7,5},{8,10},{9,11},{10,... | collective-permute-start | bytes 3145736 | tf_op jit(solution)/shard_map/ppermute | solution.py:134
  24.6 48.4 %collective-permute-start = (bf16[1024,512]{1,0:T(8,128)(2,1)S(1)}, bf16[1024,512]{1,0:T(8,128)(2,1)}, u32[]{:S(2)}, u32[]{:S(2)}) collective-permute-start(bf16[1024,512]{1,0:T(8,128)(2,1)S(1)} %get-tuple-element.51), channel_id=1, source_target_pairs={{0,1},{1,2},{2,3},{3,0},{4,5},{5,6},{6,7},{7,4},{8,9},{9,10},{10,1... | collective-permute-start | bytes 3145736 | tf_op jit(solution)/shard_map/ppermute | solution.py:134
  77.2 18.0 %copy-start.7 = (bf16[1,512,512]{2,1,0:T(8,128)(2,1)S(1)}, bf16[1,512,512]{2,1,0:T(8,128)(2,1)}, u32[]{:S(2)}) copy-start(bf16[1,512,512]{2,1,0:T(8,128)(2,1)} %param.11) | copy-start | bytes 1572868
  77.2 104.7 %all-to-all-start.1 = ((bf16[64,16,16,128]{3,2,1,0:T(8,128)(2,1)}), bf16[64,16,16,128]{3,2,1,0:T(8,128)(2,1)}, u32[]{:S(2)}, u32[]{:S(2)}) async-start(bf16[64,16,16,128]{3,2,1,0:T(8,128)(2,1)} %bitcast.60), calls=%async_computation.1 | async-start | bytes 8388608 | tf_op jit(solution)/shard_map/all_to_all | solution.py:163
  87.9 7.4 %copy-start.3 = (bf16[4096,512]{1,0:T(8,128)(2,1)S(1)}, bf16[4096,512]{1,0:T(8,128)(2,1)}, u32[]{:S(2)}) copy-start(bf16[4096,512]{1,0:T(8,128)(2,1)} %param.7) | copy-start | bytes 12582916
  88.0 7.4 %copy-start.5 = (bf16[1,512,4096]{2,1,0:T(8,128)(2,1)S(1)}, bf16[1,512,4096]{2,1,0:T(8,128)(2,1)}, u32[]{:S(2)}) copy-start(bf16[1,512,4096]{2,1,0:T(8,128)(2,1)} %param.6) | copy-start | bytes 12582916
  90.6 48.6 %collective-permute-start.5 = (bf16[464,1024]{1,0:T(8,128)(2,1)S(1)}, bf16[464,1024]{1,0:T(8,128)(2,1)S(1)}, u32[]{:S(2)}, u32[]{:S(2)}) collective-permute-start(bf16[464,1024]{1,0:T(8,128)(2,1)S(1)} %get-tuple-element.45), channel_id=1, source_target_pairs={{0,192},{64,0},{128,64},{192,128},{1,193},{65,1},{129,65},{193,129... | collective-permute-start | bytes 2850824 | tf_op jit(solution)/shard_map/ppermute | solution.py:134
  93.6 45.6 %collective-permute-start.4 = (bf16[464,1024]{1,0:T(8,128)(2,1)S(1)}, bf16[464,1024]{1,0:T(8,128)(2,1)}, u32[]{:S(2)}, u32[]{:S(2)}) collective-permute-start(bf16[464,1024]{1,0:T(8,128)(2,1)S(1)} %get-tuple-element.46), channel_id=1, source_target_pairs={{0,128},{64,192},{128,0},{192,64},{1,129},{65,193},{129,1},{193,65... | collective-permute-start | bytes 2850824 | tf_op jit(solution)/shard_map/ppermute | solution.py:134
  94.2 79.8 %collective-permute-start.3 = (bf16[464,1024]{1,0:T(8,128)(2,1)S(1)}, bf16[464,1024]{1,0:T(8,128)(2,1)}, u32[]{:S(2)}, u32[]{:S(2)}) collective-permute-start(bf16[464,1024]{1,0:T(8,128)(2,1)S(1)} %get-tuple-element.47), channel_id=1, source_target_pairs={{0,64},{64,128},{128,192},{192,0},{1,65},{65,129},{129,193},{193,1... | collective-permute-start | bytes 2850824 | tf_op jit(solution)/shard_map/ppermute | solution.py:134
  189.8 15.0 %collective-permute-start.6 = (bf16[464,512]{1,0:T(8,128)(2,1)S(1)}, bf16[464,512]{1,0:T(8,128)(2,1)}, u32[]{:S(2)}, u32[]{:S(2)}) collective-permute-start(bf16[464,512]{1,0:T(8,128)(2,1)S(1)} %concatenate.21), channel_id=1, source_target_pairs={{0,64},{64,128},{128,192},{192,0},{1,65},{65,129},{129,193},{193,1... | collective-permute-start | bytes 1425416 | tf_op jit(solution)/shard_map/ppermute | solution.py:134
  191.2 23.1 %collective-permute-start.7 = (bf16[464,512]{1,0:T(8,128)(2,1)S(1)}, bf16[464,512]{1,0:T(8,128)(2,1)}, u32[]{:S(2)}, u32[]{:S(2)}) collective-permute-start(bf16[464,512]{1,0:T(8,128)(2,1)S(1)} %concatenate.21), channel_id=1, source_target_pairs={{0,192},{64,0},{128,64},{192,128},{1,193},{65,1},{129,65},{193,129... | collective-permute-start | bytes 1425416 | tf_op jit(solution)/shard_map/ppermute | solution.py:134
  193.1 23.0 %collective-permute-start.8 = (bf16[464,512]{1,0:T(8,128)(2,1)S(1)}, bf16[464,512]{1,0:T(8,128)(2,1)}, u32[]{:S(2)}, u32[]{:S(2)}) collective-permute-start(bf16[464,512]{1,0:T(8,128)(2,1)S(1)} %concatenate.21), channel_id=1, source_target_pairs={{0,128},{64,192},{128,0},{192,64},{1,129},{65,193},{129,1},{193,65... | collective-permute-start | bytes 1425416 | tf_op jit(solution)/shard_map/ppermute | solution.py:134
  196.2 29.3 %all-to-all-start.2 = ((bf16[4,464,512]{2,1,0:T(8,128)(2,1)}), bf16[4,464,512]{2,1,0:T(8,128)(2,1)}, u32[]{:S(2)}, u32[]{:S(2)}) async-start(bf16[4,464,512]{2,1,0:T(8,128)(2,1)} %broadcast_in_dim.7), calls=%async_computation.2 | async-start | bytes 3801088 | tf_op jit(solution)/shard_map/all_to_all | solution.py:190
  219.2 3.0 %collective-permute-start.9 = (f32[8,64,512]{2,1,0:T(8,128)}, f32[8,64,512]{2,1,0:T(8,128)}, u32[]{:S(2)}, u32[]{:S(2)}) collective-permute-start(f32[8,64,512]{2,1,0:T(8,128)} %dynamic-slice_bitcast_fusion), channel_id=1, source_target_pairs={{0,4},{4,0},{1,5},{5,1},{2,6},{6,2},{3,7},{7,3},{8,12},{12,8},{9,1... | collective-permute-start | bytes 3145736 | tf_op jit(solution)/shard_map/ppermute | solution.py:134
  225.5 10.3 %copy-start.4 = (f32[8,64,512]{2,1,0:T(8,128)S(1)}, f32[8,64,512]{2,1,0:T(8,128)}, u32[]{:S(2)}) copy-start(f32[8,64,512]{2,1,0:T(8,128)} %bitcast_add_fusion) | copy-start | bytes 3145732
  226.8 7.7 %collective-permute-start.10 = (f32[4,64,256]{2,1,0:T(8,128)S(1)}, f32[4,64,256]{2,1,0:T(8,128)S(1)}, u32[]{:S(2)}, u32[]{:S(2)}) collective-permute-start(f32[4,64,256]{2,1,0:T(8,128)S(1)} %get-tuple-element.57), channel_id=1, source_target_pairs={{0,8},{8,0},{16,24},{24,16},{32,40},{40,32},{48,56},{56,48},{1,9},... | collective-permute-start | bytes 786440 | tf_op jit(solution)/shard_map/ppermute | solution.py:195
  227.8 8.0 %collective-permute-start.11 = (f32[4,64,256]{2,1,0:T(8,128)S(1)}, f32[4,64,256]{2,1,0:T(8,128)S(1)}, u32[]{:S(2)}, u32[]{:S(2)}) collective-permute-start(f32[4,64,256]{2,1,0:T(8,128)S(1)} %get-tuple-element.56), channel_id=1, source_target_pairs={{8,16},{16,8},{24,32},{32,24},{40,48},{48,40},{0,56},{56,0},{9,17}... | collective-permute-start | bytes 786440 | tf_op jit(solution)/shard_map/ppermute | solution.py:196
  227.8 17.3 %copy-start.11 = (bf16[1024,512]{1,0:T(8,128)(2,1)S(1)}, bf16[1024,512]{1,0:T(8,128)(2,1)}, u32[]{:S(2)}) copy-start(bf16[1024,512]{1,0:T(8,128)(2,1)} %copy-done.10) | copy-start | bytes 3145732
  235.9 17.6 %collective-permute-start.12 = (f32[64,512]{1,0:T(8,128)S(1)}, f32[64,512]{1,0:T(8,128)S(1)}, u32[]{:S(2)}, u32[]{:S(2)}) collective-permute-start(f32[64,512]{1,0:T(8,128)S(1)} %get-tuple-element.53), channel_id=1, source_target_pairs={{0,16},{8,24},{16,32},{24,40},{32,48},{40,56},{48,0},{56,8},{1,17}... | collective-permute-start | bytes 393224 | tf_op jit(solution)/shard_map/ppermute | solution.py:134
  238.9 14.6 %collective-permute-start.14 = (f32[64,512]{1,0:T(8,128)S(1)}, f32[64,512]{1,0:T(8,128)S(1)}, u32[]{:S(2)}, u32[]{:S(2)}) collective-permute-start(f32[64,512]{1,0:T(8,128)S(1)} %get-tuple-element.54), channel_id=1, source_target_pairs={{0,48},{8,56},{16,0},{24,8},{32,16},{40,24},{48,32},{56,40},{1,49}... | collective-permute-start | bytes 393224 | tf_op jit(solution)/shard_map/ppermute | solution.py:134
  240.1 8.8 %copy-start.6 = (bf16[1024,512]{1,0:T(8,128)(2,1)S(1)}, bf16[1024,512]{1,0:T(8,128)(2,1)}, u32[]{:S(2)}) copy-start(bf16[1024,512]{1,0:T(8,128)(2,1)} %get-tuple-element.40) | copy-start | bytes 3145732
  240.1 15.3 %collective-permute-start.13 = (f32[64,512]{1,0:T(8,128)S(1)}, f32[64,512]{1,0:T(8,128)S(1)}, u32[]{:S(2)}, u32[]{:S(2)}) collective-permute-start(f32[64,512]{1,0:T(8,128)S(1)} %get-tuple-element.55), channel_id=1, source_target_pairs={{0,32},{8,40},{16,48},{24,56},{32,0},{40,8},{48,16},{56,24},{1,33}... | collective-permute-start | bytes 393224 | tf_op jit(solution)/shard_map/ppermute | solution.py:134
  (6 other events, 10.9 us)

commit v8 on v7

--- a/solution.py
+++ b/solution.py
@@ -20,41 +20,32 @@
 BOTH_FIRST = (((0,), (0,)), ((), ()))
 
 
-def cut_kernel(owner_ref, row_ref, cache_ref, out_ref, named_ref):
+def cut_kernel(named_ref, cache_ref, out_ref):
     rows = cache_ref.shape[0]
-    _, stretches, neigh = owner_ref.shape
-    named_ref[...] = jnp.zeros_like(named_ref)
-    named_ref[:stretches, :neigh] = owner_ref[0].astype(F32)
-    named_ref[stretches : 2 * stretches, :neigh] = row_ref[0].astype(F32)
     _, heads, tiles, _, _, _ = out_ref.shape
     for head in range(heads):
         cols = slice(head * HEAD_DIM, (head + 1) * HEAD_DIM)
         for tile in range(tiles):
             out_ref[0, head, tile, :rows] = cache_ref[:, 0, tile * TILE : (tile + 1) * TILE, cols]
-            out_ref[0, head, tile, rows] = named_ref[...].astype(BF16)
-
-
-def cut(nb_owner, nb_row, cache):
+            out_ref[0, head, tile, rows] = named_ref[...]
+
+
+def cut(named, cache):
     rows, _, nb_len, width = cache.shape
-    tiles, heads, parts = nb_len // TILE, width // HEAD_DIM, 2
-    named = pl.BlockSpec(nb_owner.shape, lambda a, t: (0, 0, 0))
+    tiles, heads = nb_len // TILE, width // HEAD_DIM
     return pl.pallas_call(
         cut_kernel,
-        grid=(2, parts),
+        grid=(2,),
         in_specs=[
-            named,
-            named,
-            pl.BlockSpec((rows, 1, nb_len // parts, width), lambda a, t: (0, a, t, 0)),
+            pl.BlockSpec(named.shape, lambda a: (0, 0)),
+            pl.BlockSpec((rows, 1, nb_len, width), lambda a: (0, a, 0, 0)),
         ],
-        out_specs=pl.BlockSpec(
-            (1, heads, tiles // parts, rows + 1, TILE, HEAD_DIM), lambda a, t: (a, 0, t, 0, 0, 0)
-        ),
+        out_specs=pl.BlockSpec((1, heads, tiles, rows + 1, TILE, HEAD_DIM), lambda a: (a, 0, 0, 0, 0, 0)),
         out_shape=jax.ShapeDtypeStruct((2, heads, tiles, rows + 1, TILE, HEAD_DIM), BF16),
-        scratch_shapes=[pltpu.VMEM((TILE, HEAD_DIM), F32)],
-        compiler_params=pltpu.CompilerParams(vmem_limit_bytes=VMEM),
+        compiler_params=pltpu.CompilerParams(vmem_limit_bytes=60 << 20),
         cost_estimate=pl.CostEstimate(flops=0, bytes_accessed=4 << 20, transcendentals=0),
         name="cut",
-    )(nb_owner, nb_row, cache).reshape(-1, rows + 1, TILE, HEAD_DIM)
+    )(named, cache).reshape(-1, rows + 1, TILE, HEAD_DIM)
 
 
 def pick_kernel(ids_ref, tiles_ref, out_ref, *, slots):
@@ -81,6 +72,13 @@
 
 
 def attend_kernel(q_ref, g_ref, kv_ref, out_ref, dq_ref, *, heads):
+    for i in range(q_ref.shape[0] // STRETCH):
+        rows = pl.ds(i * STRETCH, STRETCH)
+        kv = kv_ref.at[:, :, :, :, i]
+        attend_stretch(q_ref.at[rows], g_ref.at[rows], kv, out_ref.at[rows], dq_ref.at[rows], heads)
+
+
+def attend_stretch(q_ref, g_ref, kv_ref, out_ref, dq_ref, heads):
     scale = HEAD_DIM ** (-0.5)
     cols = [slice(h * HEAD_DIM, (h + 1) * HEAD_DIM) for h in range(heads)]
     keys = [kv_ref[0, h].reshape(-1, HEAD_DIM) for h in range(heads)]
@@ -106,18 +104,20 @@
         dq_ref[:, c] = jnp.dot(dscore, k, preferred_element_type=F32).astype(BF16)
 
 
-def attend(q, g, kv, neigh):
+def attend(q, g, kv):
     rows, width = q.shape
-    count = rows // STRETCH
-    _, heads, tiles, slots, _, _ = kv.shape
-    block = pl.BlockSpec((STRETCH, width), lambda c: (c, 0))
+    count, together = rows // STRETCH, 2
+    _, heads, tiles, neigh, _, _, _ = kv.shape
+    block = pl.BlockSpec((together * STRETCH, width), lambda c: (c, 0))
     return pl.pallas_call(
         functools.partial(attend_kernel, heads=heads),
-        grid=(count,),
+        grid=(count // together,),
         in_specs=[
             block,
             block,
-            pl.BlockSpec((2, heads, tiles, neigh, TILE, HEAD_DIM), lambda c: (0, 0, 0, c, 0, 0)),
+            pl.BlockSpec(
+                (2, heads, tiles, neigh, together, TILE, HEAD_DIM), lambda c: (0, 0, 0, 0, c, 0, 0)
+            ),
         ],
         out_specs=[block, block],
         out_shape=[jax.ShapeDtypeStruct(q.shape, BF16)] * 2,
@@ -149,7 +149,9 @@
     tiles = nb_len // TILE
     real = length - LEAD
 
-    message = cut(nb_owner, nb_row, cache_kv)
+    lanes = (0, HEAD_DIM - stretches)
+    named = jnp.pad(nb_owner[0].T, ((0, TILE - neigh), lanes)) + jnp.pad(nb_row[0].T, ((neigh, TILE - 2 * neigh), lanes))
+    message = cut(named.astype(BF16), cache_kv)
     held = lax.all_to_all(message, DP, split_axis=0, concat_axis=0, tiled=True)
 
     block = d // nmp
@@ -157,8 +159,8 @@
     fans = [step(a, "mp", by) if by else a for by, a in enumerate(fans)]
     held, fans = lax.optimization_barrier((held, fans))
 
-    named = held[:, db_rows, : 2 * stretches, :neigh].astype(jnp.int32)
-    ids = named[:, :stretches] * (db_rows + 1) + named[:, stretches:]
+    named = held[:, db_rows, : 2 * neigh, :stretches].astype(jnp.int32)
+    ids = named[:, :neigh] * (db_rows + 1) + named[:, neigh:]
     send = pick(ids.reshape(-1), held.reshape(-1, TILE, HEAD_DIM))
     got = lax.all_to_all(
         send.reshape(ndp, requests, TILE, HEAD_DIM), DP, split_axis=0, concat_axis=0, tiled=True
@@ -176,12 +178,15 @@
     g = shifted(grad_rows)
     got, share, q, g = lax.optimization_barrier((got, share, q, g))
 
-    out, dq = attend(q, g, got.reshape(2, heads, tiles, requests, TILE, HEAD_DIM), neigh)
+    out, dq = attend(q, g, got.reshape(2, heads, tiles, neigh, stretches, TILE, HEAD_DIM))
     dq = jnp.concatenate([jnp.zeros((LEAD - SKIP, width), BF16), dq[:real]], 0)
 
     total = 0.0
     for by in sorted(range(nx), key=lambda by: min(by, nx - by)):
         near = step(dq, "x", by) if by else dq
+        if 2 * by == nx:
+            own = lax.dot_general(dq, fans[0], BOTH_LAST, preferred_element_type=F32).astype(BF16)
+            near, own = lax.optimization_barrier((near, own))
         total += lax.dot_general(share[by], near, BOTH_FIRST, preferred_element_type=F32)
     total = total.reshape(nz, nc, -1, width)
     mine = lax.dynamic_index_in_dim(total, mc, 1, keepdims=False)
@@ -194,15 +199,16 @@
     mine = lax.dynamic_index_in_dim(pairs, mz % 2, 1, keepdims=False)
     up = lax.ppermute(away[..., : width // 2], "z", [(i, i ^ 1) for i in range(nz)])
     down = lax.ppermute(away[..., width // 2 :], "z", [(i, ((i + 1) ^ 1) - 1) for i in range(1, nz - 1)] + [(0, nz - 1), (nz - 1, 0)])
-    groups, up = lax.optimization_barrier((groups, up))
+    parts = [own]
+    for by in range(1, nmp):
+        if by == nmp - 1:
+            up, parts, groups = lax.optimization_barrier((up, parts, groups))
+        near = lax.dynamic_index_in_dim(groups, (my - by) % nmp, 0, keepdims=False)
+        parts.append(lax.dot_general(near, fans[by], BOTH_LAST, preferred_element_type=F32).astype(BF16))
     mine += jnp.concatenate([up, down], -1)
     terms = [lax.dynamic_index_in_dim(mine, (mz // 2 + by) % (nz // 2), 0, keepdims=False) for by in range(nz // 2)]
     query_grad = sum(step(a, "z", 2 * by) if by else a for by, a in enumerate(terms))
-    part = 0.0
-    for by in range(nmp):
-        near = lax.dynamic_index_in_dim(groups, (my - by) % nmp, 0, keepdims=False)
-        part += lax.dot_general(near, fans[by], BOTH_LAST, preferred_element_type=F32).astype(BF16).astype(F32)
-    part = part.astype(BF16)
+    part = sum(a.astype(F32) for a in parts).astype(BF16)
     attended = jnp.concatenate([jnp.zeros((LEAD, width), BF16), out[:real]], 0)
     input_grad = jnp.concatenate([jnp.zeros((SKIP, d // nmp), BF16), part], 0)
     return attended[None], input_grad[None], query_grad

time: 257 us -> 255 us (level)
  matrix products: 16.3 us -> 20.1 us
  starting transfers between devices: 51.1 us -> 47.7 us
  local copies, waits for them, and re-layouts: 20.9 us -> 17.8 us
    unnamed x26 -> x16, local copies, waits for them, and re-layouts: 8.51 us -> 4.48 us
    ppermute x13, waiting for transfers between devices: 137 us -> 141 us  [step(): lax.ppermute(array, axis, [(i, (i + by) % size) for i in range(size)])]
    dot_general x1, matrix products: 2.32 us -> 5.79 us  [local(): q = shifted(jnp.dot(late, weights, preferred_element_type=F32).astype(BF16))]
    ppermute x13, starting transfers between devices: 23.5 us -> 20.6 us  [step(): lax.ppermute(array, axis, [(i, (i + by) % size) for i in range(size)])]
    dot_general x4 -> x3, matrix products: 7.35 us -> 6.01 us  [local(): lax.dot_general(near, fans[by], BOTH_LAST, preferred_element_type=F32)]
  transfers between devices with their start and end apart: 18 -> 18, of which waited for: 12 -> 11; matrix products, arithmetic and copies ran while one was open for 12% -> 14% of each run, Pallas kernels for 0% -> 0%
where the time goes in v8:
time: 255 us
  waiting for transfers between devices  153 us (60%)
  starting transfers between devices  47.7 us (19%)
  matrix products  20.1 us (8%)
  local copies, waits for them, and re-layouts  17.8 us (7%)
  Pallas kernels  10.6 us (4%)
  other arithmetic  4.53 us (2%)
    ppermute x13, waiting for transfers between devices, step(): lax.ppermute(array, axis, [(i, (i + by) % size) for i in range(size)])  141 us
    ppermute x13, starting transfers between devices, step(): lax.ppermute(array, axis, [(i, (i + by) % size) for i in range(size)])  20.6 us
    all_to_all x1, starting transfers between devices, local(): held = lax.all_to_all(message, DP, split_axis=0, concat_axis=0, tiled=True)  11.6 us
    all_to_all x1, starting transfers between devices, local(): lax.all_to_all(send.reshape(ndp, requests, TILE, HEAD_DIM), DP, split_axi...  10.5 us
    all_to_all x1, waiting for transfers between devices, local(): lax.all_to_all(send.reshape(ndp, requests, TILE, HEAD_DIM), DP, split_axi...  7.98 us
    dot_general x4, matrix products, local(): lax.dot_general(share[by], near, BOTH_FIRST, preferred_element_type=F32)  6.63 us
    dot_general x3, matrix products, local(): lax.dot_general(near, fans[by], BOTH_LAST, preferred_element_type=F32)  6.01 us
    pallas_call x1, Pallas kernels, attend(): pl.pallas_call(functools.partial(attend_kernel, heads=heads), grid=(count...  5.88 us
  transfers between devices with their start and end apart: 18, of which 11 were waited for; matrix products, arithmetic and copies ran while one was open for 14% of the time, Pallas kernels for 0%

profile of v8, /device:TPU:32, one launch (start us, length us, event | category | flops | bytes accessed | tf_op | source)
XLA Modules:
  0.0 254.6 jit_solution(12030446858745027379)
XLA Ops:
  1.9 2.8 %cut.1 = bf16[2,4,8,9,16,128]{5,4,3,2,1,0:T(8,128)(2,1)} custom-call(bf16[16,128]{1,0:T(8,128)(2,1)} %add_convert_fusion.1.named_ref, bf16[8,2,128,512]{3,2,1,0:T(8,128)(2,1)} %cache_ref.1), custom_call_target="tpu_custom_call" | custom-call | bytes 4194304 | tf_op jit(solution)/shard_map/cut/pallas_call | solution.py:36
  4.8 11.6 %all-to-all-start = ((bf16[64,9,16,128]{3,2,1,0:T(8,128)(2,1)}), bf16[64,9,16,128]{3,2,1,0:T(8,128)(2,1)S(1)}, u32[]{:S(2)}, u32[]{:S(2)}) async-start(bf16[64,9,16,128]{3,2,1,0:T(8,128)(2,1)} %bitcast.65), calls=%async_computation | async-start | bytes 4718592 | tf_op jit(solution)/shard_map/all_to_all | solution.py:155
  16.4 3.4 %constant_dynamic-slice_fusion = (bf16[1024,512]{1,0:T(8,128)(2,1)S(1)}, bf16[1024,512]{1,0:T(8,128)(2,1)S(1)}, bf16[1024,512]{1,0:T(8,128)(2,1)S(1)}, bf16[1024,512]{1,0:T(8,128)(2,1)}) fusion(bf16[4096,512]{1,0:T(8,128)(2,1)} %param.7, s32[]{:T(128)S(6)} %select_n.144, s32[]{:T(128)S(6)} %select_n.142, s32[]{:T(128)S(6)} %select_n.140, s32[]{:T(128)S(6)} %select_n.138), kind=kLoop, calls=%fused_computation.32 | loop fusion | bytes 8388624 | tf_op jit(solution)/shard_map/dynamic_slice | solution.py:158
  19.8 3.0 %collective-permute-start.2 = (bf16[1024,512]{1,0:T(8,128)(2,1)S(1)}, bf16[1024,512]{1,0:T(8,128)(2,1)S(1)}, u32[]{:S(2)}, u32[]{:S(2)}) collective-permute-start(bf16[1024,512]{1,0:T(8,128)(2,1)S(1)} %get-tuple-element.59), channel_id=1, source_target_pairs={{0,3},{1,0},{2,1},{3,2},{4,7},{5,4},{6,5},{7,6},{8,11},{9,8},{10,9... | collective-permute-start | bytes 3145736 | tf_op jit(solution)/shard_map/ppermute | solution.py:134
  24.5 43.6 %collective-permute-done.2 = bf16[1024,512]{1,0:T(8,128)(2,1)S(1)} collective-permute-done((bf16[1024,512]{1,0:T(8,128)(2,1)S(1)}, bf16[1024,512]{1,0:T(8,128)(2,1)S(1)}, u32[]{:S(2)}, u32[]{:S(2)}) %collective-permute-start.2) | collective-permute-done | bytes 1048608 | tf_op jit(solution)/shard_map/ppermute | solution.py:134
  76.0 10.5 %all-to-all-start.1 = ((bf16[64,16,16,128]{3,2,1,0:T(8,128)(2,1)}), bf16[64,16,16,128]{3,2,1,0:T(8,128)(2,1)}, u32[]{:S(2)}, u32[]{:S(2)}) async-start(bf16[64,16,16,128]{3,2,1,0:T(8,128)(2,1)} %bitcast.63), calls=%async_computation.1 | async-start | bytes 8388608 | tf_op jit(solution)/shard_map/all_to_all | solution.py:165
  86.6 3.7 %constant_dynamic-slice_fusion.4 = (bf16[464,1024]{1,0:T(8,128)(2,1)}, bf16[464,1024]{1,0:T(8,128)(2,1)}, bf16[464,1024]{1,0:T(8,128)(2,1)}, bf16[464,1024]{1,0:T(8,128)(2,1)S(1)}) fusion(bf16[512,4096]{1,0:T(8,128)(2,1)} %bitcast.70, s32[]{:T(128)S(6)} %select_n.152, s32[]{:T(128)S(6)} %select_n.150, s32[]{:T(128)S(6)} %select_n.148, s32[]{:T(128)S(6)} %select_n.146), kind=kLoop, calls=%fused_computation.36 | loop fusion | bytes 7602192 | tf_op jit(solution)/shard_map/dynamic_slice | solution.py:171
  90.3 2.9 %collective-permute-start.5 = (bf16[464,1024]{1,0:T(8,128)(2,1)}, bf16[464,1024]{1,0:T(8,128)(2,1)S(1)}, u32[]{:S(2)}, u32[]{:S(2)}) collective-permute-start(bf16[464,1024]{1,0:T(8,128)(2,1)} %get-tuple-element.55), channel_id=1, source_target_pairs={{0,192},{64,0},{128,64},{192,128},{1,193},{65,1},{129,65},{193,129... | collective-permute-start | bytes 2850824 | tf_op jit(solution)/shard_map/ppermute | solution.py:134
  95.0 5.8 %fusion.17 = bf16[512,512]{1,0:T(8,128)(2,1)S(1)} fusion(bf16[512,4096]{1,0:T(8,128)(2,1)} %bitcast.71, bf16[4096,512]{1,0:T(8,128)(2,1)} %param.7), kind=kOutput, calls=%fused_computation.46 | convolution fusion | flops 2147483648 | bytes 8912896 | tf_op jit(solution)/shard_map/dot_general | solution.py:177
  101.0 36.9 %collective-permute-done.5 = bf16[464,1024]{1,0:T(8,128)(2,1)S(1)} collective-permute-done((bf16[464,1024]{1,0:T(8,128)(2,1)}, bf16[464,1024]{1,0:T(8,128)(2,1)S(1)}, u32[]{:S(2)}, u32[]{:S(2)}) %collective-permute-start.5) | collective-permute-done | bytes 950304 | tf_op jit(solution)/shard_map/ppermute | solution.py:134
  137.8 34.8 %collective-permute-done.3 = bf16[464,1024]{1,0:T(8,128)(2,1)} collective-permute-done((bf16[464,1024]{1,0:T(8,128)(2,1)}, bf16[464,1024]{1,0:T(8,128)(2,1)}, u32[]{:S(2)}, u32[]{:S(2)}) %collective-permute-start.3) | collective-permute-done | bytes 950304 | tf_op jit(solution)/shard_map/ppermute | solution.py:134
  172.6 8.0 %all-to-all-done.1 = bf16[64,16,16,128]{3,2,1,0:T(8,128)(2,1)} async-done(((bf16[64,16,16,128]{3,2,1,0:T(8,128)(2,1)}), bf16[64,16,16,128]{3,2,1,0:T(8,128)(2,1)}, u32[]{:S(2)}, u32[]{:S(2)}) %all-to-all-start.1) | async-done | bytes 4194336 | tf_op jit(solution)/shard_map/all_to_all | solution.py:165
  180.6 5.9 %attend.1 = (bf16[512,512]{1,0:T(8,128)(2,1)S(1)}, bf16[512,512]{1,0:T(8,128)(2,1)S(1)}) custom-call(bf16[512,512]{1,0:T(8,128)(2,1)S(1)} %concatenate.18.q_ref, bf16[512,512]{1,0:T(8,128)(2,1)S(1)} %concatenate.19.g_ref, bf16[2,4,8,2,8,16,128]{6,5,4,3,2,1,0:T(8,128)(2,1)} %bitcast.11.kv_ref), custom_call_target="tpu_custom_call" | custom-call | flops 671088640 | bytes 4194304 | tf_op jit(solution)/shard_map/attend/pallas_call | solution.py:112
  186.7 2.9 %collective-permute-start.7 = (bf16[464,512]{1,0:T(8,128)(2,1)S(1)}, bf16[464,512]{1,0:T(8,128)(2,1)}, u32[]{:S(2)}, u32[]{:S(2)}) collective-permute-start(bf16[464,512]{1,0:T(8,128)(2,1)S(1)} %concatenate.21), channel_id=1, source_target_pairs={{0,192},{64,0},{128,64},{192,128},{1,193},{65,1},{129,65},{193,129... | collective-permute-start | bytes 1425416 | tf_op jit(solution)/shard_map/ppermute | solution.py:134
  189.5 2.2 collective-permute-start.8
  193.1 4.4 %all-to-all-start.2 = ((bf16[4,464,512]{2,1,0:T(8,128)(2,1)}), bf16[4,464,512]{2,1,0:T(8,128)(2,1)}, u32[]{:S(2)}, u32[]{:S(2)}) async-start(bf16[4,464,512]{2,1,0:T(8,128)(2,1)} %broadcast_in_dim.7), calls=%async_computation.2 | async-start | bytes 3801088 | tf_op jit(solution)/shard_map/all_to_all | solution.py:195
  200.5 13.2 %collective-permute-done.8 = bf16[464,512]{1,0:T(8,128)(2,1)} collective-permute-done((bf16[464,512]{1,0:T(8,128)(2,1)S(1)}, bf16[464,512]{1,0:T(8,128)(2,1)}, u32[]{:S(2)}, u32[]{:S(2)}) %collective-permute-start.8) | collective-permute-done | bytes 475168 | tf_op jit(solution)/shard_map/ppermute | solution.py:134
  224.5 2.4 bitcast_add_fusion
  230.8 2.2 convolution_convert_fusion.2
  233.0 3.6 %collective-permute-done.10 = f32[4,64,256]{2,1,0:T(8,128)S(1)} collective-permute-done((f32[4,64,256]{2,1,0:T(8,128)S(1)}, f32[4,64,256]{2,1,0:T(8,128)S(1)}, u32[]{:S(2)}, u32[]{:S(2)}) %collective-permute-start.10) | collective-permute-done | bytes 262176 | tf_op jit(solution)/shard_map/ppermute | solution.py:200
  238.2 2.8 %collective-permute-start.14 = (f32[64,512]{1,0:T(8,128)S(1)}, f32[64,512]{1,0:T(8,128)S(1)}, u32[]{:S(2)}, u32[]{:S(2)}) collective-permute-start(f32[64,512]{1,0:T(8,128)S(1)} %get-tuple-element.64), channel_id=1, source_target_pairs={{0,48},{8,56},{16,0},{24,8},{32,16},{40,24},{48,32},{56,40},{1,49}... | collective-permute-start | bytes 393224 | tf_op jit(solution)/shard_map/ppermute | solution.py:134
  241.0 2.2 collective-permute-start.13
  246.0 3.8 %collective-permute-done.14 = f32[64,512]{1,0:T(8,128)S(1)} collective-permute-done((f32[64,512]{1,0:T(8,128)S(1)}, f32[64,512]{1,0:T(8,128)S(1)}, u32[]{:S(2)}, u32[]{:S(2)}) %collective-permute-start.14) | collective-permute-done | bytes 131104 | tf_op jit(solution)/shard_map/ppermute | solution.py:134
  249.8 4.1 %collective-permute-done.13 = f32[64,512]{1,0:T(8,128)S(1)} collective-permute-done((f32[64,512]{1,0:T(8,128)S(1)}, f32[64,512]{1,0:T(8,128)S(1)}, u32[]{:S(2)}, u32[]{:S(2)}) %collective-permute-start.13) | collective-permute-done | bytes 131104 | tf_op jit(solution)/shard_map/ppermute | solution.py:134
  (63 shorter events, 36.9 us)
Async XLA Ops:
  4.8 67.1 %all-to-all-start = ((bf16[64,9,16,128]{3,2,1,0:T(8,128)(2,1)}), bf16[64,9,16,128]{3,2,1,0:T(8,128)(2,1)S(1)}, u32[]{:S(2)}, u32[]{:S(2)}) async-start(bf16[64,9,16,128]{3,2,1,0:T(8,128)(2,1)} %bitcast.65), calls=%async_computation | async-start | bytes 4718592 | tf_op jit(solution)/shard_map/all_to_all | solution.py:155
  19.8 48.2 %collective-permute-start.2 = (bf16[1024,512]{1,0:T(8,128)(2,1)S(1)}, bf16[1024,512]{1,0:T(8,128)(2,1)S(1)}, u32[]{:S(2)}, u32[]{:S(2)}) collective-permute-start(bf16[1024,512]{1,0:T(8,128)(2,1)S(1)} %get-tuple-element.59), channel_id=1, source_target_pairs={{0,3},{1,0},{2,1},{3,2},{4,7},{5,4},{6,5},{7,6},{8,11},{9,8},{10,9... | collective-permute-start | bytes 3145736 | tf_op jit(solution)/shard_map/ppermute | solution.py:134
  22.9 45.2 %collective-permute-start.1 = (bf16[1024,512]{1,0:T(8,128)(2,1)S(1)}, bf16[1024,512]{1,0:T(8,128)(2,1)S(1)}, u32[]{:S(2)}, u32[]{:S(2)}) collective-permute-start(bf16[1024,512]{1,0:T(8,128)(2,1)S(1)} %get-tuple-element.60), channel_id=1, source_target_pairs={{0,2},{1,3},{2,0},{3,1},{4,6},{5,7},{6,4},{7,5},{8,10},{9,11},{10,... | collective-permute-start | bytes 3145736 | tf_op jit(solution)/shard_map/ppermute | solution.py:134
  23.5 48.4 %collective-permute-start = (bf16[1024,512]{1,0:T(8,128)(2,1)S(1)}, bf16[1024,512]{1,0:T(8,128)(2,1)}, u32[]{:S(2)}, u32[]{:S(2)}) collective-permute-start(bf16[1024,512]{1,0:T(8,128)(2,1)S(1)} %get-tuple-element.61), channel_id=1, source_target_pairs={{0,1},{1,2},{2,3},{3,0},{4,5},{5,6},{6,7},{7,4},{8,9},{9,10},{10,1... | collective-permute-start | bytes 3145736 | tf_op jit(solution)/shard_map/ppermute | solution.py:134
  74.0 2.0 copy-start
  76.0 104.6 %all-to-all-start.1 = ((bf16[64,16,16,128]{3,2,1,0:T(8,128)(2,1)}), bf16[64,16,16,128]{3,2,1,0:T(8,128)(2,1)}, u32[]{:S(2)}, u32[]{:S(2)}) async-start(bf16[64,16,16,128]{3,2,1,0:T(8,128)(2,1)} %bitcast.63), calls=%async_computation.1 | async-start | bytes 8388608 | tf_op jit(solution)/shard_map/all_to_all | solution.py:165
  86.6 8.2 %copy-start.3 = (bf16[1,512,512]{2,1,0:T(8,128)(2,1)S(1)}, bf16[1,512,512]{2,1,0:T(8,128)(2,1)}, u32[]{:S(2)}) copy-start(bf16[1,512,512]{2,1,0:T(8,128)(2,1)} %param.11) | copy-start | bytes 1572868
  90.3 47.5 %collective-permute-start.5 = (bf16[464,1024]{1,0:T(8,128)(2,1)}, bf16[464,1024]{1,0:T(8,128)(2,1)S(1)}, u32[]{:S(2)}, u32[]{:S(2)}) collective-permute-start(bf16[464,1024]{1,0:T(8,128)(2,1)} %get-tuple-element.55), channel_id=1, source_target_pairs={{0,192},{64,0},{128,64},{192,128},{1,193},{65,1},{129,65},{193,129... | collective-permute-start | bytes 2850824 | tf_op jit(solution)/shard_map/ppermute | solution.py:134
  93.2 44.6 %collective-permute-start.4 = (bf16[464,1024]{1,0:T(8,128)(2,1)}, bf16[464,1024]{1,0:T(8,128)(2,1)}, u32[]{:S(2)}, u32[]{:S(2)}) collective-permute-start(bf16[464,1024]{1,0:T(8,128)(2,1)} %get-tuple-element.56), channel_id=1, source_target_pairs={{0,128},{64,192},{128,0},{192,64},{1,129},{65,193},{129,1},{193,65... | collective-permute-start | bytes 2850824 | tf_op jit(solution)/shard_map/ppermute | solution.py:134
  93.9 78.8 %collective-permute-start.3 = (bf16[464,1024]{1,0:T(8,128)(2,1)}, bf16[464,1024]{1,0:T(8,128)(2,1)}, u32[]{:S(2)}, u32[]{:S(2)}) collective-permute-start(bf16[464,1024]{1,0:T(8,128)(2,1)} %get-tuple-element.57), channel_id=1, source_target_pairs={{0,64},{64,128},{128,192},{192,0},{1,65},{65,129},{129,193},{193,1... | collective-permute-start | bytes 2850824 | tf_op jit(solution)/shard_map/ppermute | solution.py:134
  186.7 29.9 %collective-permute-start.7 = (bf16[464,512]{1,0:T(8,128)(2,1)S(1)}, bf16[464,512]{1,0:T(8,128)(2,1)}, u32[]{:S(2)}, u32[]{:S(2)}) collective-permute-start(bf16[464,512]{1,0:T(8,128)(2,1)S(1)} %concatenate.21), channel_id=1, source_target_pairs={{0,192},{64,0},{128,64},{192,128},{1,193},{65,1},{129,65},{193,129... | collective-permute-start | bytes 1425416 | tf_op jit(solution)/shard_map/ppermute | solution.py:134
  189.5 25.0 %collective-permute-start.6 = (bf16[464,512]{1,0:T(8,128)(2,1)S(1)}, bf16[464,512]{1,0:T(8,128)(2,1)}, u32[]{:S(2)}, u32[]{:S(2)}) collective-permute-start(bf16[464,512]{1,0:T(8,128)(2,1)S(1)} %concatenate.21), channel_id=1, source_target_pairs={{0,64},{64,128},{128,192},{192,0},{1,65},{65,129},{129,193},{193,1... | collective-permute-start | bytes 1425416 | tf_op jit(solution)/shard_map/ppermute | solution.py:134
  189.5 24.1 %collective-permute-start.8 = (bf16[464,512]{1,0:T(8,128)(2,1)S(1)}, bf16[464,512]{1,0:T(8,128)(2,1)}, u32[]{:S(2)}, u32[]{:S(2)}) collective-permute-start(bf16[464,512]{1,0:T(8,128)(2,1)S(1)} %concatenate.21), channel_id=1, source_target_pairs={{0,128},{64,192},{128,0},{192,64},{1,129},{65,193},{129,1},{193,65... | collective-permute-start | bytes 1425416 | tf_op jit(solution)/shard_map/ppermute | solution.py:134
  193.1 33.8 %all-to-all-start.2 = ((bf16[4,464,512]{2,1,0:T(8,128)(2,1)}), bf16[4,464,512]{2,1,0:T(8,128)(2,1)}, u32[]{:S(2)}, u32[]{:S(2)}) async-start(bf16[4,464,512]{2,1,0:T(8,128)(2,1)} %broadcast_in_dim.7), calls=%async_computation.2 | async-start | bytes 3801088 | tf_op jit(solution)/shard_map/all_to_all | solution.py:195
  197.6 1.2 copy-start.2
  221.5 3.0 %collective-permute-start.9 = (f32[8,64,512]{2,1,0:T(8,128)}, f32[8,64,512]{2,1,0:T(8,128)}, u32[]{:S(2)}, u32[]{:S(2)}) collective-permute-start(f32[8,64,512]{2,1,0:T(8,128)} %dynamic-slice_bitcast_fusion), channel_id=1, source_target_pairs={{0,4},{4,0},{1,5},{5,1},{2,6},{6,2},{3,7},{7,3},{8,12},{12,8},{9,1... | collective-permute-start | bytes 3145736 | tf_op jit(solution)/shard_map/ppermute | solution.py:134
  228.1 8.6 %collective-permute-start.11 = (f32[4,64,256]{2,1,0:T(8,128)S(1)}, f32[4,64,256]{2,1,0:T(8,128)S(1)}, u32[]{:S(2)}, u32[]{:S(2)}) collective-permute-start(f32[4,64,256]{2,1,0:T(8,128)S(1)} %get-tuple-element.66), channel_id=1, source_target_pairs={{8,16},{16,8},{24,32},{32,24},{40,48},{48,40},{0,56},{56,0},{9,17}... | collective-permute-start | bytes 786440 | tf_op jit(solution)/shard_map/ppermute | solution.py:201
  228.2 8.5 %copy-start.1 = (f32[8,64,512]{2,1,0:T(8,128)S(1)}, f32[8,64,512]{2,1,0:T(8,128)}, u32[]{:S(2)}) copy-start(f32[8,64,512]{2,1,0:T(8,128)} %bitcast_add_fusion) | copy-start | bytes 3145732
  228.2 8.4 %collective-permute-start.10 = (f32[4,64,256]{2,1,0:T(8,128)S(1)}, f32[4,64,256]{2,1,0:T(8,128)S(1)}, u32[]{:S(2)}, u32[]{:S(2)}) collective-permute-start(f32[4,64,256]{2,1,0:T(8,128)S(1)} %get-tuple-element.67), channel_id=1, source_target_pairs={{0,8},{8,0},{16,24},{24,16},{32,40},{40,32},{48,56},{56,48},{1,9},... | collective-permute-start | bytes 786440 | tf_op jit(solution)/shard_map/ppermute | solution.py:200
  230.8 12.4 %copy-start.5 = (bf16[1024,512]{1,0:T(8,128)(2,1)S(1)}, bf16[1024,512]{1,0:T(8,128)(2,1)}, u32[]{:S(2)}) copy-start(bf16[1024,512]{1,0:T(8,128)(2,1)} %copy-done.4) | copy-start | bytes 3145732
  230.8 12.4 %copy-start.7 = (bf16[464,1024]{1,0:T(8,128)(2,1)S(1)}, bf16[464,1024]{1,0:T(8,128)(2,1)}, u32[]{:S(2)}) copy-start(bf16[464,1024]{1,0:T(8,128)(2,1)} %convolution_convert_fusion.3) | copy-start | bytes 2850820
  236.7 9.2 %collective-permute-start.12 = (f32[64,512]{1,0:T(8,128)S(1)}, f32[64,512]{1,0:T(8,128)S(1)}, u32[]{:S(2)}, u32[]{:S(2)}) collective-permute-start(f32[64,512]{1,0:T(8,128)S(1)} %get-tuple-element.63), channel_id=1, source_target_pairs={{0,16},{8,24},{16,32},{24,40},{32,48},{40,56},{48,0},{56,8},{1,17}... | collective-permute-start | bytes 393224 | tf_op jit(solution)/shard_map/ppermute | solution.py:134
  238.2 11.6 %collective-permute-start.14 = (f32[64,512]{1,0:T(8,128)S(1)}, f32[64,512]{1,0:T(8,128)S(1)}, u32[]{:S(2)}, u32[]{:S(2)}) collective-permute-start(f32[64,512]{1,0:T(8,128)S(1)} %get-tuple-element.64), channel_id=1, source_target_pairs={{0,48},{8,56},{16,0},{24,8},{32,16},{40,24},{48,32},{56,40},{1,49}... | collective-permute-start | bytes 393224 | tf_op jit(solution)/shard_map/ppermute | solution.py:134
  241.0 12.9 %collective-permute-start.13 = (f32[64,512]{1,0:T(8,128)S(1)}, f32[64,512]{1,0:T(8,128)S(1)}, u32[]{:S(2)}, u32[]{:S(2)}) collective-permute-start(f32[64,512]{1,0:T(8,128)S(1)} %get-tuple-element.65), channel_id=1, source_target_pairs={{0,32},{8,40},{16,48},{24,56},{32,0},{40,8},{48,16},{56,24},{1,33}... | collective-permute-start | bytes 393224 | tf_op jit(solution)/shard_map/ppermute | solution.py:134
  (2 other events, 2.0 us)

commit v9 on v8

--- a/solution.py
+++ b/solution.py
@@ -129,6 +129,32 @@
     )(q, g, kv)
 
 
+def split_kernel(core_ref, share_ref, own_ref, other_ref, *, rows):
+    lane = lax.broadcasted_iota(jnp.int32, (share_ref.shape[0], 2 * rows), 1)
+    first = core_ref[0] == 0
+    for i in range(own_ref.shape[1] // (2 * rows)):
+        even = share_ref[:, 4 * i * rows : (4 * i + 2) * rows].astype(F32)
+        odd = share_ref[:, (4 * i + 2) * rows : (4 * i + 4) * rows].astype(F32)
+        low = jnp.where(lane < rows, even, pltpu.roll(odd, rows, 1)).astype(BF16)
+        high = jnp.where(lane < rows, pltpu.roll(even, rows, 1), odd).astype(BF16)
+        own_ref[:, 2 * i * rows : 2 * (i + 1) * rows] = jnp.where(first, low, high)
+        other_ref[:, 2 * i * rows : 2 * (i + 1) * rows] = jnp.where(first, high, low)
+
+
+def split(core, share, rows):
+    tokens, columns = share.shape
+    whole = pl.BlockSpec((tokens, columns // 2), lambda: (0, 0))
+    return pl.pallas_call(
+        functools.partial(split_kernel, rows=rows),
+        in_specs=[pl.BlockSpec(memory_space=pltpu.SMEM), pl.BlockSpec((tokens, columns), lambda: (0, 0))],
+        out_specs=[whole] * 2,
+        out_shape=[jax.ShapeDtypeStruct((tokens, columns // 2), BF16)] * 2,
+        compiler_params=pltpu.CompilerParams(vmem_limit_bytes=16 << 20),
+        cost_estimate=pl.CostEstimate(flops=0, bytes_accessed=4 << 20, transcendentals=0),
+        name="split",
+    )(core.reshape(1), share)
+
+
 def step(array, axis, by):
     size = lax.axis_size(axis)
     return lax.ppermute(array, axis, [(i, (i + by) % size) for i in range(size)])
@@ -169,7 +195,7 @@
     late, weights, grad_rows, _ = lax.optimization_barrier((tokens, w_query, grad_rows, held))
     block = d // nx
     share = [lax.dynamic_slice(late, (SKIP, (mx + by) % nx * block), (length - SKIP, block)) for by in range(nx)]
-    share = [step(a, "x", by) if by else a for by, a in enumerate(share)]
+    share = [split(mc, step(a, "x", by) if by else a, d // ndp) for by, a in enumerate(share)]
 
     def shifted(array):
         return jnp.concatenate([array[LEAD:], jnp.zeros((LEAD, array.shape[1]), array.dtype)], 0)
@@ -181,16 +207,18 @@
     out, dq = attend(q, g, got.reshape(2, heads, tiles, neigh, stretches, TILE, HEAD_DIM))
     dq = jnp.concatenate([jnp.zeros((LEAD - SKIP, width), BF16), dq[:real]], 0)
 
-    total = 0.0
-    for by in sorted(range(nx), key=lambda by: min(by, nx - by)):
+    mine = other = 0.0
+    order = sorted(range(nx), key=lambda by: min(by, nx - by))
+    for by in order:
         near = step(dq, "x", by) if by else dq
-        if 2 * by == nx:
+        if by == 1:
             own = lax.dot_general(dq, fans[0], BOTH_LAST, preferred_element_type=F32).astype(BF16)
             near, own = lax.optimization_barrier((near, own))
-        total += lax.dot_general(share[by], near, BOTH_FIRST, preferred_element_type=F32)
-    total = total.reshape(nz, nc, -1, width)
-    mine = lax.dynamic_index_in_dim(total, mc, 1, keepdims=False)
-    mine += step(lax.dynamic_index_in_dim(total, 1 - mc, 1, keepdims=False), "core", 1)
+        if by == order[-1]:
+            near, mine, other = lax.optimization_barrier((near, mine, other))
+        other += lax.dot_general(share[by][1], near, BOTH_FIRST, preferred_element_type=F32)
+        mine += lax.dot_general(share[by][0], near, BOTH_FIRST, preferred_element_type=F32)
+    mine += step(other, "core", 1)
     groups = jnp.broadcast_to(dq[None], (nmp,) + dq.shape)
     groups = lax.all_to_all(groups, "mp", split_axis=0, concat_axis=0, tiled=True)
     groups, mine = lax.optimization_barrier((groups, mine))

time: 255 us -> 255 us (level)
  waiting for transfers between devices: 153 us -> 136 us
  matrix products: 20.1 us -> 26.3 us
  Pallas kernels: 10.6 us -> 14.9 us
  starting transfers between devices: 47.7 us -> 51.4 us
    ppermute x13, waiting for transfers between devices: 141 us -> 122 us  [step(): lax.ppermute(array, axis, [(i, (i + by) % size) for i in range(size)])]
    dot_general x4 -> x8, matrix products: 6.63 us -> 12 us  [the longest x4 7.02 us: local(): lax.dot_general(share[by][0], near, BOTH_FIRST, preferred_element_type=F32)]
    all_to_all x1, waiting for transfers between devices: 0.01 us -> 4.69 us  [local(): lax.all_to_all(groups, 'mp', split_axis=0, concat_axis=0, tiled=True)]
    pallas_call x0 -> x4, Pallas kernels: none -> 4.3 us  [split(): pl.pallas_call(functools.partial(split_kernel, rows=rows), in_specs=[pl.B...]
    unnamed x16 -> x38, local copies, waits for them, and re-layouts: 4.48 us -> 7.13 us
  transfers between devices with their start and end apart: 18 -> 18, of which waited for: 11 -> 11; matrix products, arithmetic and copies ran while one was open for 14% -> 16% of each run, Pallas kernels for 0% -> 2%
where the time goes in v9:
time: 255 us; the launch traced here: 254 us
  waiting for transfers between devices  136 us (53%)
  starting transfers between devices  51.4 us (20%)
  matrix products  26.3 us (10%)
  local copies, waits for them, and re-layouts  20.2 us (8%)
  Pallas kernels  14.9 us (6%)
  other arithmetic  4.89 us (2%)
    ppermute x13, waiting for transfers between devices, step(): lax.ppermute(array, axis, [(i, (i + by) % size) for i in range(size)])  122 us
    ppermute x13, starting transfers between devices, step(): lax.ppermute(array, axis, [(i, (i + by) % size) for i in range(size)])  22.1 us
    all_to_all x1, starting transfers between devices, local(): held = lax.all_to_all(message, DP, split_axis=0, concat_axis=0, tiled=True)  11.6 us
    all_to_all x1, starting transfers between devices, local(): lax.all_to_all(send.reshape(ndp, requests, TILE, HEAD_DIM), DP, split_axi...  10.5 us
    unnamed x38, local copies, waits for them, and re-layouts  7.13 us
    dot_general x4, matrix products, local(): lax.dot_general(share[by][0], near, BOTH_FIRST, preferred_element_type=F32)  7.02 us
    all_to_all x1, waiting for transfers between devices, local(): lax.all_to_all(send.reshape(ndp, requests, TILE, HEAD_DIM), DP, split_axi...  5.99 us
    pallas_call x1, Pallas kernels, attend(): pl.pallas_call(functools.partial(attend_kernel, heads=heads), grid=(count...  5.88 us
  transfers between devices with their start and end apart: 18, of which 11 were waited for; matrix products, arithmetic and copies ran while one was open for 16% of the time, Pallas kernels for 2%

profile of v9, /device:TPU:32, one launch (start us, length us, event | category | flops | bytes accessed | tf_op | source)
XLA Modules:
  0.0 254.4 jit_solution(6343925421047559206)
XLA Ops:
  1.9 2.8 %cut.1 = bf16[2,4,8,9,16,128]{5,4,3,2,1,0:T(8,128)(2,1)} custom-call(bf16[16,128]{1,0:T(8,128)(2,1)} %add_convert_fusion.1.named_ref, bf16[8,2,128,512]{3,2,1,0:T(8,128)(2,1)} %cache_ref.1), custom_call_target="tpu_custom_call" | custom-call | bytes 4194304 | tf_op jit(solution)/shard_map/cut/pallas_call | solution.py:36
  4.8 11.6 %all-to-all-start = ((bf16[64,9,16,128]{3,2,1,0:T(8,128)(2,1)}), bf16[64,9,16,128]{3,2,1,0:T(8,128)(2,1)S(1)}, u32[]{:S(2)}, u32[]{:S(2)}) async-start(bf16[64,9,16,128]{3,2,1,0:T(8,128)(2,1)} %bitcast.68), calls=%async_computation | async-start | bytes 4718592 | tf_op jit(solution)/shard_map/all_to_all | solution.py:181
  16.4 3.4 %constant_dynamic-slice_fusion = (bf16[1024,512]{1,0:T(8,128)(2,1)S(1)}, bf16[1024,512]{1,0:T(8,128)(2,1)S(1)}, bf16[1024,512]{1,0:T(8,128)(2,1)S(1)}, bf16[1024,512]{1,0:T(8,128)(2,1)}) fusion(bf16[4096,512]{1,0:T(8,128)(2,1)} %param.7, s32[]{:T(128)S(6)} %select_n.137, s32[]{:T(128)S(6)} %select_n.135, s32[]{:T(128)S(6)} %select_n.133, s32[]{:T(128)S(6)} %select_n.131), kind=kLoop, calls=%fused_computation.34 | loop fusion | bytes 8388624 | tf_op jit(solution)/shard_map/dynamic_slice | solution.py:184
  19.9 3.0 %collective-permute-start.2 = (bf16[1024,512]{1,0:T(8,128)(2,1)S(1)}, bf16[1024,512]{1,0:T(8,128)(2,1)S(1)}, u32[]{:S(2)}, u32[]{:S(2)}) collective-permute-start(bf16[1024,512]{1,0:T(8,128)(2,1)S(1)} %get-tuple-element.89), channel_id=1, source_target_pairs={{0,3},{1,0},{2,1},{3,2},{4,7},{5,4},{6,5},{7,6},{8,11},{9,8},{10,9... | collective-permute-start | bytes 3145736 | tf_op jit(solution)/shard_map/ppermute | solution.py:160
  24.5 43.6 %collective-permute-done.2 = bf16[1024,512]{1,0:T(8,128)(2,1)S(1)} collective-permute-done((bf16[1024,512]{1,0:T(8,128)(2,1)S(1)}, bf16[1024,512]{1,0:T(8,128)(2,1)S(1)}, u32[]{:S(2)}, u32[]{:S(2)}) %collective-permute-start.2) | collective-permute-done | bytes 1048608 | tf_op jit(solution)/shard_map/ppermute | solution.py:160
  76.0 10.5 %all-to-all-start.1 = ((bf16[64,16,16,128]{3,2,1,0:T(8,128)(2,1)}), bf16[64,16,16,128]{3,2,1,0:T(8,128)(2,1)}, u32[]{:S(2)}, u32[]{:S(2)}) async-start(bf16[64,16,16,128]{3,2,1,0:T(8,128)(2,1)} %bitcast.66), calls=%async_computation.1 | async-start | bytes 8388608 | tf_op jit(solution)/shard_map/all_to_all | solution.py:191
  86.6 3.8 %constant_dynamic-slice_fusion.4 = (bf16[464,1024]{1,0:T(8,128)(2,1)}, bf16[464,1024]{1,0:T(8,128)(2,1)}, bf16[464,1024]{1,0:T(8,128)(2,1)}, bf16[464,1024]{1,0:T(8,128)(2,1)S(1)}) fusion(bf16[512,4096]{1,0:T(8,128)(2,1)} %bitcast.71, s32[]{:T(128)S(6)} %select_n.145, s32[]{:T(128)S(6)} %select_n.143, s32[]{:T(128)S(6)} %select_n.141, s32[]{:T(128)S(6)} %select_n.139), kind=kLoop, calls=%fused_computation.38 | loop fusion | bytes 7602192 | tf_op jit(solution)/shard_map/dynamic_slice | solution.py:197
  90.4 2.9 %collective-permute-start.5 = (bf16[464,1024]{1,0:T(8,128)(2,1)}, bf16[464,1024]{1,0:T(8,128)(2,1)}, u32[]{:S(2)}, u32[]{:S(2)}) collective-permute-start(bf16[464,1024]{1,0:T(8,128)(2,1)} %get-tuple-element.85), channel_id=1, source_target_pairs={{0,192},{64,0},{128,64},{192,128},{1,193},{65,1},{129,65},{193,129... | collective-permute-start | bytes 2850824 | tf_op jit(solution)/shard_map/ppermute | solution.py:160
  95.0 5.8 %fusion.20 = bf16[512,512]{1,0:T(8,128)(2,1)S(1)} fusion(bf16[512,4096]{1,0:T(8,128)(2,1)} %bitcast.72, bf16[4096,512]{1,0:T(8,128)(2,1)} %param.7), kind=kOutput, calls=%fused_computation.51 | convolution fusion | flops 2147483648 | bytes 8912896 | tf_op jit(solution)/shard_map/dot_general | solution.py:203
  102.3 35.7 %collective-permute-done.5.share_ref = bf16[464,1024]{1,0:T(8,128)(2,1)} collective-permute-done((bf16[464,1024]{1,0:T(8,128)(2,1)}, bf16[464,1024]{1,0:T(8,128)(2,1)}, u32[]{:S(2)}, u32[]{:S(2)}) %collective-permute-start.5) | collective-permute-done | bytes 950304 | tf_op jit(solution)/shard_map/ppermute | solution.py:160
  142.1 30.5 %collective-permute-done.3.share_ref = bf16[464,1024]{1,0:T(8,128)(2,1)S(1)} collective-permute-done((bf16[464,1024]{1,0:T(8,128)(2,1)}, bf16[464,1024]{1,0:T(8,128)(2,1)S(1)}, u32[]{:S(2)}, u32[]{:S(2)}) %collective-permute-start.3) | collective-permute-done | bytes 950304 | tf_op jit(solution)/shard_map/ppermute | solution.py:160
  174.6 6.0 %all-to-all-done.1 = bf16[64,16,16,128]{3,2,1,0:T(8,128)(2,1)} async-done(((bf16[64,16,16,128]{3,2,1,0:T(8,128)(2,1)}), bf16[64,16,16,128]{3,2,1,0:T(8,128)(2,1)}, u32[]{:S(2)}, u32[]{:S(2)}) %all-to-all-start.1) | async-done | bytes 4194336 | tf_op jit(solution)/shard_map/all_to_all | solution.py:191
  180.6 5.9 %attend.1 = (bf16[512,512]{1,0:T(8,128)(2,1)S(1)}, bf16[512,512]{1,0:T(8,128)(2,1)S(1)}) custom-call(bf16[512,512]{1,0:T(8,128)(2,1)S(1)} %concatenate.18.q_ref, bf16[512,512]{1,0:T(8,128)(2,1)S(1)} %concatenate.19.g_ref, bf16[2,4,8,2,8,16,128]{6,5,4,3,2,1,0:T(8,128)(2,1)} %bitcast.12.kv_ref), custom_call_target="tpu_custom_call" | custom-call | flops 671088640 | bytes 4194304 | tf_op jit(solution)/shard_map/attend/pallas_call | solution.py:112
  193.9 2.4 broadcast_in_dim.7
  196.4 4.5 %all-to-all-start.2 = ((bf16[4,464,512]{2,1,0:T(8,128)(2,1)}), bf16[4,464,512]{2,1,0:T(8,128)(2,1)}, u32[]{:S(2)}, u32[]{:S(2)}) async-start(bf16[4,464,512]{2,1,0:T(8,128)(2,1)} %broadcast_in_dim.7), calls=%async_computation.2 | async-start | bytes 3801088 | tf_op jit(solution)/shard_map/all_to_all | solution.py:223
  201.4 2.9 %convolution_convert_fusion.3 = bf16[464,1024]{1,0:T(8,128)(2,1)} fusion(bf16[1024,512]{1,0:T(8,128)(2,1)} %get-tuple-element.63, bf16[449,512]{1,0:T(8,128)(2,1)S(1)} %slice.33), kind=kOutput, calls=%fused_computation.4 | convolution fusion | flops 487014400 | bytes 2458624 | tf_op jit(solution)/shard_map/dot_general | solution.py:215
  207.5 2.5 convolution_add_fusion.2
  211.5 2.4 collective-permute-done.6
  221.1 4.7 %all-to-all-done.2 = bf16[4,464,512]{2,1,0:T(8,128)(2,1)} async-done(((bf16[4,464,512]{2,1,0:T(8,128)(2,1)}), bf16[4,464,512]{2,1,0:T(8,128)(2,1)}, u32[]{:S(2)}, u32[]{:S(2)}) %all-to-all-start.2) | async-done | bytes 1900576 | tf_op jit(solution)/shard_map/all_to_all | solution.py:223
  226.2 2.3 collective-permute-start.10
  232.5 2.4 collective-permute-done.10
  235.0 3.8 %collective-permute-start.12 = (f32[64,512]{1,0:T(8,128)S(1)}, f32[64,512]{1,0:T(8,128)S(1)}, u32[]{:S(2)}, u32[]{:S(2)}) collective-permute-start(f32[64,512]{1,0:T(8,128)S(1)} %get-tuple-element.93), channel_id=1, source_target_pairs={{0,16},{8,24},{16,32},{24,40},{32,48},{40,56},{48,0},{56,8},{1,17}... | collective-permute-start | bytes 393224 | tf_op jit(solution)/shard_map/ppermute | solution.py:160
  239.3 3.6 %collective-permute-start.13 = (f32[64,512]{1,0:T(8,128)S(1)}, f32[64,512]{1,0:T(8,128)S(1)}, u32[]{:S(2)}, u32[]{:S(2)}) collective-permute-start(f32[64,512]{1,0:T(8,128)S(1)} %get-tuple-element.95), channel_id=1, source_target_pairs={{0,32},{8,40},{16,48},{24,56},{32,0},{40,8},{48,16},{56,24},{1,33}... | collective-permute-start | bytes 393224 | tf_op jit(solution)/shard_map/ppermute | solution.py:160
  247.6 6.0 %collective-permute-done.13 = f32[64,512]{1,0:T(8,128)S(1)} collective-permute-done((f32[64,512]{1,0:T(8,128)S(1)}, f32[64,512]{1,0:T(8,128)S(1)}, u32[]{:S(2)}, u32[]{:S(2)}) %collective-permute-start.13) | collective-permute-done | bytes 131104 | tf_op jit(solution)/shard_map/ppermute | solution.py:160
  (93 shorter events, 50.1 us)
Async XLA Ops:
  4.8 67.1 %all-to-all-start = ((bf16[64,9,16,128]{3,2,1,0:T(8,128)(2,1)}), bf16[64,9,16,128]{3,2,1,0:T(8,128)(2,1)S(1)}, u32[]{:S(2)}, u32[]{:S(2)}) async-start(bf16[64,9,16,128]{3,2,1,0:T(8,128)(2,1)} %bitcast.68), calls=%async_computation | async-start | bytes 4718592 | tf_op jit(solution)/shard_map/all_to_all | solution.py:181
  19.9 48.2 %collective-permute-start.2 = (bf16[1024,512]{1,0:T(8,128)(2,1)S(1)}, bf16[1024,512]{1,0:T(8,128)(2,1)S(1)}, u32[]{:S(2)}, u32[]{:S(2)}) collective-permute-start(bf16[1024,512]{1,0:T(8,128)(2,1)S(1)} %get-tuple-element.89), channel_id=1, source_target_pairs={{0,3},{1,0},{2,1},{3,2},{4,7},{5,4},{6,5},{7,6},{8,11},{9,8},{10,9... | collective-permute-start | bytes 3145736 | tf_op jit(solution)/shard_map/ppermute | solution.py:160
  22.9 45.2 %collective-permute-start.1 = (bf16[1024,512]{1,0:T(8,128)(2,1)S(1)}, bf16[1024,512]{1,0:T(8,128)(2,1)S(1)}, u32[]{:S(2)}, u32[]{:S(2)}) collective-permute-start(bf16[1024,512]{1,0:T(8,128)(2,1)S(1)} %get-tuple-element.90), channel_id=1, source_target_pairs={{0,2},{1,3},{2,0},{3,1},{4,6},{5,7},{6,4},{7,5},{8,10},{9,11},{10,... | collective-permute-start | bytes 3145736 | tf_op jit(solution)/shard_map/ppermute | solution.py:160
  23.5 48.4 %collective-permute-start = (bf16[1024,512]{1,0:T(8,128)(2,1)S(1)}, bf16[1024,512]{1,0:T(8,128)(2,1)}, u32[]{:S(2)}, u32[]{:S(2)}) collective-permute-start(bf16[1024,512]{1,0:T(8,128)(2,1)S(1)} %get-tuple-element.91), channel_id=1, source_target_pairs={{0,1},{1,2},{2,3},{3,0},{4,5},{5,6},{6,7},{7,4},{8,9},{9,10},{10,1... | collective-permute-start | bytes 3145736 | tf_op jit(solution)/shard_map/ppermute | solution.py:160
  76.0 104.6 %all-to-all-start.1 = ((bf16[64,16,16,128]{3,2,1,0:T(8,128)(2,1)}), bf16[64,16,16,128]{3,2,1,0:T(8,128)(2,1)}, u32[]{:S(2)}, u32[]{:S(2)}) async-start(bf16[64,16,16,128]{3,2,1,0:T(8,128)(2,1)} %bitcast.66), calls=%async_computation.1 | async-start | bytes 8388608 | tf_op jit(solution)/shard_map/all_to_all | solution.py:191
  86.6 8.3 %copy-start.13 = (bf16[1,512,512]{2,1,0:T(8,128)(2,1)S(1)}, bf16[1,512,512]{2,1,0:T(8,128)(2,1)}, u32[]{:S(2)}) copy-start(bf16[1,512,512]{2,1,0:T(8,128)(2,1)} %param.11) | copy-start | bytes 1572868
  90.4 47.6 %collective-permute-start.5 = (bf16[464,1024]{1,0:T(8,128)(2,1)}, bf16[464,1024]{1,0:T(8,128)(2,1)}, u32[]{:S(2)}, u32[]{:S(2)}) collective-permute-start(bf16[464,1024]{1,0:T(8,128)(2,1)} %get-tuple-element.85), channel_id=1, source_target_pairs={{0,192},{64,0},{128,64},{192,128},{1,193},{65,1},{129,65},{193,129... | collective-permute-start | bytes 2850824 | tf_op jit(solution)/shard_map/ppermute | solution.py:160
  93.3 47.1 %collective-permute-start.4 = (bf16[464,1024]{1,0:T(8,128)(2,1)}, bf16[464,1024]{1,0:T(8,128)(2,1)}, u32[]{:S(2)}, u32[]{:S(2)}) collective-permute-start(bf16[464,1024]{1,0:T(8,128)(2,1)} %get-tuple-element.86), channel_id=1, source_target_pairs={{0,128},{64,192},{128,0},{192,64},{1,129},{65,193},{129,1},{193,65... | collective-permute-start | bytes 2850824 | tf_op jit(solution)/shard_map/ppermute | solution.py:160
  93.9 78.6 %collective-permute-start.3 = (bf16[464,1024]{1,0:T(8,128)(2,1)}, bf16[464,1024]{1,0:T(8,128)(2,1)S(1)}, u32[]{:S(2)}, u32[]{:S(2)}) collective-permute-start(bf16[464,1024]{1,0:T(8,128)(2,1)} %get-tuple-element.87), channel_id=1, source_target_pairs={{0,64},{64,128},{128,192},{192,0},{1,65},{65,129},{129,193},{193,1... | collective-permute-start | bytes 2850824 | tf_op jit(solution)/shard_map/ppermute | solution.py:160
  102.3 38.1 %copy-start.3 = (bf16[464,512]{1,0:T(8,128)(2,1)}, bf16[464,512]{1,0:T(8,128)(2,1)S(1)}, u32[]{:S(2)}) copy-start(bf16[464,512]{1,0:T(8,128)(2,1)S(1)} %get-tuple-element.66) | copy-start | bytes 1425412
  186.5 5.9 %copy-start.6 = (bf16[464,512]{1,0:T(8,128)(2,1)S(1)}, bf16[464,512]{1,0:T(8,128)(2,1)}, u32[]{:S(2)}) copy-start(bf16[464,512]{1,0:T(8,128)(2,1)} %copy-done.5) | copy-start | bytes 1425412
  187.5 16.8 %collective-permute-start.7 = (bf16[464,512]{1,0:T(8,128)(2,1)}, bf16[464,512]{1,0:T(8,128)(2,1)}, u32[]{:S(2)}, u32[]{:S(2)}) collective-permute-start(bf16[464,512]{1,0:T(8,128)(2,1)} %concatenate.21), channel_id=1, source_target_pairs={{0,64},{64,128},{128,192},{192,0},{1,65},{65,129},{129,193},{193,1... | collective-permute-start | bytes 1425416 | tf_op jit(solution)/shard_map/ppermute | solution.py:160
  188.8 18.6 %collective-permute-start.8 = (bf16[464,512]{1,0:T(8,128)(2,1)}, bf16[464,512]{1,0:T(8,128)(2,1)}, u32[]{:S(2)}, u32[]{:S(2)}) collective-permute-start(bf16[464,512]{1,0:T(8,128)(2,1)} %concatenate.21), channel_id=1, source_target_pairs={{0,192},{64,0},{128,64},{192,128},{1,193},{65,1},{129,65},{193,129... | collective-permute-start | bytes 1425416 | tf_op jit(solution)/shard_map/ppermute | solution.py:160
  190.7 23.2 %collective-permute-start.6 = (bf16[464,512]{1,0:T(8,128)(2,1)}, bf16[464,512]{1,0:T(8,128)(2,1)}, u32[]{:S(2)}, u32[]{:S(2)}) collective-permute-start(bf16[464,512]{1,0:T(8,128)(2,1)} %concatenate.21), channel_id=1, source_target_pairs={{0,128},{64,192},{128,0},{192,64},{1,129},{65,193},{129,1},{193,65... | collective-permute-start | bytes 1425416 | tf_op jit(solution)/shard_map/ppermute | solution.py:160
  196.4 29.5 %all-to-all-start.2 = ((bf16[4,464,512]{2,1,0:T(8,128)(2,1)}), bf16[4,464,512]{2,1,0:T(8,128)(2,1)}, u32[]{:S(2)}, u32[]{:S(2)}) async-start(bf16[4,464,512]{2,1,0:T(8,128)(2,1)} %broadcast_in_dim.7), calls=%async_computation.2 | async-start | bytes 3801088 | tf_op jit(solution)/shard_map/all_to_all | solution.py:223
  216.5 3.0 %collective-permute-start.9 = (f32[512,512]{1,0:T(8,128)}, f32[512,512]{1,0:T(8,128)}, u32[]{:S(2)}, u32[]{:S(2)}) collective-permute-start(f32[512,512]{1,0:T(8,128)} %add.227), channel_id=1, source_target_pairs={{0,4},{4,0},{1,5},{5,1},{2,6},{6,2},{3,7},{7,3},{8,12},{12,8},{9,1... | collective-permute-start | bytes 3145736 | tf_op jit(solution)/shard_map/ppermute | solution.py:160
  221.1 7.5 %copy-start.17 = (bf16[1024,512]{1,0:T(8,128)(2,1)S(1)}, bf16[1024,512]{1,0:T(8,128)(2,1)}, u32[]{:S(2)}) copy-start(bf16[1024,512]{1,0:T(8,128)(2,1)} %copy-done.16) | copy-start | bytes 3145732
  225.9 9.0 %collective-permute-start.11 = (f32[4,64,256]{2,1,0:T(8,128)S(1)}, f32[4,64,256]{2,1,0:T(8,128)S(1)}, u32[]{:S(2)}, u32[]{:S(2)}) collective-permute-start(f32[4,64,256]{2,1,0:T(8,128)S(1)} %get-tuple-element.96), channel_id=1, source_target_pairs={{8,16},{16,8},{24,32},{32,24},{40,48},{48,40},{0,56},{56,0},{9,17}... | collective-permute-start | bytes 786440 | tf_op jit(solution)/shard_map/ppermute | solution.py:229
  226.2 8.7 %collective-permute-start.10 = (f32[4,64,256]{2,1,0:T(8,128)S(1)}, f32[4,64,256]{2,1,0:T(8,128)S(1)}, u32[]{:S(2)}, u32[]{:S(2)}) collective-permute-start(f32[4,64,256]{2,1,0:T(8,128)S(1)} %get-tuple-element.97), channel_id=1, source_target_pairs={{0,8},{8,0},{16,24},{24,16},{32,40},{40,32},{48,56},{56,48},{1,9},... | collective-permute-start | bytes 786440 | tf_op jit(solution)/shard_map/ppermute | solution.py:228
  230.3 12.6 %copy-start.15 = (bf16[1024,512]{1,0:T(8,128)(2,1)S(1)}, bf16[1024,512]{1,0:T(8,128)(2,1)}, u32[]{:S(2)}) copy-start(bf16[1024,512]{1,0:T(8,128)(2,1)} %copy-done.14) | copy-start | bytes 3145732
  230.3 12.6 %copy-start.18 = (bf16[464,1024]{1,0:T(8,128)(2,1)S(1)}, bf16[464,1024]{1,0:T(8,128)(2,1)}, u32[]{:S(2)}) copy-start(bf16[464,1024]{1,0:T(8,128)(2,1)} %convolution_convert_fusion.3) | copy-start | bytes 2850820
  235.0 10.6 %collective-permute-start.12 = (f32[64,512]{1,0:T(8,128)S(1)}, f32[64,512]{1,0:T(8,128)S(1)}, u32[]{:S(2)}, u32[]{:S(2)}) collective-permute-start(f32[64,512]{1,0:T(8,128)S(1)} %get-tuple-element.93), channel_id=1, source_target_pairs={{0,16},{8,24},{16,32},{24,40},{32,48},{40,56},{48,0},{56,8},{1,17}... | collective-permute-start | bytes 393224 | tf_op jit(solution)/shard_map/ppermute | solution.py:160
  238.9 8.8 %collective-permute-start.14 = (f32[64,512]{1,0:T(8,128)S(1)}, f32[64,512]{1,0:T(8,128)S(1)}, u32[]{:S(2)}, u32[]{:S(2)}) collective-permute-start(f32[64,512]{1,0:T(8,128)S(1)} %get-tuple-element.94), channel_id=1, source_target_pairs={{0,48},{8,56},{16,0},{24,8},{32,16},{40,24},{48,32},{56,40},{1,49}... | collective-permute-start | bytes 393224 | tf_op jit(solution)/shard_map/ppermute | solution.py:160
  239.3 14.4 %collective-permute-start.13 = (f32[64,512]{1,0:T(8,128)S(1)}, f32[64,512]{1,0:T(8,128)S(1)}, u32[]{:S(2)}, u32[]{:S(2)}) collective-permute-start(f32[64,512]{1,0:T(8,128)S(1)} %get-tuple-element.95), channel_id=1, source_target_pairs={{0,32},{8,40},{16,48},{24,56},{32,0},{40,8},{48,16},{56,24},{1,33}... | collective-permute-start | bytes 393224 | tf_op jit(solution)/shard_map/ppermute | solution.py:160
  (13 other events, 24.4 us)

commit v10 on v9

--- a/solution.py
+++ b/solution.py
@@ -215,13 +215,12 @@
             own = lax.dot_general(dq, fans[0], BOTH_LAST, preferred_element_type=F32).astype(BF16)
             near, own = lax.optimization_barrier((near, own))
         if by == order[-1]:
-            near, mine, other = lax.optimization_barrier((near, mine, other))
+            near, mine, _ = lax.optimization_barrier((near, mine, other))
         other += lax.dot_general(share[by][1], near, BOTH_FIRST, preferred_element_type=F32)
         mine += lax.dot_general(share[by][0], near, BOTH_FIRST, preferred_element_type=F32)
     mine += step(other, "core", 1)
     groups = jnp.broadcast_to(dq[None], (nmp,) + dq.shape)
     groups = lax.all_to_all(groups, "mp", split_axis=0, concat_axis=0, tiled=True)
-    groups, mine = lax.optimization_barrier((groups, mine))
     pairs = mine.reshape(nz // 2, 2, -1, width)
     away = lax.dynamic_index_in_dim(pairs, 1 - mz % 2, 1, keepdims=False)
     mine = lax.dynamic_index_in_dim(pairs, mz % 2, 1, keepdims=False)
@@ -229,7 +228,7 @@
     down = lax.ppermute(away[..., width // 2 :], "z", [(i, ((i + 1) ^ 1) - 1) for i in range(1, nz - 1)] + [(0, nz - 1), (nz - 1, 0)])
     parts = [own]
     for by in range(1, nmp):
-        if by == nmp - 1:
+        if by == 2:
             up, parts, groups = lax.optimization_barrier((up, parts, groups))
         near = lax.dynamic_index_in_dim(groups, (my - by) % nmp, 0, keepdims=False)
         parts.append(lax.dot_general(near, fans[by], BOTH_LAST, preferred_element_type=F32).astype(BF16))

time: 255 us -> 269 us (1.055)
  waiting for transfers between devices: 136 us -> 158 us
  matrix products: 26.3 us -> 19.1 us
    all_to_all x1, waiting for transfers between devices: 4.69 us -> 18.5 us  [local(): lax.all_to_all(groups, 'mp', split_axis=0, concat_axis=0, tiled=True)]
    ppermute x13, waiting for transfers between devices: 122 us -> 134 us  [step(): lax.ppermute(array, axis, [(i, (i + by) % size) for i in range(size)])]
    dot_general x4, matrix products: 7.02 us -> 2.9 us  [local(): lax.dot_general(share[by][0], near, BOTH_FIRST, preferred_element_type=F32)]
    unnamed x38 -> x40, local copies, waits for them, and re-layouts: 7.13 us -> 7.12 us
  transfers between devices with their start and end apart: 18 -> 18, of which waited for: 11 -> 9; matrix products, arithmetic and copies ran while one was open for 16% -> 11% of each run, Pallas kernels for 2% -> 2%
where the time goes in v10:
time: 269 us
  waiting for transfers between devices  158 us (59%)
  starting transfers between devices  52.9 us (20%)
  matrix products  19.1 us (7%)
  local copies, waits for them, and re-layouts  18.4 us (7%)
  Pallas kernels  14.9 us (6%)
  other arithmetic  3.7 us (1%)
    ppermute x13, waiting for transfers between devices, step(): lax.ppermute(array, axis, [(i, (i + by) % size) for i in range(size)])  134 us
    ppermute x13, starting transfers between devices, step(): lax.ppermute(array, axis, [(i, (i + by) % size) for i in range(size)])  23 us
    all_to_all x1, waiting for transfers between devices, local(): lax.all_to_all(groups, 'mp', split_axis=0, concat_axis=0, tiled=True)  18.5 us
    all_to_all x1, starting transfers between devices, local(): held = lax.all_to_all(message, DP, split_axis=0, concat_axis=0, tiled=True)  11.6 us
    all_to_all x1, starting transfers between devices, local(): lax.all_to_all(send.reshape(ndp, requests, TILE, HEAD_DIM), DP, split_axi...  10.5 us
    unnamed x40, local copies, waits for them, and re-layouts  7.12 us
    all_to_all x1, waiting for transfers between devices, local(): lax.all_to_all(send.reshape(ndp, requests, TILE, HEAD_DIM), DP, split_axi...  6 us
    pallas_call x1, Pallas kernels, attend(): pl.pallas_call(functools.partial(attend_kernel, heads=heads), grid=(count...  5.89 us
  transfers between devices with their start and end apart: 18, of which 9 were waited for; matrix products, arithmetic and copies ran while one was open for 11% of the time, Pallas kernels for 2%

profile of v10, /device:TPU:32, one launch (start us, length us, event | category | flops | bytes accessed | tf_op | source)
XLA Modules:
  0.0 268.5 jit_solution(9612103173710882961)
XLA Ops:
  1.9 2.8 %cut.1 = bf16[2,4,8,9,16,128]{5,4,3,2,1,0:T(8,128)(2,1)} custom-call(bf16[16,128]{1,0:T(8,128)(2,1)} %add_convert_fusion.1.named_ref, bf16[8,2,128,512]{3,2,1,0:T(8,128)(2,1)} %cache_ref.1), custom_call_target="tpu_custom_call" | custom-call | bytes 4194304 | tf_op jit(solution)/shard_map/cut/pallas_call | solution.py:36
  4.8 11.6 %all-to-all-start = ((bf16[64,9,16,128]{3,2,1,0:T(8,128)(2,1)}), bf16[64,9,16,128]{3,2,1,0:T(8,128)(2,1)S(1)}, u32[]{:S(2)}, u32[]{:S(2)}) async-start(bf16[64,9,16,128]{3,2,1,0:T(8,128)(2,1)} %bitcast.68), calls=%async_computation | async-start | bytes 4718592 | tf_op jit(solution)/shard_map/all_to_all | solution.py:181
  16.4 3.4 %constant_dynamic-slice_fusion = (bf16[1024,512]{1,0:T(8,128)(2,1)S(1)}, bf16[1024,512]{1,0:T(8,128)(2,1)S(1)}, bf16[1024,512]{1,0:T(8,128)(2,1)S(1)}, bf16[1024,512]{1,0:T(8,128)(2,1)}) fusion(bf16[4096,512]{1,0:T(8,128)(2,1)} %param.7, s32[]{:T(128)S(6)} %select_n.137, s32[]{:T(128)S(6)} %select_n.135, s32[]{:T(128)S(6)} %select_n.133, s32[]{:T(128)S(6)} %select_n.131), kind=kLoop, calls=%fused_computation.35 | loop fusion | bytes 8388624 | tf_op jit(solution)/shard_map/dynamic_slice | solution.py:184
  19.9 3.0 %collective-permute-start.2 = (bf16[1024,512]{1,0:T(8,128)(2,1)S(1)}, bf16[1024,512]{1,0:T(8,128)(2,1)S(1)}, u32[]{:S(2)}, u32[]{:S(2)}) collective-permute-start(bf16[1024,512]{1,0:T(8,128)(2,1)S(1)} %get-tuple-element.81), channel_id=1, source_target_pairs={{0,3},{1,0},{2,1},{3,2},{4,7},{5,4},{6,5},{7,6},{8,11},{9,8},{10,9... | collective-permute-start | bytes 3145736 | tf_op jit(solution)/shard_map/ppermute | solution.py:160
  24.5 43.6 %collective-permute-done.2 = bf16[1024,512]{1,0:T(8,128)(2,1)S(1)} collective-permute-done((bf16[1024,512]{1,0:T(8,128)(2,1)S(1)}, bf16[1024,512]{1,0:T(8,128)(2,1)S(1)}, u32[]{:S(2)}, u32[]{:S(2)}) %collective-permute-start.2) | collective-permute-done | bytes 1048608 | tf_op jit(solution)/shard_map/ppermute | solution.py:160
  74.0 2.0 copy-done
  76.0 10.5 %all-to-all-start.1 = ((bf16[64,16,16,128]{3,2,1,0:T(8,128)(2,1)}), bf16[64,16,16,128]{3,2,1,0:T(8,128)(2,1)}, u32[]{:S(2)}, u32[]{:S(2)}) async-start(bf16[64,16,16,128]{3,2,1,0:T(8,128)(2,1)} %bitcast.66), calls=%async_computation.1 | async-start | bytes 8388608 | tf_op jit(solution)/shard_map/all_to_all | solution.py:191
  86.6 3.8 %constant_dynamic-slice_fusion.4 = (bf16[464,1024]{1,0:T(8,128)(2,1)}, bf16[464,1024]{1,0:T(8,128)(2,1)}, bf16[464,1024]{1,0:T(8,128)(2,1)}, bf16[464,1024]{1,0:T(8,128)(2,1)S(1)}) fusion(bf16[512,4096]{1,0:T(8,128)(2,1)} %bitcast.71, s32[]{:T(128)S(6)} %select_n.145, s32[]{:T(128)S(6)} %select_n.143, s32[]{:T(128)S(6)} %select_n.141, s32[]{:T(128)S(6)} %select_n.139), kind=kLoop, calls=%fused_computation.39 | loop fusion | bytes 7602192 | tf_op jit(solution)/shard_map/dynamic_slice | solution.py:197
  90.4 2.9 %collective-permute-start.5 = (bf16[464,1024]{1,0:T(8,128)(2,1)}, bf16[464,1024]{1,0:T(8,128)(2,1)}, u32[]{:S(2)}, u32[]{:S(2)}) collective-permute-start(bf16[464,1024]{1,0:T(8,128)(2,1)} %get-tuple-element.77), channel_id=1, source_target_pairs={{0,192},{64,0},{128,64},{192,128},{1,193},{65,1},{129,65},{193,129... | collective-permute-start | bytes 2850824 | tf_op jit(solution)/shard_map/ppermute | solution.py:160
  95.0 5.8 %fusion.20 = bf16[512,512]{1,0:T(8,128)(2,1)S(1)} fusion(bf16[512,4096]{1,0:T(8,128)(2,1)} %bitcast.72, bf16[4096,512]{1,0:T(8,128)(2,1)} %param.7), kind=kOutput, calls=%fused_computation.52 | convolution fusion | flops 2147483648 | bytes 8912896 | tf_op jit(solution)/shard_map/dot_general | solution.py:203
  102.3 35.7 %collective-permute-done.5.share_ref = bf16[464,1024]{1,0:T(8,128)(2,1)} collective-permute-done((bf16[464,1024]{1,0:T(8,128)(2,1)}, bf16[464,1024]{1,0:T(8,128)(2,1)}, u32[]{:S(2)}, u32[]{:S(2)}) %collective-permute-start.5) | collective-permute-done | bytes 950304 | tf_op jit(solution)/shard_map/ppermute | solution.py:160
  142.0 30.5 %collective-permute-done.3.share_ref = bf16[464,1024]{1,0:T(8,128)(2,1)S(1)} collective-permute-done((bf16[464,1024]{1,0:T(8,128)(2,1)}, bf16[464,1024]{1,0:T(8,128)(2,1)S(1)}, u32[]{:S(2)}, u32[]{:S(2)}) %collective-permute-start.3) | collective-permute-done | bytes 950304 | tf_op jit(solution)/shard_map/ppermute | solution.py:160
  174.6 6.0 %all-to-all-done.1 = bf16[64,16,16,128]{3,2,1,0:T(8,128)(2,1)} async-done(((bf16[64,16,16,128]{3,2,1,0:T(8,128)(2,1)}), bf16[64,16,16,128]{3,2,1,0:T(8,128)(2,1)}, u32[]{:S(2)}, u32[]{:S(2)}) %all-to-all-start.1) | async-done | bytes 4194336 | tf_op jit(solution)/shard_map/all_to_all | solution.py:191
  180.6 5.9 %attend.1 = (bf16[512,512]{1,0:T(8,128)(2,1)S(1)}, bf16[512,512]{1,0:T(8,128)(2,1)S(1)}) custom-call(bf16[512,512]{1,0:T(8,128)(2,1)S(1)} %concatenate.18.q_ref, bf16[512,512]{1,0:T(8,128)(2,1)S(1)} %concatenate.19.g_ref, bf16[2,4,8,2,8,16,128]{6,5,4,3,2,1,0:T(8,128)(2,1)} %bitcast.12.kv_ref), custom_call_target="tpu_custom_call" | custom-call | flops 671088640 | bytes 4194304 | tf_op jit(solution)/shard_map/attend/pallas_call | solution.py:112
  194.4 7.2 %collective-permute-done.7 = bf16[464,512]{1,0:T(8,128)(2,1)S(1)} collective-permute-done((bf16[464,512]{1,0:T(8,128)(2,1)S(1)}, bf16[464,512]{1,0:T(8,128)(2,1)S(1)}, u32[]{:S(2)}, u32[]{:S(2)}) %collective-permute-start.7) | collective-permute-done | bytes 475168 | tf_op jit(solution)/shard_map/ppermute | solution.py:160
  202.6 8.6 %collective-permute-done.8 = bf16[464,512]{1,0:T(8,128)(2,1)S(1)} collective-permute-done((bf16[464,512]{1,0:T(8,128)(2,1)S(1)}, bf16[464,512]{1,0:T(8,128)(2,1)S(1)}, u32[]{:S(2)}, u32[]{:S(2)}) %collective-permute-start.8) | collective-permute-done | bytes 475168 | tf_op jit(solution)/shard_map/ppermute | solution.py:160
  216.0 4.4 %all-to-all-start.2 = ((bf16[4,464,512]{2,1,0:T(8,128)(2,1)}), bf16[4,464,512]{2,1,0:T(8,128)(2,1)}, u32[]{:S(2)}, u32[]{:S(2)}) async-start(bf16[4,464,512]{2,1,0:T(8,128)(2,1)} %broadcast_in_dim.7), calls=%async_computation.2 | async-start | bytes 3801088 | tf_op jit(solution)/shard_map/all_to_all | solution.py:223
  224.1 3.1 %collective-permute-start.10 = (f32[4,64,256]{2,1,0:T(8,128)S(1)}, f32[4,64,256]{2,1,0:T(8,128)S(1)}, u32[]{:S(2)}, u32[]{:S(2)}) collective-permute-start(f32[4,64,256]{2,1,0:T(8,128)S(1)} %get-tuple-element.89), channel_id=1, source_target_pairs={{0,8},{8,0},{16,24},{24,16},{32,40},{40,32},{48,56},{56,48},{1,9},... | collective-permute-start | bytes 786440 | tf_op jit(solution)/shard_map/ppermute | solution.py:227
  227.2 18.5 %all-to-all-done.2 = bf16[4,464,512]{2,1,0:T(8,128)(2,1)} async-done(((bf16[4,464,512]{2,1,0:T(8,128)(2,1)}), bf16[4,464,512]{2,1,0:T(8,128)(2,1)}, u32[]{:S(2)}, u32[]{:S(2)}) %all-to-all-start.2) | async-done | bytes 1900576 | tf_op jit(solution)/shard_map/all_to_all | solution.py:223
  245.7 2.1 convolution_convert_fusion.2
  248.2 4.0 %collective-permute-start.14 = (f32[64,512]{1,0:T(8,128)S(1)}, f32[64,512]{1,0:T(8,128)S(1)}, u32[]{:S(2)}, u32[]{:S(2)}) collective-permute-start(f32[64,512]{1,0:T(8,128)S(1)} %get-tuple-element.86), channel_id=1, source_target_pairs={{0,48},{8,56},{16,0},{24,8},{32,16},{40,24},{48,32},{56,40},{1,49}... | collective-permute-start | bytes 393224 | tf_op jit(solution)/shard_map/ppermute | solution.py:160
  252.1 4.6 %collective-permute-start.13 = (f32[64,512]{1,0:T(8,128)S(1)}, f32[64,512]{1,0:T(8,128)S(1)}, u32[]{:S(2)}, u32[]{:S(2)}) collective-permute-start(f32[64,512]{1,0:T(8,128)S(1)} %get-tuple-element.87), channel_id=1, source_target_pairs={{0,32},{8,40},{16,48},{24,56},{32,0},{40,8},{48,16},{56,24},{1,33}... | collective-permute-start | bytes 393224 | tf_op jit(solution)/shard_map/ppermute | solution.py:160
  256.7 2.1 convolution_convert_fusion.1
  261.6 6.2 %collective-permute-done.13 = f32[64,512]{1,0:T(8,128)S(1)} collective-permute-done((f32[64,512]{1,0:T(8,128)S(1)}, f32[64,512]{1,0:T(8,128)S(1)}, u32[]{:S(2)}, u32[]{:S(2)}) %collective-permute-start.13) | collective-permute-done | bytes 131104 | tf_op jit(solution)/shard_map/ppermute | solution.py:160
  (94 shorter events, 39.0 us)
Async XLA Ops:
  4.8 67.1 %all-to-all-start = ((bf16[64,9,16,128]{3,2,1,0:T(8,128)(2,1)}), bf16[64,9,16,128]{3,2,1,0:T(8,128)(2,1)S(1)}, u32[]{:S(2)}, u32[]{:S(2)}) async-start(bf16[64,9,16,128]{3,2,1,0:T(8,128)(2,1)} %bitcast.68), calls=%async_computation | async-start | bytes 4718592 | tf_op jit(solution)/shard_map/all_to_all | solution.py:181
  19.9 48.2 %collective-permute-start.2 = (bf16[1024,512]{1,0:T(8,128)(2,1)S(1)}, bf16[1024,512]{1,0:T(8,128)(2,1)S(1)}, u32[]{:S(2)}, u32[]{:S(2)}) collective-permute-start(bf16[1024,512]{1,0:T(8,128)(2,1)S(1)} %get-tuple-element.81), channel_id=1, source_target_pairs={{0,3},{1,0},{2,1},{3,2},{4,7},{5,4},{6,5},{7,6},{8,11},{9,8},{10,9... | collective-permute-start | bytes 3145736 | tf_op jit(solution)/shard_map/ppermute | solution.py:160
  22.9 45.2 %collective-permute-start.1 = (bf16[1024,512]{1,0:T(8,128)(2,1)S(1)}, bf16[1024,512]{1,0:T(8,128)(2,1)S(1)}, u32[]{:S(2)}, u32[]{:S(2)}) collective-permute-start(bf16[1024,512]{1,0:T(8,128)(2,1)S(1)} %get-tuple-element.82), channel_id=1, source_target_pairs={{0,2},{1,3},{2,0},{3,1},{4,6},{5,7},{6,4},{7,5},{8,10},{9,11},{10,... | collective-permute-start | bytes 3145736 | tf_op jit(solution)/shard_map/ppermute | solution.py:160
  23.5 48.4 %collective-permute-start = (bf16[1024,512]{1,0:T(8,128)(2,1)S(1)}, bf16[1024,512]{1,0:T(8,128)(2,1)}, u32[]{:S(2)}, u32[]{:S(2)}) collective-permute-start(bf16[1024,512]{1,0:T(8,128)(2,1)S(1)} %get-tuple-element.83), channel_id=1, source_target_pairs={{0,1},{1,2},{2,3},{3,0},{4,5},{5,6},{6,7},{7,4},{8,9},{9,10},{10,1... | collective-permute-start | bytes 3145736 | tf_op jit(solution)/shard_map/ppermute | solution.py:160
  76.0 104.6 %all-to-all-start.1 = ((bf16[64,16,16,128]{3,2,1,0:T(8,128)(2,1)}), bf16[64,16,16,128]{3,2,1,0:T(8,128)(2,1)}, u32[]{:S(2)}, u32[]{:S(2)}) async-start(bf16[64,16,16,128]{3,2,1,0:T(8,128)(2,1)} %bitcast.66), calls=%async_computation.1 | async-start | bytes 8388608 | tf_op jit(solution)/shard_map/all_to_all | solution.py:191
  86.6 8.3 %copy-start.15 = (bf16[1,512,512]{2,1,0:T(8,128)(2,1)S(1)}, bf16[1,512,512]{2,1,0:T(8,128)(2,1)}, u32[]{:S(2)}) copy-start(bf16[1,512,512]{2,1,0:T(8,128)(2,1)} %param.11) | copy-start | bytes 1572868
  90.4 47.6 %collective-permute-start.5 = (bf16[464,1024]{1,0:T(8,128)(2,1)}, bf16[464,1024]{1,0:T(8,128)(2,1)}, u32[]{:S(2)}, u32[]{:S(2)}) collective-permute-start(bf16[464,1024]{1,0:T(8,128)(2,1)} %get-tuple-element.77), channel_id=1, source_target_pairs={{0,192},{64,0},{128,64},{192,128},{1,193},{65,1},{129,65},{193,129... | collective-permute-start | bytes 2850824 | tf_op jit(solution)/shard_map/ppermute | solution.py:160
  93.3 47.1 %collective-permute-start.4 = (bf16[464,1024]{1,0:T(8,128)(2,1)}, bf16[464,1024]{1,0:T(8,128)(2,1)}, u32[]{:S(2)}, u32[]{:S(2)}) collective-permute-start(bf16[464,1024]{1,0:T(8,128)(2,1)} %get-tuple-element.78), channel_id=1, source_target_pairs={{0,128},{64,192},{128,0},{192,64},{1,129},{65,193},{129,1},{193,65... | collective-permute-start | bytes 2850824 | tf_op jit(solution)/shard_map/ppermute | solution.py:160
  93.9 78.6 %collective-permute-start.3 = (bf16[464,1024]{1,0:T(8,128)(2,1)}, bf16[464,1024]{1,0:T(8,128)(2,1)S(1)}, u32[]{:S(2)}, u32[]{:S(2)}) collective-permute-start(bf16[464,1024]{1,0:T(8,128)(2,1)} %get-tuple-element.79), channel_id=1, source_target_pairs={{0,64},{64,128},{128,192},{192,0},{1,65},{65,129},{129,193},{193,1... | collective-permute-start | bytes 2850824 | tf_op jit(solution)/shard_map/ppermute | solution.py:160
  102.3 38.1 %copy-start.3 = (bf16[464,512]{1,0:T(8,128)(2,1)}, bf16[464,512]{1,0:T(8,128)(2,1)S(1)}, u32[]{:S(2)}) copy-start(bf16[464,512]{1,0:T(8,128)(2,1)S(1)} %get-tuple-element.62) | copy-start | bytes 1425412
  186.7 14.9 %collective-permute-start.7 = (bf16[464,512]{1,0:T(8,128)(2,1)S(1)}, bf16[464,512]{1,0:T(8,128)(2,1)S(1)}, u32[]{:S(2)}, u32[]{:S(2)}) collective-permute-start(bf16[464,512]{1,0:T(8,128)(2,1)S(1)} %concatenate.21), channel_id=1, source_target_pairs={{0,64},{64,128},{128,192},{192,0},{1,65},{65,129},{129,193},{193,1... | collective-permute-start | bytes 1425416 | tf_op jit(solution)/shard_map/ppermute | solution.py:160
  188.1 23.0 %collective-permute-start.8 = (bf16[464,512]{1,0:T(8,128)(2,1)S(1)}, bf16[464,512]{1,0:T(8,128)(2,1)S(1)}, u32[]{:S(2)}, u32[]{:S(2)}) collective-permute-start(bf16[464,512]{1,0:T(8,128)(2,1)S(1)} %concatenate.21), channel_id=1, source_target_pairs={{0,192},{64,0},{128,64},{192,128},{1,193},{65,1},{129,65},{193,129... | collective-permute-start | bytes 1425416 | tf_op jit(solution)/shard_map/ppermute | solution.py:160
  190.0 23.1 %collective-permute-start.6 = (bf16[464,512]{1,0:T(8,128)(2,1)S(1)}, bf16[464,512]{1,0:T(8,128)(2,1)S(1)}, u32[]{:S(2)}, u32[]{:S(2)}) collective-permute-start(bf16[464,512]{1,0:T(8,128)(2,1)S(1)} %concatenate.21), channel_id=1, source_target_pairs={{0,128},{64,192},{128,0},{192,64},{1,129},{65,193},{129,1},{193,65... | collective-permute-start | bytes 1425416 | tf_op jit(solution)/shard_map/ppermute | solution.py:160
  192.3 9.3 %copy-start.10 = (bf16[464,512]{1,0:T(8,128)(2,1)S(1)}, bf16[464,512]{1,0:T(8,128)(2,1)}, u32[]{:S(2)}) copy-start(bf16[464,512]{1,0:T(8,128)(2,1)} %copy-done.9) | copy-start | bytes 1425412
  202.1 9.1 %copy-start.2 = (bf16[464,512]{1,0:T(8,128)(2,1)S(1)}, bf16[464,512]{1,0:T(8,128)(2,1)}, u32[]{:S(2)}) copy-start(bf16[464,512]{1,0:T(8,128)(2,1)} %copy-done.1) | copy-start | bytes 1425412
  214.6 7.4 %collective-permute-start.9 = (f32[512,512]{1,0:T(8,128)}, f32[512,512]{1,0:T(8,128)}, u32[]{:S(2)}, u32[]{:S(2)}) collective-permute-start(f32[512,512]{1,0:T(8,128)} %convolution_add_fusion), channel_id=1, source_target_pairs={{0,4},{4,0},{1,5},{5,1},{2,6},{6,2},{3,7},{7,3},{8,12},{12,8},{9,1... | collective-permute-start | bytes 3145736 | tf_op jit(solution)/shard_map/ppermute | solution.py:160
  216.0 29.7 %all-to-all-start.2 = ((bf16[4,464,512]{2,1,0:T(8,128)(2,1)}), bf16[4,464,512]{2,1,0:T(8,128)(2,1)}, u32[]{:S(2)}, u32[]{:S(2)}) async-start(bf16[4,464,512]{2,1,0:T(8,128)(2,1)} %broadcast_in_dim.7), calls=%async_computation.2 | async-start | bytes 3801088 | tf_op jit(solution)/shard_map/all_to_all | solution.py:223
  223.8 24.0 %collective-permute-start.11 = (f32[4,64,256]{2,1,0:T(8,128)S(1)}, f32[4,64,256]{2,1,0:T(8,128)S(1)}, u32[]{:S(2)}, u32[]{:S(2)}) collective-permute-start(f32[4,64,256]{2,1,0:T(8,128)S(1)} %get-tuple-element.88), channel_id=1, source_target_pairs={{8,16},{16,8},{24,32},{32,24},{40,48},{48,40},{0,56},{56,0},{9,17}... | collective-permute-start | bytes 786440 | tf_op jit(solution)/shard_map/ppermute | solution.py:228
  224.1 23.7 %collective-permute-start.10 = (f32[4,64,256]{2,1,0:T(8,128)S(1)}, f32[4,64,256]{2,1,0:T(8,128)S(1)}, u32[]{:S(2)}, u32[]{:S(2)}) collective-permute-start(f32[4,64,256]{2,1,0:T(8,128)S(1)} %get-tuple-element.89), channel_id=1, source_target_pairs={{0,8},{8,0},{16,24},{24,16},{32,40},{40,32},{48,56},{56,48},{1,9},... | collective-permute-start | bytes 786440 | tf_op jit(solution)/shard_map/ppermute | solution.py:227
  247.9 11.0 %copy-start.17 = (bf16[1024,512]{1,0:T(8,128)(2,1)S(1)}, bf16[1024,512]{1,0:T(8,128)(2,1)}, u32[]{:S(2)}) copy-start(bf16[1024,512]{1,0:T(8,128)(2,1)} %copy-done.16) | copy-start | bytes 3145732
  247.9 11.0 %copy-start.19 = (bf16[464,1024]{1,0:T(8,128)(2,1)S(1)}, bf16[464,1024]{1,0:T(8,128)(2,1)}, u32[]{:S(2)}) copy-start(bf16[464,1024]{1,0:T(8,128)(2,1)} %convolution_convert_fusion.3) | copy-start | bytes 2850820
  247.9 13.7 %collective-permute-start.12 = (f32[64,512]{1,0:T(8,128)S(1)}, f32[64,512]{1,0:T(8,128)S(1)}, u32[]{:S(2)}, u32[]{:S(2)}) collective-permute-start(f32[64,512]{1,0:T(8,128)S(1)} %get-tuple-element.85), channel_id=1, source_target_pairs={{0,16},{8,24},{16,32},{24,40},{32,48},{40,56},{48,0},{56,8},{1,17}... | collective-permute-start | bytes 393224 | tf_op jit(solution)/shard_map/ppermute | solution.py:160
  248.2 13.5 %collective-permute-start.14 = (f32[64,512]{1,0:T(8,128)S(1)}, f32[64,512]{1,0:T(8,128)S(1)}, u32[]{:S(2)}, u32[]{:S(2)}) collective-permute-start(f32[64,512]{1,0:T(8,128)S(1)} %get-tuple-element.86), channel_id=1, source_target_pairs={{0,48},{8,56},{16,0},{24,8},{32,16},{40,24},{48,32},{56,40},{1,49}... | collective-permute-start | bytes 393224 | tf_op jit(solution)/shard_map/ppermute | solution.py:160
  252.1 15.7 %collective-permute-start.13 = (f32[64,512]{1,0:T(8,128)S(1)}, f32[64,512]{1,0:T(8,128)S(1)}, u32[]{:S(2)}, u32[]{:S(2)}) collective-permute-start(f32[64,512]{1,0:T(8,128)S(1)} %get-tuple-element.87), channel_id=1, source_target_pairs={{0,32},{8,40},{16,48},{24,56},{32,0},{40,8},{48,16},{56,24},{1,33}... | collective-permute-start | bytes 393224 | tf_op jit(solution)/shard_map/ppermute | solution.py:160
  (14 other events, 35.9 us)

commit v11 on v10

--- a/solution.py
+++ b/solution.py
@@ -207,6 +207,7 @@
     out, dq = attend(q, g, got.reshape(2, heads, tiles, neigh, stretches, TILE, HEAD_DIM))
     dq = jnp.concatenate([jnp.zeros((LEAD - SKIP, width), BF16), dq[:real]], 0)
 
+    groups = [step(dq, "mp", by) if by else dq for by in range(nmp)]
     mine = other = 0.0
     order = sorted(range(nx), key=lambda by: min(by, nx - by))
     for by in order:
@@ -215,22 +216,19 @@
             own = lax.dot_general(dq, fans[0], BOTH_LAST, preferred_element_type=F32).astype(BF16)
             near, own = lax.optimization_barrier((near, own))
         if by == order[-1]:
-            near, mine, _ = lax.optimization_barrier((near, mine, other))
+            near, mine, groups[1], _ = lax.optimization_barrier((near, mine, groups[1], other))
         other += lax.dot_general(share[by][1], near, BOTH_FIRST, preferred_element_type=F32)
         mine += lax.dot_general(share[by][0], near, BOTH_FIRST, preferred_element_type=F32)
     mine += step(other, "core", 1)
-    groups = jnp.broadcast_to(dq[None], (nmp,) + dq.shape)
-    groups = lax.all_to_all(groups, "mp", split_axis=0, concat_axis=0, tiled=True)
     pairs = mine.reshape(nz // 2, 2, -1, width)
     away = lax.dynamic_index_in_dim(pairs, 1 - mz % 2, 1, keepdims=False)
     mine = lax.dynamic_index_in_dim(pairs, mz % 2, 1, keepdims=False)
     up = lax.ppermute(away[..., : width // 2], "z", [(i, i ^ 1) for i in range(nz)])
     down = lax.ppermute(away[..., width // 2 :], "z", [(i, ((i + 1) ^ 1) - 1) for i in range(1, nz - 1)] + [(0, nz - 1), (nz - 1, 0)])
-    parts = [own]
-    for by in range(1, nmp):
-        if by == 2:
-            up, parts, groups = lax.optimization_barrier((up, parts, groups))
-        near = lax.dynamic_index_in_dim(groups, (my - by) % nmp, 0, keepdims=False)
+    parts = [own, lax.dot_general(groups[1], fans[1], BOTH_LAST, preferred_element_type=F32).astype(BF16)]
+    up, parts = lax.optimization_barrier((up, parts))
+    late, _ = lax.optimization_barrier((groups[2:], up))
+    for by, near in enumerate(late, 2):
         parts.append(lax.dot_general(near, fans[by], BOTH_LAST, preferred_element_type=F32).astype(BF16))
     mine += jnp.concatenate([up, down], -1)
     terms = [lax.dynamic_index_in_dim(mine, (mz // 2 + by) % (nz // 2), 0, keepdims=False) for by in range(nz // 2)]

time: 269 us -> 260 us (0.967)
  starting transfers between devices: 52.9 us -> 44.4 us
  waiting for transfers between devices: 158 us -> 163 us
  matrix products: 19.1 us -> 15.5 us
    all_to_all x1 -> x0, waiting for transfers between devices: 18.5 us -> none  [local(): lax.all_to_all(groups, 'mp', split_axis=0, concat_axis=0, tiled=True)]
    ppermute x13 -> x16, waiting for transfers between devices: 134 us -> 151 us  [step(): lax.ppermute(array, axis, [(i, (i + by) % size) for i in range(size)])]
    ppermute x1, waiting for transfers between devices: 0.01 us -> 5.71 us  [local(): lax.ppermute(away[..., :width // 2], 'z', [(i, i ^ 1) for i in range(nz)])]
    dot_general x3 -> x2, matrix products: 5.87 us -> 1.42 us  [local(): lax.dot_general(near, fans[by], BOTH_LAST, preferred_element_type=F32)]
    all_to_all x1 -> x0, starting transfers between devices: 4.42 us -> none  [local(): lax.all_to_all(groups, 'mp', split_axis=0, concat_axis=0, tiled=True)]
    ppermute x13 -> x16, starting transfers between devices: 23 us -> 21.6 us  [step(): lax.ppermute(array, axis, [(i, (i + by) % size) for i in range(size)])]
    unnamed x40 -> x44, local copies, waits for them, and re-layouts: 7.12 us -> 7.1 us
  transfers between devices with their start and end apart: 18 -> 20, of which waited for: 9 -> 10; matrix products, arithmetic and copies ran while one was open for 11% -> 10% of each run, Pallas kernels for 2% -> 2%
where the time goes in v11:
time: 260 us
  waiting for transfers between devices  163 us (63%)
  starting transfers between devices  44.4 us (17%)
  local copies, waits for them, and re-layouts  17 us (7%)
  matrix products  15.5 us (6%)
  Pallas kernels  15 us (6%)
  other arithmetic  3.76 us (1%)
    ppermute x16, waiting for transfers between devices, step(): lax.ppermute(array, axis, [(i, (i + by) % size) for i in range(size)])  151 us
    ppermute x16, starting transfers between devices, step(): lax.ppermute(array, axis, [(i, (i + by) % size) for i in range(size)])  21.6 us
    all_to_all x1, starting transfers between devices, local(): held = lax.all_to_all(message, DP, split_axis=0, concat_axis=0, tiled=True)  11.6 us
    all_to_all x1, starting transfers between devices, local(): lax.all_to_all(send.reshape(ndp, requests, TILE, HEAD_DIM), DP, split_axi...  10.5 us
    unnamed x44, local copies, waits for them, and re-layouts  7.1 us
    all_to_all x1, waiting for transfers between devices, local(): lax.all_to_all(send.reshape(ndp, requests, TILE, HEAD_DIM), DP, split_axi...  5.99 us
    pallas_call x1, Pallas kernels, attend(): pl.pallas_call(functools.partial(attend_kernel, heads=heads), grid=(count...  5.94 us
    dot_general x1, matrix products, local(): q = shifted(jnp.dot(late, weights, preferred_element_type=F32).astype(BF16))  5.79 us
  transfers between devices with their start and end apart: 20, of which 10 were waited for; matrix products, arithmetic and copies ran while one was open for 10% of the time, Pallas kernels for 2%

profile of v11, /device:TPU:32, one launch (start us, length us, event | category | flops | bytes accessed | tf_op | source)
XLA Modules:
  0.0 259.8 jit_solution(4972185820189144538)
XLA Ops:
  1.9 2.8 %cut.1 = bf16[2,4,8,9,16,128]{5,4,3,2,1,0:T(8,128)(2,1)} custom-call(bf16[16,128]{1,0:T(8,128)(2,1)} %add_convert_fusion.1.named_ref, bf16[8,2,128,512]{3,2,1,0:T(8,128)(2,1)} %cache_ref.1), custom_call_target="tpu_custom_call" | custom-call | bytes 4194304 | tf_op jit(solution)/shard_map/cut/pallas_call | solution.py:36
  4.8 11.6 %all-to-all-start = ((bf16[64,9,16,128]{3,2,1,0:T(8,128)(2,1)}), bf16[64,9,16,128]{3,2,1,0:T(8,128)(2,1)S(1)}, u32[]{:S(2)}, u32[]{:S(2)}) async-start(bf16[64,9,16,128]{3,2,1,0:T(8,128)(2,1)} %bitcast.62), calls=%async_computation | async-start | bytes 4718592 | tf_op jit(solution)/shard_map/all_to_all | solution.py:181
  16.4 3.4 %constant_dynamic-slice_fusion = (bf16[1024,512]{1,0:T(8,128)(2,1)S(1)}, bf16[1024,512]{1,0:T(8,128)(2,1)S(1)}, bf16[1024,512]{1,0:T(8,128)(2,1)S(1)}, bf16[1024,512]{1,0:T(8,128)(2,1)}) fusion(bf16[4096,512]{1,0:T(8,128)(2,1)} %param.7, s32[]{:T(128)S(6)} %select_n.115, s32[]{:T(128)S(6)} %select_n.113, s32[]{:T(128)S(6)} %select_n.111, s32[]{:T(128)S(6)} %select_n.109), kind=kLoop, calls=%fused_computation.26 | loop fusion | bytes 8388624 | tf_op jit(solution)/shard_map/dynamic_slice | solution.py:184
  19.8 3.0 %collective-permute-start.2 = (bf16[1024,512]{1,0:T(8,128)(2,1)S(1)}, bf16[1024,512]{1,0:T(8,128)(2,1)S(1)}, u32[]{:S(2)}, u32[]{:S(2)}) collective-permute-start(bf16[1024,512]{1,0:T(8,128)(2,1)S(1)} %get-tuple-element.85), channel_id=1, source_target_pairs={{0,3},{1,0},{2,1},{3,2},{4,7},{5,4},{6,5},{7,6},{8,11},{9,8},{10,9... | collective-permute-start | bytes 3145736 | tf_op jit(solution)/shard_map/ppermute | solution.py:160
  24.5 43.6 %collective-permute-done.2 = bf16[1024,512]{1,0:T(8,128)(2,1)S(1)} collective-permute-done((bf16[1024,512]{1,0:T(8,128)(2,1)S(1)}, bf16[1024,512]{1,0:T(8,128)(2,1)S(1)}, u32[]{:S(2)}, u32[]{:S(2)}) %collective-permute-start.2) | collective-permute-done | bytes 1048608 | tf_op jit(solution)/shard_map/ppermute | solution.py:160
  72.1 1.9 pick.1
  74.0 2.0 copy-done
  76.0 10.5 %all-to-all-start.1 = ((bf16[64,16,16,128]{3,2,1,0:T(8,128)(2,1)}), bf16[64,16,16,128]{3,2,1,0:T(8,128)(2,1)}, u32[]{:S(2)}, u32[]{:S(2)}) async-start(bf16[64,16,16,128]{3,2,1,0:T(8,128)(2,1)} %bitcast.60), calls=%async_computation.1 | async-start | bytes 8388608 | tf_op jit(solution)/shard_map/all_to_all | solution.py:191
  86.6 3.8 %constant_dynamic-slice_fusion.4 = (bf16[464,1024]{1,0:T(8,128)(2,1)}, bf16[464,1024]{1,0:T(8,128)(2,1)}, bf16[464,1024]{1,0:T(8,128)(2,1)}, bf16[464,1024]{1,0:T(8,128)(2,1)S(1)}) fusion(bf16[512,4096]{1,0:T(8,128)(2,1)} %bitcast.65, s32[]{:T(128)S(6)} %select_n.123, s32[]{:T(128)S(6)} %select_n.121, s32[]{:T(128)S(6)} %select_n.119, s32[]{:T(128)S(6)} %select_n.117), kind=kLoop, calls=%fused_computation.30 | loop fusion | bytes 7602192 | tf_op jit(solution)/shard_map/dynamic_slice | solution.py:197
  90.4 2.9 %collective-permute-start.5 = (bf16[464,1024]{1,0:T(8,128)(2,1)}, bf16[464,1024]{1,0:T(8,128)(2,1)}, u32[]{:S(2)}, u32[]{:S(2)}) collective-permute-start(bf16[464,1024]{1,0:T(8,128)(2,1)} %get-tuple-element.81), channel_id=1, source_target_pairs={{0,192},{64,0},{128,64},{192,128},{1,193},{65,1},{129,65},{193,129... | collective-permute-start | bytes 2850824 | tf_op jit(solution)/shard_map/ppermute | solution.py:160
  95.0 5.8 %fusion.11 = bf16[512,512]{1,0:T(8,128)(2,1)S(1)} fusion(bf16[512,4096]{1,0:T(8,128)(2,1)} %bitcast.66, bf16[4096,512]{1,0:T(8,128)(2,1)} %param.7), kind=kOutput, calls=%fused_computation.43 | convolution fusion | flops 2147483648 | bytes 8912896 | tf_op jit(solution)/shard_map/dot_general | solution.py:203
  102.3 35.6 %collective-permute-done.5.share_ref = bf16[464,1024]{1,0:T(8,128)(2,1)} collective-permute-done((bf16[464,1024]{1,0:T(8,128)(2,1)}, bf16[464,1024]{1,0:T(8,128)(2,1)}, u32[]{:S(2)}, u32[]{:S(2)}) %collective-permute-start.5) | collective-permute-done | bytes 950304 | tf_op jit(solution)/shard_map/ppermute | solution.py:160
  142.0 30.5 %collective-permute-done.3.share_ref = bf16[464,1024]{1,0:T(8,128)(2,1)S(1)} collective-permute-done((bf16[464,1024]{1,0:T(8,128)(2,1)}, bf16[464,1024]{1,0:T(8,128)(2,1)S(1)}, u32[]{:S(2)}, u32[]{:S(2)}) %collective-permute-start.3) | collective-permute-done | bytes 950304 | tf_op jit(solution)/shard_map/ppermute | solution.py:160
  174.6 6.0 %all-to-all-done.1 = bf16[64,16,16,128]{3,2,1,0:T(8,128)(2,1)} async-done(((bf16[64,16,16,128]{3,2,1,0:T(8,128)(2,1)}), bf16[64,16,16,128]{3,2,1,0:T(8,128)(2,1)}, u32[]{:S(2)}, u32[]{:S(2)}) %all-to-all-start.1) | async-done | bytes 4194336 | tf_op jit(solution)/shard_map/all_to_all | solution.py:191
  180.6 5.9 %attend.1 = (bf16[512,512]{1,0:T(8,128)(2,1)S(1)}, bf16[512,512]{1,0:T(8,128)(2,1)S(1)}) custom-call(bf16[512,512]{1,0:T(8,128)(2,1)S(1)} %concatenate.18.q_ref, bf16[512,512]{1,0:T(8,128)(2,1)S(1)} %concatenate.19.g_ref, bf16[2,4,8,2,8,16,128]{6,5,4,3,2,1,0:T(8,128)(2,1)} %bitcast.12.kv_ref), custom_call_target="tpu_custom_call" | custom-call | flops 671088640 | bytes 4194304 | tf_op jit(solution)/shard_map/attend/pallas_call | solution.py:112
  186.9 2.9 %collective-permute-start.8 = (bf16[464,512]{1,0:T(8,128)(2,1)S(1)}, bf16[464,512]{1,0:T(8,128)(2,1)S(1)}, u32[]{:S(2)}, u32[]{:S(2)}) collective-permute-start(bf16[464,512]{1,0:T(8,128)(2,1)S(1)} %concatenate.21), channel_id=1, source_target_pairs={{0,192},{64,0},{128,64},{192,128},{1,193},{65,1},{129,65},{193,129... | collective-permute-start | bytes 1425416 | tf_op jit(solution)/shard_map/ppermute | solution.py:160
  189.7 2.2 collective-permute-start.6
  194.6 20.0 %collective-permute-done.7 = bf16[464,512]{1,0:T(8,128)(2,1)S(1)} collective-permute-done((bf16[464,512]{1,0:T(8,128)(2,1)S(1)}, bf16[464,512]{1,0:T(8,128)(2,1)S(1)}, u32[]{:S(2)}, u32[]{:S(2)}) %collective-permute-start.7) | collective-permute-done | bytes 475168 | tf_op jit(solution)/shard_map/ppermute | solution.py:160
  218.1 2.9 %collective-permute-start.12 = (bf16[464,512]{1,0:T(8,128)(2,1)S(1)}, bf16[464,512]{1,0:T(8,128)(2,1)S(1)}, u32[]{:S(2)}, u32[]{:S(2)}) collective-permute-start(bf16[464,512]{1,0:T(8,128)(2,1)S(1)} %concatenate.21), channel_id=1, source_target_pairs={{0,2},{1,3},{2,0},{3,1},{4,6},{5,7},{6,4},{7,5},{8,10},{9,11},{10,... | collective-permute-start | bytes 1425416 | tf_op jit(solution)/shard_map/ppermute | solution.py:160
  225.1 1.9 convolution_convert_fusion.2
  227.0 5.7 %collective-permute-done.11 = f32[4,64,256]{2,1,0:T(8,128)S(1)} collective-permute-done((f32[4,64,256]{2,1,0:T(8,128)S(1)}, f32[4,64,256]{2,1,0:T(8,128)S(1)}, u32[]{:S(2)}, u32[]{:S(2)}) %collective-permute-start.11) | collective-permute-done | bytes 262176 | tf_op jit(solution)/shard_map/ppermute | solution.py:226
  232.9 10.4 %collective-permute-done.13 = bf16[464,512]{1,0:T(8,128)(2,1)S(1)} collective-permute-done((bf16[464,512]{1,0:T(8,128)(2,1)S(1)}, bf16[464,512]{1,0:T(8,128)(2,1)S(1)}, u32[]{:S(2)}, u32[]{:S(2)}) %collective-permute-start.13) | collective-permute-done | bytes 475168 | tf_op jit(solution)/shard_map/ppermute | solution.py:160
  243.7 4.0 %collective-permute-start.17 = (f32[64,512]{1,0:T(8,128)S(1)}, f32[64,512]{1,0:T(8,128)S(1)}, u32[]{:S(2)}, u32[]{:S(2)}) collective-permute-start(f32[64,512]{1,0:T(8,128)S(1)} %get-tuple-element.90), channel_id=1, source_target_pairs={{0,48},{8,56},{16,0},{24,8},{32,16},{40,24},{48,32},{56,40},{1,49}... | collective-permute-start | bytes 393224 | tf_op jit(solution)/shard_map/ppermute | solution.py:160
  250.1 9.0 %collective-permute-done.15 = f32[64,512]{1,0:T(8,128)S(1)} collective-permute-done((f32[64,512]{1,0:T(8,128)S(1)}, f32[64,512]{1,0:T(8,128)S(1)}, u32[]{:S(2)}, u32[]{:S(2)}) %collective-permute-start.15) | collective-permute-done | bytes 131104 | tf_op jit(solution)/shard_map/ppermute | solution.py:160
  (101 shorter events, 30.2 us)
Async XLA Ops:
  4.8 67.1 %all-to-all-start = ((bf16[64,9,16,128]{3,2,1,0:T(8,128)(2,1)}), bf16[64,9,16,128]{3,2,1,0:T(8,128)(2,1)S(1)}, u32[]{:S(2)}, u32[]{:S(2)}) async-start(bf16[64,9,16,128]{3,2,1,0:T(8,128)(2,1)} %bitcast.62), calls=%async_computation | async-start | bytes 4718592 | tf_op jit(solution)/shard_map/all_to_all | solution.py:181
  19.8 48.2 %collective-permute-start.2 = (bf16[1024,512]{1,0:T(8,128)(2,1)S(1)}, bf16[1024,512]{1,0:T(8,128)(2,1)S(1)}, u32[]{:S(2)}, u32[]{:S(2)}) collective-permute-start(bf16[1024,512]{1,0:T(8,128)(2,1)S(1)} %get-tuple-element.85), channel_id=1, source_target_pairs={{0,3},{1,0},{2,1},{3,2},{4,7},{5,4},{6,5},{7,6},{8,11},{9,8},{10,9... | collective-permute-start | bytes 3145736 | tf_op jit(solution)/shard_map/ppermute | solution.py:160
  22.8 45.2 %collective-permute-start.1 = (bf16[1024,512]{1,0:T(8,128)(2,1)S(1)}, bf16[1024,512]{1,0:T(8,128)(2,1)S(1)}, u32[]{:S(2)}, u32[]{:S(2)}) collective-permute-start(bf16[1024,512]{1,0:T(8,128)(2,1)S(1)} %get-tuple-element.86), channel_id=1, source_target_pairs={{0,2},{1,3},{2,0},{3,1},{4,6},{5,7},{6,4},{7,5},{8,10},{9,11},{10,... | collective-permute-start | bytes 3145736 | tf_op jit(solution)/shard_map/ppermute | solution.py:160
  23.5 48.4 %collective-permute-start = (bf16[1024,512]{1,0:T(8,128)(2,1)S(1)}, bf16[1024,512]{1,0:T(8,128)(2,1)}, u32[]{:S(2)}, u32[]{:S(2)}) collective-permute-start(bf16[1024,512]{1,0:T(8,128)(2,1)S(1)} %get-tuple-element.87), channel_id=1, source_target_pairs={{0,1},{1,2},{2,3},{3,0},{4,5},{5,6},{6,7},{7,4},{8,9},{9,10},{10,1... | collective-permute-start | bytes 3145736 | tf_op jit(solution)/shard_map/ppermute | solution.py:160
  76.0 104.6 %all-to-all-start.1 = ((bf16[64,16,16,128]{3,2,1,0:T(8,128)(2,1)}), bf16[64,16,16,128]{3,2,1,0:T(8,128)(2,1)}, u32[]{:S(2)}, u32[]{:S(2)}) async-start(bf16[64,16,16,128]{3,2,1,0:T(8,128)(2,1)} %bitcast.60), calls=%async_computation.1 | async-start | bytes 8388608 | tf_op jit(solution)/shard_map/all_to_all | solution.py:191
  90.4 47.5 %collective-permute-start.5 = (bf16[464,1024]{1,0:T(8,128)(2,1)}, bf16[464,1024]{1,0:T(8,128)(2,1)}, u32[]{:S(2)}, u32[]{:S(2)}) collective-permute-start(bf16[464,1024]{1,0:T(8,128)(2,1)} %get-tuple-element.81), channel_id=1, source_target_pairs={{0,192},{64,0},{128,64},{192,128},{1,193},{65,1},{129,65},{193,129... | collective-permute-start | bytes 2850824 | tf_op jit(solution)/shard_map/ppermute | solution.py:160
  93.3 47.1 %collective-permute-start.4 = (bf16[464,1024]{1,0:T(8,128)(2,1)}, bf16[464,1024]{1,0:T(8,128)(2,1)}, u32[]{:S(2)}, u32[]{:S(2)}) collective-permute-start(bf16[464,1024]{1,0:T(8,128)(2,1)} %get-tuple-element.82), channel_id=1, source_target_pairs={{0,128},{64,192},{128,0},{192,64},{1,129},{65,193},{129,1},{193,65... | collective-permute-start | bytes 2850824 | tf_op jit(solution)/shard_map/ppermute | solution.py:160
  93.9 78.6 %collective-permute-start.3 = (bf16[464,1024]{1,0:T(8,128)(2,1)}, bf16[464,1024]{1,0:T(8,128)(2,1)S(1)}, u32[]{:S(2)}, u32[]{:S(2)}) collective-permute-start(bf16[464,1024]{1,0:T(8,128)(2,1)} %get-tuple-element.83), channel_id=1, source_target_pairs={{0,64},{64,128},{128,192},{192,0},{1,65},{65,129},{129,193},{193,1... | collective-permute-start | bytes 2850824 | tf_op jit(solution)/shard_map/ppermute | solution.py:160
  102.3 38.1 %copy-start.3 = (bf16[464,512]{1,0:T(8,128)(2,1)}, bf16[464,512]{1,0:T(8,128)(2,1)S(1)}, u32[]{:S(2)}) copy-start(bf16[464,512]{1,0:T(8,128)(2,1)S(1)} %get-tuple-element.64) | copy-start | bytes 1425412
  186.8 29.8 %collective-permute-start.9 = (bf16[464,512]{1,0:T(8,128)(2,1)S(1)}, bf16[464,512]{1,0:T(8,128)(2,1)S(1)}, u32[]{:S(2)}, u32[]{:S(2)}) collective-permute-start(bf16[464,512]{1,0:T(8,128)(2,1)S(1)} %concatenate.21), channel_id=1, source_target_pairs={{0,1},{1,2},{2,3},{3,0},{4,5},{5,6},{6,7},{7,4},{8,9},{9,10},{10,1... | collective-permute-start | bytes 1425416 | tf_op jit(solution)/shard_map/ppermute | solution.py:160
  186.9 28.7 %collective-permute-start.8 = (bf16[464,512]{1,0:T(8,128)(2,1)S(1)}, bf16[464,512]{1,0:T(8,128)(2,1)S(1)}, u32[]{:S(2)}, u32[]{:S(2)}) collective-permute-start(bf16[464,512]{1,0:T(8,128)(2,1)S(1)} %concatenate.21), channel_id=1, source_target_pairs={{0,192},{64,0},{128,64},{192,128},{1,193},{65,1},{129,65},{193,129... | collective-permute-start | bytes 1425416 | tf_op jit(solution)/shard_map/ppermute | solution.py:160
  189.7 24.9 %collective-permute-start.7 = (bf16[464,512]{1,0:T(8,128)(2,1)S(1)}, bf16[464,512]{1,0:T(8,128)(2,1)S(1)}, u32[]{:S(2)}, u32[]{:S(2)}) collective-permute-start(bf16[464,512]{1,0:T(8,128)(2,1)S(1)} %concatenate.21), channel_id=1, source_target_pairs={{0,64},{64,128},{128,192},{192,0},{1,65},{65,129},{129,193},{193,1... | collective-permute-start | bytes 1425416 | tf_op jit(solution)/shard_map/ppermute | solution.py:160
  189.7 26.9 %collective-permute-start.6 = (bf16[464,512]{1,0:T(8,128)(2,1)S(1)}, bf16[464,512]{1,0:T(8,128)(2,1)S(1)}, u32[]{:S(2)}, u32[]{:S(2)}) collective-permute-start(bf16[464,512]{1,0:T(8,128)(2,1)S(1)} %concatenate.21), channel_id=1, source_target_pairs={{0,128},{64,192},{128,0},{192,64},{1,129},{65,193},{129,1},{193,65... | collective-permute-start | bytes 1425416 | tf_op jit(solution)/shard_map/ppermute | solution.py:160
  192.4 22.2 %copy-start.10 = (bf16[464,512]{1,0:T(8,128)(2,1)S(1)}, bf16[464,512]{1,0:T(8,128)(2,1)}, u32[]{:S(2)}) copy-start(bf16[464,512]{1,0:T(8,128)(2,1)} %copy-done.9) | copy-start | bytes 1425412
  192.9 22.2 %copy-start.8 = (bf16[464,512]{1,0:T(8,128)(2,1)S(1)}, bf16[464,512]{1,0:T(8,128)(2,1)}, u32[]{:S(2)}) copy-start(bf16[464,512]{1,0:T(8,128)(2,1)} %copy-done.7) | copy-start | bytes 1425412
  218.1 4.6 %collective-permute-start.10 = (f32[512,512]{1,0:T(8,128)}, f32[512,512]{1,0:T(8,128)}, u32[]{:S(2)}, u32[]{:S(2)}) collective-permute-start(f32[512,512]{1,0:T(8,128)} %convolution_add_fusion), channel_id=1, source_target_pairs={{0,4},{4,0},{1,5},{5,1},{2,6},{6,2},{3,7},{7,3},{8,12},{12,8},{9,1... | collective-permute-start | bytes 3145736 | tf_op jit(solution)/shard_map/ppermute | solution.py:160
  218.1 14.8 %collective-permute-start.12 = (bf16[464,512]{1,0:T(8,128)(2,1)S(1)}, bf16[464,512]{1,0:T(8,128)(2,1)S(1)}, u32[]{:S(2)}, u32[]{:S(2)}) collective-permute-start(bf16[464,512]{1,0:T(8,128)(2,1)S(1)} %concatenate.21), channel_id=1, source_target_pairs={{0,2},{1,3},{2,0},{3,1},{4,6},{5,7},{6,4},{7,5},{8,10},{9,11},{10,... | collective-permute-start | bytes 1425416 | tf_op jit(solution)/shard_map/ppermute | solution.py:160
  221.0 22.3 %collective-permute-start.13 = (bf16[464,512]{1,0:T(8,128)(2,1)S(1)}, bf16[464,512]{1,0:T(8,128)(2,1)S(1)}, u32[]{:S(2)}, u32[]{:S(2)}) collective-permute-start(bf16[464,512]{1,0:T(8,128)(2,1)S(1)} %concatenate.21), channel_id=1, source_target_pairs={{0,3},{1,0},{2,1},{3,2},{4,7},{5,4},{6,5},{7,6},{8,11},{9,8},{10,9... | collective-permute-start | bytes 1425416 | tf_op jit(solution)/shard_map/ppermute | solution.py:160
  224.4 18.9 %collective-permute-start.14 = (f32[4,64,256]{2,1,0:T(8,128)S(1)}, f32[4,64,256]{2,1,0:T(8,128)S(1)}, u32[]{:S(2)}, u32[]{:S(2)}) collective-permute-start(f32[4,64,256]{2,1,0:T(8,128)S(1)} %get-tuple-element.92), channel_id=1, source_target_pairs={{8,16},{16,8},{24,32},{32,24},{40,48},{48,40},{0,56},{56,0},{9,17}... | collective-permute-start | bytes 786440 | tf_op jit(solution)/shard_map/ppermute | solution.py:227
  224.5 23.1 %copy-start.18 = (bf16[1024,512]{1,0:T(8,128)(2,1)S(1)}, bf16[1024,512]{1,0:T(8,128)(2,1)}, u32[]{:S(2)}) copy-start(bf16[1024,512]{1,0:T(8,128)(2,1)} %copy-done.17) | copy-start | bytes 3145732
  224.5 8.2 %collective-permute-start.11 = (f32[4,64,256]{2,1,0:T(8,128)S(1)}, f32[4,64,256]{2,1,0:T(8,128)S(1)}, u32[]{:S(2)}, u32[]{:S(2)}) collective-permute-start(f32[4,64,256]{2,1,0:T(8,128)S(1)} %get-tuple-element.93), channel_id=1, source_target_pairs={{0,8},{8,0},{16,24},{24,16},{32,40},{40,32},{48,56},{56,48},{1,9},... | collective-permute-start | bytes 786440 | tf_op jit(solution)/shard_map/ppermute | solution.py:226
  243.4 15.7 %collective-permute-start.15 = (f32[64,512]{1,0:T(8,128)S(1)}, f32[64,512]{1,0:T(8,128)S(1)}, u32[]{:S(2)}, u32[]{:S(2)}) collective-permute-start(f32[64,512]{1,0:T(8,128)S(1)} %get-tuple-element.89), channel_id=1, source_target_pairs={{0,16},{8,24},{16,32},{24,40},{32,48},{40,56},{48,0},{56,8},{1,17}... | collective-permute-start | bytes 393224 | tf_op jit(solution)/shard_map/ppermute | solution.py:160
  243.7 15.5 %collective-permute-start.17 = (f32[64,512]{1,0:T(8,128)S(1)}, f32[64,512]{1,0:T(8,128)S(1)}, u32[]{:S(2)}, u32[]{:S(2)}) collective-permute-start(f32[64,512]{1,0:T(8,128)S(1)} %get-tuple-element.90), channel_id=1, source_target_pairs={{0,48},{8,56},{16,0},{24,8},{32,16},{40,24},{48,32},{56,40},{1,49}... | collective-permute-start | bytes 393224 | tf_op jit(solution)/shard_map/ppermute | solution.py:160
  247.6 11.5 %collective-permute-start.16 = (f32[64,512]{1,0:T(8,128)S(1)}, f32[64,512]{1,0:T(8,128)S(1)}, u32[]{:S(2)}, u32[]{:S(2)}) collective-permute-start(f32[64,512]{1,0:T(8,128)S(1)} %get-tuple-element.91), channel_id=1, source_target_pairs={{0,32},{8,40},{16,48},{24,56},{32,0},{40,8},{48,16},{56,24},{1,33}... | collective-permute-start | bytes 393224 | tf_op jit(solution)/shard_map/ppermute | solution.py:160
  (18 other events, 117.2 us)

commit v12 on v11

--- a/solution.py
+++ b/solution.py
@@ -227,12 +227,13 @@
     down = lax.ppermute(away[..., width // 2 :], "z", [(i, ((i + 1) ^ 1) - 1) for i in range(1, nz - 1)] + [(0, nz - 1), (nz - 1, 0)])
     parts = [own, lax.dot_general(groups[1], fans[1], BOTH_LAST, preferred_element_type=F32).astype(BF16)]
     up, parts = lax.optimization_barrier((up, parts))
-    late, _ = lax.optimization_barrier((groups[2:], up))
+    mine += jnp.concatenate([up, down], -1)
+    terms = [lax.dynamic_index_in_dim(mine, (mz // 2 + by) % (nz // 2), 0, keepdims=False) for by in range(nz // 2)]
+    terms = [step(a, "z", 2 * by) if by else a for by, a in enumerate(terms)]
+    late, _ = lax.optimization_barrier((groups[2:], terms[1]))
     for by, near in enumerate(late, 2):
         parts.append(lax.dot_general(near, fans[by], BOTH_LAST, preferred_element_type=F32).astype(BF16))
-    mine += jnp.concatenate([up, down], -1)
-    terms = [lax.dynamic_index_in_dim(mine, (mz // 2 + by) % (nz // 2), 0, keepdims=False) for by in range(nz // 2)]
-    query_grad = sum(step(a, "z", 2 * by) if by else a for by, a in enumerate(terms))
+    query_grad = sum(terms)
     part = sum(a.astype(F32) for a in parts).astype(BF16)
     attended = jnp.concatenate([jnp.zeros((LEAD, width), BF16), out[:real]], 0)
     input_grad = jnp.concatenate([jnp.zeros((SKIP, d // nmp), BF16), part], 0)

time: 260 us -> 254 us (0.977); the launches traced: 260 us -> 249 us
  waiting for transfers between devices: 163 us -> 147 us
  matrix products: 15.5 us -> 18.9 us
    ppermute x16, waiting for transfers between devices: 151 us -> 136 us  [step(): lax.ppermute(array, axis, [(i, (i + by) % size) for i in range(size)])]
  transfers between devices with their start and end apart: 20 -> 20, of which waited for: 10 -> 9; matrix products, arithmetic and copies ran while one was open for 10% -> 12% of each run, Pallas kernels for 2% -> 2%
where the time goes in v12:
time: 254 us; the launch traced here: 249 us
  waiting for transfers between devices  147 us (58%)
  starting transfers between devices  46.1 us (18%)
  matrix products  18.9 us (7%)
  local copies, waits for them, and re-layouts  17 us (7%)
  Pallas kernels  15 us (6%)
  other arithmetic  3.76 us (1%)
    ppermute x16, waiting for transfers between devices, step(): lax.ppermute(array, axis, [(i, (i + by) % size) for i in range(size)])  136 us
    ppermute x16, starting transfers between devices, step(): lax.ppermute(array, axis, [(i, (i + by) % size) for i in range(size)])  23.2 us
    all_to_all x1, starting transfers between devices, local(): held = lax.all_to_all(message, DP, split_axis=0, concat_axis=0, tiled=True)  11.6 us
    all_to_all x1, starting transfers between devices, local(): lax.all_to_all(send.reshape(ndp, requests, TILE, HEAD_DIM), DP, split_axi...  10.5 us
    unnamed x44, local copies, waits for them, and re-layouts  7.1 us
    all_to_all x1, waiting for transfers between devices, local(): lax.all_to_all(send.reshape(ndp, requests, TILE, HEAD_DIM), DP, split_axi...  5.99 us
    pallas_call x1, Pallas kernels, attend(): pl.pallas_call(functools.partial(attend_kernel, heads=heads), grid=(count...  5.94 us
    dot_general x1, matrix products, local(): q = shifted(jnp.dot(late, weights, preferred_element_type=F32).astype(BF16))  5.79 us
  transfers between devices with their start and end apart: 20, of which 9 were waited for; matrix products, arithmetic and copies ran while one was open for 12% of the time, Pallas kernels for 2%

profile of v12, /device:TPU:32, one launch (start us, length us, event | category | flops | bytes accessed | tf_op | source)
XLA Modules:
  0.0 249.0 jit_solution(3989817540274986659)
XLA Ops:
  1.9 2.8 %cut.1 = bf16[2,4,8,9,16,128]{5,4,3,2,1,0:T(8,128)(2,1)} custom-call(bf16[16,128]{1,0:T(8,128)(2,1)} %add_convert_fusion.1.named_ref, bf16[8,2,128,512]{3,2,1,0:T(8,128)(2,1)} %cache_ref.1), custom_call_target="tpu_custom_call" | custom-call | bytes 4194304 | tf_op jit(solution)/shard_map/cut/pallas_call | solution.py:36
  4.8 11.6 %all-to-all-start = ((bf16[64,9,16,128]{3,2,1,0:T(8,128)(2,1)}), bf16[64,9,16,128]{3,2,1,0:T(8,128)(2,1)S(1)}, u32[]{:S(2)}, u32[]{:S(2)}) async-start(bf16[64,9,16,128]{3,2,1,0:T(8,128)(2,1)} %bitcast.62), calls=%async_computation | async-start | bytes 4718592 | tf_op jit(solution)/shard_map/all_to_all | solution.py:181
  16.4 3.4 %constant_dynamic-slice_fusion = (bf16[1024,512]{1,0:T(8,128)(2,1)S(1)}, bf16[1024,512]{1,0:T(8,128)(2,1)S(1)}, bf16[1024,512]{1,0:T(8,128)(2,1)S(1)}, bf16[1024,512]{1,0:T(8,128)(2,1)}) fusion(bf16[4096,512]{1,0:T(8,128)(2,1)} %param.7, s32[]{:T(128)S(6)} %select_n.115, s32[]{:T(128)S(6)} %select_n.113, s32[]{:T(128)S(6)} %select_n.111, s32[]{:T(128)S(6)} %select_n.109), kind=kLoop, calls=%fused_computation.26 | loop fusion | bytes 8388624 | tf_op jit(solution)/shard_map/dynamic_slice | solution.py:184
  19.8 3.0 %collective-permute-start.2 = (bf16[1024,512]{1,0:T(8,128)(2,1)S(1)}, bf16[1024,512]{1,0:T(8,128)(2,1)S(1)}, u32[]{:S(2)}, u32[]{:S(2)}) collective-permute-start(bf16[1024,512]{1,0:T(8,128)(2,1)S(1)} %get-tuple-element.85), channel_id=1, source_target_pairs={{0,3},{1,0},{2,1},{3,2},{4,7},{5,4},{6,5},{7,6},{8,11},{9,8},{10,9... | collective-permute-start | bytes 3145736 | tf_op jit(solution)/shard_map/ppermute | solution.py:160
  24.5 43.6 %collective-permute-done.2 = bf16[1024,512]{1,0:T(8,128)(2,1)S(1)} collective-permute-done((bf16[1024,512]{1,0:T(8,128)(2,1)S(1)}, bf16[1024,512]{1,0:T(8,128)(2,1)S(1)}, u32[]{:S(2)}, u32[]{:S(2)}) %collective-permute-start.2) | collective-permute-done | bytes 1048608 | tf_op jit(solution)/shard_map/ppermute | solution.py:160
  74.0 2.0 copy-done
  76.0 10.5 %all-to-all-start.1 = ((bf16[64,16,16,128]{3,2,1,0:T(8,128)(2,1)}), bf16[64,16,16,128]{3,2,1,0:T(8,128)(2,1)}, u32[]{:S(2)}, u32[]{:S(2)}) async-start(bf16[64,16,16,128]{3,2,1,0:T(8,128)(2,1)} %bitcast.60), calls=%async_computation.1 | async-start | bytes 8388608 | tf_op jit(solution)/shard_map/all_to_all | solution.py:191
  86.6 3.8 %constant_dynamic-slice_fusion.4 = (bf16[464,1024]{1,0:T(8,128)(2,1)}, bf16[464,1024]{1,0:T(8,128)(2,1)}, bf16[464,1024]{1,0:T(8,128)(2,1)}, bf16[464,1024]{1,0:T(8,128)(2,1)S(1)}) fusion(bf16[512,4096]{1,0:T(8,128)(2,1)} %bitcast.65, s32[]{:T(128)S(6)} %select_n.123, s32[]{:T(128)S(6)} %select_n.121, s32[]{:T(128)S(6)} %select_n.119, s32[]{:T(128)S(6)} %select_n.117), kind=kLoop, calls=%fused_computation.30 | loop fusion | bytes 7602192 | tf_op jit(solution)/shard_map/dynamic_slice | solution.py:197
  90.4 2.9 %collective-permute-start.5 = (bf16[464,1024]{1,0:T(8,128)(2,1)}, bf16[464,1024]{1,0:T(8,128)(2,1)}, u32[]{:S(2)}, u32[]{:S(2)}) collective-permute-start(bf16[464,1024]{1,0:T(8,128)(2,1)} %get-tuple-element.81), channel_id=1, source_target_pairs={{0,192},{64,0},{128,64},{192,128},{1,193},{65,1},{129,65},{193,129... | collective-permute-start | bytes 2850824 | tf_op jit(solution)/shard_map/ppermute | solution.py:160
  95.0 5.8 %fusion.11 = bf16[512,512]{1,0:T(8,128)(2,1)S(1)} fusion(bf16[512,4096]{1,0:T(8,128)(2,1)} %bitcast.66, bf16[4096,512]{1,0:T(8,128)(2,1)} %param.7), kind=kOutput, calls=%fused_computation.43 | convolution fusion | flops 2147483648 | bytes 8912896 | tf_op jit(solution)/shard_map/dot_general | solution.py:203
  102.3 35.6 %collective-permute-done.5.share_ref = bf16[464,1024]{1,0:T(8,128)(2,1)} collective-permute-done((bf16[464,1024]{1,0:T(8,128)(2,1)}, bf16[464,1024]{1,0:T(8,128)(2,1)}, u32[]{:S(2)}, u32[]{:S(2)}) %collective-permute-start.5) | collective-permute-done | bytes 950304 | tf_op jit(solution)/shard_map/ppermute | solution.py:160
  142.0 30.5 %collective-permute-done.3.share_ref = bf16[464,1024]{1,0:T(8,128)(2,1)S(1)} collective-permute-done((bf16[464,1024]{1,0:T(8,128)(2,1)}, bf16[464,1024]{1,0:T(8,128)(2,1)S(1)}, u32[]{:S(2)}, u32[]{:S(2)}) %collective-permute-start.3) | collective-permute-done | bytes 950304 | tf_op jit(solution)/shard_map/ppermute | solution.py:160
  174.6 6.0 %all-to-all-done.1 = bf16[64,16,16,128]{3,2,1,0:T(8,128)(2,1)} async-done(((bf16[64,16,16,128]{3,2,1,0:T(8,128)(2,1)}), bf16[64,16,16,128]{3,2,1,0:T(8,128)(2,1)}, u32[]{:S(2)}, u32[]{:S(2)}) %all-to-all-start.1) | async-done | bytes 4194336 | tf_op jit(solution)/shard_map/all_to_all | solution.py:191
  180.6 5.9 %attend.1 = (bf16[512,512]{1,0:T(8,128)(2,1)S(1)}, bf16[512,512]{1,0:T(8,128)(2,1)S(1)}) custom-call(bf16[512,512]{1,0:T(8,128)(2,1)S(1)} %concatenate.18.q_ref, bf16[512,512]{1,0:T(8,128)(2,1)S(1)} %concatenate.19.g_ref, bf16[2,4,8,2,8,16,128]{6,5,4,3,2,1,0:T(8,128)(2,1)} %bitcast.12.kv_ref), custom_call_target="tpu_custom_call" | custom-call | flops 671088640 | bytes 4194304 | tf_op jit(solution)/shard_map/attend/pallas_call | solution.py:112
  186.9 2.9 %collective-permute-start.8 = (bf16[464,512]{1,0:T(8,128)(2,1)S(1)}, bf16[464,512]{1,0:T(8,128)(2,1)S(1)}, u32[]{:S(2)}, u32[]{:S(2)}) collective-permute-start(bf16[464,512]{1,0:T(8,128)(2,1)S(1)} %concatenate.21), channel_id=1, source_target_pairs={{0,192},{64,0},{128,64},{192,128},{1,193},{65,1},{129,65},{193,129... | collective-permute-start | bytes 1425416 | tf_op jit(solution)/shard_map/ppermute | solution.py:160
  189.7 2.2 collective-permute-start.6
  194.6 20.0 %collective-permute-done.7 = bf16[464,512]{1,0:T(8,128)(2,1)S(1)} collective-permute-done((bf16[464,512]{1,0:T(8,128)(2,1)S(1)}, bf16[464,512]{1,0:T(8,128)(2,1)S(1)}, u32[]{:S(2)}, u32[]{:S(2)}) %collective-permute-start.7) | collective-permute-done | bytes 475168 | tf_op jit(solution)/shard_map/ppermute | solution.py:160
  218.1 2.9 %collective-permute-start.12 = (bf16[464,512]{1,0:T(8,128)(2,1)S(1)}, bf16[464,512]{1,0:T(8,128)(2,1)}, u32[]{:S(2)}, u32[]{:S(2)}) collective-permute-start(bf16[464,512]{1,0:T(8,128)(2,1)S(1)} %concatenate.21), channel_id=1, source_target_pairs={{0,2},{1,3},{2,0},{3,1},{4,6},{5,7},{6,4},{7,5},{8,10},{9,11},{10,... | collective-permute-start | bytes 1425416 | tf_op jit(solution)/shard_map/ppermute | solution.py:160
  224.3 2.9 %convolution_convert_fusion.2 = bf16[464,1024]{1,0:T(8,128)(2,1)} fusion(bf16[464,512]{1,0:T(8,128)(2,1)S(1)} %copy-done.19, bf16[1024,512]{1,0:T(8,128)(2,1)} %collective-permute-done), kind=kOutput, calls=%fused_computation.3 | convolution fusion | flops 487014400 | bytes 2473984 | tf_op jit(solution)/shard_map/dot_general | solution.py:228
  227.1 4.6 %collective-permute-done.11 = f32[4,64,256]{2,1,0:T(8,128)S(1)} collective-permute-done((f32[4,64,256]{2,1,0:T(8,128)S(1)}, f32[4,64,256]{2,1,0:T(8,128)S(1)}, u32[]{:S(2)}, u32[]{:S(2)}) %collective-permute-start.11) | collective-permute-done | bytes 262176 | tf_op jit(solution)/shard_map/ppermute | solution.py:226
  232.1 2.1 collective-permute-start.15
  235.2 2.7 %collective-permute-start.16 = (f32[64,512]{1,0:T(8,128)S(1)}, f32[64,512]{1,0:T(8,128)S(1)}, u32[]{:S(2)}, u32[]{:S(2)}) collective-permute-start(f32[64,512]{1,0:T(8,128)S(1)} %get-tuple-element.89), channel_id=1, source_target_pairs={{0,32},{8,40},{16,48},{24,56},{32,0},{40,8},{48,16},{56,24},{1,33}... | collective-permute-start | bytes 393224 | tf_op jit(solution)/shard_map/ppermute | solution.py:160
  238.8 4.6 %collective-permute-done.13 = bf16[464,512]{1,0:T(8,128)(2,1)} collective-permute-done((bf16[464,512]{1,0:T(8,128)(2,1)S(1)}, bf16[464,512]{1,0:T(8,128)(2,1)}, u32[]{:S(2)}, u32[]{:S(2)}) %collective-permute-start.13) | collective-permute-done | bytes 475168 | tf_op jit(solution)/shard_map/ppermute | solution.py:160
  243.4 2.1 convolution_convert_fusion.1
  (101 shorter events, 33.4 us)
Async XLA Ops:
  4.8 67.1 %all-to-all-start = ((bf16[64,9,16,128]{3,2,1,0:T(8,128)(2,1)}), bf16[64,9,16,128]{3,2,1,0:T(8,128)(2,1)S(1)}, u32[]{:S(2)}, u32[]{:S(2)}) async-start(bf16[64,9,16,128]{3,2,1,0:T(8,128)(2,1)} %bitcast.62), calls=%async_computation | async-start | bytes 4718592 | tf_op jit(solution)/shard_map/all_to_all | solution.py:181
  19.8 48.2 %collective-permute-start.2 = (bf16[1024,512]{1,0:T(8,128)(2,1)S(1)}, bf16[1024,512]{1,0:T(8,128)(2,1)S(1)}, u32[]{:S(2)}, u32[]{:S(2)}) collective-permute-start(bf16[1024,512]{1,0:T(8,128)(2,1)S(1)} %get-tuple-element.85), channel_id=1, source_target_pairs={{0,3},{1,0},{2,1},{3,2},{4,7},{5,4},{6,5},{7,6},{8,11},{9,8},{10,9... | collective-permute-start | bytes 3145736 | tf_op jit(solution)/shard_map/ppermute | solution.py:160
  22.8 45.2 %collective-permute-start.1 = (bf16[1024,512]{1,0:T(8,128)(2,1)S(1)}, bf16[1024,512]{1,0:T(8,128)(2,1)S(1)}, u32[]{:S(2)}, u32[]{:S(2)}) collective-permute-start(bf16[1024,512]{1,0:T(8,128)(2,1)S(1)} %get-tuple-element.86), channel_id=1, source_target_pairs={{0,2},{1,3},{2,0},{3,1},{4,6},{5,7},{6,4},{7,5},{8,10},{9,11},{10,... | collective-permute-start | bytes 3145736 | tf_op jit(solution)/shard_map/ppermute | solution.py:160
  23.5 48.4 %collective-permute-start = (bf16[1024,512]{1,0:T(8,128)(2,1)S(1)}, bf16[1024,512]{1,0:T(8,128)(2,1)}, u32[]{:S(2)}, u32[]{:S(2)}) collective-permute-start(bf16[1024,512]{1,0:T(8,128)(2,1)S(1)} %get-tuple-element.87), channel_id=1, source_target_pairs={{0,1},{1,2},{2,3},{3,0},{4,5},{5,6},{6,7},{7,4},{8,9},{9,10},{10,1... | collective-permute-start | bytes 3145736 | tf_op jit(solution)/shard_map/ppermute | solution.py:160
  76.0 104.6 %all-to-all-start.1 = ((bf16[64,16,16,128]{3,2,1,0:T(8,128)(2,1)}), bf16[64,16,16,128]{3,2,1,0:T(8,128)(2,1)}, u32[]{:S(2)}, u32[]{:S(2)}) async-start(bf16[64,16,16,128]{3,2,1,0:T(8,128)(2,1)} %bitcast.60), calls=%async_computation.1 | async-start | bytes 8388608 | tf_op jit(solution)/shard_map/all_to_all | solution.py:191
  90.4 47.5 %collective-permute-start.5 = (bf16[464,1024]{1,0:T(8,128)(2,1)}, bf16[464,1024]{1,0:T(8,128)(2,1)}, u32[]{:S(2)}, u32[]{:S(2)}) collective-permute-start(bf16[464,1024]{1,0:T(8,128)(2,1)} %get-tuple-element.81), channel_id=1, source_target_pairs={{0,192},{64,0},{128,64},{192,128},{1,193},{65,1},{129,65},{193,129... | collective-permute-start | bytes 2850824 | tf_op jit(solution)/shard_map/ppermute | solution.py:160
  93.3 47.1 %collective-permute-start.4 = (bf16[464,1024]{1,0:T(8,128)(2,1)}, bf16[464,1024]{1,0:T(8,128)(2,1)}, u32[]{:S(2)}, u32[]{:S(2)}) collective-permute-start(bf16[464,1024]{1,0:T(8,128)(2,1)} %get-tuple-element.82), channel_id=1, source_target_pairs={{0,128},{64,192},{128,0},{192,64},{1,129},{65,193},{129,1},{193,65... | collective-permute-start | bytes 2850824 | tf_op jit(solution)/shard_map/ppermute | solution.py:160
  93.9 78.6 %collective-permute-start.3 = (bf16[464,1024]{1,0:T(8,128)(2,1)}, bf16[464,1024]{1,0:T(8,128)(2,1)S(1)}, u32[]{:S(2)}, u32[]{:S(2)}) collective-permute-start(bf16[464,1024]{1,0:T(8,128)(2,1)} %get-tuple-element.83), channel_id=1, source_target_pairs={{0,64},{64,128},{128,192},{192,0},{1,65},{65,129},{129,193},{193,1... | collective-permute-start | bytes 2850824 | tf_op jit(solution)/shard_map/ppermute | solution.py:160
  102.3 38.1 %copy-start.3 = (bf16[464,512]{1,0:T(8,128)(2,1)}, bf16[464,512]{1,0:T(8,128)(2,1)S(1)}, u32[]{:S(2)}) copy-start(bf16[464,512]{1,0:T(8,128)(2,1)S(1)} %get-tuple-element.64) | copy-start | bytes 1425412
  186.8 29.8 %collective-permute-start.9 = (bf16[464,512]{1,0:T(8,128)(2,1)S(1)}, bf16[464,512]{1,0:T(8,128)(2,1)S(1)}, u32[]{:S(2)}, u32[]{:S(2)}) collective-permute-start(bf16[464,512]{1,0:T(8,128)(2,1)S(1)} %concatenate.21), channel_id=1, source_target_pairs={{0,1},{1,2},{2,3},{3,0},{4,5},{5,6},{6,7},{7,4},{8,9},{9,10},{10,1... | collective-permute-start | bytes 1425416 | tf_op jit(solution)/shard_map/ppermute | solution.py:160
  186.9 28.7 %collective-permute-start.8 = (bf16[464,512]{1,0:T(8,128)(2,1)S(1)}, bf16[464,512]{1,0:T(8,128)(2,1)S(1)}, u32[]{:S(2)}, u32[]{:S(2)}) collective-permute-start(bf16[464,512]{1,0:T(8,128)(2,1)S(1)} %concatenate.21), channel_id=1, source_target_pairs={{0,192},{64,0},{128,64},{192,128},{1,193},{65,1},{129,65},{193,129... | collective-permute-start | bytes 1425416 | tf_op jit(solution)/shard_map/ppermute | solution.py:160
  189.7 24.9 %collective-permute-start.7 = (bf16[464,512]{1,0:T(8,128)(2,1)S(1)}, bf16[464,512]{1,0:T(8,128)(2,1)S(1)}, u32[]{:S(2)}, u32[]{:S(2)}) collective-permute-start(bf16[464,512]{1,0:T(8,128)(2,1)S(1)} %concatenate.21), channel_id=1, source_target_pairs={{0,64},{64,128},{128,192},{192,0},{1,65},{65,129},{129,193},{193,1... | collective-permute-start | bytes 1425416 | tf_op jit(solution)/shard_map/ppermute | solution.py:160
  189.7 26.9 %collective-permute-start.6 = (bf16[464,512]{1,0:T(8,128)(2,1)S(1)}, bf16[464,512]{1,0:T(8,128)(2,1)S(1)}, u32[]{:S(2)}, u32[]{:S(2)}) collective-permute-start(bf16[464,512]{1,0:T(8,128)(2,1)S(1)} %concatenate.21), channel_id=1, source_target_pairs={{0,128},{64,192},{128,0},{192,64},{1,129},{65,193},{129,1},{193,65... | collective-permute-start | bytes 1425416 | tf_op jit(solution)/shard_map/ppermute | solution.py:160
  192.4 22.2 %copy-start.10 = (bf16[464,512]{1,0:T(8,128)(2,1)S(1)}, bf16[464,512]{1,0:T(8,128)(2,1)}, u32[]{:S(2)}) copy-start(bf16[464,512]{1,0:T(8,128)(2,1)} %copy-done.9) | copy-start | bytes 1425412
  192.9 22.2 %copy-start.8 = (bf16[464,512]{1,0:T(8,128)(2,1)S(1)}, bf16[464,512]{1,0:T(8,128)(2,1)}, u32[]{:S(2)}) copy-start(bf16[464,512]{1,0:T(8,128)(2,1)} %copy-done.7) | copy-start | bytes 1425412
  194.6 21.0 %copy-start.2 = (bf16[464,512]{1,0:T(8,128)(2,1)S(1)}, bf16[464,512]{1,0:T(8,128)(2,1)}, u32[]{:S(2)}) copy-start(bf16[464,512]{1,0:T(8,128)(2,1)} %copy-done.1) | copy-start | bytes 1425412
  218.1 3.6 %collective-permute-start.10 = (f32[512,512]{1,0:T(8,128)}, f32[512,512]{1,0:T(8,128)}, u32[]{:S(2)}, u32[]{:S(2)}) collective-permute-start(f32[512,512]{1,0:T(8,128)} %convolution_add_fusion), channel_id=1, source_target_pairs={{0,4},{4,0},{1,5},{5,1},{2,6},{6,2},{3,7},{7,3},{8,12},{12,8},{9,1... | collective-permute-start | bytes 3145736 | tf_op jit(solution)/shard_map/ppermute | solution.py:160
  218.1 20.7 %collective-permute-start.12 = (bf16[464,512]{1,0:T(8,128)(2,1)S(1)}, bf16[464,512]{1,0:T(8,128)(2,1)}, u32[]{:S(2)}, u32[]{:S(2)}) collective-permute-start(bf16[464,512]{1,0:T(8,128)(2,1)S(1)} %concatenate.21), channel_id=1, source_target_pairs={{0,2},{1,3},{2,0},{3,1},{4,6},{5,7},{6,4},{7,5},{8,10},{9,11},{10,... | collective-permute-start | bytes 1425416 | tf_op jit(solution)/shard_map/ppermute | solution.py:160
  220.9 22.4 %collective-permute-start.13 = (bf16[464,512]{1,0:T(8,128)(2,1)S(1)}, bf16[464,512]{1,0:T(8,128)(2,1)}, u32[]{:S(2)}, u32[]{:S(2)}) collective-permute-start(bf16[464,512]{1,0:T(8,128)(2,1)S(1)} %concatenate.21), channel_id=1, source_target_pairs={{0,3},{1,0},{2,1},{3,2},{4,7},{5,4},{6,5},{7,6},{8,11},{9,8},{10,9... | collective-permute-start | bytes 1425416 | tf_op jit(solution)/shard_map/ppermute | solution.py:160
  223.5 8.2 %collective-permute-start.11 = (f32[4,64,256]{2,1,0:T(8,128)S(1)}, f32[4,64,256]{2,1,0:T(8,128)S(1)}, u32[]{:S(2)}, u32[]{:S(2)}) collective-permute-start(f32[4,64,256]{2,1,0:T(8,128)S(1)} %get-tuple-element.92), channel_id=1, source_target_pairs={{0,8},{8,0},{16,24},{24,16},{32,40},{40,32},{48,56},{56,48},{1,9},... | collective-permute-start | bytes 786440 | tf_op jit(solution)/shard_map/ppermute | solution.py:226
  224.0 7.9 %collective-permute-start.14 = (f32[4,64,256]{2,1,0:T(8,128)S(1)}, f32[4,64,256]{2,1,0:T(8,128)S(1)}, u32[]{:S(2)}, u32[]{:S(2)}) collective-permute-start(f32[4,64,256]{2,1,0:T(8,128)S(1)} %get-tuple-element.93), channel_id=1, source_target_pairs={{8,16},{16,8},{24,32},{32,24},{40,48},{48,40},{0,56},{56,0},{9,17}... | collective-permute-start | bytes 786440 | tf_op jit(solution)/shard_map/ppermute | solution.py:227
  232.1 11.3 %collective-permute-start.15 = (f32[64,512]{1,0:T(8,128)S(1)}, f32[64,512]{1,0:T(8,128)S(1)}, u32[]{:S(2)}, u32[]{:S(2)}) collective-permute-start(f32[64,512]{1,0:T(8,128)S(1)} %get-tuple-element.91), channel_id=1, source_target_pairs={{0,16},{8,24},{16,32},{24,40},{32,48},{40,56},{48,0},{56,8},{1,17}... | collective-permute-start | bytes 393224 | tf_op jit(solution)/shard_map/ppermute | solution.py:160
  235.2 13.2 %collective-permute-start.16 = (f32[64,512]{1,0:T(8,128)S(1)}, f32[64,512]{1,0:T(8,128)S(1)}, u32[]{:S(2)}, u32[]{:S(2)}) collective-permute-start(f32[64,512]{1,0:T(8,128)S(1)} %get-tuple-element.89), channel_id=1, source_target_pairs={{0,32},{8,40},{16,48},{24,56},{32,0},{40,8},{48,16},{56,24},{1,33}... | collective-permute-start | bytes 393224 | tf_op jit(solution)/shard_map/ppermute | solution.py:160
  237.9 10.4 %collective-permute-start.17 = (f32[64,512]{1,0:T(8,128)S(1)}, f32[64,512]{1,0:T(8,128)S(1)}, u32[]{:S(2)}, u32[]{:S(2)}) collective-permute-start(f32[64,512]{1,0:T(8,128)S(1)} %get-tuple-element.90), channel_id=1, source_target_pairs={{0,48},{8,56},{16,0},{24,8},{32,16},{40,24},{48,32},{56,40},{1,49}... | collective-permute-start | bytes 393224 | tf_op jit(solution)/shard_map/ppermute | solution.py:160
  (18 other events, 95.2 us)

commit v13 on v12

--- a/solution.py
+++ b/solution.py
@@ -230,7 +230,7 @@
     mine += jnp.concatenate([up, down], -1)
     terms = [lax.dynamic_index_in_dim(mine, (mz // 2 + by) % (nz // 2), 0, keepdims=False) for by in range(nz // 2)]
     terms = [step(a, "z", 2 * by) if by else a for by, a in enumerate(terms)]
-    late, _ = lax.optimization_barrier((groups[2:], terms[1]))
+    late, _ = lax.optimization_barrier((groups[2:], mine))
     for by, near in enumerate(late, 2):
         parts.append(lax.dot_general(near, fans[by], BOTH_LAST, preferred_element_type=F32).astype(BF16))
     query_grad = sum(terms)

time: 254 us -> 260 us (1.024); the launches traced: 249 us -> 260 us
  waiting for transfers between devices: 147 us -> 163 us
  matrix products: 18.9 us -> 15.6 us
    ppermute x16, waiting for transfers between devices: 136 us -> 151 us  [step(): lax.ppermute(array, axis, [(i, (i + by) % size) for i in range(size)])]
  transfers between devices with their start and end apart: 20 -> 20, of which waited for: 9 -> 10; matrix products, arithmetic and copies ran while one was open for 12% -> 10% of each run, Pallas kernels for 2% -> 2%
where the time goes in v13:
time: 260 us
  waiting for transfers between devices  163 us (63%)
  starting transfers between devices  44.6 us (17%)
  local copies, waits for them, and re-layouts  17 us (7%)
  matrix products  15.6 us (6%)
  Pallas kernels  15 us (6%)
  other arithmetic  3.76 us (1%)
    ppermute x16, waiting for transfers between devices, step(): lax.ppermute(array, axis, [(i, (i + by) % size) for i in range(size)])  151 us
    ppermute x16, starting transfers between devices, step(): lax.ppermute(array, axis, [(i, (i + by) % size) for i in range(size)])  21.6 us
    all_to_all x1, starting transfers between devices, local(): held = lax.all_to_all(message, DP, split_axis=0, concat_axis=0, tiled=True)  11.6 us
    all_to_all x1, starting transfers between devices, local(): lax.all_to_all(send.reshape(ndp, requests, TILE, HEAD_DIM), DP, split_axi...  10.5 us
    unnamed x44, local copies, waits for them, and re-layouts  7.1 us
    all_to_all x1, waiting for transfers between devices, local(): lax.all_to_all(send.reshape(ndp, requests, TILE, HEAD_DIM), DP, split_axi...  5.99 us
    pallas_call x1, Pallas kernels, attend(): pl.pallas_call(functools.partial(attend_kernel, heads=heads), grid=(count...  5.94 us
    dot_general x1, matrix products, local(): q = shifted(jnp.dot(late, weights, preferred_element_type=F32).astype(BF16))  5.79 us
  transfers between devices with their start and end apart: 20, of which 10 were waited for; matrix products, arithmetic and copies ran while one was open for 10% of the time, Pallas kernels for 2%

profile of v13, /device:TPU:32, one launch (start us, length us, event | category | flops | bytes accessed | tf_op | source)
XLA Modules:
  0.0 259.7 jit_solution(13475041382620354326)
XLA Ops:
  1.9 2.8 %cut.1 = bf16[2,4,8,9,16,128]{5,4,3,2,1,0:T(8,128)(2,1)} custom-call(bf16[16,128]{1,0:T(8,128)(2,1)} %add_convert_fusion.1.named_ref, bf16[8,2,128,512]{3,2,1,0:T(8,128)(2,1)} %cache_ref.1), custom_call_target="tpu_custom_call" | custom-call | bytes 4194304 | tf_op jit(solution)/shard_map/cut/pallas_call | solution.py:36
  4.8 11.6 %all-to-all-start = ((bf16[64,9,16,128]{3,2,1,0:T(8,128)(2,1)}), bf16[64,9,16,128]{3,2,1,0:T(8,128)(2,1)S(1)}, u32[]{:S(2)}, u32[]{:S(2)}) async-start(bf16[64,9,16,128]{3,2,1,0:T(8,128)(2,1)} %bitcast.62), calls=%async_computation | async-start | bytes 4718592 | tf_op jit(solution)/shard_map/all_to_all | solution.py:181
  16.4 3.4 %constant_dynamic-slice_fusion = (bf16[1024,512]{1,0:T(8,128)(2,1)S(1)}, bf16[1024,512]{1,0:T(8,128)(2,1)S(1)}, bf16[1024,512]{1,0:T(8,128)(2,1)S(1)}, bf16[1024,512]{1,0:T(8,128)(2,1)}) fusion(bf16[4096,512]{1,0:T(8,128)(2,1)} %param.7, s32[]{:T(128)S(6)} %select_n.115, s32[]{:T(128)S(6)} %select_n.113, s32[]{:T(128)S(6)} %select_n.111, s32[]{:T(128)S(6)} %select_n.109), kind=kLoop, calls=%fused_computation.26 | loop fusion | bytes 8388624 | tf_op jit(solution)/shard_map/dynamic_slice | solution.py:184
  19.8 3.0 %collective-permute-start.2 = (bf16[1024,512]{1,0:T(8,128)(2,1)S(1)}, bf16[1024,512]{1,0:T(8,128)(2,1)S(1)}, u32[]{:S(2)}, u32[]{:S(2)}) collective-permute-start(bf16[1024,512]{1,0:T(8,128)(2,1)S(1)} %get-tuple-element.85), channel_id=1, source_target_pairs={{0,3},{1,0},{2,1},{3,2},{4,7},{5,4},{6,5},{7,6},{8,11},{9,8},{10,9... | collective-permute-start | bytes 3145736 | tf_op jit(solution)/shard_map/ppermute | solution.py:160
  24.5 43.6 %collective-permute-done.2 = bf16[1024,512]{1,0:T(8,128)(2,1)S(1)} collective-permute-done((bf16[1024,512]{1,0:T(8,128)(2,1)S(1)}, bf16[1024,512]{1,0:T(8,128)(2,1)S(1)}, u32[]{:S(2)}, u32[]{:S(2)}) %collective-permute-start.2) | collective-permute-done | bytes 1048608 | tf_op jit(solution)/shard_map/ppermute | solution.py:160
  72.1 1.9 pick.1
  74.0 2.0 copy-done
  76.0 10.5 %all-to-all-start.1 = ((bf16[64,16,16,128]{3,2,1,0:T(8,128)(2,1)}), bf16[64,16,16,128]{3,2,1,0:T(8,128)(2,1)}, u32[]{:S(2)}, u32[]{:S(2)}) async-start(bf16[64,16,16,128]{3,2,1,0:T(8,128)(2,1)} %bitcast.60), calls=%async_computation.1 | async-start | bytes 8388608 | tf_op jit(solution)/shard_map/all_to_all | solution.py:191
  86.6 3.8 %constant_dynamic-slice_fusion.4 = (bf16[464,1024]{1,0:T(8,128)(2,1)}, bf16[464,1024]{1,0:T(8,128)(2,1)}, bf16[464,1024]{1,0:T(8,128)(2,1)}, bf16[464,1024]{1,0:T(8,128)(2,1)S(1)}) fusion(bf16[512,4096]{1,0:T(8,128)(2,1)} %bitcast.65, s32[]{:T(128)S(6)} %select_n.123, s32[]{:T(128)S(6)} %select_n.121, s32[]{:T(128)S(6)} %select_n.119, s32[]{:T(128)S(6)} %select_n.117), kind=kLoop, calls=%fused_computation.30 | loop fusion | bytes 7602192 | tf_op jit(solution)/shard_map/dynamic_slice | solution.py:197
  90.4 2.9 %collective-permute-start.5 = (bf16[464,1024]{1,0:T(8,128)(2,1)}, bf16[464,1024]{1,0:T(8,128)(2,1)}, u32[]{:S(2)}, u32[]{:S(2)}) collective-permute-start(bf16[464,1024]{1,0:T(8,128)(2,1)} %get-tuple-element.81), channel_id=1, source_target_pairs={{0,192},{64,0},{128,64},{192,128},{1,193},{65,1},{129,65},{193,129... | collective-permute-start | bytes 2850824 | tf_op jit(solution)/shard_map/ppermute | solution.py:160
  95.0 5.8 %fusion.11 = bf16[512,512]{1,0:T(8,128)(2,1)S(1)} fusion(bf16[512,4096]{1,0:T(8,128)(2,1)} %bitcast.66, bf16[4096,512]{1,0:T(8,128)(2,1)} %param.7), kind=kOutput, calls=%fused_computation.43 | convolution fusion | flops 2147483648 | bytes 8912896 | tf_op jit(solution)/shard_map/dot_general | solution.py:203
  102.3 35.6 %collective-permute-done.5.share_ref = bf16[464,1024]{1,0:T(8,128)(2,1)} collective-permute-done((bf16[464,1024]{1,0:T(8,128)(2,1)}, bf16[464,1024]{1,0:T(8,128)(2,1)}, u32[]{:S(2)}, u32[]{:S(2)}) %collective-permute-start.5) | collective-permute-done | bytes 950304 | tf_op jit(solution)/shard_map/ppermute | solution.py:160
  142.0 30.5 %collective-permute-done.3.share_ref = bf16[464,1024]{1,0:T(8,128)(2,1)S(1)} collective-permute-done((bf16[464,1024]{1,0:T(8,128)(2,1)}, bf16[464,1024]{1,0:T(8,128)(2,1)S(1)}, u32[]{:S(2)}, u32[]{:S(2)}) %collective-permute-start.3) | collective-permute-done | bytes 950304 | tf_op jit(solution)/shard_map/ppermute | solution.py:160
  174.6 6.0 %all-to-all-done.1 = bf16[64,16,16,128]{3,2,1,0:T(8,128)(2,1)} async-done(((bf16[64,16,16,128]{3,2,1,0:T(8,128)(2,1)}), bf16[64,16,16,128]{3,2,1,0:T(8,128)(2,1)}, u32[]{:S(2)}, u32[]{:S(2)}) %all-to-all-start.1) | async-done | bytes 4194336 | tf_op jit(solution)/shard_map/all_to_all | solution.py:191
  180.6 5.9 %attend.1 = (bf16[512,512]{1,0:T(8,128)(2,1)S(1)}, bf16[512,512]{1,0:T(8,128)(2,1)S(1)}) custom-call(bf16[512,512]{1,0:T(8,128)(2,1)S(1)} %concatenate.18.q_ref, bf16[512,512]{1,0:T(8,128)(2,1)S(1)} %concatenate.19.g_ref, bf16[2,4,8,2,8,16,128]{6,5,4,3,2,1,0:T(8,128)(2,1)} %bitcast.12.kv_ref), custom_call_target="tpu_custom_call" | custom-call | flops 671088640 | bytes 4194304 | tf_op jit(solution)/shard_map/attend/pallas_call | solution.py:112
  186.9 2.9 %collective-permute-start.8 = (bf16[464,512]{1,0:T(8,128)(2,1)S(1)}, bf16[464,512]{1,0:T(8,128)(2,1)S(1)}, u32[]{:S(2)}, u32[]{:S(2)}) collective-permute-start(bf16[464,512]{1,0:T(8,128)(2,1)S(1)} %concatenate.21), channel_id=1, source_target_pairs={{0,192},{64,0},{128,64},{192,128},{1,193},{65,1},{129,65},{193,129... | collective-permute-start | bytes 1425416 | tf_op jit(solution)/shard_map/ppermute | solution.py:160
  189.7 2.2 collective-permute-start.6
  194.6 20.0 %collective-permute-done.7 = bf16[464,512]{1,0:T(8,128)(2,1)S(1)} collective-permute-done((bf16[464,512]{1,0:T(8,128)(2,1)S(1)}, bf16[464,512]{1,0:T(8,128)(2,1)S(1)}, u32[]{:S(2)}, u32[]{:S(2)}) %collective-permute-start.7) | collective-permute-done | bytes 475168 | tf_op jit(solution)/shard_map/ppermute | solution.py:160
  218.1 2.9 %collective-permute-start.12 = (bf16[464,512]{1,0:T(8,128)(2,1)S(1)}, bf16[464,512]{1,0:T(8,128)(2,1)S(1)}, u32[]{:S(2)}, u32[]{:S(2)}) collective-permute-start(bf16[464,512]{1,0:T(8,128)(2,1)S(1)} %concatenate.21), channel_id=1, source_target_pairs={{0,2},{1,3},{2,0},{3,1},{4,6},{5,7},{6,4},{7,5},{8,10},{9,11},{10,... | collective-permute-start | bytes 1425416 | tf_op jit(solution)/shard_map/ppermute | solution.py:160
  225.2 2.0 convolution_convert_fusion.2
  227.2 5.4 %collective-permute-done.11 = f32[4,64,256]{2,1,0:T(8,128)S(1)} collective-permute-done((f32[4,64,256]{2,1,0:T(8,128)S(1)}, f32[4,64,256]{2,1,0:T(8,128)S(1)}, u32[]{:S(2)}, u32[]{:S(2)}) %collective-permute-start.11) | collective-permute-done | bytes 262176 | tf_op jit(solution)/shard_map/ppermute | solution.py:226
  233.0 10.3 %collective-permute-done.13 = bf16[464,512]{1,0:T(8,128)(2,1)S(1)} collective-permute-done((bf16[464,512]{1,0:T(8,128)(2,1)S(1)}, bf16[464,512]{1,0:T(8,128)(2,1)S(1)}, u32[]{:S(2)}, u32[]{:S(2)}) %collective-permute-start.13) | collective-permute-done | bytes 475168 | tf_op jit(solution)/shard_map/ppermute | solution.py:160
  243.6 4.0 %collective-permute-start.17 = (f32[64,512]{1,0:T(8,128)S(1)}, f32[64,512]{1,0:T(8,128)S(1)}, u32[]{:S(2)}, u32[]{:S(2)}) collective-permute-start(f32[64,512]{1,0:T(8,128)S(1)} %get-tuple-element.90), channel_id=1, source_target_pairs={{0,48},{8,56},{16,0},{24,8},{32,16},{40,24},{48,32},{56,40},{1,49}... | collective-permute-start | bytes 393224 | tf_op jit(solution)/shard_map/ppermute | solution.py:160
  250.1 9.0 %collective-permute-done.15 = f32[64,512]{1,0:T(8,128)S(1)} collective-permute-done((f32[64,512]{1,0:T(8,128)S(1)}, f32[64,512]{1,0:T(8,128)S(1)}, u32[]{:S(2)}, u32[]{:S(2)}) %collective-permute-start.15) | collective-permute-done | bytes 131104 | tf_op jit(solution)/shard_map/ppermute | solution.py:160
  (101 shorter events, 30.5 us)
Async XLA Ops:
  4.8 67.1 %all-to-all-start = ((bf16[64,9,16,128]{3,2,1,0:T(8,128)(2,1)}), bf16[64,9,16,128]{3,2,1,0:T(8,128)(2,1)S(1)}, u32[]{:S(2)}, u32[]{:S(2)}) async-start(bf16[64,9,16,128]{3,2,1,0:T(8,128)(2,1)} %bitcast.62), calls=%async_computation | async-start | bytes 4718592 | tf_op jit(solution)/shard_map/all_to_all | solution.py:181
  19.8 48.2 %collective-permute-start.2 = (bf16[1024,512]{1,0:T(8,128)(2,1)S(1)}, bf16[1024,512]{1,0:T(8,128)(2,1)S(1)}, u32[]{:S(2)}, u32[]{:S(2)}) collective-permute-start(bf16[1024,512]{1,0:T(8,128)(2,1)S(1)} %get-tuple-element.85), channel_id=1, source_target_pairs={{0,3},{1,0},{2,1},{3,2},{4,7},{5,4},{6,5},{7,6},{8,11},{9,8},{10,9... | collective-permute-start | bytes 3145736 | tf_op jit(solution)/shard_map/ppermute | solution.py:160
  22.8 45.2 %collective-permute-start.1 = (bf16[1024,512]{1,0:T(8,128)(2,1)S(1)}, bf16[1024,512]{1,0:T(8,128)(2,1)S(1)}, u32[]{:S(2)}, u32[]{:S(2)}) collective-permute-start(bf16[1024,512]{1,0:T(8,128)(2,1)S(1)} %get-tuple-element.86), channel_id=1, source_target_pairs={{0,2},{1,3},{2,0},{3,1},{4,6},{5,7},{6,4},{7,5},{8,10},{9,11},{10,... | collective-permute-start | bytes 3145736 | tf_op jit(solution)/shard_map/ppermute | solution.py:160
  23.5 48.4 %collective-permute-start = (bf16[1024,512]{1,0:T(8,128)(2,1)S(1)}, bf16[1024,512]{1,0:T(8,128)(2,1)}, u32[]{:S(2)}, u32[]{:S(2)}) collective-permute-start(bf16[1024,512]{1,0:T(8,128)(2,1)S(1)} %get-tuple-element.87), channel_id=1, source_target_pairs={{0,1},{1,2},{2,3},{3,0},{4,5},{5,6},{6,7},{7,4},{8,9},{9,10},{10,1... | collective-permute-start | bytes 3145736 | tf_op jit(solution)/shard_map/ppermute | solution.py:160
  76.0 104.6 %all-to-all-start.1 = ((bf16[64,16,16,128]{3,2,1,0:T(8,128)(2,1)}), bf16[64,16,16,128]{3,2,1,0:T(8,128)(2,1)}, u32[]{:S(2)}, u32[]{:S(2)}) async-start(bf16[64,16,16,128]{3,2,1,0:T(8,128)(2,1)} %bitcast.60), calls=%async_computation.1 | async-start | bytes 8388608 | tf_op jit(solution)/shard_map/all_to_all | solution.py:191
  90.4 47.5 %collective-permute-start.5 = (bf16[464,1024]{1,0:T(8,128)(2,1)}, bf16[464,1024]{1,0:T(8,128)(2,1)}, u32[]{:S(2)}, u32[]{:S(2)}) collective-permute-start(bf16[464,1024]{1,0:T(8,128)(2,1)} %get-tuple-element.81), channel_id=1, source_target_pairs={{0,192},{64,0},{128,64},{192,128},{1,193},{65,1},{129,65},{193,129... | collective-permute-start | bytes 2850824 | tf_op jit(solution)/shard_map/ppermute | solution.py:160
  93.3 47.1 %collective-permute-start.4 = (bf16[464,1024]{1,0:T(8,128)(2,1)}, bf16[464,1024]{1,0:T(8,128)(2,1)}, u32[]{:S(2)}, u32[]{:S(2)}) collective-permute-start(bf16[464,1024]{1,0:T(8,128)(2,1)} %get-tuple-element.82), channel_id=1, source_target_pairs={{0,128},{64,192},{128,0},{192,64},{1,129},{65,193},{129,1},{193,65... | collective-permute-start | bytes 2850824 | tf_op jit(solution)/shard_map/ppermute | solution.py:160
  93.9 78.6 %collective-permute-start.3 = (bf16[464,1024]{1,0:T(8,128)(2,1)}, bf16[464,1024]{1,0:T(8,128)(2,1)S(1)}, u32[]{:S(2)}, u32[]{:S(2)}) collective-permute-start(bf16[464,1024]{1,0:T(8,128)(2,1)} %get-tuple-element.83), channel_id=1, source_target_pairs={{0,64},{64,128},{128,192},{192,0},{1,65},{65,129},{129,193},{193,1... | collective-permute-start | bytes 2850824 | tf_op jit(solution)/shard_map/ppermute | solution.py:160
  102.3 38.1 %copy-start.3 = (bf16[464,512]{1,0:T(8,128)(2,1)}, bf16[464,512]{1,0:T(8,128)(2,1)S(1)}, u32[]{:S(2)}) copy-start(bf16[464,512]{1,0:T(8,128)(2,1)S(1)} %get-tuple-element.64) | copy-start | bytes 1425412
  186.8 29.8 %collective-permute-start.9 = (bf16[464,512]{1,0:T(8,128)(2,1)S(1)}, bf16[464,512]{1,0:T(8,128)(2,1)S(1)}, u32[]{:S(2)}, u32[]{:S(2)}) collective-permute-start(bf16[464,512]{1,0:T(8,128)(2,1)S(1)} %concatenate.21), channel_id=1, source_target_pairs={{0,1},{1,2},{2,3},{3,0},{4,5},{5,6},{6,7},{7,4},{8,9},{9,10},{10,1... | collective-permute-start | bytes 1425416 | tf_op jit(solution)/shard_map/ppermute | solution.py:160
  186.9 28.7 %collective-permute-start.8 = (bf16[464,512]{1,0:T(8,128)(2,1)S(1)}, bf16[464,512]{1,0:T(8,128)(2,1)S(1)}, u32[]{:S(2)}, u32[]{:S(2)}) collective-permute-start(bf16[464,512]{1,0:T(8,128)(2,1)S(1)} %concatenate.21), channel_id=1, source_target_pairs={{0,192},{64,0},{128,64},{192,128},{1,193},{65,1},{129,65},{193,129... | collective-permute-start | bytes 1425416 | tf_op jit(solution)/shard_map/ppermute | solution.py:160
  189.7 24.9 %collective-permute-start.7 = (bf16[464,512]{1,0:T(8,128)(2,1)S(1)}, bf16[464,512]{1,0:T(8,128)(2,1)S(1)}, u32[]{:S(2)}, u32[]{:S(2)}) collective-permute-start(bf16[464,512]{1,0:T(8,128)(2,1)S(1)} %concatenate.21), channel_id=1, source_target_pairs={{0,64},{64,128},{128,192},{192,0},{1,65},{65,129},{129,193},{193,1... | collective-permute-start | bytes 1425416 | tf_op jit(solution)/shard_map/ppermute | solution.py:160
  189.7 26.9 %collective-permute-start.6 = (bf16[464,512]{1,0:T(8,128)(2,1)S(1)}, bf16[464,512]{1,0:T(8,128)(2,1)S(1)}, u32[]{:S(2)}, u32[]{:S(2)}) collective-permute-start(bf16[464,512]{1,0:T(8,128)(2,1)S(1)} %concatenate.21), channel_id=1, source_target_pairs={{0,128},{64,192},{128,0},{192,64},{1,129},{65,193},{129,1},{193,65... | collective-permute-start | bytes 1425416 | tf_op jit(solution)/shard_map/ppermute | solution.py:160
  192.4 22.2 %copy-start.10 = (bf16[464,512]{1,0:T(8,128)(2,1)S(1)}, bf16[464,512]{1,0:T(8,128)(2,1)}, u32[]{:S(2)}) copy-start(bf16[464,512]{1,0:T(8,128)(2,1)} %copy-done.9) | copy-start | bytes 1425412
  192.9 22.2 %copy-start.8 = (bf16[464,512]{1,0:T(8,128)(2,1)S(1)}, bf16[464,512]{1,0:T(8,128)(2,1)}, u32[]{:S(2)}) copy-start(bf16[464,512]{1,0:T(8,128)(2,1)} %copy-done.7) | copy-start | bytes 1425412
  218.1 4.6 %collective-permute-start.10 = (f32[512,512]{1,0:T(8,128)}, f32[512,512]{1,0:T(8,128)}, u32[]{:S(2)}, u32[]{:S(2)}) collective-permute-start(f32[512,512]{1,0:T(8,128)} %convolution_add_fusion), channel_id=1, source_target_pairs={{0,4},{4,0},{1,5},{5,1},{2,6},{6,2},{3,7},{7,3},{8,12},{12,8},{9,1... | collective-permute-start | bytes 3145736 | tf_op jit(solution)/shard_map/ppermute | solution.py:160
  218.1 14.9 %collective-permute-start.12 = (bf16[464,512]{1,0:T(8,128)(2,1)S(1)}, bf16[464,512]{1,0:T(8,128)(2,1)S(1)}, u32[]{:S(2)}, u32[]{:S(2)}) collective-permute-start(bf16[464,512]{1,0:T(8,128)(2,1)S(1)} %concatenate.21), channel_id=1, source_target_pairs={{0,2},{1,3},{2,0},{3,1},{4,6},{5,7},{6,4},{7,5},{8,10},{9,11},{10,... | collective-permute-start | bytes 1425416 | tf_op jit(solution)/shard_map/ppermute | solution.py:160
  221.0 22.3 %collective-permute-start.13 = (bf16[464,512]{1,0:T(8,128)(2,1)S(1)}, bf16[464,512]{1,0:T(8,128)(2,1)S(1)}, u32[]{:S(2)}, u32[]{:S(2)}) collective-permute-start(bf16[464,512]{1,0:T(8,128)(2,1)S(1)} %concatenate.21), channel_id=1, source_target_pairs={{0,3},{1,0},{2,1},{3,2},{4,7},{5,4},{6,5},{7,6},{8,11},{9,8},{10,9... | collective-permute-start | bytes 1425416 | tf_op jit(solution)/shard_map/ppermute | solution.py:160
  224.4 8.2 %collective-permute-start.11 = (f32[4,64,256]{2,1,0:T(8,128)S(1)}, f32[4,64,256]{2,1,0:T(8,128)S(1)}, u32[]{:S(2)}, u32[]{:S(2)}) collective-permute-start(f32[4,64,256]{2,1,0:T(8,128)S(1)} %get-tuple-element.92), channel_id=1, source_target_pairs={{0,8},{8,0},{16,24},{24,16},{32,40},{40,32},{48,56},{56,48},{1,9},... | collective-permute-start | bytes 786440 | tf_op jit(solution)/shard_map/ppermute | solution.py:226
  225.0 22.6 %copy-start.18 = (bf16[1024,512]{1,0:T(8,128)(2,1)S(1)}, bf16[1024,512]{1,0:T(8,128)(2,1)}, u32[]{:S(2)}) copy-start(bf16[1024,512]{1,0:T(8,128)(2,1)} %copy-done.17) | copy-start | bytes 3145732
  225.0 7.9 %collective-permute-start.14 = (f32[4,64,256]{2,1,0:T(8,128)S(1)}, f32[4,64,256]{2,1,0:T(8,128)S(1)}, u32[]{:S(2)}, u32[]{:S(2)}) collective-permute-start(f32[4,64,256]{2,1,0:T(8,128)S(1)} %get-tuple-element.93), channel_id=1, source_target_pairs={{8,16},{16,8},{24,32},{32,24},{40,48},{48,40},{0,56},{56,0},{9,17}... | collective-permute-start | bytes 786440 | tf_op jit(solution)/shard_map/ppermute | solution.py:227
  243.3 15.7 %collective-permute-start.15 = (f32[64,512]{1,0:T(8,128)S(1)}, f32[64,512]{1,0:T(8,128)S(1)}, u32[]{:S(2)}, u32[]{:S(2)}) collective-permute-start(f32[64,512]{1,0:T(8,128)S(1)} %get-tuple-element.89), channel_id=1, source_target_pairs={{0,16},{8,24},{16,32},{24,40},{32,48},{40,56},{48,0},{56,8},{1,17}... | collective-permute-start | bytes 393224 | tf_op jit(solution)/shard_map/ppermute | solution.py:160
  243.6 15.5 %collective-permute-start.17 = (f32[64,512]{1,0:T(8,128)S(1)}, f32[64,512]{1,0:T(8,128)S(1)}, u32[]{:S(2)}, u32[]{:S(2)}) collective-permute-start(f32[64,512]{1,0:T(8,128)S(1)} %get-tuple-element.90), channel_id=1, source_target_pairs={{0,48},{8,56},{16,0},{24,8},{32,16},{40,24},{48,32},{56,40},{1,49}... | collective-permute-start | bytes 393224 | tf_op jit(solution)/shard_map/ppermute | solution.py:160
  247.5 11.5 %collective-permute-start.16 = (f32[64,512]{1,0:T(8,128)S(1)}, f32[64,512]{1,0:T(8,128)S(1)}, u32[]{:S(2)}, u32[]{:S(2)}) collective-permute-start(f32[64,512]{1,0:T(8,128)S(1)} %get-tuple-element.91), channel_id=1, source_target_pairs={{0,32},{8,40},{16,48},{24,56},{32,0},{40,8},{48,16},{56,24},{1,33}... | collective-permute-start | bytes 393224 | tf_op jit(solution)/shard_map/ppermute | solution.py:160
  (18 other events, 116.8 us)

commit v14 on v13

--- a/solution.py
+++ b/solution.py
@@ -230,8 +230,8 @@
     mine += jnp.concatenate([up, down], -1)
     terms = [lax.dynamic_index_in_dim(mine, (mz // 2 + by) % (nz // 2), 0, keepdims=False) for by in range(nz // 2)]
     terms = [step(a, "z", 2 * by) if by else a for by, a in enumerate(terms)]
-    late, _ = lax.optimization_barrier((groups[2:], mine))
-    for by, near in enumerate(late, 2):
+    for by in range(2, nmp):
+        near, _ = lax.optimization_barrier((groups[by], mine if by < nmp - 1 else terms[1]))
         parts.append(lax.dot_general(near, fans[by], BOTH_LAST, preferred_element_type=F32).astype(BF16))
     query_grad = sum(terms)
     part = sum(a.astype(F32) for a in parts).astype(BF16)

time: 260 us -> 253 us (0.973)
  waiting for transfers between devices: 163 us -> 153 us
    ppermute x16, waiting for transfers between devices: 151 us -> 142 us  [step(): lax.ppermute(array, axis, [(i, (i + by) % size) for i in range(size)])]
where the time goes in v14:
time: 253 us; the launch traced here: 252 us
  waiting for transfers between devices  153 us (60%)
  starting transfers between devices  46.1 us (18%)
  local copies, waits for them, and re-layouts  17 us (7%)
  matrix products  15.6 us (6%)
  Pallas kernels  15 us (6%)
  other arithmetic  3.76 us (1%)
    ppermute x16, waiting for transfers between devices, step(): lax.ppermute(array, axis, [(i, (i + by) % size) for i in range(size)])  142 us
    ppermute x16, starting transfers between devices, step(): lax.ppermute(array, axis, [(i, (i + by) % size) for i in range(size)])  23.2 us
    all_to_all x1, starting transfers between devices, local(): held = lax.all_to_all(message, DP, split_axis=0, concat_axis=0, tiled=True)  11.6 us
    all_to_all x1, starting transfers between devices, local(): lax.all_to_all(send.reshape(ndp, requests, TILE, HEAD_DIM), DP, split_axi...  10.5 us
    unnamed x44, local copies, waits for them, and re-layouts  7.1 us
    all_to_all x1, waiting for transfers between devices, local(): lax.all_to_all(send.reshape(ndp, requests, TILE, HEAD_DIM), DP, split_axi...  5.99 us
    pallas_call x1, Pallas kernels, attend(): pl.pallas_call(functools.partial(attend_kernel, heads=heads), grid=(count...  5.94 us
    dot_general x1, matrix products, local(): q = shifted(jnp.dot(late, weights, preferred_element_type=F32).astype(BF16))  5.79 us
  transfers between devices with their start and end apart: 20, of which 10 were waited for; matrix products, arithmetic and copies ran while one was open for 10% of the time, Pallas kernels for 2%

profile of v14, /device:TPU:32, one launch (start us, length us, event | category | flops | bytes accessed | tf_op | source)
XLA Modules:
  0.0 251.9 jit_solution(13068442499711899029)
XLA Ops:
  1.9 2.8 %cut.1 = bf16[2,4,8,9,16,128]{5,4,3,2,1,0:T(8,128)(2,1)} custom-call(bf16[16,128]{1,0:T(8,128)(2,1)} %add_convert_fusion.1.named_ref, bf16[8,2,128,512]{3,2,1,0:T(8,128)(2,1)} %cache_ref.1), custom_call_target="tpu_custom_call" | custom-call | bytes 4194304 | tf_op jit(solution)/shard_map/cut/pallas_call | solution.py:36
  4.8 11.6 %all-to-all-start = ((bf16[64,9,16,128]{3,2,1,0:T(8,128)(2,1)}), bf16[64,9,16,128]{3,2,1,0:T(8,128)(2,1)S(1)}, u32[]{:S(2)}, u32[]{:S(2)}) async-start(bf16[64,9,16,128]{3,2,1,0:T(8,128)(2,1)} %bitcast.62), calls=%async_computation | async-start | bytes 4718592 | tf_op jit(solution)/shard_map/all_to_all | solution.py:181
  16.4 3.4 %constant_dynamic-slice_fusion = (bf16[1024,512]{1,0:T(8,128)(2,1)S(1)}, bf16[1024,512]{1,0:T(8,128)(2,1)S(1)}, bf16[1024,512]{1,0:T(8,128)(2,1)S(1)}, bf16[1024,512]{1,0:T(8,128)(2,1)}) fusion(bf16[4096,512]{1,0:T(8,128)(2,1)} %param.7, s32[]{:T(128)S(6)} %select_n.115, s32[]{:T(128)S(6)} %select_n.113, s32[]{:T(128)S(6)} %select_n.111, s32[]{:T(128)S(6)} %select_n.109), kind=kLoop, calls=%fused_computation.26 | loop fusion | bytes 8388624 | tf_op jit(solution)/shard_map/dynamic_slice | solution.py:184
  19.8 3.0 %collective-permute-start.2 = (bf16[1024,512]{1,0:T(8,128)(2,1)S(1)}, bf16[1024,512]{1,0:T(8,128)(2,1)S(1)}, u32[]{:S(2)}, u32[]{:S(2)}) collective-permute-start(bf16[1024,512]{1,0:T(8,128)(2,1)S(1)} %get-tuple-element.85), channel_id=1, source_target_pairs={{0,3},{1,0},{2,1},{3,2},{4,7},{5,4},{6,5},{7,6},{8,11},{9,8},{10,9... | collective-permute-start | bytes 3145736 | tf_op jit(solution)/shard_map/ppermute | solution.py:160
  24.5 43.6 %collective-permute-done.2 = bf16[1024,512]{1,0:T(8,128)(2,1)S(1)} collective-permute-done((bf16[1024,512]{1,0:T(8,128)(2,1)S(1)}, bf16[1024,512]{1,0:T(8,128)(2,1)S(1)}, u32[]{:S(2)}, u32[]{:S(2)}) %collective-permute-start.2) | collective-permute-done | bytes 1048608 | tf_op jit(solution)/shard_map/ppermute | solution.py:160
  72.1 1.9 pick.1
  74.0 2.0 copy-done
  76.0 10.5 %all-to-all-start.1 = ((bf16[64,16,16,128]{3,2,1,0:T(8,128)(2,1)}), bf16[64,16,16,128]{3,2,1,0:T(8,128)(2,1)}, u32[]{:S(2)}, u32[]{:S(2)}) async-start(bf16[64,16,16,128]{3,2,1,0:T(8,128)(2,1)} %bitcast.60), calls=%async_computation.1 | async-start | bytes 8388608 | tf_op jit(solution)/shard_map/all_to_all | solution.py:191
  86.6 3.8 %constant_dynamic-slice_fusion.4 = (bf16[464,1024]{1,0:T(8,128)(2,1)}, bf16[464,1024]{1,0:T(8,128)(2,1)}, bf16[464,1024]{1,0:T(8,128)(2,1)}, bf16[464,1024]{1,0:T(8,128)(2,1)S(1)}) fusion(bf16[512,4096]{1,0:T(8,128)(2,1)} %bitcast.65, s32[]{:T(128)S(6)} %select_n.123, s32[]{:T(128)S(6)} %select_n.121, s32[]{:T(128)S(6)} %select_n.119, s32[]{:T(128)S(6)} %select_n.117), kind=kLoop, calls=%fused_computation.30 | loop fusion | bytes 7602192 | tf_op jit(solution)/shard_map/dynamic_slice | solution.py:197
  90.4 2.9 %collective-permute-start.5 = (bf16[464,1024]{1,0:T(8,128)(2,1)}, bf16[464,1024]{1,0:T(8,128)(2,1)}, u32[]{:S(2)}, u32[]{:S(2)}) collective-permute-start(bf16[464,1024]{1,0:T(8,128)(2,1)} %get-tuple-element.81), channel_id=1, source_target_pairs={{0,192},{64,0},{128,64},{192,128},{1,193},{65,1},{129,65},{193,129... | collective-permute-start | bytes 2850824 | tf_op jit(solution)/shard_map/ppermute | solution.py:160
  95.0 5.8 %fusion.11 = bf16[512,512]{1,0:T(8,128)(2,1)S(1)} fusion(bf16[512,4096]{1,0:T(8,128)(2,1)} %bitcast.66, bf16[4096,512]{1,0:T(8,128)(2,1)} %param.7), kind=kOutput, calls=%fused_computation.43 | convolution fusion | flops 2147483648 | bytes 8912896 | tf_op jit(solution)/shard_map/dot_general | solution.py:203
  102.3 35.6 %collective-permute-done.5.share_ref = bf16[464,1024]{1,0:T(8,128)(2,1)} collective-permute-done((bf16[464,1024]{1,0:T(8,128)(2,1)}, bf16[464,1024]{1,0:T(8,128)(2,1)}, u32[]{:S(2)}, u32[]{:S(2)}) %collective-permute-start.5) | collective-permute-done | bytes 950304 | tf_op jit(solution)/shard_map/ppermute | solution.py:160
  142.0 30.5 %collective-permute-done.3.share_ref = bf16[464,1024]{1,0:T(8,128)(2,1)S(1)} collective-permute-done((bf16[464,1024]{1,0:T(8,128)(2,1)}, bf16[464,1024]{1,0:T(8,128)(2,1)S(1)}, u32[]{:S(2)}, u32[]{:S(2)}) %collective-permute-start.3) | collective-permute-done | bytes 950304 | tf_op jit(solution)/shard_map/ppermute | solution.py:160
  174.6 6.0 %all-to-all-done.1 = bf16[64,16,16,128]{3,2,1,0:T(8,128)(2,1)} async-done(((bf16[64,16,16,128]{3,2,1,0:T(8,128)(2,1)}), bf16[64,16,16,128]{3,2,1,0:T(8,128)(2,1)}, u32[]{:S(2)}, u32[]{:S(2)}) %all-to-all-start.1) | async-done | bytes 4194336 | tf_op jit(solution)/shard_map/all_to_all | solution.py:191
  180.6 5.9 %attend.1 = (bf16[512,512]{1,0:T(8,128)(2,1)S(1)}, bf16[512,512]{1,0:T(8,128)(2,1)S(1)}) custom-call(bf16[512,512]{1,0:T(8,128)(2,1)S(1)} %concatenate.18.q_ref, bf16[512,512]{1,0:T(8,128)(2,1)S(1)} %concatenate.19.g_ref, bf16[2,4,8,2,8,16,128]{6,5,4,3,2,1,0:T(8,128)(2,1)} %bitcast.12.kv_ref), custom_call_target="tpu_custom_call" | custom-call | flops 671088640 | bytes 4194304 | tf_op jit(solution)/shard_map/attend/pallas_call | solution.py:112
  186.9 2.9 %collective-permute-start.8 = (bf16[464,512]{1,0:T(8,128)(2,1)S(1)}, bf16[464,512]{1,0:T(8,128)(2,1)S(1)}, u32[]{:S(2)}, u32[]{:S(2)}) collective-permute-start(bf16[464,512]{1,0:T(8,128)(2,1)S(1)} %concatenate.21), channel_id=1, source_target_pairs={{0,192},{64,0},{128,64},{192,128},{1,193},{65,1},{129,65},{193,129... | collective-permute-start | bytes 1425416 | tf_op jit(solution)/shard_map/ppermute | solution.py:160
  189.7 2.2 collective-permute-start.6
  194.6 20.0 %collective-permute-done.7 = bf16[464,512]{1,0:T(8,128)(2,1)S(1)} collective-permute-done((bf16[464,512]{1,0:T(8,128)(2,1)S(1)}, bf16[464,512]{1,0:T(8,128)(2,1)S(1)}, u32[]{:S(2)}, u32[]{:S(2)}) %collective-permute-start.7) | collective-permute-done | bytes 475168 | tf_op jit(solution)/shard_map/ppermute | solution.py:160
  218.1 2.9 %collective-permute-start.12 = (bf16[464,512]{1,0:T(8,128)(2,1)S(1)}, bf16[464,512]{1,0:T(8,128)(2,1)S(1)}, u32[]{:S(2)}, u32[]{:S(2)}) collective-permute-start(bf16[464,512]{1,0:T(8,128)(2,1)S(1)} %concatenate.21), channel_id=1, source_target_pairs={{0,2},{1,3},{2,0},{3,1},{4,6},{5,7},{6,4},{7,5},{8,10},{9,11},{10,... | collective-permute-start | bytes 1425416 | tf_op jit(solution)/shard_map/ppermute | solution.py:160
  225.2 2.0 convolution_convert_fusion.2
  227.2 5.4 %collective-permute-done.11 = f32[4,64,256]{2,1,0:T(8,128)S(1)} collective-permute-done((f32[4,64,256]{2,1,0:T(8,128)S(1)}, f32[4,64,256]{2,1,0:T(8,128)S(1)}, u32[]{:S(2)}, u32[]{:S(2)}) %collective-permute-start.11) | collective-permute-done | bytes 262176 | tf_op jit(solution)/shard_map/ppermute | solution.py:226
  234.3 4.5 %collective-permute-start.17 = (f32[64,512]{1,0:T(8,128)S(1)}, f32[64,512]{1,0:T(8,128)S(1)}, u32[]{:S(2)}, u32[]{:S(2)}) collective-permute-start(f32[64,512]{1,0:T(8,128)S(1)} %get-tuple-element.90), channel_id=1, source_target_pairs={{0,48},{8,56},{16,0},{24,8},{32,16},{40,24},{48,32},{56,40},{1,49}... | collective-permute-start | bytes 393224 | tf_op jit(solution)/shard_map/ppermute | solution.py:160
  239.4 3.8 %collective-permute-done.14 = bf16[464,512]{1,0:T(8,128)(2,1)S(1)} collective-permute-done((bf16[464,512]{1,0:T(8,128)(2,1)S(1)}, bf16[464,512]{1,0:T(8,128)(2,1)S(1)}, u32[]{:S(2)}, u32[]{:S(2)}) %collective-permute-start.14) | collective-permute-done | bytes 475168 | tf_op jit(solution)/shard_map/ppermute | solution.py:160
  243.3 6.1 %collective-permute-done.15 = f32[64,512]{1,0:T(8,128)S(1)} collective-permute-done((f32[64,512]{1,0:T(8,128)S(1)}, f32[64,512]{1,0:T(8,128)S(1)}, u32[]{:S(2)}, u32[]{:S(2)}) %collective-permute-start.15) | collective-permute-done | bytes 131104 | tf_op jit(solution)/shard_map/ppermute | solution.py:160
  (101 shorter events, 31.5 us)
Async XLA Ops:
  4.8 67.1 %all-to-all-start = ((bf16[64,9,16,128]{3,2,1,0:T(8,128)(2,1)}), bf16[64,9,16,128]{3,2,1,0:T(8,128)(2,1)S(1)}, u32[]{:S(2)}, u32[]{:S(2)}) async-start(bf16[64,9,16,128]{3,2,1,0:T(8,128)(2,1)} %bitcast.62), calls=%async_computation | async-start | bytes 4718592 | tf_op jit(solution)/shard_map/all_to_all | solution.py:181
  19.8 48.2 %collective-permute-start.2 = (bf16[1024,512]{1,0:T(8,128)(2,1)S(1)}, bf16[1024,512]{1,0:T(8,128)(2,1)S(1)}, u32[]{:S(2)}, u32[]{:S(2)}) collective-permute-start(bf16[1024,512]{1,0:T(8,128)(2,1)S(1)} %get-tuple-element.85), channel_id=1, source_target_pairs={{0,3},{1,0},{2,1},{3,2},{4,7},{5,4},{6,5},{7,6},{8,11},{9,8},{10,9... | collective-permute-start | bytes 3145736 | tf_op jit(solution)/shard_map/ppermute | solution.py:160
  22.8 45.2 %collective-permute-start.1 = (bf16[1024,512]{1,0:T(8,128)(2,1)S(1)}, bf16[1024,512]{1,0:T(8,128)(2,1)S(1)}, u32[]{:S(2)}, u32[]{:S(2)}) collective-permute-start(bf16[1024,512]{1,0:T(8,128)(2,1)S(1)} %get-tuple-element.86), channel_id=1, source_target_pairs={{0,2},{1,3},{2,0},{3,1},{4,6},{5,7},{6,4},{7,5},{8,10},{9,11},{10,... | collective-permute-start | bytes 3145736 | tf_op jit(solution)/shard_map/ppermute | solution.py:160
  23.5 48.4 %collective-permute-start = (bf16[1024,512]{1,0:T(8,128)(2,1)S(1)}, bf16[1024,512]{1,0:T(8,128)(2,1)}, u32[]{:S(2)}, u32[]{:S(2)}) collective-permute-start(bf16[1024,512]{1,0:T(8,128)(2,1)S(1)} %get-tuple-element.87), channel_id=1, source_target_pairs={{0,1},{1,2},{2,3},{3,0},{4,5},{5,6},{6,7},{7,4},{8,9},{9,10},{10,1... | collective-permute-start | bytes 3145736 | tf_op jit(solution)/shard_map/ppermute | solution.py:160
  76.0 104.6 %all-to-all-start.1 = ((bf16[64,16,16,128]{3,2,1,0:T(8,128)(2,1)}), bf16[64,16,16,128]{3,2,1,0:T(8,128)(2,1)}, u32[]{:S(2)}, u32[]{:S(2)}) async-start(bf16[64,16,16,128]{3,2,1,0:T(8,128)(2,1)} %bitcast.60), calls=%async_computation.1 | async-start | bytes 8388608 | tf_op jit(solution)/shard_map/all_to_all | solution.py:191
  90.4 47.5 %collective-permute-start.5 = (bf16[464,1024]{1,0:T(8,128)(2,1)}, bf16[464,1024]{1,0:T(8,128)(2,1)}, u32[]{:S(2)}, u32[]{:S(2)}) collective-permute-start(bf16[464,1024]{1,0:T(8,128)(2,1)} %get-tuple-element.81), channel_id=1, source_target_pairs={{0,192},{64,0},{128,64},{192,128},{1,193},{65,1},{129,65},{193,129... | collective-permute-start | bytes 2850824 | tf_op jit(solution)/shard_map/ppermute | solution.py:160
  93.3 47.1 %collective-permute-start.4 = (bf16[464,1024]{1,0:T(8,128)(2,1)}, bf16[464,1024]{1,0:T(8,128)(2,1)}, u32[]{:S(2)}, u32[]{:S(2)}) collective-permute-start(bf16[464,1024]{1,0:T(8,128)(2,1)} %get-tuple-element.82), channel_id=1, source_target_pairs={{0,128},{64,192},{128,0},{192,64},{1,129},{65,193},{129,1},{193,65... | collective-permute-start | bytes 2850824 | tf_op jit(solution)/shard_map/ppermute | solution.py:160
  93.9 78.6 %collective-permute-start.3 = (bf16[464,1024]{1,0:T(8,128)(2,1)}, bf16[464,1024]{1,0:T(8,128)(2,1)S(1)}, u32[]{:S(2)}, u32[]{:S(2)}) collective-permute-start(bf16[464,1024]{1,0:T(8,128)(2,1)} %get-tuple-element.83), channel_id=1, source_target_pairs={{0,64},{64,128},{128,192},{192,0},{1,65},{65,129},{129,193},{193,1... | collective-permute-start | bytes 2850824 | tf_op jit(solution)/shard_map/ppermute | solution.py:160
  102.3 38.1 %copy-start.3 = (bf16[464,512]{1,0:T(8,128)(2,1)}, bf16[464,512]{1,0:T(8,128)(2,1)S(1)}, u32[]{:S(2)}) copy-start(bf16[464,512]{1,0:T(8,128)(2,1)S(1)} %get-tuple-element.64) | copy-start | bytes 1425412
  186.8 29.8 %collective-permute-start.9 = (bf16[464,512]{1,0:T(8,128)(2,1)S(1)}, bf16[464,512]{1,0:T(8,128)(2,1)S(1)}, u32[]{:S(2)}, u32[]{:S(2)}) collective-permute-start(bf16[464,512]{1,0:T(8,128)(2,1)S(1)} %concatenate.21), channel_id=1, source_target_pairs={{0,1},{1,2},{2,3},{3,0},{4,5},{5,6},{6,7},{7,4},{8,9},{9,10},{10,1... | collective-permute-start | bytes 1425416 | tf_op jit(solution)/shard_map/ppermute | solution.py:160
  186.9 28.7 %collective-permute-start.8 = (bf16[464,512]{1,0:T(8,128)(2,1)S(1)}, bf16[464,512]{1,0:T(8,128)(2,1)S(1)}, u32[]{:S(2)}, u32[]{:S(2)}) collective-permute-start(bf16[464,512]{1,0:T(8,128)(2,1)S(1)} %concatenate.21), channel_id=1, source_target_pairs={{0,192},{64,0},{128,64},{192,128},{1,193},{65,1},{129,65},{193,129... | collective-permute-start | bytes 1425416 | tf_op jit(solution)/shard_map/ppermute | solution.py:160
  189.7 24.9 %collective-permute-start.7 = (bf16[464,512]{1,0:T(8,128)(2,1)S(1)}, bf16[464,512]{1,0:T(8,128)(2,1)S(1)}, u32[]{:S(2)}, u32[]{:S(2)}) collective-permute-start(bf16[464,512]{1,0:T(8,128)(2,1)S(1)} %concatenate.21), channel_id=1, source_target_pairs={{0,64},{64,128},{128,192},{192,0},{1,65},{65,129},{129,193},{193,1... | collective-permute-start | bytes 1425416 | tf_op jit(solution)/shard_map/ppermute | solution.py:160
  189.7 26.9 %collective-permute-start.6 = (bf16[464,512]{1,0:T(8,128)(2,1)S(1)}, bf16[464,512]{1,0:T(8,128)(2,1)S(1)}, u32[]{:S(2)}, u32[]{:S(2)}) collective-permute-start(bf16[464,512]{1,0:T(8,128)(2,1)S(1)} %concatenate.21), channel_id=1, source_target_pairs={{0,128},{64,192},{128,0},{192,64},{1,129},{65,193},{129,1},{193,65... | collective-permute-start | bytes 1425416 | tf_op jit(solution)/shard_map/ppermute | solution.py:160
  192.4 22.2 %copy-start.10 = (bf16[464,512]{1,0:T(8,128)(2,1)S(1)}, bf16[464,512]{1,0:T(8,128)(2,1)}, u32[]{:S(2)}) copy-start(bf16[464,512]{1,0:T(8,128)(2,1)} %copy-done.9) | copy-start | bytes 1425412
  192.9 22.2 %copy-start.8 = (bf16[464,512]{1,0:T(8,128)(2,1)S(1)}, bf16[464,512]{1,0:T(8,128)(2,1)}, u32[]{:S(2)}) copy-start(bf16[464,512]{1,0:T(8,128)(2,1)} %copy-done.7) | copy-start | bytes 1425412
  218.1 4.6 %collective-permute-start.10 = (f32[512,512]{1,0:T(8,128)}, f32[512,512]{1,0:T(8,128)}, u32[]{:S(2)}, u32[]{:S(2)}) collective-permute-start(f32[512,512]{1,0:T(8,128)} %convolution_add_fusion), channel_id=1, source_target_pairs={{0,4},{4,0},{1,5},{5,1},{2,6},{6,2},{3,7},{7,3},{8,12},{12,8},{9,1... | collective-permute-start | bytes 3145736 | tf_op jit(solution)/shard_map/ppermute | solution.py:160
  218.1 14.9 %collective-permute-start.12 = (bf16[464,512]{1,0:T(8,128)(2,1)S(1)}, bf16[464,512]{1,0:T(8,128)(2,1)S(1)}, u32[]{:S(2)}, u32[]{:S(2)}) collective-permute-start(bf16[464,512]{1,0:T(8,128)(2,1)S(1)} %concatenate.21), channel_id=1, source_target_pairs={{0,2},{1,3},{2,0},{3,1},{4,6},{5,7},{6,4},{7,5},{8,10},{9,11},{10,... | collective-permute-start | bytes 1425416 | tf_op jit(solution)/shard_map/ppermute | solution.py:160
  221.0 22.3 %collective-permute-start.14 = (bf16[464,512]{1,0:T(8,128)(2,1)S(1)}, bf16[464,512]{1,0:T(8,128)(2,1)S(1)}, u32[]{:S(2)}, u32[]{:S(2)}) collective-permute-start(bf16[464,512]{1,0:T(8,128)(2,1)S(1)} %concatenate.21), channel_id=1, source_target_pairs={{0,3},{1,0},{2,1},{3,2},{4,7},{5,4},{6,5},{7,6},{8,11},{9,8},{10,9... | collective-permute-start | bytes 1425416 | tf_op jit(solution)/shard_map/ppermute | solution.py:160
  224.4 8.2 %collective-permute-start.11 = (f32[4,64,256]{2,1,0:T(8,128)S(1)}, f32[4,64,256]{2,1,0:T(8,128)S(1)}, u32[]{:S(2)}, u32[]{:S(2)}) collective-permute-start(f32[4,64,256]{2,1,0:T(8,128)S(1)} %get-tuple-element.92), channel_id=1, source_target_pairs={{0,8},{8,0},{16,24},{24,16},{32,40},{40,32},{48,56},{56,48},{1,9},... | collective-permute-start | bytes 786440 | tf_op jit(solution)/shard_map/ppermute | solution.py:226
  225.0 7.9 %collective-permute-start.13 = (f32[4,64,256]{2,1,0:T(8,128)S(1)}, f32[4,64,256]{2,1,0:T(8,128)S(1)}, u32[]{:S(2)}, u32[]{:S(2)}) collective-permute-start(f32[4,64,256]{2,1,0:T(8,128)S(1)} %get-tuple-element.93), channel_id=1, source_target_pairs={{8,16},{16,8},{24,32},{32,24},{40,48},{48,40},{0,56},{56,0},{9,17}... | collective-permute-start | bytes 786440 | tf_op jit(solution)/shard_map/ppermute | solution.py:227
  227.2 22.1 %copy-start.16 = (bf16[1024,512]{1,0:T(8,128)(2,1)S(1)}, bf16[1024,512]{1,0:T(8,128)(2,1)}, u32[]{:S(2)}) copy-start(bf16[1024,512]{1,0:T(8,128)(2,1)} %copy-done.15) | copy-start | bytes 3145732
  233.0 18.1 %collective-permute-start.16 = (f32[64,512]{1,0:T(8,128)S(1)}, f32[64,512]{1,0:T(8,128)S(1)}, u32[]{:S(2)}, u32[]{:S(2)}) collective-permute-start(f32[64,512]{1,0:T(8,128)S(1)} %get-tuple-element.89), channel_id=1, source_target_pairs={{0,32},{8,40},{16,48},{24,56},{32,0},{40,8},{48,16},{56,24},{1,33}... | collective-permute-start | bytes 393224 | tf_op jit(solution)/shard_map/ppermute | solution.py:160
  234.3 16.9 %collective-permute-start.17 = (f32[64,512]{1,0:T(8,128)S(1)}, f32[64,512]{1,0:T(8,128)S(1)}, u32[]{:S(2)}, u32[]{:S(2)}) collective-permute-start(f32[64,512]{1,0:T(8,128)S(1)} %get-tuple-element.90), channel_id=1, source_target_pairs={{0,48},{8,56},{16,0},{24,8},{32,16},{40,24},{48,32},{56,40},{1,49}... | collective-permute-start | bytes 393224 | tf_op jit(solution)/shard_map/ppermute | solution.py:160
  238.7 10.6 %collective-permute-start.15 = (f32[64,512]{1,0:T(8,128)S(1)}, f32[64,512]{1,0:T(8,128)S(1)}, u32[]{:S(2)}, u32[]{:S(2)}) collective-permute-start(f32[64,512]{1,0:T(8,128)S(1)} %get-tuple-element.91), channel_id=1, source_target_pairs={{0,16},{8,24},{16,32},{24,40},{32,48},{40,56},{48,0},{56,8},{1,17}... | collective-permute-start | bytes 393224 | tf_op jit(solution)/shard_map/ppermute | solution.py:160
  (18 other events, 110.7 us)

commit v15 on v14

--- a/solution.py
+++ b/solution.py
@@ -55,7 +55,7 @@
 
 
 def pick(ids, tiles):
-    count, slots = ids.shape[0], 64
+    count, slots = ids.shape[0], 128
     return pl.pallas_call(
         functools.partial(pick_kernel, slots=slots),
         grid_spec=pltpu.PrefetchScalarGridSpec(
@@ -106,7 +106,7 @@
 
 def attend(q, g, kv):
     rows, width = q.shape
-    count, together = rows // STRETCH, 2
+    count, together = rows // STRETCH, 4
     _, heads, tiles, neigh, _, _, _ = kv.shape
     block = pl.BlockSpec((together * STRETCH, width), lambda c: (c, 0))
     return pl.pallas_call(

time: 253 us -> 253 us (level)
  no operation moved by 1% of the time
where the time goes in v15:
time: 253 us; the launch traced here: 252 us
  waiting for transfers between devices  154 us (61%)
  starting transfers between devices  45.9 us (18%)
  local copies, waits for them, and re-layouts  17 us (7%)
  matrix products  15.6 us (6%)
  Pallas kernels  14.8 us (6%)
  other arithmetic  3.76 us (1%)
    ppermute x16, waiting for transfers between devices, step(): lax.ppermute(array, axis, [(i, (i + by) % size) for i in range(size)])  142 us
    ppermute x16, starting transfers between devices, step(): lax.ppermute(array, axis, [(i, (i + by) % size) for i in range(size)])  23 us
    all_to_all x1, starting transfers between devices, local(): held = lax.all_to_all(message, DP, split_axis=0, concat_axis=0, tiled=True)  11.6 us
    all_to_all x1, starting transfers between devices, local(): lax.all_to_all(send.reshape(ndp, requests, TILE, HEAD_DIM), DP, split_axi...  10.5 us
    unnamed x44, local copies, waits for them, and re-layouts  7.1 us
    all_to_all x1, waiting for transfers between devices, local(): lax.all_to_all(send.reshape(ndp, requests, TILE, HEAD_DIM), DP, split_axi...  5.99 us
    pallas_call x1, Pallas kernels, attend(): pl.pallas_call(functools.partial(attend_kernel, heads=heads), grid=(count...  5.84 us
    dot_general x1, matrix products, local(): q = shifted(jnp.dot(late, weights, preferred_element_type=F32).astype(BF16))  5.79 us
  transfers between devices with their start and end apart: 20, of which 10 were waited for; matrix products, arithmetic and copies ran while one was open for 10% of the time, Pallas kernels for 2%

profile of v15, /device:TPU:32, one launch (start us, length us, event | category | flops | bytes accessed | tf_op | source)
XLA Modules:
  0.0 251.9 jit_solution(385497162917064461)
XLA Ops:
  1.9 2.8 %cut.1 = bf16[2,4,8,9,16,128]{5,4,3,2,1,0:T(8,128)(2,1)} custom-call(bf16[16,128]{1,0:T(8,128)(2,1)} %add_convert_fusion.1.named_ref, bf16[8,2,128,512]{3,2,1,0:T(8,128)(2,1)} %cache_ref.1), custom_call_target="tpu_custom_call" | custom-call | bytes 4194304 | tf_op jit(solution)/shard_map/cut/pallas_call | solution.py:36
  4.8 11.6 %all-to-all-start = ((bf16[64,9,16,128]{3,2,1,0:T(8,128)(2,1)}), bf16[64,9,16,128]{3,2,1,0:T(8,128)(2,1)S(1)}, u32[]{:S(2)}, u32[]{:S(2)}) async-start(bf16[64,9,16,128]{3,2,1,0:T(8,128)(2,1)} %bitcast.62), calls=%async_computation | async-start | bytes 4718592 | tf_op jit(solution)/shard_map/all_to_all | solution.py:181
  16.4 3.4 %constant_dynamic-slice_fusion = (bf16[1024,512]{1,0:T(8,128)(2,1)S(1)}, bf16[1024,512]{1,0:T(8,128)(2,1)S(1)}, bf16[1024,512]{1,0:T(8,128)(2,1)S(1)}, bf16[1024,512]{1,0:T(8,128)(2,1)}) fusion(bf16[4096,512]{1,0:T(8,128)(2,1)} %param.7, s32[]{:T(128)S(6)} %select_n.115, s32[]{:T(128)S(6)} %select_n.113, s32[]{:T(128)S(6)} %select_n.111, s32[]{:T(128)S(6)} %select_n.109), kind=kLoop, calls=%fused_computation.26 | loop fusion | bytes 8388624 | tf_op jit(solution)/shard_map/dynamic_slice | solution.py:184
  19.8 3.0 %collective-permute-start.2 = (bf16[1024,512]{1,0:T(8,128)(2,1)S(1)}, bf16[1024,512]{1,0:T(8,128)(2,1)S(1)}, u32[]{:S(2)}, u32[]{:S(2)}) collective-permute-start(bf16[1024,512]{1,0:T(8,128)(2,1)S(1)} %get-tuple-element.85), channel_id=1, source_target_pairs={{0,3},{1,0},{2,1},{3,2},{4,7},{5,4},{6,5},{7,6},{8,11},{9,8},{10,9... | collective-permute-start | bytes 3145736 | tf_op jit(solution)/shard_map/ppermute | solution.py:160
  24.5 43.6 %collective-permute-done.2 = bf16[1024,512]{1,0:T(8,128)(2,1)S(1)} collective-permute-done((bf16[1024,512]{1,0:T(8,128)(2,1)S(1)}, bf16[1024,512]{1,0:T(8,128)(2,1)S(1)}, u32[]{:S(2)}, u32[]{:S(2)}) %collective-permute-start.2) | collective-permute-done | bytes 1048608 | tf_op jit(solution)/shard_map/ppermute | solution.py:160
  70.0 1.9 collective-permute-done
  73.9 2.0 copy-done
  75.9 10.5 %all-to-all-start.1 = ((bf16[64,16,16,128]{3,2,1,0:T(8,128)(2,1)}), bf16[64,16,16,128]{3,2,1,0:T(8,128)(2,1)}, u32[]{:S(2)}, u32[]{:S(2)}) async-start(bf16[64,16,16,128]{3,2,1,0:T(8,128)(2,1)} %bitcast.60), calls=%async_computation.1 | async-start | bytes 8388608 | tf_op jit(solution)/shard_map/all_to_all | solution.py:191
  86.5 3.8 %constant_dynamic-slice_fusion.4 = (bf16[464,1024]{1,0:T(8,128)(2,1)}, bf16[464,1024]{1,0:T(8,128)(2,1)}, bf16[464,1024]{1,0:T(8,128)(2,1)}, bf16[464,1024]{1,0:T(8,128)(2,1)S(1)}) fusion(bf16[512,4096]{1,0:T(8,128)(2,1)} %bitcast.65, s32[]{:T(128)S(6)} %select_n.123, s32[]{:T(128)S(6)} %select_n.121, s32[]{:T(128)S(6)} %select_n.119, s32[]{:T(128)S(6)} %select_n.117), kind=kLoop, calls=%fused_computation.30 | loop fusion | bytes 7602192 | tf_op jit(solution)/shard_map/dynamic_slice | solution.py:197
  90.3 2.9 %collective-permute-start.5 = (bf16[464,1024]{1,0:T(8,128)(2,1)}, bf16[464,1024]{1,0:T(8,128)(2,1)}, u32[]{:S(2)}, u32[]{:S(2)}) collective-permute-start(bf16[464,1024]{1,0:T(8,128)(2,1)} %get-tuple-element.81), channel_id=1, source_target_pairs={{0,192},{64,0},{128,64},{192,128},{1,193},{65,1},{129,65},{193,129... | collective-permute-start | bytes 2850824 | tf_op jit(solution)/shard_map/ppermute | solution.py:160
  94.9 5.8 %fusion.11 = bf16[512,512]{1,0:T(8,128)(2,1)S(1)} fusion(bf16[512,4096]{1,0:T(8,128)(2,1)} %bitcast.66, bf16[4096,512]{1,0:T(8,128)(2,1)} %param.7), kind=kOutput, calls=%fused_computation.43 | convolution fusion | flops 2147483648 | bytes 8912896 | tf_op jit(solution)/shard_map/dot_general | solution.py:203
  102.2 35.6 %collective-permute-done.5.share_ref = bf16[464,1024]{1,0:T(8,128)(2,1)} collective-permute-done((bf16[464,1024]{1,0:T(8,128)(2,1)}, bf16[464,1024]{1,0:T(8,128)(2,1)}, u32[]{:S(2)}, u32[]{:S(2)}) %collective-permute-start.5) | collective-permute-done | bytes 950304 | tf_op jit(solution)/shard_map/ppermute | solution.py:160
  141.9 30.5 %collective-permute-done.3.share_ref = bf16[464,1024]{1,0:T(8,128)(2,1)S(1)} collective-permute-done((bf16[464,1024]{1,0:T(8,128)(2,1)}, bf16[464,1024]{1,0:T(8,128)(2,1)S(1)}, u32[]{:S(2)}, u32[]{:S(2)}) %collective-permute-start.3) | collective-permute-done | bytes 950304 | tf_op jit(solution)/shard_map/ppermute | solution.py:160
  174.5 6.0 %all-to-all-done.1 = bf16[64,16,16,128]{3,2,1,0:T(8,128)(2,1)} async-done(((bf16[64,16,16,128]{3,2,1,0:T(8,128)(2,1)}), bf16[64,16,16,128]{3,2,1,0:T(8,128)(2,1)}, u32[]{:S(2)}, u32[]{:S(2)}) %all-to-all-start.1) | async-done | bytes 4194336 | tf_op jit(solution)/shard_map/all_to_all | solution.py:191
  180.5 5.8 %attend.1 = (bf16[512,512]{1,0:T(8,128)(2,1)S(1)}, bf16[512,512]{1,0:T(8,128)(2,1)S(1)}) custom-call(bf16[512,512]{1,0:T(8,128)(2,1)S(1)} %concatenate.18.q_ref, bf16[512,512]{1,0:T(8,128)(2,1)S(1)} %concatenate.19.g_ref, bf16[2,4,8,2,8,16,128]{6,5,4,3,2,1,0:T(8,128)(2,1)} %bitcast.12.kv_ref), custom_call_target="tpu_custom_call" | custom-call | flops 671088640 | bytes 4194304 | tf_op jit(solution)/shard_map/attend/pallas_call | solution.py:112
  186.7 2.9 %collective-permute-start.8 = (bf16[464,512]{1,0:T(8,128)(2,1)S(1)}, bf16[464,512]{1,0:T(8,128)(2,1)S(1)}, u32[]{:S(2)}, u32[]{:S(2)}) collective-permute-start(bf16[464,512]{1,0:T(8,128)(2,1)S(1)} %concatenate.21), channel_id=1, source_target_pairs={{0,192},{64,0},{128,64},{192,128},{1,193},{65,1},{129,65},{193,129... | collective-permute-start | bytes 1425416 | tf_op jit(solution)/shard_map/ppermute | solution.py:160
  189.5 2.2 collective-permute-start.6
  194.4 20.0 %collective-permute-done.7 = bf16[464,512]{1,0:T(8,128)(2,1)S(1)} collective-permute-done((bf16[464,512]{1,0:T(8,128)(2,1)S(1)}, bf16[464,512]{1,0:T(8,128)(2,1)S(1)}, u32[]{:S(2)}, u32[]{:S(2)}) %collective-permute-start.7) | collective-permute-done | bytes 475168 | tf_op jit(solution)/shard_map/ppermute | solution.py:160
  217.9 2.9 %collective-permute-start.12 = (bf16[464,512]{1,0:T(8,128)(2,1)S(1)}, bf16[464,512]{1,0:T(8,128)(2,1)S(1)}, u32[]{:S(2)}, u32[]{:S(2)}) collective-permute-start(bf16[464,512]{1,0:T(8,128)(2,1)S(1)} %concatenate.21), channel_id=1, source_target_pairs={{0,2},{1,3},{2,0},{3,1},{4,6},{5,7},{6,4},{7,5},{8,10},{9,11},{10,... | collective-permute-start | bytes 1425416 | tf_op jit(solution)/shard_map/ppermute | solution.py:160
  224.8 2.0 convolution_convert_fusion.2
  226.8 5.6 %collective-permute-done.11 = f32[4,64,256]{2,1,0:T(8,128)S(1)} collective-permute-done((f32[4,64,256]{2,1,0:T(8,128)S(1)}, f32[4,64,256]{2,1,0:T(8,128)S(1)}, u32[]{:S(2)}, u32[]{:S(2)}) %collective-permute-start.11) | collective-permute-done | bytes 262176 | tf_op jit(solution)/shard_map/ppermute | solution.py:226
  234.1 4.5 %collective-permute-start.17 = (f32[64,512]{1,0:T(8,128)S(1)}, f32[64,512]{1,0:T(8,128)S(1)}, u32[]{:S(2)}, u32[]{:S(2)}) collective-permute-start(f32[64,512]{1,0:T(8,128)S(1)} %get-tuple-element.90), channel_id=1, source_target_pairs={{0,48},{8,56},{16,0},{24,8},{32,16},{40,24},{48,32},{56,40},{1,49}... | collective-permute-start | bytes 393224 | tf_op jit(solution)/shard_map/ppermute | solution.py:160
  239.2 3.8 %collective-permute-done.14 = bf16[464,512]{1,0:T(8,128)(2,1)S(1)} collective-permute-done((bf16[464,512]{1,0:T(8,128)(2,1)S(1)}, bf16[464,512]{1,0:T(8,128)(2,1)S(1)}, u32[]{:S(2)}, u32[]{:S(2)}) %collective-permute-start.14) | collective-permute-done | bytes 475168 | tf_op jit(solution)/shard_map/ppermute | solution.py:160
  243.1 6.3 %collective-permute-done.15 = f32[64,512]{1,0:T(8,128)S(1)} collective-permute-done((f32[64,512]{1,0:T(8,128)S(1)}, f32[64,512]{1,0:T(8,128)S(1)}, u32[]{:S(2)}, u32[]{:S(2)}) %collective-permute-start.15) | collective-permute-done | bytes 131104 | tf_op jit(solution)/shard_map/ppermute | solution.py:160
  (101 shorter events, 31.1 us)
Async XLA Ops:
  4.8 67.1 %all-to-all-start = ((bf16[64,9,16,128]{3,2,1,0:T(8,128)(2,1)}), bf16[64,9,16,128]{3,2,1,0:T(8,128)(2,1)S(1)}, u32[]{:S(2)}, u32[]{:S(2)}) async-start(bf16[64,9,16,128]{3,2,1,0:T(8,128)(2,1)} %bitcast.62), calls=%async_computation | async-start | bytes 4718592 | tf_op jit(solution)/shard_map/all_to_all | solution.py:181
  19.8 48.2 %collective-permute-start.2 = (bf16[1024,512]{1,0:T(8,128)(2,1)S(1)}, bf16[1024,512]{1,0:T(8,128)(2,1)S(1)}, u32[]{:S(2)}, u32[]{:S(2)}) collective-permute-start(bf16[1024,512]{1,0:T(8,128)(2,1)S(1)} %get-tuple-element.85), channel_id=1, source_target_pairs={{0,3},{1,0},{2,1},{3,2},{4,7},{5,4},{6,5},{7,6},{8,11},{9,8},{10,9... | collective-permute-start | bytes 3145736 | tf_op jit(solution)/shard_map/ppermute | solution.py:160
  22.8 45.2 %collective-permute-start.1 = (bf16[1024,512]{1,0:T(8,128)(2,1)S(1)}, bf16[1024,512]{1,0:T(8,128)(2,1)S(1)}, u32[]{:S(2)}, u32[]{:S(2)}) collective-permute-start(bf16[1024,512]{1,0:T(8,128)(2,1)S(1)} %get-tuple-element.86), channel_id=1, source_target_pairs={{0,2},{1,3},{2,0},{3,1},{4,6},{5,7},{6,4},{7,5},{8,10},{9,11},{10,... | collective-permute-start | bytes 3145736 | tf_op jit(solution)/shard_map/ppermute | solution.py:160
  23.5 48.4 %collective-permute-start = (bf16[1024,512]{1,0:T(8,128)(2,1)S(1)}, bf16[1024,512]{1,0:T(8,128)(2,1)}, u32[]{:S(2)}, u32[]{:S(2)}) collective-permute-start(bf16[1024,512]{1,0:T(8,128)(2,1)S(1)} %get-tuple-element.87), channel_id=1, source_target_pairs={{0,1},{1,2},{2,3},{3,0},{4,5},{5,6},{6,7},{7,4},{8,9},{9,10},{10,1... | collective-permute-start | bytes 3145736 | tf_op jit(solution)/shard_map/ppermute | solution.py:160
  75.9 104.6 %all-to-all-start.1 = ((bf16[64,16,16,128]{3,2,1,0:T(8,128)(2,1)}), bf16[64,16,16,128]{3,2,1,0:T(8,128)(2,1)}, u32[]{:S(2)}, u32[]{:S(2)}) async-start(bf16[64,16,16,128]{3,2,1,0:T(8,128)(2,1)} %bitcast.60), calls=%async_computation.1 | async-start | bytes 8388608 | tf_op jit(solution)/shard_map/all_to_all | solution.py:191
  90.3 47.5 %collective-permute-start.5 = (bf16[464,1024]{1,0:T(8,128)(2,1)}, bf16[464,1024]{1,0:T(8,128)(2,1)}, u32[]{:S(2)}, u32[]{:S(2)}) collective-permute-start(bf16[464,1024]{1,0:T(8,128)(2,1)} %get-tuple-element.81), channel_id=1, source_target_pairs={{0,192},{64,0},{128,64},{192,128},{1,193},{65,1},{129,65},{193,129... | collective-permute-start | bytes 2850824 | tf_op jit(solution)/shard_map/ppermute | solution.py:160
  93.2 47.1 %collective-permute-start.4 = (bf16[464,1024]{1,0:T(8,128)(2,1)}, bf16[464,1024]{1,0:T(8,128)(2,1)}, u32[]{:S(2)}, u32[]{:S(2)}) collective-permute-start(bf16[464,1024]{1,0:T(8,128)(2,1)} %get-tuple-element.82), channel_id=1, source_target_pairs={{0,128},{64,192},{128,0},{192,64},{1,129},{65,193},{129,1},{193,65... | collective-permute-start | bytes 2850824 | tf_op jit(solution)/shard_map/ppermute | solution.py:160
  93.8 78.6 %collective-permute-start.3 = (bf16[464,1024]{1,0:T(8,128)(2,1)}, bf16[464,1024]{1,0:T(8,128)(2,1)S(1)}, u32[]{:S(2)}, u32[]{:S(2)}) collective-permute-start(bf16[464,1024]{1,0:T(8,128)(2,1)} %get-tuple-element.83), channel_id=1, source_target_pairs={{0,64},{64,128},{128,192},{192,0},{1,65},{65,129},{129,193},{193,1... | collective-permute-start | bytes 2850824 | tf_op jit(solution)/shard_map/ppermute | solution.py:160
  102.2 38.1 %copy-start.3 = (bf16[464,512]{1,0:T(8,128)(2,1)}, bf16[464,512]{1,0:T(8,128)(2,1)S(1)}, u32[]{:S(2)}) copy-start(bf16[464,512]{1,0:T(8,128)(2,1)S(1)} %get-tuple-element.64) | copy-start | bytes 1425412
  186.6 29.8 %collective-permute-start.9 = (bf16[464,512]{1,0:T(8,128)(2,1)S(1)}, bf16[464,512]{1,0:T(8,128)(2,1)S(1)}, u32[]{:S(2)}, u32[]{:S(2)}) collective-permute-start(bf16[464,512]{1,0:T(8,128)(2,1)S(1)} %concatenate.21), channel_id=1, source_target_pairs={{0,1},{1,2},{2,3},{3,0},{4,5},{5,6},{6,7},{7,4},{8,9},{9,10},{10,1... | collective-permute-start | bytes 1425416 | tf_op jit(solution)/shard_map/ppermute | solution.py:160
  186.7 28.7 %collective-permute-start.8 = (bf16[464,512]{1,0:T(8,128)(2,1)S(1)}, bf16[464,512]{1,0:T(8,128)(2,1)S(1)}, u32[]{:S(2)}, u32[]{:S(2)}) collective-permute-start(bf16[464,512]{1,0:T(8,128)(2,1)S(1)} %concatenate.21), channel_id=1, source_target_pairs={{0,192},{64,0},{128,64},{192,128},{1,193},{65,1},{129,65},{193,129... | collective-permute-start | bytes 1425416 | tf_op jit(solution)/shard_map/ppermute | solution.py:160
  189.5 24.9 %collective-permute-start.7 = (bf16[464,512]{1,0:T(8,128)(2,1)S(1)}, bf16[464,512]{1,0:T(8,128)(2,1)S(1)}, u32[]{:S(2)}, u32[]{:S(2)}) collective-permute-start(bf16[464,512]{1,0:T(8,128)(2,1)S(1)} %concatenate.21), channel_id=1, source_target_pairs={{0,64},{64,128},{128,192},{192,0},{1,65},{65,129},{129,193},{193,1... | collective-permute-start | bytes 1425416 | tf_op jit(solution)/shard_map/ppermute | solution.py:160
  189.5 26.9 %collective-permute-start.6 = (bf16[464,512]{1,0:T(8,128)(2,1)S(1)}, bf16[464,512]{1,0:T(8,128)(2,1)S(1)}, u32[]{:S(2)}, u32[]{:S(2)}) collective-permute-start(bf16[464,512]{1,0:T(8,128)(2,1)S(1)} %concatenate.21), channel_id=1, source_target_pairs={{0,128},{64,192},{128,0},{192,64},{1,129},{65,193},{129,1},{193,65... | collective-permute-start | bytes 1425416 | tf_op jit(solution)/shard_map/ppermute | solution.py:160
  192.2 22.2 %copy-start.10 = (bf16[464,512]{1,0:T(8,128)(2,1)S(1)}, bf16[464,512]{1,0:T(8,128)(2,1)}, u32[]{:S(2)}) copy-start(bf16[464,512]{1,0:T(8,128)(2,1)} %copy-done.9) | copy-start | bytes 1425412
  217.9 4.4 %collective-permute-start.10 = (f32[512,512]{1,0:T(8,128)}, f32[512,512]{1,0:T(8,128)}, u32[]{:S(2)}, u32[]{:S(2)}) collective-permute-start(f32[512,512]{1,0:T(8,128)} %convolution_add_fusion), channel_id=1, source_target_pairs={{0,4},{4,0},{1,5},{5,1},{2,6},{6,2},{3,7},{7,3},{8,12},{12,8},{9,1... | collective-permute-start | bytes 3145736 | tf_op jit(solution)/shard_map/ppermute | solution.py:160
  217.9 14.9 %collective-permute-start.12 = (bf16[464,512]{1,0:T(8,128)(2,1)S(1)}, bf16[464,512]{1,0:T(8,128)(2,1)S(1)}, u32[]{:S(2)}, u32[]{:S(2)}) collective-permute-start(bf16[464,512]{1,0:T(8,128)(2,1)S(1)} %concatenate.21), channel_id=1, source_target_pairs={{0,2},{1,3},{2,0},{3,1},{4,6},{5,7},{6,4},{7,5},{8,10},{9,11},{10,... | collective-permute-start | bytes 1425416 | tf_op jit(solution)/shard_map/ppermute | solution.py:160
  220.8 22.3 %collective-permute-start.14 = (bf16[464,512]{1,0:T(8,128)(2,1)S(1)}, bf16[464,512]{1,0:T(8,128)(2,1)S(1)}, u32[]{:S(2)}, u32[]{:S(2)}) collective-permute-start(bf16[464,512]{1,0:T(8,128)(2,1)S(1)} %concatenate.21), channel_id=1, source_target_pairs={{0,3},{1,0},{2,1},{3,2},{4,7},{5,4},{6,5},{7,6},{8,11},{9,8},{10,9... | collective-permute-start | bytes 1425416 | tf_op jit(solution)/shard_map/ppermute | solution.py:160
  224.0 8.5 %collective-permute-start.11 = (f32[4,64,256]{2,1,0:T(8,128)S(1)}, f32[4,64,256]{2,1,0:T(8,128)S(1)}, u32[]{:S(2)}, u32[]{:S(2)}) collective-permute-start(f32[4,64,256]{2,1,0:T(8,128)S(1)} %get-tuple-element.92), channel_id=1, source_target_pairs={{0,8},{8,0},{16,24},{24,16},{32,40},{40,32},{48,56},{56,48},{1,9},... | collective-permute-start | bytes 786440 | tf_op jit(solution)/shard_map/ppermute | solution.py:226
  224.8 7.9 %collective-permute-start.13 = (f32[4,64,256]{2,1,0:T(8,128)S(1)}, f32[4,64,256]{2,1,0:T(8,128)S(1)}, u32[]{:S(2)}, u32[]{:S(2)}) collective-permute-start(f32[4,64,256]{2,1,0:T(8,128)S(1)} %get-tuple-element.93), channel_id=1, source_target_pairs={{8,16},{16,8},{24,32},{32,24},{40,48},{48,40},{0,56},{56,0},{9,17}... | collective-permute-start | bytes 786440 | tf_op jit(solution)/shard_map/ppermute | solution.py:227
  226.8 22.6 %copy-start.16 = (bf16[1024,512]{1,0:T(8,128)(2,1)S(1)}, bf16[1024,512]{1,0:T(8,128)(2,1)}, u32[]{:S(2)}) copy-start(bf16[1024,512]{1,0:T(8,128)(2,1)} %copy-done.15) | copy-start | bytes 3145732
  226.8 22.6 %copy-start.21 = (bf16[464,1024]{1,0:T(8,128)(2,1)S(1)}, bf16[464,1024]{1,0:T(8,128)(2,1)}, u32[]{:S(2)}) copy-start(bf16[464,1024]{1,0:T(8,128)(2,1)} %convolution_convert_fusion.3) | copy-start | bytes 2850820
  232.8 18.4 %collective-permute-start.16 = (f32[64,512]{1,0:T(8,128)S(1)}, f32[64,512]{1,0:T(8,128)S(1)}, u32[]{:S(2)}, u32[]{:S(2)}) collective-permute-start(f32[64,512]{1,0:T(8,128)S(1)} %get-tuple-element.89), channel_id=1, source_target_pairs={{0,32},{8,40},{16,48},{24,56},{32,0},{40,8},{48,16},{56,24},{1,33}... | collective-permute-start | bytes 393224 | tf_op jit(solution)/shard_map/ppermute | solution.py:160
  234.1 17.2 %collective-permute-start.17 = (f32[64,512]{1,0:T(8,128)S(1)}, f32[64,512]{1,0:T(8,128)S(1)}, u32[]{:S(2)}, u32[]{:S(2)}) collective-permute-start(f32[64,512]{1,0:T(8,128)S(1)} %get-tuple-element.90), channel_id=1, source_target_pairs={{0,48},{8,56},{16,0},{24,8},{32,16},{40,24},{48,32},{56,40},{1,49}... | collective-permute-start | bytes 393224 | tf_op jit(solution)/shard_map/ppermute | solution.py:160
  238.5 10.9 %collective-permute-start.15 = (f32[64,512]{1,0:T(8,128)S(1)}, f32[64,512]{1,0:T(8,128)S(1)}, u32[]{:S(2)}, u32[]{:S(2)}) collective-permute-start(f32[64,512]{1,0:T(8,128)S(1)} %get-tuple-element.91), channel_id=1, source_target_pairs={{0,16},{8,24},{16,32},{24,40},{32,48},{40,56},{48,0},{56,8},{1,17}... | collective-permute-start | bytes 393224 | tf_op jit(solution)/shard_map/ppermute | solution.py:160
  (18 other events, 110.5 us)
